TPU v7x, 32 devices: a whole 2x2x4 slice. The times are simulated.
32 devices in a mesh: member: 2 (over y), frow: 4 (over x, core), fcol: 4 (over z).
Axes of the slice: x: 2, y: 2, z: 4, core: 2. Of those that a mesh axis runs over, the one named last changes fastest.
Arguments:
- latlon_cot: float32 [3, 16, 65536], P(None, None, ('member', 'frow', 'fcol')), parts along dimension 2, may hold values from -6 to 6
- dest_tile: int32 [32768, 1], P(('frow', 'fcol')), may hold values from 0 to 15; in each aligned block of 2048 rows (0 to 2047, 2048 to 4095, ...) at most 256 rows name the same one
- base_cell: int32 [32768], P(('frow', 'fcol')), may hold values from 0 to 888
- corner_frac: float32 [2, 32768], P(None, ('frow', 'fcol')), may hold values from 0 to 1
- saved_states: float32 [2, 2, 3, 16, 64, 512], P(None, None, None, None, ('member', 'frow'), 'fcol'), parts along dimension 4, may hold values from -1.2 to 1.7, as said below
- gravity: float32 [16], replicated, may hold values from 0.5 to 4
Outputs:
- sensitivity: float32 [3, 16, 64, 512], P(None, None, ('member', 'frow'), 'fcol'), parts along dimension 2
There are 2 independent parts, one for each index of `member`. A program takes and returns all parts, laid end to end along the dimension named above; an argument that names none is the same for every part. Nothing has to cross between parts.
Inputs may be any that keep to these rules, and one draw needn't show every extreme that they name: `dest_tile`: the tile index is frow index times 4 plus fcol index; of the points of one tile's block at most 256 name one tile, and in every draw some tile is named that often. `base_cell`: the cell r * 127 + c for tile row r and tile column c; the other three corners are one row and one column further, inside the same tile. saved_states[n, k] is the state entering section k of step n; the height field lies in 0.3 to 1.7 and the winds in -1.2 to 1.2.
All inputs are finite; a program needn't handle non-finite values.
Results may differ from a plain program's by a relative error of at most 0.0003.
Values sent between devices are 32-bit elements; how exact they have to be, the bound alone decides.
No kernel may reach another device: no remote copies, remote signals or barrier semaphores. Data moves between devices by JAX's collectives and lax.ppermute only.
A program may use at most 64 MiB of HBM per device.

v0:
```python
import math

import jax
import jax.numpy as jnp
from jax import lax
from jax.sharding import PartitionSpec as P

time_step = 0.25
coriolis_peak = 0.8


def extended(block, sides, width):
    for axis, dim in sides:
        count = lax.axis_size(axis)
        forward = [(i, i + 1) for i in range(count - 1)]
        forward.append((count - 1, 0))
        backward = [(target, source) for source, target in forward]
        low = lax.ppermute(
            lax.slice_in_dim(block, block.shape[dim] - width, None, axis=dim), axis, forward
        )
        high = lax.ppermute(lax.slice_in_dim(block, 0, width, axis=dim), axis, backward)
        block = jnp.concatenate([low, block, high], axis=dim)
    return block


def coriolis(grid_rows, total_rows):
    return coriolis_peak * (2.0 * (grid_rows + 0.5) / total_rows - 1.0)


def along_x(values):
    return 0.5 * (values[:, 1:-1, 2:] - values[:, 1:-1, :-2])


def along_y(values):
    return 0.5 * (values[:, 2:, 1:-1] - values[:, :-2, 1:-1])


def centre(values):
    return values[:, 1:-1, 1:-1]


def tendency(current, gravity, rotation):
    height, east_wind, north_wind = (current[0], current[1], current[2])
    gravity_col = gravity[:, None, None]
    east_mid = centre(east_wind)
    north_mid = centre(north_wind)
    height_rate = -(along_x(height * east_wind) + along_y(height * north_wind))
    east_rate = (
        -gravity_col * along_x(height)
        - east_mid * along_x(east_wind)
        - north_mid * along_y(east_wind)
        + rotation * north_mid
    )
    north_rate = (
        -gravity_col * along_y(height)
        - east_mid * along_x(north_wind)
        - north_mid * along_y(north_wind)
        - rotation * east_mid
    )
    return jnp.stack([height_rate, east_rate, north_rate])


def corner_weights(along_rows, along_cols):
    return (
        (0, 0, (1.0 - along_rows) * (1.0 - along_cols)),
        (0, 1, (1.0 - along_rows) * along_cols),
        (1, 0, along_rows * (1.0 - along_cols)),
        (1, 1, along_rows * along_cols),
    )


def per_device(latlon_cot, dest_tile, base_cell, corner_frac, saved_states, gravity):
    n_row = lax.axis_size("frow")
    n_col = lax.axis_size("fcol")
    tile_count = n_row * n_col
    levels = gravity.shape[0]
    tile_rows = saved_states.shape[4]
    columns = saved_states.shape[5]
    channels = 3 * levels
    points = base_cell.shape[0]
    capacity = 2 * points // tile_count
    target = dest_tile[:, 0]
    block_rows = math.gcd(points, 512)
    lower_ones = (jnp.arange(block_rows)[:, None] > jnp.arange(block_rows)[None, :]).astype(
        jnp.bfloat16
    )

    def rank_block(counts, target_block):
        onehot = (target_block[:, None] == jnp.arange(tile_count)[None, :]).astype(jnp.bfloat16)
        before = jnp.dot(lower_ones, onehot, preferred_element_type=jnp.float32)
        onehot_wide = onehot.astype(jnp.float32)
        ranked = jnp.sum((before + counts[None, :]) * onehot_wide, axis=1)
        return (counts + jnp.sum(onehot_wide, axis=0), ranked)

    _, ranked = lax.scan(
        rank_block, jnp.zeros((tile_count,), jnp.float32), target.reshape(-1, block_rows)
    )
    position = target * capacity + ranked.reshape(-1).astype(jnp.int32)
    slot_total = tile_count * capacity
    send_values = (
        jnp.zeros((channels, slot_total), jnp.float32)
        .at[:, position]
        .set(latlon_cot.reshape(channels, points))
        .reshape(channels, tile_count, capacity)
    )
    send_frac = (
        jnp.zeros((2, slot_total), jnp.float32)
        .at[:, position]
        .set(corner_frac)
        .reshape(2, tile_count, capacity)
    )
    send_base = (
        jnp.zeros((1, slot_total), jnp.int32)
        .at[:, position]
        .set(base_cell[None, :])
        .reshape(1, tile_count, capacity)
    )
    got_values, got_frac, got_base = (
        lax.all_to_all(send_values, ("frow", "fcol"), split_axis=1, concat_axis=1, tiled=True),
        lax.all_to_all(send_frac, ("frow", "fcol"), split_axis=1, concat_axis=1, tiled=True),
        lax.all_to_all(send_base, ("frow", "fcol"), split_axis=1, concat_axis=1, tiled=True),
    )
    flat_values = got_values.reshape(channels, -1)
    corner = got_base.reshape(-1)
    anchor = corner // (columns - 1) * columns + corner % (columns - 1)
    canvas = jnp.zeros((channels, tile_rows * columns), jnp.float32)
    for row_step, col_step, weight in corner_weights(
        got_frac[0].reshape(-1), got_frac[1].reshape(-1)
    ):
        canvas = canvas.at[:, anchor + row_step * columns + col_step].add(
            flat_values * weight[None, :]
        )
    adjoint = canvas.reshape(3, levels, tile_rows, columns)
    base_row = lax.axis_index("frow") * tile_rows
    total_rows = tile_rows * n_row

    def row_mask(width):
        global_rows = base_row - width + jnp.arange(tile_rows + 2 * width)
        return ((global_rows >= 0) & (global_rows < total_rows)).astype(jnp.float32)[:, None]

    def pull_back(state_ext, adjoint_ext, width):
        out_rows = (base_row - width + jnp.arange(tile_rows + 2 * width)).astype(jnp.float32)
        rotation = coriolis(out_rows, total_rows)[:, None]
        _, pullback = jax.vjp(lambda current: tendency(current, gravity, rotation), state_ext)
        return pullback(adjoint_ext)[0][:, :, 2:-2, 2:-2]

    saved_ext = extended(saved_states, (("frow", 4), ("fcol", 5)), 2) * row_mask(2)

    def rim_one(values):
        return extended(values, (("frow", 2), ("fcol", 3)), 1) * row_mask(1)

    for which_step in (1, 0):
        middle = 0.5 * adjoint + 0.5 * time_step * pull_back(
            saved_ext[which_step, 1], rim_one(adjoint), 1
        )
        adjoint = (
            0.5 * adjoint
            + middle
            + time_step * pull_back(saved_ext[which_step, 0], rim_one(middle), 1)
        )
    return adjoint


def solution(mesh):
    placed = (
        P(None, None, ("member", "frow", "fcol")),
        P(("frow", "fcol"), None),
        P(("frow", "fcol")),
        P(None, ("frow", "fcol")),
        P(None, None, None, None, ("member", "frow"), "fcol"),
        P(),
    )
    return jax.shard_map(
        per_device,
        mesh=mesh,
        in_specs=placed,
        out_specs=P(None, None, ("member", "frow"), "fcol"),
        check_vma=False,
    )
```

profile of v0, /device:TPU:0, one launch (start us, length us, event | category | flops | bytes accessed | tf_op | source)
XLA Modules:
  0.0 325.4 jit_solution(3295347900530901524)
XLA Ops:
  1.9 1.9 while.13
  4.6 8.8 %scatter_custom_fusion = s32[4096]{0:T(1024)} fusion(s32[2048]{0:T(1024)S(1)} %bitcast.321, s32[2048]{0:T(1024)} %param.10, s32[]{:T(128)} %constant.34.clone.1), kind=kCustom, calls=%fused_computation.217 | custom fusion | bytes 16896 | tf_op jit(solution)/shard_map/scatter | solution.py:115
  13.4 7.4 %all-to-all-start = ((s32[1,16,256]{2,0,1:T(1,128)}), s32[1,16,256]{2,0,1:T(1,128)S(1)}, u32[]{:S(2)}, u32[]{:S(2)}) async-start(s32[1,16,256]{2,0,1:T(1,128)} %bitcast.1), calls=%async_computation | async-start | bytes 32768 | tf_op jit(solution)/shard_map/all_to_all | solution.py:121
  20.8 2.3 fusion.122
  26.8 6.2 %scatter_custom_fusion.2 = f32[2,4096]{0,1:T(8,128)S(1)} fusion(s32[2048]{0:T(1024)} %bitcast.322, f32[2048,2]{1,0:T(8,128)S(1)} %copy.29, f32[]{:T(128)} %constant.33.clone.1), kind=kCustom, calls=%fused_computation.24 | custom fusion | bytes 33280 | tf_op jit(solution)/shard_map/scatter | solution.py:109
  35.6 6.3 %scatter_custom_fusion.1 = f32[48,4096]{0,1:T(8,128)S(1)} fusion(s32[2048]{0:T(1024)} %bitcast.323, f32[48,2048]{0,1:T(8,128)S(1)} %copy.26, f32[]{:T(128)} %constant.33.clone.1), kind=kCustom, calls=%fused_computation.22 | custom fusion | bytes 1180160 | tf_op jit(solution)/shard_map/scatter | solution.py:103
  41.9 1.5 copy.27
  43.9 6.0 %all-to-all-start.2 = ((f32[2,16,256]{2,0,1:T(2,128)}), f32[2,16,256]{2,0,1:T(2,128)S(1)}, u32[]{:S(2)}, u32[]{:S(2)}) async-start(f32[2,16,256]{2,0,1:T(2,128)} %copy.30), calls=%async_computation.2 | async-start | bytes 65536 | tf_op jit(solution)/shard_map/all_to_all | solution.py:120
  50.2 6.3 %all-to-all-done.2 = f32[2,16,256]{2,0,1:T(2,128)S(1)} async-done(((f32[2,16,256]{2,0,1:T(2,128)}), f32[2,16,256]{2,0,1:T(2,128)S(1)}, u32[]{:S(2)}, u32[]{:S(2)}) %all-to-all-start.2) | async-done | bytes 32800 | tf_op jit(solution)/shard_map/all_to_all | solution.py:120
  56.5 4.3 %all-to-all-start.1 = ((f32[48,16,256]{2,0,1:T(8,128)}), f32[48,16,256]{2,0,1:T(8,128)}, u32[]{:S(2)}, u32[]{:S(2)}) async-start(f32[48,16,256]{2,0,1:T(8,128)} %copy.27), calls=%async_computation.1 | async-start | bytes 1572864 | tf_op jit(solution)/shard_map/all_to_all | solution.py:119
  62.9 1.6 copy.36
  64.5 1.8 collective-permute-start.2
  67.2 2.6 collective-permute-start.3
  71.1 10.7 %collective-permute-done.2 = f32[2,2,3,16,12,2]{3,5,4,2,1,0:T(2,128)S(1)} collective-permute-done((f32[2,2,3,16,12,2]{3,5,4,2,1,0:T(2,128)}, f32[2,2,3,16,12,2]{3,5,4,2,1,0:T(2,128)S(1)}, u32[]{:S(2)}, u32[]{:S(2)}) %collective-permute-start.2) | collective-permute-done | bytes 18464 | tf_op jit(solution)/shard_map/ppermute | solution.py:18
  82.8 2.1 copy.39
  86.5 2.3 multiply_bitcast_fusion
  88.8 3.1 copy.31
  91.9 3.1 copy.32
  95.0 2.0 copy.33
  97.0 2.0 copy.34
  99.0 25.9 %scatter_custom_fusion.3 = f32[48,1024]{0,1:T(8,128)S(1)} fusion(s32[4096]{0:T(1024)} %bitcast.320, f32[4096,48]{1,0:T(8,128)} %copy.31, f32[]{:T(128)} %constant.33.clone.1), kind=kCustom, calls=%fused_computation.179 | custom fusion | flops 196608 | bytes 197120 | tf_op jit(solution)/shard_map/scatter-add | solution.py:130
  125.0 26.0 %scatter_fusion = f32[48,1024]{0,1:T(8,128)S(1)} fusion(f32[48,1024]{0,1:T(8,128)S(1)} %scatter_custom_fusion.3, s32[4096]{0:T(1024)S(1)} %bitcast.311, f32[4096,48]{1,0:T(8,128)} %copy.32), kind=kCustom, calls=%fused_computation.4 | custom fusion | flops 196608 | bytes 2375680 | tf_op jit(solution)/shard_map/scatter-add | solution.py:130
  151.0 26.0 %scatter_fusion.1 = f32[48,1024]{0,1:T(8,128)S(1)} fusion(f32[48,1024]{0,1:T(8,128)S(1)} %scatter_fusion, s32[4096]{0:T(1024)S(1)} %bitcast.310, f32[4096,48]{1,0:T(8,128)} %copy.33), kind=kCustom, calls=%fused_computation.5 | custom fusion | flops 196608 | bytes 2375680 | tf_op jit(solution)/shard_map/scatter-add | solution.py:130
  177.1 26.1 %scatter_fusion.2 = f32[48,1024]{0,1:T(8,128)S(1)} fusion(f32[48,1024]{0,1:T(8,128)S(1)} %scatter_fusion.1, s32[4096]{0:T(1024)S(1)} %bitcast.309, f32[4096,48]{1,0:T(8,128)} %copy.34), kind=kCustom, calls=%fused_computation.6 | custom fusion | flops 196608 | bytes 2375680 | tf_op jit(solution)/shard_map/scatter-add | solution.py:130
  203.5 3.9 %collective-permute-start.4 = (f32[3,16,1,128]{3,2,1,0:T(1,128)S(1)}, f32[3,16,1,128]{3,2,1,0:T(1,128)S(1)}, u32[]{:S(2)}, u32[]{:S(2)}) collective-permute-start(f32[3,16,1,128]{3,2,1,0:T(1,128)S(1)} %get-tuple-element.208), channel_id=1, source_target_pairs={{0,4},{4,8},{8,12},{12,0},{1,5},{5,9},{9,13},{13,1},{2,6},{6,10},{... | collective-permute-start | bytes 73736 | tf_op jit(solution)/shard_map/ppermute | solution.py:18
  207.4 2.9 collective-permute-start.5
  210.3 3.5 %maximum_multiply_fusion = f32[2,2,3,16,12,132]{5,4,3,2,1,0:T(8,128)S(1)} fusion(f32[2,2,3,16,12,2]{5,4,3,2,1,0:T(8,128)} %copy.39, f32[2,2,3,16,2,128]{5,4,3,2,1,0:T(2,128)S(1)} %collective-permute-done.1, f32[2,2,3,16,8,128]{5,4,3,2,1,0:T(8,128)S(1)} %copy-done.1, f32[2,2,3,16,2,128]{5,4,3,2,1,0:T(2,128)S(1)} %collective-permute-done, ...), kind=kLoop, calls=%fused_computation.20 | loop fusion | flops 1520640 | bytes 2433072 | tf_op jit(solution)/shard_map/mul | solution.py:147
  214.1 1.7 collective-permute-start.6
  215.8 2.2 collective-permute-start.7
  218.1 8.8 %collective-permute-done.6 = f32[3,16,10,1]{3,2,1,0:T(8,128)S(1)} collective-permute-done((f32[3,16,10,1]{3,2,1,0:T(8,128)S(1)}, f32[3,16,10,1]{3,2,1,0:T(8,128)S(1)}, u32[]{:S(2)}, u32[]{:S(2)}) %collective-permute-start.6) | collective-permute-done | bytes 1952 | tf_op jit(solution)/shard_map/ppermute | solution.py:18
  226.9 6.8 %collective-permute-done.7 = f32[3,16,10,1]{3,2,1,0:T(8,128)S(1)} collective-permute-done((f32[3,16,10,1]{3,2,1,0:T(8,128)S(1)}, f32[3,16,10,1]{3,2,1,0:T(8,128)S(1)}, u32[]{:S(2)}, u32[]{:S(2)}) %collective-permute-start.7) | collective-permute-done | bytes 1952 | tf_op jit(solution)/shard_map/ppermute | solution.py:21
  237.1 2.0 collective-permute-start.9
  239.1 1.4 collective-permute-done.8
  240.9 4.7 %collective-permute-start.10 = (f32[3,16,10,1]{3,2,1,0:T(8,128)S(1)}, f32[3,16,10,1]{3,2,1,0:T(8,128)S(1)}, u32[]{:S(2)}, u32[]{:S(2)}) collective-permute-start(f32[3,16,10,1]{3,2,1,0:T(8,128)S(1)} %get-tuple-element.198), channel_id=1, source_target_pairs={{0,1},{1,2},{2,3},{3,0},{4,5},{5,6},{6,7},{7,4},{8,9},{9,10},{10,1... | collective-permute-start | bytes 5768 | tf_op jit(solution)/shard_map/ppermute | solution.py:18
  245.6 2.1 collective-permute-start.11
  247.7 9.9 %collective-permute-done.10 = f32[3,16,10,1]{3,2,1,0:T(8,128)S(1)} collective-permute-done((f32[3,16,10,1]{3,2,1,0:T(8,128)S(1)}, f32[3,16,10,1]{3,2,1,0:T(8,128)S(1)}, u32[]{:S(2)}, u32[]{:S(2)}) %collective-permute-start.10) | collective-permute-done | bytes 1952 | tf_op jit(solution)/shard_map/ppermute | solution.py:18
  257.7 8.3 %collective-permute-done.11 = f32[3,16,10,1]{3,2,1,0:T(8,128)S(1)} collective-permute-done((f32[3,16,10,1]{3,2,1,0:T(8,128)S(1)}, f32[3,16,10,1]{3,2,1,0:T(8,128)S(1)}, u32[]{:S(2)}, u32[]{:S(2)}) %collective-permute-start.11) | collective-permute-done | bytes 1952 | tf_op jit(solution)/shard_map/ppermute | solution.py:21
  269.0 1.6 collective-permute-start.13
  270.7 1.5 collective-permute-done.12
  273.0 3.5 %collective-permute-start.15 = (f32[3,16,10,1]{3,2,1,0:T(8,128)S(1)}, f32[3,16,10,1]{3,2,1,0:T(8,128)S(1)}, u32[]{:S(2)}, u32[]{:S(2)}) collective-permute-start(f32[3,16,10,1]{3,2,1,0:T(8,128)S(1)} %get-tuple-element.197), channel_id=1, source_target_pairs={{1,0},{2,1},{3,2},{0,3},{5,4},{6,5},{7,6},{4,7},{9,8},{10,9},{11,1... | collective-permute-start | bytes 5768 | tf_op jit(solution)/shard_map/ppermute | solution.py:21
  276.5 9.8 %collective-permute-done.14 = f32[3,16,10,1]{3,2,1,0:T(8,128)S(1)} collective-permute-done((f32[3,16,10,1]{3,2,1,0:T(8,128)S(1)}, f32[3,16,10,1]{3,2,1,0:T(8,128)S(1)}, u32[]{:S(2)}, u32[]{:S(2)}) %collective-permute-start.14) | collective-permute-done | bytes 1952 | tf_op jit(solution)/shard_map/ppermute | solution.py:18
  286.3 7.1 %collective-permute-done.15 = f32[3,16,10,1]{3,2,1,0:T(8,128)S(1)} collective-permute-done((f32[3,16,10,1]{3,2,1,0:T(8,128)S(1)}, f32[3,16,10,1]{3,2,1,0:T(8,128)S(1)}, u32[]{:S(2)}, u32[]{:S(2)}) %collective-permute-start.15) | collective-permute-done | bytes 1952 | tf_op jit(solution)/shard_map/ppermute | solution.py:21
  296.4 1.7 collective-permute-start.17
  298.1 1.5 collective-permute-done.16
  299.9 1.6 collective-permute-start.18
  301.5 2.3 collective-permute-start.19
  303.8 9.9 %collective-permute-done.18 = f32[3,16,10,1]{3,2,1,0:T(8,128)S(1)} collective-permute-done((f32[3,16,10,1]{3,2,1,0:T(8,128)S(1)}, f32[3,16,10,1]{3,2,1,0:T(8,128)S(1)}, u32[]{:S(2)}, u32[]{:S(2)}) %collective-permute-start.18) | collective-permute-done | bytes 1952 | tf_op jit(solution)/shard_map/ppermute | solution.py:18
  313.7 7.9 %collective-permute-done.19 = f32[3,16,10,1]{3,2,1,0:T(8,128)S(1)} collective-permute-done((f32[3,16,10,1]{3,2,1,0:T(8,128)S(1)}, f32[3,16,10,1]{3,2,1,0:T(8,128)S(1)}, u32[]{:S(2)}, u32[]{:S(2)}) %collective-permute-start.19) | collective-permute-done | bytes 1952 | tf_op jit(solution)/shard_map/ppermute | solution.py:21
  (127 shorter events, 33.5 us)
Async XLA Ops:
  0.0 26.4 %copy-start.4 = (f32[2,2048]{1,0:T(2,128)S(1)}, f32[2,2048]{1,0:T(2,128)}, u32[]{:S(2)}) copy-start(f32[2,2048]{1,0:T(2,128)} %param.11) | copy-start | bytes 49156
  4.6 21.8 %copy-start.6 = (s32[2048,1]{0,1:T(1,128)}, s32[2048,1]{0,1:T(1,128)S(1)}, u32[]{:S(2)}) copy-start(s32[2048,1]{0,1:T(1,128)S(1)} %compare_select_fusion.4) | copy-start | bytes 24580
  13.4 30.5 %all-to-all-start = ((s32[1,16,256]{2,0,1:T(1,128)}), s32[1,16,256]{2,0,1:T(1,128)S(1)}, u32[]{:S(2)}, u32[]{:S(2)}) async-start(s32[1,16,256]{2,0,1:T(1,128)} %bitcast.1), calls=%async_computation | async-start | bytes 32768 | tf_op jit(solution)/shard_map/all_to_all | solution.py:121
  23.1 38.9 %collective-permute-start = (f32[2,2,3,16,2,128]{5,4,3,2,1,0:T(2,128)}, f32[2,2,3,16,2,128]{5,4,3,2,1,0:T(2,128)S(1)}, u32[]{:S(2)}, u32[]{:S(2)}) collective-permute-start(f32[2,2,3,16,2,128]{5,4,3,2,1,0:T(2,128)} %get-tuple-element.188), channel_id=1, source_target_pairs={{0,4},{4,8},{8,12},{12,0},{1,5},{5,9},{9,13},{13,1},{2,6},{6,10},{... | collective-permute-start | bytes 589832 | tf_op jit(solution)/shard_map/ppermute | solution.py:18
  23.5 38.5 %collective-permute-start.1 = (f32[2,2,3,16,2,128]{5,4,3,2,1,0:T(2,128)}, f32[2,2,3,16,2,128]{5,4,3,2,1,0:T(2,128)S(1)}, u32[]{:S(2)}, u32[]{:S(2)}) collective-permute-start(f32[2,2,3,16,2,128]{5,4,3,2,1,0:T(2,128)} %get-tuple-element.189), channel_id=1, source_target_pairs={{4,0},{8,4},{12,8},{0,12},{5,1},{9,5},{13,9},{1,13},{6,2},{10,6},{... | collective-permute-start | bytes 589832 | tf_op jit(solution)/shard_map/ppermute | solution.py:21
  41.9 1.5 copy-start.10
  41.9 20.1 %copy-start = (f32[2,2,3,16,8,128]{5,4,3,2,1,0:T(8,128)S(1)}, f32[2,2,3,16,8,128]{5,4,3,2,1,0:T(8,128)}, u32[]{:S(2)}) copy-start(f32[2,2,3,16,8,128]{5,4,3,2,1,0:T(8,128)} %param.12) | copy-start | bytes 2359300
  43.9 12.5 %all-to-all-start.2 = ((f32[2,16,256]{2,0,1:T(2,128)}), f32[2,16,256]{2,0,1:T(2,128)S(1)}, u32[]{:S(2)}, u32[]{:S(2)}) async-start(f32[2,16,256]{2,0,1:T(2,128)} %copy.30), calls=%async_computation.2 | async-start | bytes 65536 | tf_op jit(solution)/shard_map/all_to_all | solution.py:120
  56.5 28.8 %all-to-all-start.1 = ((f32[48,16,256]{2,0,1:T(8,128)}), f32[48,16,256]{2,0,1:T(8,128)}, u32[]{:S(2)}, u32[]{:S(2)}) async-start(f32[48,16,256]{2,0,1:T(8,128)} %copy.27), calls=%async_computation.1 | async-start | bytes 1572864 | tf_op jit(solution)/shard_map/all_to_all | solution.py:119
  64.5 17.4 %collective-permute-start.2 = (f32[2,2,3,16,12,2]{3,5,4,2,1,0:T(2,128)}, f32[2,2,3,16,12,2]{3,5,4,2,1,0:T(2,128)S(1)}, u32[]{:S(2)}, u32[]{:S(2)}) collective-permute-start(f32[2,2,3,16,12,2]{3,5,4,2,1,0:T(2,128)} %copy.36), channel_id=1, source_target_pairs={{0,1},{1,2},{2,3},{3,0},{4,5},{5,6},{6,7},{7,4},{8,9},{9,10},{10,1... | collective-permute-start | bytes 55304 | tf_op jit(solution)/shard_map/ppermute | solution.py:18
  67.2 15.6 %collective-permute-start.3 = (f32[2,2,3,16,12,2]{3,5,4,2,1,0:T(2,128)S(1)}, f32[2,2,3,16,12,2]{3,5,4,2,1,0:T(2,128)S(1)}, u32[]{:S(2)}, u32[]{:S(2)}) collective-permute-start(f32[2,2,3,16,12,2]{3,5,4,2,1,0:T(2,128)S(1)} %copy.37), channel_id=1, source_target_pairs={{1,0},{2,1},{3,2},{0,3},{5,4},{6,5},{7,6},{4,7},{9,8},{10,9},{11,1... | collective-permute-start | bytes 55304 | tf_op jit(solution)/shard_map/ppermute | solution.py:21
  97.0 28.0 %copy-start.3 = (s32[4096,1]{0,1:T(1,128)S(1)}, s32[4096,1]{0,1:T(1,128)}, u32[]{:S(2)}) copy-start(s32[4096,1]{0,1:T(1,128)} %get-tuple-element.218) | copy-start | bytes 49156
  124.9 26.1 %copy-start.2 = (s32[4096,1]{0,1:T(1,128)S(1)}, s32[4096,1]{0,1:T(1,128)}, u32[]{:S(2)}) copy-start(s32[4096,1]{0,1:T(1,128)} %get-tuple-element.216) | copy-start | bytes 49156
  177.1 33.2 %copy-start.1 = (f32[2,2,3,16,8,128]{5,4,3,2,1,0:T(8,128)S(1)}, f32[2,2,3,16,8,128]{5,4,3,2,1,0:T(8,128)}, u32[]{:S(2)}) copy-start(f32[2,2,3,16,8,128]{5,4,3,2,1,0:T(8,128)} %param.12) | copy-start | bytes 2359300
  177.1 33.2 %copy-start.9 = (f32[12]{0:T(128)S(1)}, f32[12]{0:T(128)}, u32[]{:S(2)}) copy-start(f32[12]{0:T(128)} %and_convert_fusion.1) | copy-start | bytes 148
  203.5 10.3 %collective-permute-start.4 = (f32[3,16,1,128]{3,2,1,0:T(1,128)S(1)}, f32[3,16,1,128]{3,2,1,0:T(1,128)S(1)}, u32[]{:S(2)}, u32[]{:S(2)}) collective-permute-start(f32[3,16,1,128]{3,2,1,0:T(1,128)S(1)} %get-tuple-element.208), channel_id=1, source_target_pairs={{0,4},{4,8},{8,12},{12,0},{1,5},{5,9},{9,13},{13,1},{2,6},{6,10},{... | collective-permute-start | bytes 73736 | tf_op jit(solution)/shard_map/ppermute | solution.py:18
  207.4 6.4 %collective-permute-start.5 = (f32[3,16,1,128]{3,2,1,0:T(1,128)S(1)}, f32[3,16,1,128]{3,2,1,0:T(1,128)S(1)}, u32[]{:S(2)}, u32[]{:S(2)}) collective-permute-start(f32[3,16,1,128]{3,2,1,0:T(1,128)S(1)} %get-tuple-element.209), channel_id=1, source_target_pairs={{4,0},{8,4},{12,8},{0,12},{5,1},{9,5},{13,9},{1,13},{6,2},{10,6},{... | collective-permute-start | bytes 73736 | tf_op jit(solution)/shard_map/ppermute | solution.py:21
  214.1 12.9 %collective-permute-start.6 = (f32[3,16,10,1]{3,2,1,0:T(8,128)S(1)}, f32[3,16,10,1]{3,2,1,0:T(8,128)S(1)}, u32[]{:S(2)}, u32[]{:S(2)}) collective-permute-start(f32[3,16,10,1]{3,2,1,0:T(8,128)S(1)} %get-tuple-element.200), channel_id=1, source_target_pairs={{0,1},{1,2},{2,3},{3,0},{4,5},{5,6},{6,7},{7,4},{8,9},{9,10},{10,1... | collective-permute-start | bytes 5768 | tf_op jit(solution)/shard_map/ppermute | solution.py:18
  215.8 18.0 %copy-start.7 = (f32[10]{0:T(128)S(1)}, f32[10]{0:T(128)}, u32[]{:S(2)}) copy-start(f32[10]{0:T(128)} %and_convert_fusion) | copy-start | bytes 124
  215.8 18.0 %collective-permute-start.7 = (f32[3,16,10,1]{3,2,1,0:T(8,128)S(1)}, f32[3,16,10,1]{3,2,1,0:T(8,128)S(1)}, u32[]{:S(2)}, u32[]{:S(2)}) collective-permute-start(f32[3,16,10,1]{3,2,1,0:T(8,128)S(1)} %get-tuple-element.201), channel_id=1, source_target_pairs={{1,0},{2,1},{3,2},{0,3},{5,4},{6,5},{7,6},{4,7},{9,8},{10,9},{11,1... | collective-permute-start | bytes 5768 | tf_op jit(solution)/shard_map/ppermute | solution.py:21
  218.1 16.3 %copy-start.5 = (f32[16]{0:T(128)S(1)}, f32[16]{0:T(128)}, u32[]{:S(2)}) copy-start(f32[16]{0:T(128)} %neg.159) | copy-start | bytes 196
  234.4 0.6 copy-start.8
  237.0 3.6 %collective-permute-start.8 = (f32[3,16,1,128]{3,2,1,0:T(1,128)S(1)}, f32[3,16,1,128]{3,2,1,0:T(1,128)S(1)}, u32[]{:S(2)}, u32[]{:S(2)}) collective-permute-start(f32[3,16,1,128]{3,2,1,0:T(1,128)S(1)} %get-tuple-element.206), channel_id=1, source_target_pairs={{0,4},{4,8},{8,12},{12,0},{1,5},{5,9},{9,13},{13,1},{2,6},{6,10},{... | collective-permute-start | bytes 73736 | tf_op jit(solution)/shard_map/ppermute | solution.py:18
  237.1 3.5 %collective-permute-start.9 = (f32[3,16,1,128]{3,2,1,0:T(1,128)S(1)}, f32[3,16,1,128]{3,2,1,0:T(1,128)S(1)}, u32[]{:S(2)}, u32[]{:S(2)}) collective-permute-start(f32[3,16,1,128]{3,2,1,0:T(1,128)S(1)} %get-tuple-element.207), channel_id=1, source_target_pairs={{4,0},{8,4},{12,8},{0,12},{5,1},{9,5},{13,9},{1,13},{6,2},{10,6},{... | collective-permute-start | bytes 73736 | tf_op jit(solution)/shard_map/ppermute | solution.py:21
  240.9 16.7 %collective-permute-start.10 = (f32[3,16,10,1]{3,2,1,0:T(8,128)S(1)}, f32[3,16,10,1]{3,2,1,0:T(8,128)S(1)}, u32[]{:S(2)}, u32[]{:S(2)}) collective-permute-start(f32[3,16,10,1]{3,2,1,0:T(8,128)S(1)} %get-tuple-element.198), channel_id=1, source_target_pairs={{0,1},{1,2},{2,3},{3,0},{4,5},{5,6},{6,7},{7,4},{8,9},{9,10},{10,1... | collective-permute-start | bytes 5768 | tf_op jit(solution)/shard_map/ppermute | solution.py:18
  245.6 20.3 %collective-permute-start.11 = (f32[3,16,10,1]{3,2,1,0:T(8,128)S(1)}, f32[3,16,10,1]{3,2,1,0:T(8,128)S(1)}, u32[]{:S(2)}, u32[]{:S(2)}) collective-permute-start(f32[3,16,10,1]{3,2,1,0:T(8,128)S(1)} %get-tuple-element.199), channel_id=1, source_target_pairs={{1,0},{2,1},{3,2},{0,3},{5,4},{6,5},{7,6},{4,7},{9,8},{10,9},{11,1... | collective-permute-start | bytes 5768 | tf_op jit(solution)/shard_map/ppermute | solution.py:21
  268.9 3.3 %collective-permute-start.12 = (f32[3,16,1,128]{3,2,1,0:T(1,128)S(1)}, f32[3,16,1,128]{3,2,1,0:T(1,128)S(1)}, u32[]{:S(2)}, u32[]{:S(2)}) collective-permute-start(f32[3,16,1,128]{3,2,1,0:T(1,128)S(1)} %get-tuple-element.204), channel_id=1, source_target_pairs={{0,4},{4,8},{8,12},{12,0},{1,5},{5,9},{9,13},{13,1},{2,6},{6,10},{... | collective-permute-start | bytes 73736 | tf_op jit(solution)/shard_map/ppermute | solution.py:18
  269.0 3.2 collective-permute-start.13
  272.4 13.9 %collective-permute-start.14 = (f32[3,16,10,1]{3,2,1,0:T(8,128)S(1)}, f32[3,16,10,1]{3,2,1,0:T(8,128)S(1)}, u32[]{:S(2)}, u32[]{:S(2)}) collective-permute-start(f32[3,16,10,1]{3,2,1,0:T(8,128)S(1)} %get-tuple-element.196), channel_id=1, source_target_pairs={{0,1},{1,2},{2,3},{3,0},{4,5},{5,6},{6,7},{7,4},{8,9},{9,10},{10,1... | collective-permute-start | bytes 5768 | tf_op jit(solution)/shard_map/ppermute | solution.py:18
  273.0 20.4 %collective-permute-start.15 = (f32[3,16,10,1]{3,2,1,0:T(8,128)S(1)}, f32[3,16,10,1]{3,2,1,0:T(8,128)S(1)}, u32[]{:S(2)}, u32[]{:S(2)}) collective-permute-start(f32[3,16,10,1]{3,2,1,0:T(8,128)S(1)} %get-tuple-element.197), channel_id=1, source_target_pairs={{1,0},{2,1},{3,2},{0,3},{5,4},{6,5},{7,6},{4,7},{9,8},{10,9},{11,1... | collective-permute-start | bytes 5768 | tf_op jit(solution)/shard_map/ppermute | solution.py:21
  296.3 3.3 %collective-permute-start.16 = (f32[3,16,1,128]{3,2,1,0:T(1,128)S(1)}, f32[3,16,1,128]{3,2,1,0:T(1,128)S(1)}, u32[]{:S(2)}, u32[]{:S(2)}) collective-permute-start(f32[3,16,1,128]{3,2,1,0:T(1,128)S(1)} %get-tuple-element.202), channel_id=1, source_target_pairs={{0,4},{4,8},{8,12},{12,0},{1,5},{5,9},{9,13},{13,1},{2,6},{6,10},{... | collective-permute-start | bytes 73736 | tf_op jit(solution)/shard_map/ppermute | solution.py:18
  296.4 3.3 collective-permute-start.17
  299.9 13.8 %collective-permute-start.18 = (f32[3,16,10,1]{3,2,1,0:T(8,128)S(1)}, f32[3,16,10,1]{3,2,1,0:T(8,128)S(1)}, u32[]{:S(2)}, u32[]{:S(2)}) collective-permute-start(f32[3,16,10,1]{3,2,1,0:T(8,128)S(1)} %get-tuple-element.194), channel_id=1, source_target_pairs={{0,1},{1,2},{2,3},{3,0},{4,5},{5,6},{6,7},{7,4},{8,9},{9,10},{10,1... | collective-permute-start | bytes 5768 | tf_op jit(solution)/shard_map/ppermute | solution.py:18
  301.5 20.1 %collective-permute-start.19 = (f32[3,16,10,1]{3,2,1,0:T(8,128)S(1)}, f32[3,16,10,1]{3,2,1,0:T(8,128)S(1)}, u32[]{:S(2)}, u32[]{:S(2)}) collective-permute-start(f32[3,16,10,1]{3,2,1,0:T(8,128)S(1)} %get-tuple-element.195), channel_id=1, source_target_pairs={{1,0},{2,1},{3,2},{0,3},{5,4},{6,5},{7,6},{4,7},{9,8},{10,9},{11,1... | collective-permute-start | bytes 5768 | tf_op jit(solution)/shard_map/ppermute | solution.py:21
where the time goes:
time: 332 us; the launch traced here: 325 us
  other arithmetic  130 us (39%)
  waiting for transfers between devices  90.5 us (27%)
  starting transfers between devices  54.8 us (17%)
  local copies, waits for them, and re-layouts  48.6 us (15%)
    scatter-add x4, other arithmetic, per_device(): canvas.at[:, anchor + row_step * columns + col_step]  104 us
    ppermute x10, waiting for transfers between devices, extended(): lax.ppermute(lax.slice_in_dim(block, block.shape[dim] - width, None, axis...  53.6 us
    ppermute x10, waiting for transfers between devices, extended(): lax.ppermute(lax.slice_in_dim(block, 0, width, axis=dim), axis, backward)  30.2 us
    ppermute x10, starting transfers between devices, extended(): lax.ppermute(lax.slice_in_dim(block, 0, width, axis=dim), axis, backward)  22.2 us
    ppermute x10, starting transfers between devices, extended(): lax.ppermute(lax.slice_in_dim(block, block.shape[dim] - width, None, axis...  15 us
    mul x4, local copies, waits for them, and re-layouts, per_device(): flat_values * weight[None, :]  10.2 us
    scatter x1, local copies, waits for them, and re-layouts, per_device(): send_base = jnp.zeros((1, slot_total), jnp.int32).at[:, position].set(bas...  8.78 us
    all_to_all x1, starting transfers between devices, per_device(): lax.all_to_all(send_base, ('frow', 'fcol'), split_axis=1, concat_axis=1,...  7.36 us
  transfers between devices with their start and end apart: 23, of which 15 were waited for; matrix products, arithmetic and copies ran while one was open for 11% of the time, Pallas kernels for 0%

commit v1 on v0

v1 whole, which is shorter than its diff:
```python
import functools

import jax
import jax.numpy as jnp
from jax import lax
from jax.experimental import pallas as pl
from jax.experimental.pallas import tpu as pltpu
from jax.sharding import PartitionSpec as P

time_step = 0.25
coriolis_peak = 0.8

HALO = 4
GROUP = 256
LANES = 128
F32 = jnp.float32
BF16 = jnp.bfloat16
PARAMS = pltpu.CompilerParams(vmem_limit_bytes=40 * 1024 * 1024)


def split(values):
    high = values.astype(BF16)
    return high, (values - high.astype(F32)).astype(BF16)


def dot_nt(a, b):
    return lax.dot_general(a, b, (((1,), (1,)), ((), ())), preferred_element_type=F32)


def pack_kernel(capacity, tile_count, tile_rows, columns, cot, dest, base, frac, out, ranks, onehot, high, low):
    channels, points = cot.shape
    groups = out.shape[0]
    target = dest[...]
    corner = base[...]
    row = jnp.zeros_like(corner)
    for k in range(1, tile_rows - 1):
        row = row + (corner >= k * (columns - 1)).astype(jnp.int32)
    col = corner - row * (columns - 1)

    before = (
        lax.broadcasted_iota(jnp.int32, (GROUP, GROUP), 0)
        < lax.broadcasted_iota(jnp.int32, (GROUP, GROUP), 1)
    ).astype(F32).astype(BF16)
    tiles = lax.broadcasted_iota(jnp.int32, (tile_count, GROUP), 0)
    first = (tiles * capacity).astype(F32)
    count = jnp.zeros((tile_count, 1), F32)
    for b in range(points // GROUP):
        part = slice(b * GROUP, (b + 1) * GROUP)
        named = (tiles == target[:, part]).astype(F32)
        ahead = jnp.dot(named.astype(BF16), before, preferred_element_type=F32)
        place = jnp.sum(named * (ahead + count + first), axis=0, keepdims=True)
        count = count + jnp.sum(named, axis=1, keepdims=True)
        ranks[:, part] = place.astype(jnp.int32)
    place = ranks[...]
    group = place // GROUP
    lane = place - group * GROUP
    slots = lax.broadcasted_iota(jnp.int32, (GROUP, points), 0)
    onehot[...] = (slots == lane).astype(F32).astype(BF16)

    coords = jnp.concatenate([row.astype(F32), col.astype(F32), frac[...]], axis=0)
    data = jnp.concatenate([cot[...], coords, coords], axis=0)
    data_high, data_low = split(data)
    rows = data.shape[0]
    for g in range(groups):
        mine = (group == g).astype(F32).astype(BF16)
        high[g * rows : (g + 1) * rows, :] = data_high * mine
        low[g * rows : (g + 1) * rows, :] = data_low * mine
    upper = lax.broadcasted_iota(jnp.int32, (8, LANES), 0) < 4
    packed = dot_nt(high[...], onehot[...]) + dot_nt(low[...], onehot[...])
    for g in range(groups):
        block = packed[g * rows : (g + 1) * rows, :]
        out[g, :channels, :] = block[:channels, :LANES]
        out[g, channels : 2 * channels, :] = block[:channels, LANES:]
        out[g, 2 * channels :, :] = jnp.where(upper, block[channels:, :LANES], block[channels:, LANES:])


def pack(cot, dest, base, frac, capacity, tile_count, tile_rows, columns):
    channels, points = cot.shape
    groups = tile_count * capacity // GROUP
    rows = channels + 8
    return pl.pallas_call(
        functools.partial(pack_kernel, capacity, tile_count, tile_rows, columns),
        out_shape=jax.ShapeDtypeStruct((groups, 2 * channels + 8, LANES), F32),
        scratch_shapes=[
            pltpu.VMEM((1, points), jnp.int32),
            pltpu.VMEM((GROUP, points), BF16),
            pltpu.VMEM((groups * rows, points), BF16),
            pltpu.VMEM((groups * rows, points), BF16),
        ],
        compiler_params=PARAMS,
        name="pack_points",
    )(cot, dest, base, frac)


def scatter_kernel(got, canvas, north, south, high, low, weight):
    groups = got.shape[0]
    tile_rows, channels, columns = canvas.shape
    cells = lax.broadcasted_iota(jnp.int32, (columns, LANES), 0).astype(F32)
    lines = lax.broadcasted_iota(jnp.int32, (tile_rows, LANES), 0).astype(F32)

    def hat(index, corner, fraction):
        away = index - corner
        return jnp.where(away == 0.0, 1.0 - fraction, jnp.where(away == 1.0, fraction, 0.0))

    for g in range(groups):
        for half in range(2):
            part = slice((2 * g + half) * LANES, (2 * g + half + 1) * LANES)
            coords = got[g, 2 * channels + 4 * half : 2 * channels + 4 * half + 4, :]
            row, col, along_rows, along_cols = (coords[k : k + 1, :] for k in range(4))
            weight_high, weight_low = split(hat(cells, col, along_cols))
            weight[:columns, part] = weight_high
            weight[columns:, part] = weight_low
            values = got[g, half * channels : (half + 1) * channels, :]
            row_weight = hat(lines, row, along_rows)
            for r in range(tile_rows):
                product_high, product_low = split(values * row_weight[r : r + 1, :])
                high[r * channels : (r + 1) * channels, part] = product_high
                low[r * channels : (r + 1) * channels, part] = product_low
    both = dot_nt(high[...], weight[...])
    total = both[:, :columns] + both[:, columns:] + dot_nt(low[...], weight[:columns, :])
    for r in range(tile_rows):
        line = total[r * channels : (r + 1) * channels, :]
        canvas[r] = line
        if r < HALO:
            north[r] = line
        if r >= tile_rows - HALO:
            south[r - tile_rows + HALO] = line


def scatter(got, channels, tile_rows, columns):
    slots = got.shape[0] * GROUP
    return pl.pallas_call(
        scatter_kernel,
        out_shape=(
            jax.ShapeDtypeStruct((tile_rows, channels, columns), F32),
            jax.ShapeDtypeStruct((HALO, channels, columns), F32),
            jax.ShapeDtypeStruct((HALO, channels, columns), F32),
        ),
        scratch_shapes=[
            pltpu.VMEM((tile_rows * channels, slots), BF16),
            pltpu.VMEM((tile_rows * channels, slots), BF16),
            pltpu.VMEM((2 * columns, slots), BF16),
        ],
        compiler_params=PARAMS,
        name="scatter_points",
    )(got)


def edge_columns(lines):
    lane = lax.broadcasted_iota(jnp.int32, lines[0][1].shape, 1)
    owner = ((lane + 4) // 8) % 16
    result = jnp.zeros_like(lines[0][1])
    for k, line in lines:
        result = jnp.where(owner == k, pltpu.roll(line, (8 * k) % LANES, 1), result)
    return result


def beside(from_left, from_right):
    lane = lax.broadcasted_iota(jnp.int32, from_left.shape, 1)
    return jnp.where(lane % 8 < 4, from_right, from_left)


def row_mask(n_row):
    at = lax.axis_index("frow")
    return jnp.where(at > 0, 1.0, 0.0).astype(F32), jnp.where(at < n_row - 1, 1.0, 0.0).astype(F32)


def adjoint_edges_kernel(n_row, canvas, above, below, edges):
    tile_rows = canvas.shape[0]
    keep_above, keep_below = row_mask(n_row)
    lines = [(k, above[k] * keep_above) for k in range(HALO)]
    lines += [(HALO + k, canvas[k]) for k in range(tile_rows)]
    lines += [(HALO + tile_rows + k, below[k] * keep_below) for k in range(HALO)]
    edges[...] = edge_columns(lines)


def adjoint_edges(canvas, above, below, n_row):
    return pl.pallas_call(
        functools.partial(adjoint_edges_kernel, n_row),
        out_shape=jax.ShapeDtypeStruct(canvas.shape[1:], F32),
        compiler_params=PARAMS,
        name="adjoint_edges",
    )(canvas, above, below)


def first_row(which):
    return sum(HALO - k for k in range(which))


def turn_states_kernel(order, states, turned, north, south):
    tile_rows = turned.shape[1]
    channels = turned.shape[2]
    for which, source in enumerate(order):
        width = HALO - which
        for r in range(tile_rows):
            line = states[source, pl.ds(r, channels, stride=tile_rows), :]
            turned[which, r] = line
            if r < width:
                north[first_row(which) + r] = line
            if r >= tile_rows - width:
                south[first_row(which) + r - tile_rows + width] = line


def turn_states(states, order, channels, tile_rows, columns):
    stages = len(order)
    rim = first_row(stages)
    return pl.pallas_call(
        functools.partial(turn_states_kernel, order),
        out_shape=(
            jax.ShapeDtypeStruct((stages, tile_rows, channels, columns), F32),
            jax.ShapeDtypeStruct((rim, channels, columns), F32),
            jax.ShapeDtypeStruct((rim, channels, columns), F32),
        ),
        compiler_params=PARAMS,
        name="turn_states",
    )(states)


def state_lines(which, turned, above, below, keep_above, keep_below):
    tile_rows = turned.shape[1]
    width = HALO - which
    at = first_row(which)
    lines = [(HALO - width + k, above[at + k] * keep_above) for k in range(width)]
    lines += [(HALO + k, turned[which, k]) for k in range(tile_rows)]
    lines += [(HALO + tile_rows + k, below[at + k] * keep_below) for k in range(width)]
    return lines


def state_edges_kernel(n_row, turned, above, below, edges):
    keep_above, keep_below = row_mask(n_row)
    for which in range(turned.shape[0]):
        edges[which] = edge_columns(state_lines(which, turned, above, below, keep_above, keep_below))


def state_edges(turned, above, below, n_row):
    stages, _, channels, columns = turned.shape
    return pl.pallas_call(
        functools.partial(state_edges_kernel, n_row),
        out_shape=jax.ShapeDtypeStruct((stages, channels, columns), F32),
        compiler_params=PARAMS,
        name="state_edges",
    )(turned, above, below)


def widen_states_kernel(n_row, turned, above, below, from_left, from_right, wide):
    columns = turned.shape[3]
    keep_above, keep_below = row_mask(n_row)
    for which in range(turned.shape[0]):
        rim = beside(from_left[which], from_right[which])
        for k, line in state_lines(which, turned, above, below, keep_above, keep_below):
            wide[which, k, :, :columns] = line
            wide[which, k, :, columns:] = pltpu.roll(rim, (-8 * k) % LANES, 1)


def widen_states(turned, above, below, from_left, from_right, n_row):
    stages, tile_rows, channels, columns = turned.shape
    return pl.pallas_call(
        functools.partial(widen_states_kernel, n_row),
        out_shape=jax.ShapeDtypeStruct((stages, tile_rows + 2 * HALO, channels, 2 * columns), F32),
        compiler_params=PARAMS,
        name="widen_states",
    )(turned, above, below, from_left, from_right)


def steps_kernel(n_row, canvas, above, below, from_left, from_right, wide, gravity, out, start, middle, after, last):
    tile_rows, channels, columns = canvas.shape
    levels = channels // 3
    total_rows = tile_rows * n_row
    base_row = lax.axis_index("frow") * tile_rows
    keep_above, keep_below = row_mask(n_row)
    rim = beside(from_left[...], from_right[...])
    lines = [(k, above[k] * keep_above) for k in range(HALO)]
    lines += [(HALO + k, canvas[k]) for k in range(tile_rows)]
    lines += [(HALO + tile_rows + k, below[k] * keep_below) for k in range(HALO)]
    for k, line in lines:
        start[k, :, :columns] = line
        start[k, :, columns:] = pltpu.roll(rim, (-8 * k) % LANES, 1)
    pull = jnp.broadcast_to(gravity[...], (levels, 2 * columns))

    def along_x(values):
        return 0.5 * (pltpu.roll(values, 2 * columns - 1, 1) - pltpu.roll(values, 1, 1))

    def field(ref, k, which):
        return ref[k, which * levels : (which + 1) * levels, :]

    def pull_back(stage, adjoint, k):
        a, b, c = (field(adjoint, k, w) for w in range(3))
        a_up, b_up, c_up = (field(adjoint, k - 1, w) for w in range(3))
        a_down, b_down, c_down = (field(adjoint, k + 1, w) for w in range(3))
        state = wide.at[stage]
        h, u, v = (field(state, k, w) for w in range(3))
        u_up, v_up = (field(state, k - 1, w) for w in (1, 2))
        u_down, v_down = (field(state, k + 1, w) for w in (1, 2))
        rotation = coriolis_peak * (2.0 * ((base_row + k - HALO).astype(F32) + 0.5) / total_rows - 1.0)
        a_x = along_x(a)
        a_y = 0.5 * (a_down - a_up)
        height = u * a_x + v * a_y + pull * (along_x(b) + 0.5 * (c_down - c_up))
        east = (
            h * a_x
            + along_x(u * b)
            + 0.5 * (v_down * b_down - v_up * b_up)
            - b * along_x(u)
            - c * along_x(v)
            - rotation * c
        )
        north = (
            h * a_y
            + along_x(u * c)
            + 0.5 * (v_down * c_down - v_up * c_up)
            - b * (0.5 * (u_down - u_up))
            - c * (0.5 * (v_down - v_up))
            + rotation * b
        )
        return (a, b, c), (height, east, north)

    def keep(k):
        row = base_row + k - HALO
        return jnp.where((row >= 0) & (row < total_rows), 1.0, 0.0).astype(F32)

    def half_step(stage, adjoint, result):
        def body(k, _):
            old, change = pull_back(stage, adjoint, k)
            for w in range(3):
                result[k, w * levels : (w + 1) * levels, :] = keep(k) * (
                    0.5 * old[w] + (0.5 * time_step) * change[w]
                )
            return 0

        width = HALO - 1 - stage
        lax.fori_loop(HALO - width, HALO + tile_rows + width, body, 0, unroll=2)

    def full_step(stage, adjoint, mid, store):
        def body(k, _):
            mids, change = pull_back(stage, mid, k)
            for w in range(3):
                store(k, w, 0.5 * field(adjoint, k, w) + mids[w] + time_step * change[w])
            return 0

        width = HALO - 1 - stage
        lax.fori_loop(HALO - width, HALO + tile_rows + width, body, 0, unroll=2)

    def to_after(k, w, value):
        after[k, w * levels : (w + 1) * levels, :] = keep(k) * value

    def to_out(k, w, value):
        out[pl.ds(w * levels * tile_rows + k - HALO, levels, stride=tile_rows), :] = value[:, :columns]

    half_step(0, start, middle)
    full_step(1, start, middle, to_after)
    half_step(2, after, last)
    full_step(3, after, last, to_out)


def steps(canvas, above, below, from_left, from_right, wide, gravity, n_row):
    tile_rows, channels, columns = canvas.shape
    extended = pltpu.VMEM((tile_rows + 2 * HALO, channels, 2 * columns), F32)
    return pl.pallas_call(
        functools.partial(steps_kernel, n_row),
        out_shape=jax.ShapeDtypeStruct((channels * tile_rows, columns), F32),
        scratch_shapes=[extended] * 4,
        compiler_params=PARAMS,
        name="adjoint_steps",
    )(canvas, above, below, from_left, from_right, wide, gravity)


def shifted(values, axis, by):
    count = lax.axis_size(axis)
    return lax.ppermute(values, axis, [(i, (i + by) % count) for i in range(count)])


def to_partners(packed, channels, capacity, tile_count):
    if capacity == GROUP:
        return lax.all_to_all(packed, ("frow", "fcol"), split_axis=0, concat_axis=0, tiled=True)
    groups = packed.shape[0]
    rows = channels + 4
    halves = [
        jnp.concatenate(
            [
                packed[:, h * channels : (h + 1) * channels],
                packed[:, 2 * channels + 4 * h : 2 * channels + 4 * h + 4],
            ],
            axis=1,
        )
        for h in range(2)
    ]
    slots = jnp.stack(halves, axis=2).transpose(1, 0, 2, 3).reshape(rows, tile_count, capacity)
    slots = lax.all_to_all(slots, ("frow", "fcol"), split_axis=1, concat_axis=1, tiled=True)
    slots = slots.reshape(rows, groups, 2, LANES).transpose(1, 2, 0, 3)
    return jnp.concatenate(
        [slots[:, 0, :channels], slots[:, 1, :channels], slots[:, 0, channels:], slots[:, 1, channels:]], axis=1
    )


def per_device(latlon_cot, dest_tile, base_cell, corner_frac, saved_states, gravity):
    n_row = lax.axis_size("frow")
    tile_count = n_row * lax.axis_size("fcol")
    levels = gravity.shape[0]
    tile_rows = saved_states.shape[4]
    columns = saved_states.shape[5]
    channels = 3 * levels
    points = base_cell.shape[0]
    capacity = 2 * points // tile_count

    packed = pack(
        latlon_cot.reshape(channels, points),
        dest_tile.reshape(1, points),
        base_cell.reshape(1, points),
        corner_frac,
        capacity,
        tile_count,
        tile_rows,
        columns,
    )
    got = to_partners(packed, channels, capacity, tile_count)

    turned, north, south = turn_states(
        saved_states.reshape(4, channels * tile_rows, columns), (3, 2, 1, 0), channels, tile_rows, columns
    )
    state_above = shifted(south, "frow", 1)
    state_below = shifted(north, "frow", -1)
    edges = state_edges(turned, state_above, state_below, n_row)
    wide = widen_states(
        turned, state_above, state_below, shifted(edges, "fcol", 1), shifted(edges, "fcol", -1), n_row
    )

    canvas, north, south = scatter(got, channels, tile_rows, columns)
    above = shifted(south, "frow", 1)
    below = shifted(north, "frow", -1)
    edges = adjoint_edges(canvas, above, below, n_row)
    result = steps(
        canvas,
        above,
        below,
        shifted(edges, "fcol", 1),
        shifted(edges, "fcol", -1),
        wide,
        gravity.reshape(levels, 1),
        n_row,
    )
    return result.reshape(3, levels, tile_rows, columns)


def solution(mesh):
    placed = (
        P(None, None, ("member", "frow", "fcol")),
        P(("frow", "fcol"), None),
        P(("frow", "fcol")),
        P(None, ("frow", "fcol")),
        P(None, None, None, None, ("member", "frow"), "fcol"),
        P(),
    )
    return jax.shard_map(
        per_device,
        mesh=mesh,
        in_specs=placed,
        out_specs=P(None, None, ("member", "frow"), "fcol"),
        check_vma=False,
    )
```

time: 332 us -> 57.2 us (0.17); the launches traced: 325 us -> 56.9 us
  other arithmetic: 130 us -> 0 us
  waiting for transfers between devices: 90.5 us -> 22.1 us
  local copies, waits for them, and re-layouts: 48.6 us -> 3.27 us
  starting transfers between devices: 54.8 us -> 18.7 us
  Pallas kernels: 0 us -> 12.8 us
    scatter-add x4 -> x0, other arithmetic: 104 us -> none  [per_device(): canvas.at[:, anchor + row_step * columns + col_step]]
    ppermute x20 -> x8, waiting for transfers between devices: 83.8 us -> 1.29 us  [shifted(): lax.ppermute(values, axis, [(i, (i + by) % count) for i in range(count)])]
    ppermute x20 -> x8, starting transfers between devices: 37.2 us -> 11.3 us  [shifted(): lax.ppermute(values, axis, [(i, (i + by) % count) for i in range(count)])]
    scatter x3 -> x0, local copies, waits for them, and re-layouts: 21.3 us -> none  [the longest x1 8.78 us: per_device(): send_base = jnp.zeros((1, slot_total), jnp.int32).at[:, position].set(bas...]
    all_to_all x3 -> x1, waiting for transfers between devices: 6.64 us -> 20.8 us  [to_partners(): lax.all_to_all(packed, ('frow', 'fcol'), split_axis=0, concat_axis=0, til...]
    pallas_call x0 -> x7, Pallas kernels: none -> 12.8 us  [the longest x1 4.83 us: steps(): pl.pallas_call(functools.partial(steps_kernel, n_row), out_shape=jax.Shap...]
    all_to_all x3 -> x1, starting transfers between devices: 17.7 us -> 7.36 us  [to_partners(): lax.all_to_all(packed, ('frow', 'fcol'), split_axis=0, concat_axis=0, til...]
    mul x4 -> x0, local copies, waits for them, and re-layouts: 10.2 us -> none  [per_device(): flat_values * weight[None, :]]
  transfers between devices with their start and end apart: 23 -> 9, of which waited for: 15 -> 2; matrix products, arithmetic and copies ran while one was open for 11% -> 0% of each run, Pallas kernels for 0% -> 8%
where the time goes in v1:
time: 57.2 us; the launch traced here: 56.9 us
  waiting for transfers between devices  22.1 us (39%)
  starting transfers between devices  18.7 us (33%)
  Pallas kernels  12.8 us (22%)
  local copies, waits for them, and re-layouts  3.27 us (6%)
    all_to_all x1, waiting for transfers between devices, to_partners(): lax.all_to_all(packed, ('frow', 'fcol'), split_axis=0, concat_axis=0, til...  20.8 us
    ppermute x8, starting transfers between devices, shifted(): lax.ppermute(values, axis, [(i, (i + by) % count) for i in range(count)])  11.3 us
    all_to_all x1, starting transfers between devices, to_partners(): lax.all_to_all(packed, ('frow', 'fcol'), split_axis=0, concat_axis=0, til...  7.36 us
    pallas_call x1, Pallas kernels, steps(): pl.pallas_call(functools.partial(steps_kernel, n_row), out_shape=jax.Shap...  4.83 us
    pallas_call x1, Pallas kernels, scatter(): pl.pallas_call(scatter_kernel, out_shape=(jax.ShapeDtypeStruct((tile_rows...  3.56 us
    pallas_call x1, Pallas kernels, pack(): pl.pallas_call(functools.partial(pack_kernel, capacity, tile_count, tile_...  3.23 us
    unnamed x12, local copies, waits for them, and re-layouts  3.19 us
    ppermute x8, waiting for transfers between devices, shifted(): lax.ppermute(values, axis, [(i, (i + by) % count) for i in range(count)])  1.29 us
  transfers between devices with their start and end apart: 9, of which 2 were waited for; matrix products, arithmetic and copies ran while one was open for 0% of the time, Pallas kernels for 8%

profile of v1, /device:TPU:0, one launch (start us, length us, event | category | flops | bytes accessed | tf_op | source)
XLA Modules:
  0.0 56.9 jit_solution(1167647897470494907)
XLA Ops:
  0.0 0.0 copy-start
  0.0 0.0 copy-start.1
  0.0 1.1 %copy-done.1 = f32[3,16,2048]{2,1,0:T(8,128)S(1)} copy-done((f32[3,16,2048]{2,1,0:T(8,128)S(1)}, f32[3,16,2048]{2,1,0:T(8,128)}, u32[]{:S(2)}) %copy-start.1) | copy-done | bytes 393240
  1.1 0.0 copy-start.2
  1.1 0.7 %copy-done.2 = f32[2,2048]{1,0:T(2,128)S(1)} copy-done((f32[2,2048]{1,0:T(2,128)S(1)}, f32[2,2048]{1,0:T(2,128)}, u32[]{:S(2)}) %copy-start.2) | copy-done | bytes 16408
  1.8 0.0 copy-start.3
  1.8 0.7 %copy-done.3 = s32[2048,1]{0,1:T(1,128)S(1)} copy-done((s32[2048,1]{0,1:T(1,128)S(1)}, s32[2048,1]{0,1:T(1,128)}, u32[]{:S(2)}) %copy-start.3) | copy-done | bytes 8216
  2.5 0.0 copy-start.4
  2.5 0.7 %copy-done.4 = s32[2048]{0:T(1024)S(1)} copy-done((s32[2048]{0:T(1024)S(1)}, s32[2048]{0:T(1024)}, u32[]{:S(2)}) %copy-start.4) | copy-done | bytes 8216
  3.2 0.0 copy-start.5
  3.2 3.2 %pack_points.1 = f32[16,104,128]{2,1,0:T(8,128)} custom-call(f32[48,2048]{1,0:T(8,128)S(1)} %bitcast.7, s32[1,2048]{1,0:T(1,128)S(1)} %bitcast.8, s32[1,2048]{1,0:T(1,128)S(1)} %bitcast.9, f32[2,2048]{1,0:T(2,128)S(1)} %copy-done.2), custom_call_target="tpu_custom_call" | custom-call | tf_op jit(solution)/shard_map/pack_points/pallas_call | solution.py:81
  6.4 7.4 %all-to-all-start = ((f32[16,104,128]{2,1,0:T(8,128)}), f32[16,104,128]{2,1,0:T(8,128)S(1)}, u32[]{:S(2)}, u32[]{:S(2)}) async-start(f32[16,104,128]{2,1,0:T(8,128)} %pack_points.1), calls=%async_computation | async-start | bytes 1703936 | tf_op jit(solution)/shard_map/all_to_all | solution.py:373
  13.8 0.0 copy-done
  13.8 0.1 turn_states.1
  13.9 0.5 collective-permute-start.4
  14.4 1.3 %collective-permute-start.5 = (f32[10,48,128]{2,1,0:T(8,128)S(1)}, f32[10,48,128]{2,1,0:T(8,128)S(1)}, u32[]{:S(2)}, u32[]{:S(2)}) collective-permute-start(f32[10,48,128]{2,1,0:T(8,128)S(1)} %get-tuple-element.16), channel_id=1, source_target_pairs={{0,12},{4,0},{8,4},{12,8},{1,13},{5,1},{9,5},{13,9},{2,14},{6,2},{... | collective-permute-start | bytes 737288 | tf_op jit(solution)/shard_map/ppermute | solution.py:368
  15.7 20.8 %all-to-all-done.got = f32[16,104,128]{2,1,0:T(8,128)S(1)} async-done(((f32[16,104,128]{2,1,0:T(8,128)}), f32[16,104,128]{2,1,0:T(8,128)S(1)}, u32[]{:S(2)}, u32[]{:S(2)}) %all-to-all-start) | async-done | bytes 852000 | tf_op jit(solution)/shard_map/all_to_all | solution.py:373
  36.5 3.6 %scatter_points.1 = (f32[8,48,128]{2,1,0:T(8,128)S(1)}, f32[4,48,128]{2,1,0:T(8,128)S(1)}, f32[4,48,128]{2,1,0:T(8,128)S(1)}) custom-call(f32[16,104,128]{2,1,0:T(8,128)S(1)} %all-to-all-done.got), custom_call_target="tpu_custom_call" | custom-call | tf_op jit(solution)/shard_map/scatter_points/pallas_call | solution.py:132
  40.1 0.1 collective-permute-start
  40.2 1.7 %collective-permute-start.1 = (f32[4,48,128]{2,1,0:T(8,128)S(1)}, f32[4,48,128]{2,1,0:T(8,128)S(1)}, u32[]{:S(2)}, u32[]{:S(2)}) collective-permute-start(f32[4,48,128]{2,1,0:T(8,128)S(1)} %get-tuple-element.13), channel_id=1, source_target_pairs={{0,12},{4,0},{8,4},{12,8},{1,13},{5,1},{9,5},{13,9},{2,14},{6,2},{... | collective-permute-start | bytes 294920 | tf_op jit(solution)/shard_map/ppermute | solution.py:368
  41.9 0.0 collective-permute-done.4.above
  41.9 0.0 collective-permute-done.5.below
  41.9 0.4 state_edges.1
  42.3 0.1 collective-permute-start.6
  42.4 3.8 %collective-permute-start.7 = (f32[4,48,128]{2,1,0:T(8,128)S(1)}, f32[4,48,128]{2,1,0:T(8,128)S(1)}, u32[]{:S(2)}, u32[]{:S(2)}) collective-permute-start(f32[4,48,128]{2,1,0:T(8,128)S(1)} %state_edges.1), channel_id=1, source_target_pairs={{0,3},{1,0},{2,1},{3,2},{4,7},{5,4},{6,5},{7,6},{8,11},{9,8},{10,9... | collective-permute-start | bytes 294920 | tf_op jit(solution)/shard_map/ppermute | solution.py:368
  46.2 0.0 collective-permute-done.above
  46.2 0.0 collective-permute-done.1.below
  46.2 0.2 adjoint_edges.1
  46.4 0.1 collective-permute-start.2
  46.4 3.8 %collective-permute-start.3 = (f32[48,128]{1,0:T(8,128)S(1)}, f32[48,128]{1,0:T(8,128)S(1)}, u32[]{:S(2)}, u32[]{:S(2)}) collective-permute-start(f32[48,128]{1,0:T(8,128)S(1)} %adjoint_edges.1), channel_id=1, source_target_pairs={{0,3},{1,0},{2,1},{3,2},{4,7},{5,4},{6,5},{7,6},{8,11},{9,8},{10,9... | collective-permute-start | bytes 73736 | tf_op jit(solution)/shard_map/ppermute | solution.py:368
  50.2 0.0 copy-done.5
  50.2 0.1 copy.7.gravity
  50.3 0.0 collective-permute-done.6.from_left
  50.3 0.0 collective-permute-done.7.from_right
  50.3 0.4 widen_states.1.wide
  50.8 1.3 %collective-permute-done.2.from_left = f32[48,128]{1,0:T(8,128)S(1)} collective-permute-done((f32[48,128]{1,0:T(8,128)S(1)}, f32[48,128]{1,0:T(8,128)S(1)}, u32[]{:S(2)}, u32[]{:S(2)}) %collective-permute-start.2) | collective-permute-done | bytes 24608 | tf_op jit(solution)/shard_map/ppermute | solution.py:368
  52.0 0.0 collective-permute-done.3.from_right
  52.0 4.8 %adjoint_steps.1 = f32[384,128]{1,0:T(8,128)} custom-call(f32[8,48,128]{2,1,0:T(8,128)S(1)} %get-tuple-element.11.canvas, f32[4,48,128]{2,1,0:T(8,128)S(1)} %collective-permute-done.above, f32[4,48,128]{2,1,0:T(8,128)S(1)} %collective-permute-done.1.below, f32[48,128]{1,0:T(8,128)S(1)} %collective-permute-done.2.from_left, ...), custom_call_target="tpu_custom_call" | custom-call | tf_op jit(solution)/shard_map/adjoint_steps/pallas_call | solution.py:357
Async XLA Ops:
  0.0 13.8 %copy-start = (f32[2,2,3,16,8,128]{5,4,3,2,1,0:T(8,128)S(1)}, f32[2,2,3,16,8,128]{5,4,3,2,1,0:T(8,128)}, u32[]{:S(2)}) copy-start(f32[2,2,3,16,8,128]{5,4,3,2,1,0:T(8,128)} %param.10) | copy-start | bytes 2359300
  0.0 1.1 %copy-start.1 = (f32[3,16,2048]{2,1,0:T(8,128)S(1)}, f32[3,16,2048]{2,1,0:T(8,128)}, u32[]{:S(2)}) copy-start(f32[3,16,2048]{2,1,0:T(8,128)} %param.6) | copy-start | bytes 1179652
  1.1 0.7 %copy-start.2 = (f32[2,2048]{1,0:T(2,128)S(1)}, f32[2,2048]{1,0:T(2,128)}, u32[]{:S(2)}) copy-start(f32[2,2048]{1,0:T(2,128)} %frac.1) | copy-start | bytes 49156
  1.8 0.7 %copy-start.3 = (s32[2048,1]{0,1:T(1,128)S(1)}, s32[2048,1]{0,1:T(1,128)}, u32[]{:S(2)}) copy-start(s32[2048,1]{0,1:T(1,128)} %param.7) | copy-start | bytes 24580
  2.5 0.7 %copy-start.4 = (s32[2048]{0:T(1024)S(1)}, s32[2048]{0:T(1024)}, u32[]{:S(2)}) copy-start(s32[2048]{0:T(1024)} %param.8) | copy-start | bytes 24580
  3.2 47.1 %copy-start.5 = (f32[16]{0:T(128)S(1)}, f32[16]{0:T(128)}, u32[]{:S(2)}) copy-start(f32[16]{0:T(128)} %param.11) | copy-start | bytes 196
  6.4 30.1 %all-to-all-start = ((f32[16,104,128]{2,1,0:T(8,128)}), f32[16,104,128]{2,1,0:T(8,128)S(1)}, u32[]{:S(2)}, u32[]{:S(2)}) async-start(f32[16,104,128]{2,1,0:T(8,128)} %pack_points.1), calls=%async_computation | async-start | bytes 1703936 | tf_op jit(solution)/shard_map/all_to_all | solution.py:373
  13.9 28.0 %collective-permute-start.4 = (f32[10,48,128]{2,1,0:T(8,128)S(1)}, f32[10,48,128]{2,1,0:T(8,128)S(1)}, u32[]{:S(2)}, u32[]{:S(2)}) collective-permute-start(f32[10,48,128]{2,1,0:T(8,128)S(1)} %get-tuple-element.15), channel_id=1, source_target_pairs={{0,4},{4,8},{8,12},{12,0},{1,5},{5,9},{9,13},{13,1},{2,6},{6,10},{... | collective-permute-start | bytes 737288 | tf_op jit(solution)/shard_map/ppermute | solution.py:368
  14.4 27.5 %collective-permute-start.5 = (f32[10,48,128]{2,1,0:T(8,128)S(1)}, f32[10,48,128]{2,1,0:T(8,128)S(1)}, u32[]{:S(2)}, u32[]{:S(2)}) collective-permute-start(f32[10,48,128]{2,1,0:T(8,128)S(1)} %get-tuple-element.16), channel_id=1, source_target_pairs={{0,12},{4,0},{8,4},{12,8},{1,13},{5,1},{9,5},{13,9},{2,14},{6,2},{... | collective-permute-start | bytes 737288 | tf_op jit(solution)/shard_map/ppermute | solution.py:368
  40.1 6.1 %collective-permute-start = (f32[4,48,128]{2,1,0:T(8,128)S(1)}, f32[4,48,128]{2,1,0:T(8,128)S(1)}, u32[]{:S(2)}, u32[]{:S(2)}) collective-permute-start(f32[4,48,128]{2,1,0:T(8,128)S(1)} %get-tuple-element.12), channel_id=1, source_target_pairs={{0,4},{4,8},{8,12},{12,0},{1,5},{5,9},{9,13},{13,1},{2,6},{6,10},{... | collective-permute-start | bytes 294920 | tf_op jit(solution)/shard_map/ppermute | solution.py:368
  40.2 6.0 %collective-permute-start.1 = (f32[4,48,128]{2,1,0:T(8,128)S(1)}, f32[4,48,128]{2,1,0:T(8,128)S(1)}, u32[]{:S(2)}, u32[]{:S(2)}) collective-permute-start(f32[4,48,128]{2,1,0:T(8,128)S(1)} %get-tuple-element.13), channel_id=1, source_target_pairs={{0,12},{4,0},{8,4},{12,8},{1,13},{5,1},{9,5},{13,9},{2,14},{6,2},{... | collective-permute-start | bytes 294920 | tf_op jit(solution)/shard_map/ppermute | solution.py:368
  42.3 8.0 %collective-permute-start.6 = (f32[4,48,128]{2,1,0:T(8,128)S(1)}, f32[4,48,128]{2,1,0:T(8,128)S(1)}, u32[]{:S(2)}, u32[]{:S(2)}) collective-permute-start(f32[4,48,128]{2,1,0:T(8,128)S(1)} %state_edges.1), channel_id=1, source_target_pairs={{0,1},{1,2},{2,3},{3,0},{4,5},{5,6},{6,7},{7,4},{8,9},{9,10},{10,1... | collective-permute-start | bytes 294920 | tf_op jit(solution)/shard_map/ppermute | solution.py:368
  42.4 8.0 %collective-permute-start.7 = (f32[4,48,128]{2,1,0:T(8,128)S(1)}, f32[4,48,128]{2,1,0:T(8,128)S(1)}, u32[]{:S(2)}, u32[]{:S(2)}) collective-permute-start(f32[4,48,128]{2,1,0:T(8,128)S(1)} %state_edges.1), channel_id=1, source_target_pairs={{0,3},{1,0},{2,1},{3,2},{4,7},{5,4},{6,5},{7,6},{8,11},{9,8},{10,9... | collective-permute-start | bytes 294920 | tf_op jit(solution)/shard_map/ppermute | solution.py:368
  46.4 5.7 %collective-permute-start.2 = (f32[48,128]{1,0:T(8,128)S(1)}, f32[48,128]{1,0:T(8,128)S(1)}, u32[]{:S(2)}, u32[]{:S(2)}) collective-permute-start(f32[48,128]{1,0:T(8,128)S(1)} %adjoint_edges.1), channel_id=1, source_target_pairs={{0,1},{1,2},{2,3},{3,0},{4,5},{5,6},{6,7},{7,4},{8,9},{9,10},{10,1... | collective-permute-start | bytes 73736 | tf_op jit(solution)/shard_map/ppermute | solution.py:368
  46.4 5.6 %collective-permute-start.3 = (f32[48,128]{1,0:T(8,128)S(1)}, f32[48,128]{1,0:T(8,128)S(1)}, u32[]{:S(2)}, u32[]{:S(2)}) collective-permute-start(f32[48,128]{1,0:T(8,128)S(1)} %adjoint_edges.1), channel_id=1, source_target_pairs={{0,3},{1,0},{2,1},{3,2},{4,7},{5,4},{6,5},{7,6},{8,11},{9,8},{10,9... | collective-permute-start | bytes 73736 | tf_op jit(solution)/shard_map/ppermute | solution.py:368

commit v2 on v1

--- a/solution.py
+++ b/solution.py
@@ -27,74 +27,145 @@
     return lax.dot_general(a, b, (((1,), (1,)), ((), ())), preferred_element_type=F32)
 
 
-def pack_kernel(capacity, tile_count, tile_rows, columns, cot, dest, base, frac, out, ranks, onehot, high, low):
+def slot_blocks(cot, where, group, lane, groups, tile_rows, columns, onehot, high, low):
     channels, points = cot.shape
-    groups = out.shape[0]
-    target = dest[...]
-    corner = base[...]
+    corner = where[1:2, :]
     row = jnp.zeros_like(corner)
     for k in range(1, tile_rows - 1):
-        row = row + (corner >= k * (columns - 1)).astype(jnp.int32)
-    col = corner - row * (columns - 1)
-
+        row = row + (corner >= float(k * (columns - 1))).astype(F32)
+    col = corner - row * float(columns - 1)
+    coords = jnp.concatenate([row, col, where[2:, :]], axis=0)
+    data = jnp.concatenate([cot[...], coords, coords], axis=0)
+    data_high, data_low = split(data)
+    slots = lax.broadcasted_iota(jnp.int32, (GROUP, points), 0)
+    onehot[...] = (slots == lane).astype(F32).astype(BF16)
+    rows = channels + 8
+    for g in range(groups):
+        mine = (group == g).astype(F32).astype(BF16)
+        high[g * rows : (g + 1) * rows, :] = data_high * mine
+        low[g * rows : (g + 1) * rows, :] = data_low * mine
+    packed = dot_nt(high[...], onehot[...]) + dot_nt(low[...], onehot[...])
+    upper = lax.broadcasted_iota(jnp.int32, (8, LANES), 0) < 4
+    for g in range(groups):
+        block = packed[g * rows : (g + 1) * rows, :]
+        yield (
+            block[:channels, :LANES],
+            block[:channels, LANES:],
+            jnp.where(upper, block[channels:, :LANES], block[channels:, LANES:]),
+        )
+
+
+def count_ahead(target, tiles, base, place):
     before = (
         lax.broadcasted_iota(jnp.int32, (GROUP, GROUP), 0)
         < lax.broadcasted_iota(jnp.int32, (GROUP, GROUP), 1)
     ).astype(F32).astype(BF16)
-    tiles = lax.broadcasted_iota(jnp.int32, (tile_count, GROUP), 0)
-    first = (tiles * capacity).astype(F32)
-    count = jnp.zeros((tile_count, 1), F32)
-    for b in range(points // GROUP):
+    count = jnp.zeros((tiles.shape[0], 1), F32)
+    for b in range(target.shape[1] // GROUP):
         part = slice(b * GROUP, (b + 1) * GROUP)
         named = (tiles == target[:, part]).astype(F32)
         ahead = jnp.dot(named.astype(BF16), before, preferred_element_type=F32)
-        place = jnp.sum(named * (ahead + count + first), axis=0, keepdims=True)
+        found = jnp.sum(named * (ahead + count + base + 1.0), axis=0, keepdims=True)
         count = count + jnp.sum(named, axis=1, keepdims=True)
-        ranks[:, part] = place.astype(jnp.int32)
-    place = ranks[...]
-    group = place // GROUP
-    lane = place - group * GROUP
-    slots = lax.broadcasted_iota(jnp.int32, (GROUP, points), 0)
-    onehot[...] = (slots == lane).astype(F32).astype(BF16)
-
-    coords = jnp.concatenate([row.astype(F32), col.astype(F32), frac[...]], axis=0)
-    data = jnp.concatenate([cot[...], coords, coords], axis=0)
-    data_high, data_low = split(data)
-    rows = data.shape[0]
-    for g in range(groups):
-        mine = (group == g).astype(F32).astype(BF16)
-        high[g * rows : (g + 1) * rows, :] = data_high * mine
-        low[g * rows : (g + 1) * rows, :] = data_low * mine
-    upper = lax.broadcasted_iota(jnp.int32, (8, LANES), 0) < 4
-    packed = dot_nt(high[...], onehot[...]) + dot_nt(low[...], onehot[...])
-    for g in range(groups):
-        block = packed[g * rows : (g + 1) * rows, :]
-        out[g, :channels, :] = block[:channels, :LANES]
-        out[g, channels : 2 * channels, :] = block[:channels, LANES:]
-        out[g, 2 * channels :, :] = jnp.where(upper, block[channels:, :LANES], block[channels:, LANES:])
-
-
-def pack(cot, dest, base, frac, capacity, tile_count, tile_rows, columns):
+        place[:, part] = found.astype(jnp.int32) - 1
+
+
+def store_block(out, at, pieces):
+    channels = pieces[0].shape[0]
+    out[at : at + channels, :] = pieces[0]
+    out[at + channels : at + 2 * channels, :] = pieces[1]
+    out[at + 2 * channels : at + 2 * channels + 8, :] = pieces[2]
+
+
+def pack_scratch(channels, points, groups):
+    return [
+        pltpu.VMEM((1, points), jnp.int32),
+        pltpu.VMEM((GROUP, points), BF16),
+        pltpu.VMEM((groups * (channels + 8), points), BF16),
+        pltpu.VMEM((groups * (channels + 8), points), BF16),
+    ]
+
+
+def pack_all_kernel(capacity, tile_count, tile_rows, columns, cot, where, out, place, onehot, high, low):
+    tiles = lax.broadcasted_iota(jnp.int32, (tile_count, GROUP), 0)
+    count_ahead(where[0:1, :].astype(jnp.int32), tiles, (tiles * capacity).astype(F32), place)
+    slot = place[...]
+    group = slot // GROUP
+    blocks = slot_blocks(
+        cot, where, group, slot - group * GROUP, out.shape[0], tile_rows, columns, onehot, high, low
+    )
+    for g, pieces in enumerate(blocks):
+        store_block(out.at[g], 0, pieces)
+
+
+def pack_all(cot, where, capacity, tile_count, tile_rows, columns):
     channels, points = cot.shape
     groups = tile_count * capacity // GROUP
-    rows = channels + 8
-    return pl.pallas_call(
-        functools.partial(pack_kernel, capacity, tile_count, tile_rows, columns),
+    return pl.pallas_call(
+        functools.partial(pack_all_kernel, capacity, tile_count, tile_rows, columns),
         out_shape=jax.ShapeDtypeStruct((groups, 2 * channels + 8, LANES), F32),
-        scratch_shapes=[
-            pltpu.VMEM((1, points), jnp.int32),
-            pltpu.VMEM((GROUP, points), BF16),
-            pltpu.VMEM((groups * rows, points), BF16),
-            pltpu.VMEM((groups * rows, points), BF16),
-        ],
+        scratch_shapes=pack_scratch(channels, points, groups),
         compiler_params=PARAMS,
         name="pack_points",
-    )(cot, dest, base, frac)
-
-
-def scatter_kernel(got, canvas, north, south, high, low, weight):
-    groups = got.shape[0]
-    tile_rows, channels, columns = canvas.shape
+    )(cot, where)
+
+
+def chip_offsets(n_row, n_col):
+    offsets = [(0, 0)]
+    for step in sorted(range(n_col), key=lambda z: -(z & -z) if z else 1):
+        offsets += [(other, step) for other in range(0, n_row, 2) if (other, step) != (0, 0)]
+    return offsets
+
+
+def pack_chips_kernel(offsets, n_col, tile_rows, columns, cot, where, *refs):
+    outs, (place, onehot, high, low) = refs[:-4], refs[-4:]
+    own = None
+    if len(outs) > 1:
+        own, outs = outs[0], outs[1:]
+    groups = len(offsets)
+    at_row, at_col = lax.axis_index("frow"), lax.axis_index("fcol")
+    index = lax.broadcasted_iota(jnp.int32, (groups, GROUP), 0)
+    tiles = jnp.zeros((groups, GROUP), jnp.int32)
+    for g, (df, dz) in enumerate(offsets):
+        tiles = jnp.where(index == g, (at_row ^ df) * n_col + (at_col ^ dz), tiles)
+    count_ahead(where[0:1, :].astype(jnp.int32), tiles, (index * GROUP).astype(F32), place)
+    slot = place[...]
+    group = jnp.where(slot < 0, groups, slot // GROUP)
+    blocks = slot_blocks(
+        cot, where, group, slot - group * GROUP, groups, tile_rows, columns, onehot, high, low
+    )
+    for g, pieces in enumerate(blocks):
+        if own is None:
+            store_block(outs[0].at[g], 0, pieces)
+        else:
+            size = own.shape[1]
+            outs[g][:size, :] = own[g]
+            store_block(outs[g], size, pieces)
+
+
+def pack_chips(cot, where, own, offsets, n_col, tile_rows, columns):
+    channels, points = cot.shape
+    rows, groups = 2 * channels + 8, len(offsets)
+    if own is None:
+        shapes = jax.ShapeDtypeStruct((groups, rows, LANES), F32)
+    else:
+        shapes = [jax.ShapeDtypeStruct((2 * rows, LANES), F32)] * groups
+    return pl.pallas_call(
+        functools.partial(pack_chips_kernel, offsets, n_col, tile_rows, columns),
+        out_shape=shapes,
+        scratch_shapes=pack_scratch(channels, points, groups),
+        compiler_params=PARAMS,
+        name="pack_own" if own is None else "pack_partner",
+    )(cot, where, *([] if own is None else [own]))
+
+
+def scatter_kernel(count, first, last, *refs):
+    blocks, refs = refs[:count], refs[count:]
+    if not first:
+        total, refs = refs[0], refs[1:]
+    outs, (high, low, weight) = refs[:-3], refs[-3:]
+    tile_rows, channels, columns = outs[0].shape
+    rows = 2 * channels + 8
     cells = lax.broadcasted_iota(jnp.int32, (columns, LANES), 0).astype(F32)
     lines = lax.broadcasted_iota(jnp.int32, (tile_rows, LANES), 0).astype(F32)
 
@@ -102,40 +173,46 @@
         away = index - corner
         return jnp.where(away == 0.0, 1.0 - fraction, jnp.where(away == 1.0, fraction, 0.0))
 
-    for g in range(groups):
-        for half in range(2):
-            part = slice((2 * g + half) * LANES, (2 * g + half + 1) * LANES)
-            coords = got[g, 2 * channels + 4 * half : 2 * channels + 4 * half + 4, :]
-            row, col, along_rows, along_cols = (coords[k : k + 1, :] for k in range(4))
-            weight_high, weight_low = split(hat(cells, col, along_cols))
-            weight[:columns, part] = weight_high
-            weight[columns:, part] = weight_low
-            values = got[g, half * channels : (half + 1) * channels, :]
-            row_weight = hat(lines, row, along_rows)
-            for r in range(tile_rows):
-                product_high, product_low = split(values * row_weight[r : r + 1, :])
-                high[r * channels : (r + 1) * channels, part] = product_high
-                low[r * channels : (r + 1) * channels, part] = product_low
+    at = 0
+    for block in blocks:
+        for source in range(block.shape[0] // rows):
+            for half in range(2):
+                part = slice(at, at + LANES)
+                at += LANES
+                begin = source * rows + 2 * channels + 4 * half
+                coords = block[begin : begin + 4, :]
+                row, col, along_rows, along_cols = (coords[k : k + 1, :] for k in range(4))
+                weight_high, weight_low = split(hat(cells, col, along_cols))
+                weight[:columns, part] = weight_high
+                weight[columns:, part] = weight_low
+                begin = source * rows + half * channels
+                values = block[begin : begin + channels, :]
+                row_weight = hat(lines, row, along_rows)
+                for r in range(tile_rows):
+                    product_high, product_low = split(values * row_weight[r : r + 1, :])
+                    high[r * channels : (r + 1) * channels, part] = product_high
+                    low[r * channels : (r + 1) * channels, part] = product_low
     both = dot_nt(high[...], weight[...])
-    total = both[:, :columns] + both[:, columns:] + dot_nt(low[...], weight[:columns, :])
+    sums = both[:, :columns] + both[:, columns:] + dot_nt(low[...], weight[:columns, :])
     for r in range(tile_rows):
-        line = total[r * channels : (r + 1) * channels, :]
-        canvas[r] = line
-        if r < HALO:
-            north[r] = line
-        if r >= tile_rows - HALO:
-            south[r - tile_rows + HALO] = line
-
-
-def scatter(got, channels, tile_rows, columns):
-    slots = got.shape[0] * GROUP
-    return pl.pallas_call(
-        scatter_kernel,
-        out_shape=(
-            jax.ShapeDtypeStruct((tile_rows, channels, columns), F32),
-            jax.ShapeDtypeStruct((HALO, channels, columns), F32),
-            jax.ShapeDtypeStruct((HALO, channels, columns), F32),
-        ),
+        line = sums[r * channels : (r + 1) * channels, :]
+        if not first:
+            line = line + total[r]
+        outs[0][r] = line
+        if last and r < HALO:
+            outs[1][r] = line
+        if last and r >= tile_rows - HALO:
+            outs[2][r - tile_rows + HALO] = line
+
+
+def scatter(blocks, total, last, channels, tile_rows, columns):
+    slots = sum(block.shape[0] for block in blocks) // (2 * channels + 8) * GROUP
+    shapes = [jax.ShapeDtypeStruct((tile_rows, channels, columns), F32)]
+    if last:
+        shapes += [jax.ShapeDtypeStruct((HALO, channels, columns), F32)] * 2
+    return pl.pallas_call(
+        functools.partial(scatter_kernel, len(blocks), total is None, last),
+        out_shape=shapes,
         scratch_shapes=[
             pltpu.VMEM((tile_rows * channels, slots), BF16),
             pltpu.VMEM((tile_rows * channels, slots), BF16),
@@ -143,7 +220,7 @@
         ],
         compiler_params=PARAMS,
         name="scatter_points",
-    )(got)
+    )(*blocks, *([] if total is None else [total]))
 
 
 def edge_columns(lines):
@@ -368,9 +445,7 @@
     return lax.ppermute(values, axis, [(i, (i + by) % count) for i in range(count)])
 
 
-def to_partners(packed, channels, capacity, tile_count):
-    if capacity == GROUP:
-        return lax.all_to_all(packed, ("frow", "fcol"), split_axis=0, concat_axis=0, tiled=True)
+def from_everyone(packed, channels, capacity, tile_count):
     groups = packed.shape[0]
     rows = channels + 4
     halves = [
@@ -391,9 +466,15 @@
     )
 
 
+def exchanged(values, offset, n_row, n_col):
+    df, dz = offset
+    pairs = [(f * n_col + z, (f ^ df) * n_col + (z ^ dz)) for f in range(n_row) for z in range(n_col)]
+    return lax.ppermute(values, ("frow", "fcol"), pairs)
+
+
 def per_device(latlon_cot, dest_tile, base_cell, corner_frac, saved_states, gravity):
-    n_row = lax.axis_size("frow")
-    tile_count = n_row * lax.axis_size("fcol")
+    n_row, n_col = lax.axis_size("frow"), lax.axis_size("fcol")
+    tile_count = n_row * n_col
     levels = gravity.shape[0]
     tile_rows = saved_states.shape[4]
     columns = saved_states.shape[5]
@@ -401,17 +482,30 @@
     points = base_cell.shape[0]
     capacity = 2 * points // tile_count
 
-    packed = pack(
-        latlon_cot.reshape(channels, points),
-        dest_tile.reshape(1, points),
-        base_cell.reshape(1, points),
-        corner_frac,
-        capacity,
-        tile_count,
-        tile_rows,
-        columns,
-    )
-    got = to_partners(packed, channels, capacity, tile_count)
+    cot = latlon_cot.reshape(channels, points)
+    where = jnp.concatenate(
+        [dest_tile.reshape(1, points).astype(F32), base_cell.reshape(1, points).astype(F32), corner_frac], axis=0
+    )
+    size = (channels, tile_rows, columns)
+    if capacity == GROUP and n_row & (n_row - 1) == 0 and n_col & (n_col - 1) == 0:
+        offsets = chip_offsets(n_row, n_col)
+        partner_cot = exchanged(cot, (1, 0), n_row, n_col)
+        partner_where = exchanged(where, (1, 0), n_row, n_col)
+        own = pack_chips(cot, where, None, offsets, n_col, tile_rows, columns)
+        packed = pack_chips(partner_cot, partner_where, own, offsets, n_col, tile_rows, columns)
+        got = [packed[0]] + [
+            exchanged(block, offset, n_row, n_col) for block, offset in zip(packed[1:], offsets[1:])
+        ]
+        total = None
+        for begin, end in ((0, 3), (3, 6), (6, len(got))):
+            last = end == len(got)
+            canvas = scatter(got[begin:end], total, last, *size)
+            total = canvas[0]
+        canvas, north_rim, south_rim = canvas
+    else:
+        packed = pack_all(cot, where, capacity, tile_count, tile_rows, columns)
+        got = from_everyone(packed, channels, capacity, tile_count)
+        canvas, north_rim, south_rim = scatter([got.reshape(-1, LANES)], None, True, *size)
 
     turned, north, south = turn_states(
         saved_states.reshape(4, channels * tile_rows, columns), (3, 2, 1, 0), channels, tile_rows, columns
@@ -423,9 +517,8 @@
         turned, state_above, state_below, shifted(edges, "fcol", 1), shifted(edges, "fcol", -1), n_row
     )
 
-    canvas, north, south = scatter(got, channels, tile_rows, columns)
-    above = shifted(south, "frow", 1)
-    below = shifted(north, "frow", -1)
+    above = shifted(south_rim, "frow", 1)
+    below = shifted(north_rim, "frow", -1)
     edges = adjoint_edges(canvas, above, below, n_row)
     result = steps(
         canvas,

time: 57.2 us -> 50.6 us (0.88)
  waiting for transfers between devices: 22.1 us -> 7.33 us
  starting transfers between devices: 18.7 us -> 26.4 us
  other arithmetic: 0 us -> 2.14 us
  local copies, waits for them, and re-layouts: 3.27 us -> 2.21 us
  Pallas kernels: 12.8 us -> 12.1 us
    all_to_all x1 -> x0, waiting for transfers between devices: 20.8 us -> none  [to_partners(): lax.all_to_all(packed, ('frow', 'fcol'), split_axis=0, concat_axis=0, til...]
    ppermute x0 -> x9, starting transfers between devices: none -> 16.3 us  [exchanged(): return lax.ppermute(values, ('frow', 'fcol'), pairs)]
    all_to_all x1 -> x0, starting transfers between devices: 7.36 us -> none  [to_partners(): lax.all_to_all(packed, ('frow', 'fcol'), split_axis=0, concat_axis=0, til...]
    ppermute x0 -> x9, waiting for transfers between devices: none -> 5.93 us  [exchanged(): return lax.ppermute(values, ('frow', 'fcol'), pairs)]
    convert_element_type x0 -> x2, other arithmetic: none -> 1.4 us  [the longest x1 0.7 us: per_device(): dest_tile.reshape(1, points).astype(F32)]
    ppermute x8, starting transfers between devices: 11.3 us -> 10.1 us  [shifted(): lax.ppermute(values, axis, [(i, (i + by) % count) for i in range(count)])]
    unnamed x12 -> x6, local copies, waits for them, and re-layouts: 3.19 us -> 2.13 us
    concatenate x0 -> x1, other arithmetic: none -> 0.74 us  [per_device(): jnp.concatenate([dest_tile.reshape(1, points).astype(F32), base_cell.resh...]
  transfers between devices with their start and end apart: 9 -> 17, of which waited for: 2 -> 5; matrix products, arithmetic and copies ran while one was open for 0% -> 4% of each run, Pallas kernels for 8% -> 12%
where the time goes in v2:
time: 50.6 us; the launch traced here: 50.3 us
  starting transfers between devices  26.4 us (52%)
  Pallas kernels  12.1 us (24%)
  waiting for transfers between devices  7.33 us (14%)
  local copies, waits for them, and re-layouts  2.21 us (4%)
  other arithmetic  2.14 us (4%)
    ppermute x9, starting transfers between devices, exchanged(): return lax.ppermute(values, ('frow', 'fcol'), pairs)  16.3 us
    ppermute x8, starting transfers between devices, shifted(): lax.ppermute(values, axis, [(i, (i + by) % count) for i in range(count)])  10.1 us
    ppermute x9, waiting for transfers between devices, exchanged(): return lax.ppermute(values, ('frow', 'fcol'), pairs)  5.93 us
    pallas_call x1, Pallas kernels, steps(): pl.pallas_call(functools.partial(steps_kernel, n_row), out_shape=jax.Shap...  4.83 us
    pallas_call x3, Pallas kernels, scatter(): pl.pallas_call(functools.partial(scatter_kernel, len(blocks), total is No...  3.41 us
    pallas_call x2, Pallas kernels, pack_chips(): pl.pallas_call(functools.partial(pack_chips_kernel, offsets, n_col, tile_...  2.73 us
    unnamed x6, local copies, waits for them, and re-layouts  2.13 us
    ppermute x8, waiting for transfers between devices, shifted(): lax.ppermute(values, axis, [(i, (i + by) % count) for i in range(count)])  1.4 us
  transfers between devices with their start and end apart: 17, of which 5 were waited for; matrix products, arithmetic and copies ran while one was open for 4% of the time, Pallas kernels for 12%

profile of v2, /device:TPU:0, one launch (start us, length us, event | category | flops | bytes accessed | tf_op | source)
XLA Modules:
  0.0 50.3 jit_solution(14882234030447975784)
XLA Ops:
  0.0 0.5 collective-permute-start
  0.5 0.7 %convert_bitcast_fusion = f32[1,2048]{1,0:T(1,128)S(1)} fusion(s32[2048,1]{0,1:T(1,128)} %param.7), kind=kLoop, calls=%fused_computation.1 | loop fusion | flops 2048 | bytes 16384 | tf_op jit(solution)/shard_map/convert_element_type | solution.py:487
  1.2 0.7 %convert_element_type.22 = f32[2048]{0:T(1024)S(1)} convert(s32[2048]{0:T(1024)} %param.8) | non-fusion elementwise | flops 2048 | bytes 16384 | tf_op jit(solution)/shard_map/convert_element_type | solution.py:487
  1.9 0.7 %pad_maximum_fusion.where = f32[4,2048]{1,0:T(4,128)S(1)} fusion(f32[2,2048]{1,0:T(2,128)} %param.9, f32[1,2048]{1,0:T(1,128)S(1)} %bitcast.10, f32[1,2048]{1,0:T(1,128)S(1)} %convert_bitcast_fusion), kind=kLoop, calls=%fused_computation | loop fusion | flops 16384 | bytes 65536 | tf_op jit(solution)/shard_map/concatenate | solution.py:486
  2.6 0.1 collective-permute-start.1
  2.7 1.0 %copy-done.1 = f32[3,16,2048]{2,1,0:T(8,128)S(1)} copy-done((f32[3,16,2048]{2,1,0:T(8,128)S(1)}, f32[3,16,2048]{2,1,0:T(8,128)}, u32[]{:S(2)}) %copy-start.1) | copy-done | bytes 393240
  3.7 1.4 %pack_own.1.refs_0_ = f32[8,104,128]{2,1,0:T(8,128)S(1)} custom-call(f32[48,2048]{1,0:T(8,128)S(1)} %bitcast.9, f32[4,2048]{1,0:T(4,128)S(1)} %pad_maximum_fusion.where), custom_call_target="tpu_custom_call" | custom-call | tf_op jit(solution)/shard_map/pack_own/pallas_call | solution.py:153
  5.1 0.0 collective-permute-done.1.where
  5.1 0.0 collective-permute-done.cot
  5.1 1.4 %pack_partner.1 = (f32[208,128]{1,0:T(8,128)S(1)}, f32[208,128]{1,0:T(8,128)S(1)}, f32[208,128]{1,0:T(8,128)S(1)}, f32[208,128]{1,0:T(8,128)S(1)}, f32[208,128]{...) custom-call(f32[48,2048]{1,0:T(8,128)S(1)} %collective-permute-done.cot, ...), custom_call_target="tpu_custom_call" | custom-call | tf_op jit(solution)/shard_map/pack_partner/pallas_call | solution.py:153
  6.5 4.1 %collective-permute-start.7 = (f32[208,128]{1,0:T(8,128)S(1)}, f32[208,128]{1,0:T(8,128)S(1)}, u32[]{:S(2)}, u32[]{:S(2)}) collective-permute-start(f32[208,128]{1,0:T(8,128)S(1)} %get-tuple-element.25), channel_id=1, source_target_pairs={{0,2},{1,3},{2,0},{3,1},{4,6},{5,7},{6,4},{7,5},{8,10},{9,11},{10,... | collective-permute-start | bytes 319496 | tf_op jit(solution)/shard_map/ppermute | solution.py:472
  10.6 1.1 %copy-done = f32[2,2,3,16,8,128]{5,4,3,2,1,0:T(8,128)S(1)} copy-done((f32[2,2,3,16,8,128]{5,4,3,2,1,0:T(8,128)S(1)}, f32[2,2,3,16,8,128]{5,4,3,2,1,0:T(8,128)}, u32[]{:S(2)}) %copy-start) | copy-done | bytes 786456
  11.7 0.1 turn_states.1
  11.9 0.1 collective-permute-start.13
  11.9 1.7 %collective-permute-start.14 = (f32[10,48,128]{2,1,0:T(8,128)S(1)}, f32[10,48,128]{2,1,0:T(8,128)S(1)}, u32[]{:S(2)}, u32[]{:S(2)}) collective-permute-start(f32[10,48,128]{2,1,0:T(8,128)S(1)} %get-tuple-element.32), channel_id=1, source_target_pairs={{0,12},{4,0},{8,4},{12,8},{1,13},{5,1},{9,5},{13,9},{2,14},{6,2},{... | collective-permute-start | bytes 737288 | tf_op jit(solution)/shard_map/ppermute | solution.py:445
  13.7 1.2 %collective-permute-start.8 = (f32[208,128]{1,0:T(8,128)S(1)}, f32[208,128]{1,0:T(8,128)S(1)}, u32[]{:S(2)}, u32[]{:S(2)}) collective-permute-start(f32[208,128]{1,0:T(8,128)S(1)} %get-tuple-element.26), channel_id=1, source_target_pairs={{0,10},{1,11},{2,8},{3,9},{4,14},{5,15},{6,12},{7,13},{8,2},{9,3},... | collective-permute-start | bytes 319496 | tf_op jit(solution)/shard_map/ppermute | solution.py:472
  14.9 1.6 %collective-permute-start.4 = (f32[208,128]{1,0:T(8,128)S(1)}, f32[208,128]{1,0:T(8,128)S(1)}, u32[]{:S(2)}, u32[]{:S(2)}) collective-permute-start(f32[208,128]{1,0:T(8,128)S(1)} %get-tuple-element.21), channel_id=1, source_target_pairs={{0,1},{1,0},{2,3},{3,2},{4,5},{5,4},{6,7},{7,6},{8,9},{9,8},{10,11... | collective-permute-start | bytes 319496 | tf_op jit(solution)/shard_map/ppermute | solution.py:472
  16.5 3.5 %collective-permute-start.5 = (f32[208,128]{1,0:T(8,128)S(1)}, f32[208,128]{1,0:T(8,128)S(1)}, u32[]{:S(2)}, u32[]{:S(2)}) collective-permute-start(f32[208,128]{1,0:T(8,128)S(1)} %get-tuple-element.22), channel_id=1, source_target_pairs={{0,9},{1,8},{2,11},{3,10},{4,13},{5,12},{6,15},{7,14},{8,1},{9,0},... | collective-permute-start | bytes 319496 | tf_op jit(solution)/shard_map/ppermute | solution.py:472
  20.0 2.6 %collective-permute-done.8.refs_2_ = f32[208,128]{1,0:T(8,128)S(1)} collective-permute-done((f32[208,128]{1,0:T(8,128)S(1)}, f32[208,128]{1,0:T(8,128)S(1)}, u32[]{:S(2)}, u32[]{:S(2)}) %collective-permute-start.8) | collective-permute-done | bytes 106528 | tf_op jit(solution)/shard_map/ppermute | solution.py:472
  22.6 2.6 %collective-permute-start.6 = (f32[208,128]{1,0:T(8,128)S(1)}, f32[208,128]{1,0:T(8,128)S(1)}, u32[]{:S(2)}, u32[]{:S(2)}) collective-permute-start(f32[208,128]{1,0:T(8,128)S(1)} %get-tuple-element.23), channel_id=1, source_target_pairs={{0,3},{1,2},{2,1},{3,0},{4,7},{5,6},{6,5},{7,4},{8,11},{9,10},{10,... | collective-permute-start | bytes 319496 | tf_op jit(solution)/shard_map/ppermute | solution.py:472
  25.2 0.0 collective-permute-done.4.refs_0_
  25.2 2.1 %collective-permute-start.2 = (f32[208,128]{1,0:T(8,128)S(1)}, f32[208,128]{1,0:T(8,128)S(1)}, u32[]{:S(2)}, u32[]{:S(2)}) collective-permute-start(f32[208,128]{1,0:T(8,128)S(1)} %get-tuple-element.19), channel_id=1, source_target_pairs={{0,11},{1,10},{2,9},{3,8},{4,15},{5,14},{6,13},{7,12},{8,3},{9,2},... | collective-permute-start | bytes 319496 | tf_op jit(solution)/shard_map/ppermute | solution.py:472
  27.3 0.6 %collective-permute-start.3 = (f32[208,128]{1,0:T(8,128)S(1)}, f32[208,128]{1,0:T(8,128)S(1)}, u32[]{:S(2)}, u32[]{:S(2)}) collective-permute-start(f32[208,128]{1,0:T(8,128)S(1)} %get-tuple-element.20), channel_id=1, source_target_pairs={{0,8},{1,9},{2,10},{3,11},{4,12},{5,13},{6,14},{7,15},{8,0},{9,1},... | collective-permute-start | bytes 319496 | tf_op jit(solution)/shard_map/ppermute | solution.py:472
  27.9 1.2 %scatter_points.3.refs_3_ = f32[8,48,128]{2,1,0:T(8,128)S(1)} custom-call(f32[208,128]{1,0:T(8,128)S(1)} %get-tuple-element.24.refs_0_, f32[208,128]{1,0:T(8,128)S(1)} %collective-permute-done.7.refs_1_, f32[208,128]{1,0:T(8,128)S(1)} %collective-permute-done.8.refs_2_), custom_call_target="tpu_custom_call" | custom-call | tf_op jit(solution)/shard_map/scatter_points/pallas_call | solution.py:213
  29.1 0.1 collective-permute-done.6.refs_2_
  29.2 1.2 %scatter_points.4.refs_2_ = f32[8,48,128]{2,1,0:T(8,128)S(1)} custom-call(f32[208,128]{1,0:T(8,128)S(1)} %collective-permute-done.4.refs_0_, f32[208,128]{1,0:T(8,128)S(1)} %collective-permute-done.5.refs_1_, f32[208,128]{1,0:T(8,128)S(1)} %collective-permute-done.6.refs_2_, f32[8,48,128]{2,1,0:T(8,128)S(1)} %scatter_points.3.refs_3_), custom_call_target="tpu_custom_call" | custom-call | tf_op jit(solution)/shard_map/scatter_points/pallas_call | solution.py:213
  30.4 2.2 %collective-permute-done.2.refs_0_ = f32[208,128]{1,0:T(8,128)S(1)} collective-permute-done((f32[208,128]{1,0:T(8,128)S(1)}, f32[208,128]{1,0:T(8,128)S(1)}, u32[]{:S(2)}, u32[]{:S(2)}) %collective-permute-start.2) | collective-permute-done | bytes 106528 | tf_op jit(solution)/shard_map/ppermute | solution.py:472
  32.6 1.0 %collective-permute-done.3.refs_1_ = f32[208,128]{1,0:T(8,128)S(1)} collective-permute-done((f32[208,128]{1,0:T(8,128)S(1)}, f32[208,128]{1,0:T(8,128)S(1)}, u32[]{:S(2)}, u32[]{:S(2)}) %collective-permute-start.3) | collective-permute-done | bytes 106528 | tf_op jit(solution)/shard_map/ppermute | solution.py:472
  33.6 1.0 %scatter_points.5 = (f32[8,48,128]{2,1,0:T(8,128)S(1)}, f32[4,48,128]{2,1,0:T(8,128)S(1)}, f32[4,48,128]{2,1,0:T(8,128)S(1)}) custom-call(f32[208,128]{1,0:T(8,128)S(1)} %collective-permute-done.2.refs_0_, f32[208,128]{1,0:T(8,128)S(1)} %collective-permute-done.3.refs_1_, f32[8,48,128]{2,1,0:T(8,128)S(1)} %scatter_points.4.refs_2_), custom_call_target="tpu_custom_call" | custom-call | tf_op jit(solution)/shard_map/scatter_points/pallas_call | solution.py:213
  34.6 0.1 collective-permute-start.10
  34.7 0.5 collective-permute-start.9
  35.2 0.0 collective-permute-done.13.above
  35.2 0.0 collective-permute-done.14.below
  35.2 0.4 state_edges.1
  35.6 0.9 %collective-permute-start.15 = (f32[4,48,128]{2,1,0:T(8,128)S(1)}, f32[4,48,128]{2,1,0:T(8,128)S(1)}, u32[]{:S(2)}, u32[]{:S(2)}) collective-permute-start(f32[4,48,128]{2,1,0:T(8,128)S(1)} %state_edges.1), channel_id=1, source_target_pairs={{0,1},{1,2},{2,3},{3,0},{4,5},{5,6},{6,7},{7,4},{8,9},{9,10},{10,1... | collective-permute-start | bytes 294920 | tf_op jit(solution)/shard_map/ppermute | solution.py:445
  36.5 3.0 %collective-permute-start.16 = (f32[4,48,128]{2,1,0:T(8,128)S(1)}, f32[4,48,128]{2,1,0:T(8,128)S(1)}, u32[]{:S(2)}, u32[]{:S(2)}) collective-permute-start(f32[4,48,128]{2,1,0:T(8,128)S(1)} %state_edges.1), channel_id=1, source_target_pairs={{0,3},{1,0},{2,1},{3,2},{4,7},{5,4},{6,5},{7,6},{8,11},{9,8},{10,9... | collective-permute-start | bytes 294920 | tf_op jit(solution)/shard_map/ppermute | solution.py:445
  39.5 0.0 collective-permute-done.10.below
  39.5 0.0 collective-permute-done.9.above
  39.5 0.2 adjoint_edges.1
  39.6 0.4 collective-permute-start.11
  40.0 3.5 %collective-permute-start.12 = (f32[48,128]{1,0:T(8,128)S(1)}, f32[48,128]{1,0:T(8,128)S(1)}, u32[]{:S(2)}, u32[]{:S(2)}) collective-permute-start(f32[48,128]{1,0:T(8,128)S(1)} %adjoint_edges.1), channel_id=1, source_target_pairs={{0,3},{1,0},{2,1},{3,2},{4,7},{5,4},{6,5},{7,6},{8,11},{9,8},{10,9... | collective-permute-start | bytes 73736 | tf_op jit(solution)/shard_map/ppermute | solution.py:445
  43.5 0.1 copy.7.gravity
  43.6 0.0 collective-permute-done.15.from_left
  43.6 0.0 collective-permute-done.16.from_right
  43.6 0.4 widen_states.1.wide
  44.0 1.4 %collective-permute-done.11.from_left = f32[48,128]{1,0:T(8,128)S(1)} collective-permute-done((f32[48,128]{1,0:T(8,128)S(1)}, f32[48,128]{1,0:T(8,128)S(1)}, u32[]{:S(2)}, u32[]{:S(2)}) %collective-permute-start.11) | collective-permute-done | bytes 24608 | tf_op jit(solution)/shard_map/ppermute | solution.py:445
  45.4 0.0 collective-permute-done.12.from_right
  45.4 4.8 %adjoint_steps.1 = f32[384,128]{1,0:T(8,128)} custom-call(f32[8,48,128]{2,1,0:T(8,128)S(1)} %get-tuple-element.27.canvas, f32[4,48,128]{2,1,0:T(8,128)S(1)} %collective-permute-done.9.above, f32[4,48,128]{2,1,0:T(8,128)S(1)} %collective-permute-done.10.below, f32[48,128]{1,0:T(8,128)S(1)} %collective-permute-done.11.from_left, ...), custom_call_target="tpu_custom_call" | custom-call | tf_op jit(solution)/shard_map/adjoint_steps/pallas_call | solution.py:434
  (6 shorter events, 0.0 us)
Async XLA Ops:
  0.0 43.5 %copy-start.2 = (f32[16]{0:T(128)S(1)}, f32[16]{0:T(128)}, u32[]{:S(2)}) copy-start(f32[16]{0:T(128)} %param.11) | copy-start | bytes 196
  0.0 5.1 %collective-permute-start = (f32[48,2048]{1,0:T(8,128)}, f32[48,2048]{1,0:T(8,128)S(1)}, u32[]{:S(2)}, u32[]{:S(2)}) collective-permute-start(f32[48,2048]{1,0:T(8,128)} %bitcast.8), channel_id=1, source_target_pairs={{0,4},{1,5},{2,6},{3,7},{4,0},{5,1},{6,2},{7,3},{8,12},{9,13},{10,... | collective-permute-start | bytes 1179656 | tf_op jit(solution)/shard_map/ppermute | solution.py:472
  2.6 2.5 %collective-permute-start.1 = (f32[4,2048]{1,0:T(4,128)S(1)}, f32[4,2048]{1,0:T(4,128)S(1)}, u32[]{:S(2)}, u32[]{:S(2)}) collective-permute-start(f32[4,2048]{1,0:T(4,128)S(1)} %pad_maximum_fusion.where), channel_id=1, source_target_pairs={{0,4},{1,5},{2,6},{3,7},{4,0},{5,1},{6,2},{7,3},{8,12},{9,13},{10,... | collective-permute-start | bytes 98312 | tf_op jit(solution)/shard_map/ppermute | solution.py:472
  2.7 1.0 %copy-start.1 = (f32[3,16,2048]{2,1,0:T(8,128)S(1)}, f32[3,16,2048]{2,1,0:T(8,128)}, u32[]{:S(2)}) copy-start(f32[3,16,2048]{2,1,0:T(8,128)} %param.6) | copy-start | bytes 1179652
  6.5 10.0 %collective-permute-start.7 = (f32[208,128]{1,0:T(8,128)S(1)}, f32[208,128]{1,0:T(8,128)S(1)}, u32[]{:S(2)}, u32[]{:S(2)}) collective-permute-start(f32[208,128]{1,0:T(8,128)S(1)} %get-tuple-element.25), channel_id=1, source_target_pairs={{0,2},{1,3},{2,0},{3,1},{4,6},{5,7},{6,4},{7,5},{8,10},{9,11},{10,... | collective-permute-start | bytes 319496 | tf_op jit(solution)/shard_map/ppermute | solution.py:472
  10.6 1.1 %copy-start = (f32[2,2,3,16,8,128]{5,4,3,2,1,0:T(8,128)S(1)}, f32[2,2,3,16,8,128]{5,4,3,2,1,0:T(8,128)}, u32[]{:S(2)}) copy-start(f32[2,2,3,16,8,128]{5,4,3,2,1,0:T(8,128)} %param.10) | copy-start | bytes 2359300
  11.9 23.3 %collective-permute-start.13 = (f32[10,48,128]{2,1,0:T(8,128)S(1)}, f32[10,48,128]{2,1,0:T(8,128)S(1)}, u32[]{:S(2)}, u32[]{:S(2)}) collective-permute-start(f32[10,48,128]{2,1,0:T(8,128)S(1)} %get-tuple-element.31), channel_id=1, source_target_pairs={{0,4},{4,8},{8,12},{12,0},{1,5},{5,9},{9,13},{13,1},{2,6},{6,10},{... | collective-permute-start | bytes 737288 | tf_op jit(solution)/shard_map/ppermute | solution.py:445
  11.9 23.2 %collective-permute-start.14 = (f32[10,48,128]{2,1,0:T(8,128)S(1)}, f32[10,48,128]{2,1,0:T(8,128)S(1)}, u32[]{:S(2)}, u32[]{:S(2)}) collective-permute-start(f32[10,48,128]{2,1,0:T(8,128)S(1)} %get-tuple-element.32), channel_id=1, source_target_pairs={{0,12},{4,0},{8,4},{12,8},{1,13},{5,1},{9,5},{13,9},{2,14},{6,2},{... | collective-permute-start | bytes 737288 | tf_op jit(solution)/shard_map/ppermute | solution.py:445
  13.7 8.9 %collective-permute-start.8 = (f32[208,128]{1,0:T(8,128)S(1)}, f32[208,128]{1,0:T(8,128)S(1)}, u32[]{:S(2)}, u32[]{:S(2)}) collective-permute-start(f32[208,128]{1,0:T(8,128)S(1)} %get-tuple-element.26), channel_id=1, source_target_pairs={{0,10},{1,11},{2,8},{3,9},{4,14},{5,15},{6,12},{7,13},{8,2},{9,3},... | collective-permute-start | bytes 319496 | tf_op jit(solution)/shard_map/ppermute | solution.py:472
  14.9 10.2 %collective-permute-start.4 = (f32[208,128]{1,0:T(8,128)S(1)}, f32[208,128]{1,0:T(8,128)S(1)}, u32[]{:S(2)}, u32[]{:S(2)}) collective-permute-start(f32[208,128]{1,0:T(8,128)S(1)} %get-tuple-element.21), channel_id=1, source_target_pairs={{0,1},{1,0},{2,3},{3,2},{4,5},{5,4},{6,7},{7,6},{8,9},{9,8},{10,11... | collective-permute-start | bytes 319496 | tf_op jit(solution)/shard_map/ppermute | solution.py:472
  16.5 10.8 %collective-permute-start.5 = (f32[208,128]{1,0:T(8,128)S(1)}, f32[208,128]{1,0:T(8,128)S(1)}, u32[]{:S(2)}, u32[]{:S(2)}) collective-permute-start(f32[208,128]{1,0:T(8,128)S(1)} %get-tuple-element.22), channel_id=1, source_target_pairs={{0,9},{1,8},{2,11},{3,10},{4,13},{5,12},{6,15},{7,14},{8,1},{9,0},... | collective-permute-start | bytes 319496 | tf_op jit(solution)/shard_map/ppermute | solution.py:472
  22.6 6.6 %collective-permute-start.6 = (f32[208,128]{1,0:T(8,128)S(1)}, f32[208,128]{1,0:T(8,128)S(1)}, u32[]{:S(2)}, u32[]{:S(2)}) collective-permute-start(f32[208,128]{1,0:T(8,128)S(1)} %get-tuple-element.23), channel_id=1, source_target_pairs={{0,3},{1,2},{2,1},{3,0},{4,7},{5,6},{6,5},{7,4},{8,11},{9,10},{10,... | collective-permute-start | bytes 319496 | tf_op jit(solution)/shard_map/ppermute | solution.py:472
  25.2 7.5 %collective-permute-start.2 = (f32[208,128]{1,0:T(8,128)S(1)}, f32[208,128]{1,0:T(8,128)S(1)}, u32[]{:S(2)}, u32[]{:S(2)}) collective-permute-start(f32[208,128]{1,0:T(8,128)S(1)} %get-tuple-element.19), channel_id=1, source_target_pairs={{0,11},{1,10},{2,9},{3,8},{4,15},{5,14},{6,13},{7,12},{8,3},{9,2},... | collective-permute-start | bytes 319496 | tf_op jit(solution)/shard_map/ppermute | solution.py:472
  27.3 6.4 %collective-permute-start.3 = (f32[208,128]{1,0:T(8,128)S(1)}, f32[208,128]{1,0:T(8,128)S(1)}, u32[]{:S(2)}, u32[]{:S(2)}) collective-permute-start(f32[208,128]{1,0:T(8,128)S(1)} %get-tuple-element.20), channel_id=1, source_target_pairs={{0,8},{1,9},{2,10},{3,11},{4,12},{5,13},{6,14},{7,15},{8,0},{9,1},... | collective-permute-start | bytes 319496 | tf_op jit(solution)/shard_map/ppermute | solution.py:472
  34.6 4.8 %collective-permute-start.10 = (f32[4,48,128]{2,1,0:T(8,128)S(1)}, f32[4,48,128]{2,1,0:T(8,128)S(1)}, u32[]{:S(2)}, u32[]{:S(2)}) collective-permute-start(f32[4,48,128]{2,1,0:T(8,128)S(1)} %get-tuple-element.29), channel_id=1, source_target_pairs={{0,12},{4,0},{8,4},{12,8},{1,13},{5,1},{9,5},{13,9},{2,14},{6,2},{... | collective-permute-start | bytes 294920 | tf_op jit(solution)/shard_map/ppermute | solution.py:445
  34.7 4.8 %collective-permute-start.9 = (f32[4,48,128]{2,1,0:T(8,128)S(1)}, f32[4,48,128]{2,1,0:T(8,128)S(1)}, u32[]{:S(2)}, u32[]{:S(2)}) collective-permute-start(f32[4,48,128]{2,1,0:T(8,128)S(1)} %get-tuple-element.28), channel_id=1, source_target_pairs={{0,4},{4,8},{8,12},{12,0},{1,5},{5,9},{9,13},{13,1},{2,6},{6,10},{... | collective-permute-start | bytes 294920 | tf_op jit(solution)/shard_map/ppermute | solution.py:445
  35.6 8.0 %collective-permute-start.15 = (f32[4,48,128]{2,1,0:T(8,128)S(1)}, f32[4,48,128]{2,1,0:T(8,128)S(1)}, u32[]{:S(2)}, u32[]{:S(2)}) collective-permute-start(f32[4,48,128]{2,1,0:T(8,128)S(1)} %state_edges.1), channel_id=1, source_target_pairs={{0,1},{1,2},{2,3},{3,0},{4,5},{5,6},{6,7},{7,4},{8,9},{9,10},{10,1... | collective-permute-start | bytes 294920 | tf_op jit(solution)/shard_map/ppermute | solution.py:445
  36.5 7.1 %collective-permute-start.16 = (f32[4,48,128]{2,1,0:T(8,128)S(1)}, f32[4,48,128]{2,1,0:T(8,128)S(1)}, u32[]{:S(2)}, u32[]{:S(2)}) collective-permute-start(f32[4,48,128]{2,1,0:T(8,128)S(1)} %state_edges.1), channel_id=1, source_target_pairs={{0,3},{1,0},{2,1},{3,2},{4,7},{5,4},{6,5},{7,6},{8,11},{9,8},{10,9... | collective-permute-start | bytes 294920 | tf_op jit(solution)/shard_map/ppermute | solution.py:445
  39.6 5.8 %collective-permute-start.11 = (f32[48,128]{1,0:T(8,128)S(1)}, f32[48,128]{1,0:T(8,128)S(1)}, u32[]{:S(2)}, u32[]{:S(2)}) collective-permute-start(f32[48,128]{1,0:T(8,128)S(1)} %adjoint_edges.1), channel_id=1, source_target_pairs={{0,1},{1,2},{2,3},{3,0},{4,5},{5,6},{6,7},{7,4},{8,9},{9,10},{10,1... | collective-permute-start | bytes 73736 | tf_op jit(solution)/shard_map/ppermute | solution.py:445
  40.0 5.4 %collective-permute-start.12 = (f32[48,128]{1,0:T(8,128)S(1)}, f32[48,128]{1,0:T(8,128)S(1)}, u32[]{:S(2)}, u32[]{:S(2)}) collective-permute-start(f32[48,128]{1,0:T(8,128)S(1)} %adjoint_edges.1), channel_id=1, source_target_pairs={{0,3},{1,0},{2,1},{3,2},{4,7},{5,4},{6,5},{7,6},{8,11},{9,8},{10,9... | collective-permute-start | bytes 73736 | tf_op jit(solution)/shard_map/ppermute | solution.py:445

commit v3 on v0

v3 whole, which is shorter than its diff:
```python
import functools

import jax
import jax.numpy as jnp
from jax import lax
from jax.experimental import pallas as pl
from jax.experimental.pallas import tpu as pltpu
from jax.sharding import PartitionSpec as P

time_step = 0.25
coriolis_peak = 0.8

HALO = 4
GROUP = 256
LANES = 128
F32 = jnp.float32
BF16 = jnp.bfloat16
PARAMS = pltpu.CompilerParams(vmem_limit_bytes=16 * 1024 * 1024)


def split(values):
    high = values.astype(BF16)
    return high, (values - high.astype(F32)).astype(BF16)


def dot_nt(a, b):
    return lax.dot_general(a, b, (((1,), (1,)), ((), ())), preferred_element_type=F32)


def first_of_pair(axis="frow"):
    return lax.rem(lax.axis_index(axis), 2) == 0


def row_masks(n_row):
    at = lax.axis_index("frow")
    return jnp.where(at > 0, 1.0, 0.0).astype(F32), jnp.where(at < n_row - 1, 1.0, 0.0).astype(F32)


def extended_rows(tile, pair, cross, width, lower, masks):
    tile_rows = len(tile)
    lines = [(HALO - width + k, jnp.where(lower, cross[k], pair[k]) * masks[0]) for k in range(width)]
    lines += [(HALO + k, tile[k]) for k in range(tile_rows)]
    lines += [(HALO + tile_rows + k, jnp.where(lower, pair[k], cross[k]) * masks[1]) for k in range(width)]
    return lines


def edge_columns(lines):
    lane = lax.broadcasted_iota(jnp.int32, lines[0][1].shape, 1)
    owner = ((lane + 4) // 8) % 16
    result = jnp.zeros_like(lines[0][1])
    for k, line in lines:
        result = jnp.where(owner == k, pltpu.roll(line, (8 * k) % LANES, 1), result)
    return result


def first_lanes(like):
    return lax.broadcasted_iota(jnp.int32, like.shape, 1) % 8 < 4


def from_sides(one, other, paired):
    if not paired:
        return one, other
    lower = first_of_pair("fcol")
    return jnp.where(lower, other, one), jnp.where(lower, one, other)


def first_row(which):
    return sum(HALO - k for k in range(which))


def prepare_kernel(order, dest, base, frac, states, cot, sent, cross, turned, cot_out, dest_v, base_v, frac_v, states_v, sems):
    moves = ((dest, dest_v), (base, base_v), (frac, frac_v), (states, states_v), (cot, cot_out))
    copies = [pltpu.make_async_copy(source, target, sems.at[i]) for i, (source, target) in enumerate(moves)]
    for copy in copies:
        copy.start()
    for copy in copies[:3]:
        copy.wait()
    lines = dest_v.shape[0]
    sent[:lines, :] = dest_v[...].astype(F32)
    sent[lines : 2 * lines, :] = base_v[...].astype(F32)
    for k in range(2):
        for i in range(lines):
            sent[(2 + k) * lines + i : (2 + k) * lines + i + 1, :] = frac_v[k : k + 1, i * LANES : (i + 1) * LANES]
    copies[3].wait()
    _, tile_rows, channels, _ = turned.shape
    lower = first_of_pair()
    for which, source in enumerate(order):
        for r in range(tile_rows):
            turned[which, r] = states_v[source, pl.ds(r, channels, stride=tile_rows), :]
        width = HALO - which
        for k in range(width):
            top, bottom = turned[which, k], turned[which, tile_rows - width + k]
            at = (first_row(which) + k) * channels
            sent[4 * lines + at : 4 * lines + at + channels, :] = jnp.where(lower, bottom, top)
            cross[at : at + channels, :] = jnp.where(lower, top, bottom)
    copies[4].wait()


def prepare(dest, base, frac, states, cot, order, tile_rows):
    channels, points = cot.shape
    columns = states.shape[2]
    stages = len(order)
    rim = first_row(stages) * channels
    lines = points // LANES
    in_hbm = pl.BlockSpec(memory_space=pltpu.HBM)
    return pl.pallas_call(
        functools.partial(prepare_kernel, order),
        in_specs=[in_hbm] * 5,
        out_shape=(
            jax.ShapeDtypeStruct((4 * lines + rim, LANES), F32),
            jax.ShapeDtypeStruct((rim, columns), F32),
            jax.ShapeDtypeStruct((stages, tile_rows, channels, columns), F32),
            jax.ShapeDtypeStruct(cot.shape, F32),
        ),
        scratch_shapes=[
            pltpu.VMEM(dest.shape, jnp.int32),
            pltpu.VMEM(base.shape, jnp.int32),
            pltpu.VMEM(frac.shape, F32),
            pltpu.VMEM(states.shape, F32),
            pltpu.SemaphoreType.DMA((5,)),
        ],
        compiler_params=PARAMS,
        name="prepare",
    )(*(pltpu.with_memory_space_constraint(x, pltpu.HBM) for x in (dest, base, frac, states, cot)))


def state_rows(which, turned, pair, pair_at, cross, lower, masks):
    _, tile_rows, channels, _ = turned.shape
    width = HALO - which

    def rim(ref, start):
        at = [start + (first_row(which) + k) * channels for k in range(width)]
        return [ref[i : i + channels, :] for i in at]

    tile = [turned[which, r] for r in range(tile_rows)]
    return extended_rows(tile, rim(pair, pair_at), rim(cross, 0), width, lower, masks)


def edge_plan(stages, tile_rows):
    plan, lane = [], 0
    for which in range(stages):
        width = HALO - which
        for k in range(HALO - width, HALO + tile_rows + width):
            count = width - max(HALO - k, k - (HALO + tile_rows - 1), 0)
            if count > 0:
                plan.append((which, k, count, lane))
                lane += count
    return plan


def state_edges(n_row, turned, pair, pair_at, cross):
    stages, tile_rows, channels, _ = turned.shape
    lower, masks = first_of_pair(), row_masks(n_row)
    lane = lax.broadcasted_iota(jnp.int32, (channels, LANES), 1)
    first = last = jnp.zeros((channels, LANES), F32)
    lines = [dict(state_rows(which, turned, pair, pair_at, cross, lower, masks)) for which in range(stages)]
    for which, k, count, at in edge_plan(stages, tile_rows):
        here = (lane >= at) & (lane < at + count)
        first = jnp.where(here, pltpu.roll(lines[which][k], at, 1), first)
        last = jnp.where(here, pltpu.roll(lines[which][k], (at + count) % LANES, 1), last)
    return first, last


def state_edges_kernel(n_row, pair_at, paired, turned, pair, cross, one, other):
    first, last = state_edges(n_row, turned, pair, pair_at, cross)
    if paired:
        lower = first_of_pair("fcol")
        first, last = jnp.where(lower, last, first), jnp.where(lower, first, last)
    one[...], other[...] = first, last


def all_state_edges(n_row, pair_at, paired, turned, pair, cross):
    return pl.pallas_call(
        functools.partial(state_edges_kernel, n_row, pair_at, paired),
        out_shape=[jax.ShapeDtypeStruct((turned.shape[2], LANES), F32)] * 2,
        compiler_params=PARAMS,
        name="state_edges",
    )(turned, pair, cross)


FIELDS = 7


def stage_weight(which):
    return 0.5 * time_step if which % 2 == 0 else time_step


def widen_kernel(n_row, pair_at, edge_at, paired, turned, pair, cross, one, other, gravity, *refs):
    wide, pull = refs[-2:]
    _, tile_rows, channels, columns = turned.shape
    levels = channels // 3
    total_rows = tile_rows * n_row
    base_row = lax.axis_index("frow") * tile_rows
    lower, masks = first_of_pair(), row_masks(n_row)

    level = lax.broadcasted_iota(jnp.int32, pull.shape, 0)
    pulls = jnp.zeros(pull.shape, F32)
    for i in range(levels):
        pulls = jnp.where(level == i, gravity[i], pulls)
    pull[...] = pulls

    def along_x(values):
        return pltpu.roll(values, 2 * columns - 1, 1) - pltpu.roll(values, 1, 1)

    left, right = from_sides(one[edge_at : edge_at + channels, :], other[...], paired)
    lane = lax.broadcasted_iota(jnp.int32, (channels, columns), 1)
    rims = {
        (which, k): jnp.where(
            lane < columns // 2,
            pltpu.roll(right, (-at) % columns, 1),
            pltpu.roll(left, (-at - count) % columns, 1),
        )
        for which, k, count, at in edge_plan(turned.shape[0], tile_rows)
    }

    for which in range(turned.shape[0]):
        weight = stage_weight(which)
        lines = state_rows(which, turned, pair, pair_at, cross, lower, masks)
        first, final = lines[0][0], lines[-1][0]
        for k, line in lines:
            rim = rims.get((which, k), jnp.zeros_like(line))
            scaled = (0.5 * weight) * jnp.concatenate([line, rim], axis=1)
            wide[which, k, :channels, :] = scaled
        for k in range(first + 1, final):
            winds = slice(levels, channels)
            change = along_x(wide[which, k, winds, :])
            slope = wide[which, k + 1, winds, :] - wide[which, k - 1, winds, :]
            row = (base_row + k - HALO).astype(F32)
            rotation = weight * (coriolis_peak * (2.0 * (row + 0.5) / total_rows - 1.0))
            begin = channels
            for value in (change[:levels], change[levels:] + rotation, slope[:levels] - rotation, slope[levels:]):
                wide[which, k, begin : begin + levels, :] = value
                begin += levels


def widen(n_row, pair_at, edge_at, paired, turned, pair, cross, one, other, gravity, after=()):
    stages, tile_rows, channels, columns = turned.shape
    in_vmem = pl.BlockSpec(memory_space=pltpu.VMEM)
    return pl.pallas_call(
        functools.partial(widen_kernel, n_row, pair_at, edge_at, paired),
        in_specs=[in_vmem] * 5 + [pl.BlockSpec(memory_space=pltpu.SMEM)] + [in_vmem] * len(after),
        out_shape=(
            jax.ShapeDtypeStruct((stages, tile_rows + 2 * HALO, channels // 3 * FIELDS, 2 * columns), F32),
            jax.ShapeDtypeStruct((channels // 3, 2 * columns), F32),
        ),
        compiler_params=PARAMS,
        name="widen_states",
    )(turned, pair, cross, one, other, gravity, *after)


def slot_blocks(cot, where, tiles, share, tile_rows, columns, onehot, high, low):
    channels, points = cot.shape
    lines = points // LANES
    groups = tiles.shape[0] // share
    corner = where[lines : 2 * lines, :]
    row = jnp.zeros_like(corner)
    for k in range(1, tile_rows - 1):
        row = row + (corner >= float(k * (columns - 1))).astype(F32)
    col = corner - row * float(columns - 1)
    target = where[:lines, :]
    offsets = [where[k * lines : (k + 1) * lines, :] for k in (2, 3)]

    before = (
        lax.broadcasted_iota(jnp.int32, (GROUP, GROUP), 0)
        < lax.broadcasted_iota(jnp.int32, (GROUP, GROUP), 1)
    ).astype(F32).astype(BF16)
    index = lax.broadcasted_iota(jnp.int32, tiles.shape, 0)
    begin = ((index % share) * (GROUP // share)).astype(F32)
    slots = lax.broadcasted_iota(jnp.int32, (GROUP, GROUP), 0).astype(F32)
    count = jnp.zeros((tiles.shape[0], 1), F32)
    rows = channels + 8
    for b in range(points // GROUP):
        part = slice(b * GROUP, (b + 1) * GROUP)

        def across(values):
            return jnp.concatenate([values[2 * b : 2 * b + 1, :], values[2 * b + 1 : 2 * b + 2, :]], axis=1)

        named = (tiles == across(target)).astype(F32)
        ahead = jnp.dot(named.astype(BF16), before, preferred_element_type=F32)
        lane = jnp.sum(named * (ahead + count + begin), axis=0, keepdims=True)
        count = count + jnp.sum(named, axis=1, keepdims=True)
        onehot[:, part] = (slots == lane).astype(F32).astype(BF16)
        coords = [across(values) for values in (row, col, *offsets)]
        data_high, data_low = split(jnp.concatenate([cot[:, part], *coords, *coords], axis=0))
        for g in range(groups):
            mine = named[g * share : g * share + 1, :]
            for i in range(1, share):
                mine = mine + named[g * share + i : g * share + i + 1, :]
            mine = mine.astype(BF16)
            high[g * rows : (g + 1) * rows, part] = data_high * mine
            low[g * rows : (g + 1) * rows, part] = data_low * mine
    packed = dot_nt(high[...], onehot[...]) + dot_nt(low[...], onehot[...])
    upper = lax.broadcasted_iota(jnp.int32, (8, LANES), 0) < 4
    for g in range(groups):
        block = packed[g * rows : (g + 1) * rows, :]
        yield (
            block[:channels, :LANES],
            block[:channels, LANES:],
            jnp.where(upper, block[channels:, :LANES], block[channels:, LANES:]),
        )


def store_block(out, at, pieces):
    channels = pieces[0].shape[0]
    out[at : at + channels, :] = pieces[0]
    out[at + channels : at + 2 * channels, :] = pieces[1]
    out[at + 2 * channels : at + 2 * channels + 8, :] = pieces[2]


def pack_scratch(channels, points, groups):
    return [
        pltpu.VMEM((GROUP, points), BF16),
        pltpu.VMEM((groups * (channels + 8), points), BF16),
        pltpu.VMEM((groups * (channels + 8), points), BF16),
    ]


def pack_all_kernel(tile_count, share, tile_rows, columns, cot, where, out, *scratch):
    tiles = lax.broadcasted_iota(jnp.int32, (tile_count, GROUP), 0).astype(F32)
    for g, pieces in enumerate(slot_blocks(cot, where, tiles, share, tile_rows, columns, *scratch)):
        store_block(out.at[g], 0, pieces)


def pack_all(cot, where, tile_count, share, tile_rows, columns):
    channels, points = cot.shape
    groups = tile_count // share
    return pl.pallas_call(
        functools.partial(pack_all_kernel, tile_count, share, tile_rows, columns),
        out_shape=jax.ShapeDtypeStruct((groups, 2 * channels + 8, LANES), F32),
        scratch_shapes=pack_scratch(channels, points, groups),
        compiler_params=PARAMS,
        name="pack_points",
    )(cot, where)


NEAR = ((0, 0), (2, 0), (0, 1), (2, 1))
FAR = ((0, 2), (2, 2), (0, 3), (2, 3))


def partner_tiles(partners):
    at_row, at_col = lax.axis_index("frow"), lax.axis_index("fcol")
    n_col = lax.axis_size("fcol")
    index = lax.broadcasted_iota(jnp.int32, (len(partners), GROUP), 0)
    tiles = jnp.zeros(index.shape, jnp.int32)
    for g, (df, dz) in enumerate(partners):
        tiles = jnp.where(index == g, (at_row ^ df) * n_col + (at_col ^ dz), tiles)
    return tiles.astype(F32)


def pack_own_kernel(tiles, tile_rows, columns, cot, where, out, *scratch):
    for g, pieces in enumerate(slot_blocks(cot, where, partner_tiles(tiles), 1, tile_rows, columns, *scratch)):
        store_block(out.at[g], 0, pieces)


def pack_own(tiles, cot, where, tile_rows, columns):
    channels, points = cot.shape
    groups = len(tiles)
    return pl.pallas_call(
        functools.partial(pack_own_kernel, tiles, tile_rows, columns),
        out_shape=jax.ShapeDtypeStruct((groups, 2 * channels + 8, LANES), F32),
        scratch_shapes=pack_scratch(channels, points, groups),
        compiler_params=PARAMS,
        name="pack_own",
    )(cot, where)


def pack_partner_kernel(tiles, tailed, tile_rows, columns, cot, where, own, *refs):
    if tailed is not None:
        tail, *refs = refs
    outs, scratch = refs[:-3], refs[-3:]
    size = own.shape[1]
    blocks = slot_blocks(cot, where, partner_tiles(tiles), 1, tile_rows, columns, *scratch)
    for g, pieces in enumerate(blocks):
        outs[g][:size, :] = own[g]
        store_block(outs[g], size, pieces)
        if tiles[g] == tailed:
            outs[g][2 * size :, :] = tail[...]


def pack_partner(tiles, cot, where, own, tile_rows, columns, tailed=None, tail=None):
    channels, points = cot.shape
    rows = 2 * own.shape[1]
    sizes = [rows + (tail.shape[0] if tile == tailed else 0) for tile in tiles]
    blocks = pl.pallas_call(
        functools.partial(pack_partner_kernel, tiles, tailed, tile_rows, columns),
        out_shape=[jax.ShapeDtypeStruct((size, LANES), F32) for size in sizes],
        scratch_shapes=pack_scratch(channels, points, len(tiles)),
        compiler_params=PARAMS,
        name="pack_partner",
    )(cot, where, own, *([] if tail is None else [tail]))
    return dict(zip(tiles, blocks))


def scatter_kernel(count, first, later, *refs):
    blocks, refs = refs[:count], refs[count:]
    if not first:
        total, refs = refs[0], refs[1:]
    outs, (high, low, weight) = refs[later:-3], refs[-3:]
    part_rows, channels, columns = outs[0].shape
    tile_rows = part_rows * len(outs)
    rows = 2 * channels + 8
    cells = lax.broadcasted_iota(jnp.int32, (columns, LANES), 0).astype(F32)
    lines = lax.broadcasted_iota(jnp.int32, (tile_rows, LANES), 0).astype(F32)

    def hat(index, corner, fraction):
        away = index - corner
        return jnp.where(away == 0.0, 1.0 - fraction, jnp.where(away == 1.0, fraction, 0.0))

    at = 0
    for block in blocks:
        for source in range(block.shape[0] // rows):
            for half in range(2):
                part = slice(at, at + LANES)
                at += LANES
                begin = source * rows + 2 * channels + 4 * half
                coords = block[begin : begin + 4, :]
                row, col, along_rows, along_cols = (coords[k : k + 1, :] for k in range(4))
                weight_high, weight_low = split(hat(cells, col, along_cols))
                weight[:columns, part] = weight_high
                weight[columns:, part] = weight_low
                begin = source * rows + half * channels
                values = block[begin : begin + channels, :]
                row_weight = hat(lines, row, along_rows)
                for r in range(tile_rows):
                    product_high, product_low = split(values * row_weight[r : r + 1, :])
                    high[r * channels : (r + 1) * channels, part] = product_high
                    low[r * channels : (r + 1) * channels, part] = product_low
    both = dot_nt(high[...], weight[...])
    sums = both[:, :columns] + both[:, columns:] + dot_nt(low[...], weight[:columns, :])
    for r in range(tile_rows):
        line = sums[r * channels : (r + 1) * channels, :]
        if not first:
            line = line + total[r]
        outs[r // part_rows][r % part_rows] = line


def scatter(blocks, total, channels, tile_rows, columns, after=(), parts=1):
    slots = sum(block.shape[0] // (2 * channels + 8) for block in blocks) * GROUP
    return pl.pallas_call(
        functools.partial(scatter_kernel, len(blocks), total is None, len(after)),
        out_shape=[jax.ShapeDtypeStruct((tile_rows // parts, channels, columns), F32)] * parts,
        scratch_shapes=[
            pltpu.VMEM((tile_rows * channels, slots), BF16),
            pltpu.VMEM((tile_rows * channels, slots), BF16),
            pltpu.VMEM((2 * columns, slots), BF16),
        ],
        compiler_params=PARAMS,
        name="scatter_points",
    )(*blocks, *([] if total is None else [total]), *after)


def finish_kernel(count, total, *refs):
    parts, (canvas, to_pair, to_cross) = refs[:count], refs[-3:]
    tile_rows = canvas.shape[0]
    for r in range(tile_rows):
        line = total[r]
        if parts:
            size = parts[0].shape[0]
            line = line + parts[r // size][r % size]
        canvas[r] = line
    lower = first_of_pair()
    for k in range(HALO):
        top, bottom = canvas[k], canvas[tile_rows - HALO + k]
        to_pair[k] = jnp.where(lower, bottom, top)
        to_cross[k] = jnp.where(lower, top, bottom)


def finish(total, parts=(), after=()):
    _, channels, columns = total.shape
    rim = jax.ShapeDtypeStruct((HALO, channels, columns), F32)
    return pl.pallas_call(
        functools.partial(finish_kernel, len(parts)),
        out_shape=(jax.ShapeDtypeStruct(total.shape, F32), rim, rim),
        compiler_params=PARAMS,
        name="finish_canvas",
    )(total, *parts, *after)


def adjoint_rows(n_row, canvas, pair, cross):
    tile = [canvas[r] for r in range(canvas.shape[0])]
    rims = ([ref[k] for k in range(HALO)] for ref in (pair, cross))
    return extended_rows(tile, *rims, HALO, first_of_pair(), row_masks(n_row))


def adjoint_edges_kernel(n_row, canvas, pair, cross, edges):
    edges[...] = edge_columns(adjoint_rows(n_row, canvas, pair, cross))


def adjoint_edges(n_row, canvas, pair, cross):
    return pl.pallas_call(
        functools.partial(adjoint_edges_kernel, n_row),
        out_shape=jax.ShapeDtypeStruct(canvas.shape[1:], F32),
        compiler_params=PARAMS,
        name="adjoint_edges",
    )(canvas, pair, cross)


def steps_kernel(n_row, paired, canvas, pair, cross, one, other, gravity, wide, out, start, middle, after, last):
    tile_rows, channels, columns = canvas.shape
    levels = channels // 3
    part = 8
    masks = row_masks(n_row)
    left, right = from_sides(one[...], other[...], paired)
    rim = jnp.where(first_lanes(left), right, left)
    for k, line in adjoint_rows(n_row, canvas, pair, cross):
        start[k, :, :columns] = line
        start[k, :, columns:] = pltpu.roll(rim, (-8 * k) % LANES, 1)

    def along_x(values):
        return pltpu.roll(values, 2 * columns - 1, 1) - pltpu.roll(values, 1, 1)

    def run(stage, adjoint, store):
        width = HALO - 1 - stage
        begin, end = HALO - width, HALO + tile_rows + width
        for low in range(0, levels, part):
            pull = (0.5 * stage_weight(stage)) * gravity[low : low + part, :]

            def state(k, which):
                return wide[stage, k, which * levels + low : which * levels + low + part, :]

            def line(k):
                a, b, c = (adjoint[k, w * levels + low : w * levels + low + part, :] for w in range(3))
                v = state(k, 2)
                return a, b, c, v, v * b, v * c

            up, here = line(begin - 1), line(begin)
            for k in range(begin, end):
                down = line(k + 1)
                a, b, c, v = here[:4]
                h, u = state(k, 0), state(k, 1)
                a_x, a_y = along_x(a), down[0] - up[0]
                height = u * a_x + v * a_y + pull * (along_x(b) + (down[2] - up[2]))
                east = h * a_x + along_x(u * b) + (down[4] - up[4]) - b * state(k, 3) - c * state(k, 4)
                north = h * a_y + along_x(u * c) + (down[5] - up[5]) - b * state(k, 5) - c * state(k, 6)
                for w, (old, change) in enumerate(zip((a, b, c), (height, east, north))):
                    store(k, w, low, old, change)
                up, here = here, down

    def kept(k, value):
        if k < HALO:
            return value * masks[0]
        if k >= HALO + tile_rows:
            return value * masks[1]
        return value

    def half_into(result):
        def store(k, w, low, old, change):
            result[k, w * levels + low : w * levels + low + part, :] = kept(k, 0.5 * old + change)

        return store

    def after_step(adjoint, k, w, low, old, change):
        return 0.5 * adjoint[k, w * levels + low : w * levels + low + part, :] + old + change

    def to_after(k, w, low, old, change):
        after[k, w * levels + low : w * levels + low + part, :] = kept(k, after_step(start, k, w, low, old, change))

    def to_out(k, w, low, old, change):
        place = pl.ds((w * levels + low) * tile_rows + k - HALO, part, stride=tile_rows)
        out[place, :] = after_step(after, k, w, low, old, change)[:, :columns]

    run(0, start, half_into(middle))
    run(1, middle, to_after)
    run(2, after, half_into(last))
    run(3, last, to_out)


def steps(n_row, paired, canvas, pair, cross, one, other, wide, gravity):
    tile_rows, channels, columns = canvas.shape
    extended = pltpu.VMEM((tile_rows + 2 * HALO, channels, 2 * columns), F32)
    return pl.pallas_call(
        functools.partial(steps_kernel, n_row, paired),
        out_shape=jax.ShapeDtypeStruct((channels * tile_rows, columns), F32),
        scratch_shapes=[extended] * 4,
        compiler_params=PARAMS,
        name="adjoint_steps",
    )(canvas, pair, cross, one, other, gravity, wide)


def shifted(values, axis, by):
    count = lax.axis_size(axis)
    return lax.ppermute(values, axis, [(i, (i + by) % count) for i in range(count)])


def exchanged(values, offset):
    n_row, n_col = lax.axis_size("frow"), lax.axis_size("fcol")
    df, dz = offset
    pairs = [(f * n_col + z, (f ^ df) * n_col + (z ^ dz)) for f in range(n_row) for z in range(n_col)]
    return lax.ppermute(values, ("frow", "fcol"), pairs)


def exchanged_across(values):
    n_row = lax.axis_size("frow")
    return lax.ppermute(values, "frow", [(f, ((f + 1) ^ 1) - 1) for f in range(1, n_row - 1)])


def from_everyone(packed, channels, tile_count):
    groups = packed.shape[0]
    rows = channels + 4
    halves = [
        jnp.concatenate(
            [
                packed[:, h * channels : (h + 1) * channels],
                packed[:, 2 * channels + 4 * h : 2 * channels + 4 * h + 4],
            ],
            axis=1,
        )
        for h in range(2)
    ]
    slots = jnp.stack(halves, axis=2).transpose(1, 0, 2, 3).reshape(rows, tile_count, -1)
    slots = lax.all_to_all(slots, ("frow", "fcol"), split_axis=1, concat_axis=1, tiled=True)
    slots = slots.reshape(rows, groups, 2, LANES).transpose(1, 2, 0, 3)
    return jnp.concatenate(
        [slots[:, 0, :channels], slots[:, 1, :channels], slots[:, 0, channels:], slots[:, 1, channels:]], axis=1
    )


def per_device(latlon_cot, dest_tile, base_cell, corner_frac, saved_states, gravity):
    n_row, n_col = lax.axis_size("frow"), lax.axis_size("fcol")
    tile_count = n_row * n_col
    levels = gravity.shape[0]
    tile_rows = saved_states.shape[4]
    columns = saved_states.shape[5]
    channels = 3 * levels
    points = base_cell.shape[0]
    lines = points // LANES
    share = GROUP * tile_count // (2 * points)
    paired = share == 1 and n_row == 4 and n_col == 4
    size = (channels, tile_rows, columns)

    cot = latlon_cot.reshape(channels, points)
    partner_cot = exchanged(cot, (1, 0)) if paired else None
    sent, to_cross, turned, cot = prepare(
        dest_tile.reshape(lines, LANES),
        base_cell.reshape(lines, LANES),
        corner_frac,
        saved_states.reshape(4, channels * tile_rows, columns),
        cot,
        (3, 2, 1, 0),
        tile_rows,
    )
    pair_at = 4 * lines
    pair = exchanged(sent, (1, 0))
    cross = exchanged_across(to_cross)
    if paired:
        own = pack_own(FAR, cot, sent, tile_rows, columns)
        packed = pack_partner(FAR, partner_cot, pair, own, tile_rows, columns)
        got = [packed[0, 2]] + [exchanged(packed[tile], (tile[0], tile[1] ^ 2)) for tile in FAR[1:]]
        one, other = all_state_edges(n_row, pair_at, paired, turned, pair, cross)
        own = pack_own(NEAR, cot, sent, tile_rows, columns)
        packed = pack_partner(NEAR, partner_cot, pair, own, tile_rows, columns, (0, 1), one)
        total = scatter(got[:2], None, *size, [packed[0, 0]])[0]
        far = [exchanged(part, (0, 2)) for part in scatter(got[2:], total, *size, parts=2)]
        got = {tile: exchanged(packed[tile], tile) for tile in NEAR[1:]}
        other = exchanged(other, (0, 3))
        total = scatter([packed[0, 0], got[2, 0]], None, *size)[0]
        total = scatter([got[0, 1], got[2, 1]], total, *size)[0]
        wide, pull = widen(
            n_row, pair_at, 2 * own.shape[1], paired, turned, pair, cross, got[0, 1], other, gravity, [total]
        )
        canvas = finish(total, far, [pull])
    else:
        packed = pack_all(cot, sent, tile_count, share, tile_rows, columns)
        got = from_everyone(packed, channels, tile_count)
        one, other = all_state_edges(n_row, pair_at, paired, turned, pair, cross)
        one, other = shifted(one, "fcol", 1), shifted(other, "fcol", -1)
        wide, pull = widen(n_row, pair_at, 0, paired, turned, pair, cross, one, other, gravity)
        canvas = finish(scatter([got.reshape(-1, LANES)], None, *size)[0])

    canvas, to_pair, to_cross = canvas
    pair, cross = exchanged(to_pair, (1, 0)), exchanged_across(to_cross)
    edges = adjoint_edges(n_row, canvas, pair, cross)
    if paired:
        sides = exchanged(edges, (0, 1)), exchanged(edges, (0, 3))
    else:
        sides = shifted(edges, "fcol", 1), shifted(edges, "fcol", -1)
    result = steps(n_row, paired, canvas, pair, cross, *sides, wide, pull)
    return result.reshape(3, levels, tile_rows, columns)


def solution(mesh):
    placed = (
        P(None, None, ("member", "frow", "fcol")),
        P(("frow", "fcol"), None),
        P(("frow", "fcol")),
        P(None, ("frow", "fcol")),
        P(None, None, None, None, ("member", "frow"), "fcol"),
        P(),
    )
    return jax.shard_map(
        per_device,
        mesh=mesh,
        in_specs=placed,
        out_specs=P(None, None, ("member", "frow"), "fcol"),
        check_vma=False,
    )
```

time: 332 us -> 46.9 us (0.14)
  the two profiles are of different devices: /device:TPU:0 before, /device:TPU:1 now
where the time goes in v3:
time: 46.9 us; the launch traced here: 46.7 us
  starting transfers between devices  24.9 us (53%)
  Pallas kernels  14.6 us (31%)
  waiting for transfers between devices  7.08 us (15%)
    ppermute x14, starting transfers between devices, exchanged(): return lax.ppermute(values, ('frow', 'fcol'), pairs)  17.4 us
    ppermute x2, starting transfers between devices, exchanged_across(): lax.ppermute(values, 'frow', [(f, (f + 1 ^ 1) - 1) for f in range(1, n_ro...  7.52 us
    ppermute x14, waiting for transfers between devices, exchanged(): return lax.ppermute(values, ('frow', 'fcol'), pairs)  3.91 us
    pallas_call x4, Pallas kernels, scatter(): pl.pallas_call(functools.partial(scatter_kernel, len(blocks), total is No...  3.85 us
    ppermute x2, waiting for transfers between devices, exchanged_across(): lax.ppermute(values, 'frow', [(f, (f + 1 ^ 1) - 1) for f in range(1, n_ro...  3.18 us
    pallas_call x1, Pallas kernels, steps(): pl.pallas_call(functools.partial(steps_kernel, n_row, paired), out_shape=...  2.6 us
    pallas_call x2, Pallas kernels, pack_partner(): pl.pallas_call(functools.partial(pack_partner_kernel, tiles, tailed, tile...  1.99 us
    pallas_call x2, Pallas kernels, pack_own(): pl.pallas_call(functools.partial(pack_own_kernel, tiles, tile_rows, colum...  1.99 us
  transfers between devices with their start and end apart: 16, of which 4 were waited for; matrix products, arithmetic and copies ran while one was open for 0% of the time, Pallas kernels for 25%

profile of v3, /device:TPU:1, one launch (start us, length us, event | category | flops | bytes accessed | tf_op | source)
XLA Modules:
  0.0 46.7 jit_solution(6322763855036039867)
XLA Ops:
  0.0 0.0 copy-start
  0.0 0.1 collective-permute-start
  0.1 1.4 %prepare.1 = (f32[544,128]{1,0:T(8,128)S(1)}, f32[480,128]{1,0:T(8,128)S(1)}, f32[4,8,48,128]{3,2,1,0:T(8,128)S(1)}, f32[48,2048]{1,0:T(8,128)S(1)}) custom-call(s32[16,128]{1,0:T(8,128)} %bitcast.8, s32[16,128]{1,0:T(8,128)} %bitcast.9, f32[2,2048]{1,0:T(2,128)} %frac.1, f32[4,384,128]{2,1,0:T(8,128)} %bitcast.5, f32[48,2048]{1,0:T(8,128)} %bitcast.7), custom_call_target="tpu_custom_call" | custom-call | tf_op jit(solution)/shard_map/prepare/pallas_call | solution.py:106
  1.4 0.5 %collective-permute-start.1 = (f32[544,128]{1,0:T(8,128)S(1)}, f32[544,128]{1,0:T(8,128)S(1)}, u32[]{:S(2)}, u32[]{:S(2)}) collective-permute-start(f32[544,128]{1,0:T(8,128)S(1)} %get-tuple-element.26.where), channel_id=1, source_target_pairs={{0,4},{1,5},{2,6},{3,7},{4,0},{5,1},{6,2},{7,3},{8,12},{9,13},{10,... | collective-permute-start | bytes 835592 | tf_op jit(solution)/shard_map/ppermute | solution.py:589
  2.0 4.5 %collective-permute-start.2 = (f32[480,128]{1,0:T(8,128)S(1)}, f32[480,128]{1,0:T(8,128)S(1)}, u32[]{:S(2)}, u32[]{:S(2)}) collective-permute-start(f32[480,128]{1,0:T(8,128)S(1)} %get-tuple-element.29), channel_id=1, source_target_pairs={{4,8},{8,4},{5,9},{9,5},{6,10},{10,6},{7,11},{11,7},{20,24},{24,20... | collective-permute-start | bytes 737288 | tf_op jit(solution)/shard_map/ppermute | solution.py:594
  6.5 1.0 %pack_own.3.own = f32[4,104,128]{2,1,0:T(8,128)S(1)} custom-call(f32[48,2048]{1,0:T(8,128)S(1)} %get-tuple-element.27.cot, f32[544,128]{1,0:T(8,128)S(1)} %get-tuple-element.26.where), custom_call_target="tpu_custom_call" | custom-call | tf_op jit(solution)/shard_map/pack_own/pallas_call | solution.py:358
  7.5 0.0 collective-permute-done.1.pair.where
  7.5 0.0 collective-permute-done.cot
  7.5 1.0 %pack_partner.3 = (f32[208,128]{1,0:T(8,128)S(1)}, f32[208,128]{1,0:T(8,128)S(1)}, f32[208,128]{1,0:T(8,128)S(1)}, f32[208,128]{1,0:T(8,128)S(1)}) custom-call(f32[48,2048]{1,0:T(8,128)S(1)} %collective-permute-done.cot, f32[544,128]{1,0:T(8,128)S(1)} %collective-permute-done.1.pair.where, f32[4,104,128]{2,1,0:T(8,128)S(1)} %pack_own.3.own), custom_call_target="tpu_custom_call" | custom-call | tf_op jit(solution)/shard_map/pack_partner/pallas_call | solution.py:384
  8.5 0.1 collective-permute-start.8
  8.6 1.4 %collective-permute-start.6 = (f32[208,128]{1,0:T(8,128)S(1)}, f32[208,128]{1,0:T(8,128)S(1)}, u32[]{:S(2)}, u32[]{:S(2)}) collective-permute-start(f32[208,128]{1,0:T(8,128)S(1)} %get-tuple-element.35), channel_id=1, source_target_pairs={{0,1},{1,0},{2,3},{3,2},{4,5},{5,4},{6,7},{7,6},{8,9},{9,8},{10,11... | collective-permute-start | bytes 319496 | tf_op jit(solution)/shard_map/ppermute | solution.py:589
  9.9 1.3 %collective-permute-start.7 = (f32[208,128]{1,0:T(8,128)S(1)}, f32[208,128]{1,0:T(8,128)S(1)}, u32[]{:S(2)}, u32[]{:S(2)}) collective-permute-start(f32[208,128]{1,0:T(8,128)S(1)} %get-tuple-element.36), channel_id=1, source_target_pairs={{0,9},{1,8},{2,11},{3,10},{4,13},{5,12},{6,15},{7,14},{8,1},{9,0},... | collective-permute-start | bytes 319496 | tf_op jit(solution)/shard_map/ppermute | solution.py:589
  11.2 1.0 %pack_own.2.own = f32[4,104,128]{2,1,0:T(8,128)S(1)} custom-call(f32[48,2048]{1,0:T(8,128)S(1)} %get-tuple-element.27.cot, f32[544,128]{1,0:T(8,128)S(1)} %get-tuple-element.26.where), custom_call_target="tpu_custom_call" | custom-call | tf_op jit(solution)/shard_map/pack_own/pallas_call | solution.py:358
  12.2 0.0 collective-permute-done.2.cross
  12.2 0.6 %state_edges.1 = (f32[48,128]{1,0:T(8,128)S(1)}, f32[48,128]{1,0:T(8,128)S(1)}) custom-call(f32[4,8,48,128]{3,2,1,0:T(8,128)S(1)} %get-tuple-element.28.turned, f32[544,128]{1,0:T(8,128)S(1)} %collective-permute-done.1.pair.where, f32[480,128]{1,0:T(8,128)S(1)} %collective-permute-done.2.cross), custom_call_target="tpu_custom_call" | custom-call | tf_op jit(solution)/shard_map/state_edges/pallas_call | solution.py:173
  12.9 1.0 %pack_partner.2 = (f32[208,128]{1,0:T(8,128)S(1)}, f32[208,128]{1,0:T(8,128)S(1)}, f32[256,128]{1,0:T(8,128)S(1)}, f32[208,128]{1,0:T(8,128)S(1)}) custom-call(f32[48,2048]{1,0:T(8,128)S(1)} %collective-permute-done.cot, f32[544,128]{1,0:T(8,128)S(1)} %collective-permute-done.1.pair.where, f32[4,104,128]{2,1,0:T(8,128)S(1)} %pack_own.2.own, ...), custom_call_target="tpu_custom_call" | custom-call | tf_op jit(solution)/shard_map/pack_partner/pallas_call | solution.py:384
  13.9 0.2 collective-permute-start.5
  14.1 1.3 %collective-permute-start.3 = (f32[256,128]{1,0:T(8,128)S(1)}, f32[256,128]{1,0:T(8,128)S(1)}, u32[]{:S(2)}, u32[]{:S(2)}) collective-permute-start(f32[256,128]{1,0:T(8,128)S(1)} %get-tuple-element.31), channel_id=1, source_target_pairs={{0,1},{1,0},{2,3},{3,2},{4,5},{5,4},{6,7},{7,6},{8,9},{9,8},{10,11... | collective-permute-start | bytes 393224 | tf_op jit(solution)/shard_map/ppermute | solution.py:589
  15.3 0.0 collective-permute-done.8.refs_1_
  15.3 1.3 %collective-permute-start.4 = (f32[208,128]{1,0:T(8,128)S(1)}, f32[208,128]{1,0:T(8,128)S(1)}, u32[]{:S(2)}, u32[]{:S(2)}) collective-permute-start(f32[208,128]{1,0:T(8,128)S(1)} %get-tuple-element.32), channel_id=1, source_target_pairs={{0,9},{1,8},{2,11},{3,10},{4,13},{5,12},{6,15},{7,14},{8,1},{9,0},... | collective-permute-start | bytes 319496 | tf_op jit(solution)/shard_map/ppermute | solution.py:589
  16.6 1.0 %scatter_points.6.refs_2_ = f32[8,48,128]{2,1,0:T(8,128)S(1)} custom-call(f32[208,128]{1,0:T(8,128)S(1)} %get-tuple-element.37.refs_0_, f32[208,128]{1,0:T(8,128)S(1)} %collective-permute-done.8.refs_1_, f32[208,128]{1,0:T(8,128)S(1)} %get-tuple-element.33.refs_0_.refs_2_), custom_call_target="tpu_custom_call" | custom-call | tf_op jit(solution)/shard_map/scatter_points/pallas_call | solution.py:439
  17.6 0.0 collective-permute-done.6.refs_0_
  17.6 0.0 collective-permute-done.7.refs_1_
  17.6 1.0 %scatter_points.7 = (f32[4,48,128]{2,1,0:T(8,128)S(1)}, f32[4,48,128]{2,1,0:T(8,128)S(1)}) custom-call(f32[208,128]{1,0:T(8,128)S(1)} %collective-permute-done.6.refs_0_, f32[208,128]{1,0:T(8,128)S(1)} %collective-permute-done.7.refs_1_, f32[8,48,128]{2,1,0:T(8,128)S(1)} %scatter_points.6.refs_2_), custom_call_target="tpu_custom_call" | custom-call | tf_op jit(solution)/shard_map/scatter_points/pallas_call | solution.py:439
  18.6 2.4 %collective-permute-start.9 = (f32[4,48,128]{2,1,0:T(8,128)S(1)}, f32[4,48,128]{2,1,0:T(8,128)S(1)}, u32[]{:S(2)}, u32[]{:S(2)}) collective-permute-start(f32[4,48,128]{2,1,0:T(8,128)S(1)} %get-tuple-element.39), channel_id=1, source_target_pairs={{0,2},{1,3},{2,0},{3,1},{4,6},{5,7},{6,4},{7,5},{8,10},{9,11},{10,... | collective-permute-start | bytes 294920 | tf_op jit(solution)/shard_map/ppermute | solution.py:589
  20.9 0.1 collective-permute-start.10
  21.0 0.0 collective-permute-done.5.refs_1_
  21.0 3.3 %collective-permute-start.11 = (f32[48,128]{1,0:T(8,128)S(1)}, f32[48,128]{1,0:T(8,128)S(1)}, u32[]{:S(2)}, u32[]{:S(2)}) collective-permute-start(f32[48,128]{1,0:T(8,128)S(1)} %get-tuple-element.41), channel_id=1, source_target_pairs={{0,3},{1,2},{2,1},{3,0},{4,7},{5,6},{6,5},{7,4},{8,11},{9,10},{10,... | collective-permute-start | bytes 73736 | tf_op jit(solution)/shard_map/ppermute | solution.py:589
  24.3 1.0 %scatter_points.4.refs_2_ = f32[8,48,128]{2,1,0:T(8,128)S(1)} custom-call(f32[208,128]{1,0:T(8,128)S(1)} %get-tuple-element.33.refs_0_.refs_2_, f32[208,128]{1,0:T(8,128)S(1)} %collective-permute-done.5.refs_1_), custom_call_target="tpu_custom_call" | custom-call | tf_op jit(solution)/shard_map/scatter_points/pallas_call | solution.py:439
  25.3 0.0 collective-permute-done.4.refs_1_
  25.3 0.0 collective-permute-done.3.refs_0_.one
  25.3 1.0 %scatter_points.5.refs_0_.total = f32[8,48,128]{2,1,0:T(8,128)S(1)} custom-call(f32[256,128]{1,0:T(8,128)S(1)} %collective-permute-done.3.refs_0_.one, f32[208,128]{1,0:T(8,128)S(1)} %collective-permute-done.4.refs_1_, f32[8,48,128]{2,1,0:T(8,128)S(1)} %scatter_points.4.refs_2_), custom_call_target="tpu_custom_call" | custom-call | tf_op jit(solution)/shard_map/scatter_points/pallas_call | solution.py:439
  26.3 1.8 %collective-permute-done.11.other = f32[48,128]{1,0:T(8,128)S(1)} collective-permute-done((f32[48,128]{1,0:T(8,128)S(1)}, f32[48,128]{1,0:T(8,128)S(1)}, u32[]{:S(2)}, u32[]{:S(2)}) %collective-permute-start.11) | collective-permute-done | bytes 24608 | tf_op jit(solution)/shard_map/ppermute | solution.py:589
  28.1 0.0 copy-done
  28.1 1.9 %widen_states.1 = (f32[4,16,112,256]{3,2,1,0:T(8,128)S(1)}, f32[16,256]{1,0:T(8,128)S(1)}) custom-call(f32[4,8,48,128]{3,2,1,0:T(8,128)S(1)} %get-tuple-element.28.turned, f32[544,128]{1,0:T(8,128)S(1)} %collective-permute-done.1.pair.where, f32[480,128]{1,0:T(8,128)S(1)} %collective-permute-done.2.cross, f32[256,128]{1,0:T(8,128)S(1)} %collective-permute-done.3.refs_0_.one, ...), custom_call_target="tpu_custom_call" | custom-call | tf_op jit(solution)/shard_map/widen_states/pallas_call | solution.py:239
  30.0 0.0 collective-permute-done.9.refs_0_
  30.0 0.9 %collective-permute-done.10.refs_1_ = f32[4,48,128]{2,1,0:T(8,128)S(1)} collective-permute-done((f32[4,48,128]{2,1,0:T(8,128)S(1)}, f32[4,48,128]{2,1,0:T(8,128)S(1)}, u32[]{:S(2)}, u32[]{:S(2)}) %collective-permute-start.10) | collective-permute-done | bytes 98336 | tf_op jit(solution)/shard_map/ppermute | solution.py:589
  30.9 1.0 %collective-permute-start.12 = (f32[4,48,128]{2,1,0:T(8,128)S(1)}, f32[4,48,128]{2,1,0:T(8,128)S(1)}, u32[]{:S(2)}, u32[]{:S(2)}) collective-permute-start(f32[4,48,128]{2,1,0:T(8,128)S(1)} %get-tuple-element.44), channel_id=1, source_target_pairs={{0,4},{1,5},{2,6},{3,7},{4,0},{5,1},{6,2},{7,3},{8,12},{9,13},{10,... | collective-permute-start | bytes 294920 | tf_op jit(solution)/shard_map/ppermute | solution.py:589
  31.9 3.0 %collective-permute-start.13 = (f32[4,48,128]{2,1,0:T(8,128)S(1)}, f32[4,48,128]{2,1,0:T(8,128)S(1)}, u32[]{:S(2)}, u32[]{:S(2)}) collective-permute-start(f32[4,48,128]{2,1,0:T(8,128)S(1)} %get-tuple-element.45), channel_id=1, source_target_pairs={{4,8},{8,4},{5,9},{9,5},{6,10},{10,6},{7,11},{11,7},{20,24},{24,20... | collective-permute-start | bytes 294920 | tf_op jit(solution)/shard_map/ppermute | solution.py:594
  35.0 0.0 collective-permute-done.12.pair
  35.0 3.2 %collective-permute-done.13.cross = f32[4,48,128]{2,1,0:T(8,128)S(1)} collective-permute-done((f32[4,48,128]{2,1,0:T(8,128)S(1)}, f32[4,48,128]{2,1,0:T(8,128)S(1)}, u32[]{:S(2)}, u32[]{:S(2)}) %collective-permute-start.13) | collective-permute-done | bytes 98336 | tf_op jit(solution)/shard_map/ppermute | solution.py:594
  38.2 0.2 adjoint_edges.1
  38.3 3.1 %collective-permute-start.15 = (f32[48,128]{1,0:T(8,128)S(1)}, f32[48,128]{1,0:T(8,128)S(1)}, u32[]{:S(2)}, u32[]{:S(2)}) collective-permute-start(f32[48,128]{1,0:T(8,128)S(1)} %adjoint_edges.1), channel_id=1, source_target_pairs={{0,3},{1,2},{2,1},{3,0},{4,7},{5,6},{6,5},{7,4},{8,11},{9,10},{10,... | collective-permute-start | bytes 73736 | tf_op jit(solution)/shard_map/ppermute | solution.py:589
  41.4 1.5 %collective-permute-start.14 = (f32[48,128]{1,0:T(8,128)S(1)}, f32[48,128]{1,0:T(8,128)S(1)}, u32[]{:S(2)}, u32[]{:S(2)}) collective-permute-start(f32[48,128]{1,0:T(8,128)S(1)} %adjoint_edges.1), channel_id=1, source_target_pairs={{0,1},{1,0},{2,3},{3,2},{4,5},{5,4},{6,7},{7,6},{8,9},{9,8},{10,11... | collective-permute-start | bytes 73736 | tf_op jit(solution)/shard_map/ppermute | solution.py:589
  42.9 0.0 collective-permute-done.15.other
  42.9 1.2 %collective-permute-done.14.one = f32[48,128]{1,0:T(8,128)S(1)} collective-permute-done((f32[48,128]{1,0:T(8,128)S(1)}, f32[48,128]{1,0:T(8,128)S(1)}, u32[]{:S(2)}, u32[]{:S(2)}) %collective-permute-start.14) | collective-permute-done | bytes 24608 | tf_op jit(solution)/shard_map/ppermute | solution.py:589
  44.1 2.6 %adjoint_steps.1 = f32[384,128]{1,0:T(8,128)} custom-call(f32[8,48,128]{2,1,0:T(8,128)S(1)} %get-tuple-element.43.canvas, f32[4,48,128]{2,1,0:T(8,128)S(1)} %collective-permute-done.12.pair, f32[4,48,128]{2,1,0:T(8,128)S(1)} %collective-permute-done.13.cross, f32[48,128]{1,0:T(8,128)S(1)} %collective-permute-done.14.one, ...), custom_call_target="tpu_custom_call" | custom-call | tf_op jit(solution)/shard_map/adjoint_steps/pallas_call | solution.py:571
  (1 shorter events, 0.0 us)
Async XLA Ops:
  0.0 28.1 %copy-start = (f32[16]{0:T(128)S(1)}, f32[16]{0:T(128)}, u32[]{:S(2)}) copy-start(f32[16]{0:T(128)} %gravity.1) | copy-start | bytes 196
  0.0 7.5 %collective-permute-start = (f32[48,2048]{1,0:T(8,128)}, f32[48,2048]{1,0:T(8,128)S(1)}, u32[]{:S(2)}, u32[]{:S(2)}) collective-permute-start(f32[48,2048]{1,0:T(8,128)} %bitcast.6), channel_id=1, source_target_pairs={{0,4},{1,5},{2,6},{3,7},{4,0},{5,1},{6,2},{7,3},{8,12},{9,13},{10,... | collective-permute-start | bytes 1179656 | tf_op jit(solution)/shard_map/ppermute | solution.py:589
  1.4 6.0 %collective-permute-start.1 = (f32[544,128]{1,0:T(8,128)S(1)}, f32[544,128]{1,0:T(8,128)S(1)}, u32[]{:S(2)}, u32[]{:S(2)}) collective-permute-start(f32[544,128]{1,0:T(8,128)S(1)} %get-tuple-element.26.where), channel_id=1, source_target_pairs={{0,4},{1,5},{2,6},{3,7},{4,0},{5,1},{6,2},{7,3},{8,12},{9,13},{10,... | collective-permute-start | bytes 835592 | tf_op jit(solution)/shard_map/ppermute | solution.py:589
  2.0 10.2 %collective-permute-start.2 = (f32[480,128]{1,0:T(8,128)S(1)}, f32[480,128]{1,0:T(8,128)S(1)}, u32[]{:S(2)}, u32[]{:S(2)}) collective-permute-start(f32[480,128]{1,0:T(8,128)S(1)} %get-tuple-element.29), channel_id=1, source_target_pairs={{4,8},{8,4},{5,9},{9,5},{6,10},{10,6},{7,11},{11,7},{20,24},{24,20... | collective-permute-start | bytes 737288 | tf_op jit(solution)/shard_map/ppermute | solution.py:594
  8.5 6.8 %collective-permute-start.8 = (f32[208,128]{1,0:T(8,128)S(1)}, f32[208,128]{1,0:T(8,128)S(1)}, u32[]{:S(2)}, u32[]{:S(2)}) collective-permute-start(f32[208,128]{1,0:T(8,128)S(1)} %get-tuple-element.38), channel_id=1, source_target_pairs={{0,8},{1,9},{2,10},{3,11},{4,12},{5,13},{6,14},{7,15},{8,0},{9,1},... | collective-permute-start | bytes 319496 | tf_op jit(solution)/shard_map/ppermute | solution.py:589
  8.6 9.0 %collective-permute-start.6 = (f32[208,128]{1,0:T(8,128)S(1)}, f32[208,128]{1,0:T(8,128)S(1)}, u32[]{:S(2)}, u32[]{:S(2)}) collective-permute-start(f32[208,128]{1,0:T(8,128)S(1)} %get-tuple-element.35), channel_id=1, source_target_pairs={{0,1},{1,0},{2,3},{3,2},{4,5},{5,4},{6,7},{7,6},{8,9},{9,8},{10,11... | collective-permute-start | bytes 319496 | tf_op jit(solution)/shard_map/ppermute | solution.py:589
  9.9 7.6 %collective-permute-start.7 = (f32[208,128]{1,0:T(8,128)S(1)}, f32[208,128]{1,0:T(8,128)S(1)}, u32[]{:S(2)}, u32[]{:S(2)}) collective-permute-start(f32[208,128]{1,0:T(8,128)S(1)} %get-tuple-element.36), channel_id=1, source_target_pairs={{0,9},{1,8},{2,11},{3,10},{4,13},{5,12},{6,15},{7,14},{8,1},{9,0},... | collective-permute-start | bytes 319496 | tf_op jit(solution)/shard_map/ppermute | solution.py:589
  13.9 7.1 %collective-permute-start.5 = (f32[208,128]{1,0:T(8,128)S(1)}, f32[208,128]{1,0:T(8,128)S(1)}, u32[]{:S(2)}, u32[]{:S(2)}) collective-permute-start(f32[208,128]{1,0:T(8,128)S(1)} %get-tuple-element.34), channel_id=1, source_target_pairs={{0,8},{1,9},{2,10},{3,11},{4,12},{5,13},{6,14},{7,15},{8,0},{9,1},... | collective-permute-start | bytes 319496 | tf_op jit(solution)/shard_map/ppermute | solution.py:589
  14.1 11.2 %collective-permute-start.3 = (f32[256,128]{1,0:T(8,128)S(1)}, f32[256,128]{1,0:T(8,128)S(1)}, u32[]{:S(2)}, u32[]{:S(2)}) collective-permute-start(f32[256,128]{1,0:T(8,128)S(1)} %get-tuple-element.31), channel_id=1, source_target_pairs={{0,1},{1,0},{2,3},{3,2},{4,5},{5,4},{6,7},{7,6},{8,9},{9,8},{10,11... | collective-permute-start | bytes 393224 | tf_op jit(solution)/shard_map/ppermute | solution.py:589
  15.3 10.0 %collective-permute-start.4 = (f32[208,128]{1,0:T(8,128)S(1)}, f32[208,128]{1,0:T(8,128)S(1)}, u32[]{:S(2)}, u32[]{:S(2)}) collective-permute-start(f32[208,128]{1,0:T(8,128)S(1)} %get-tuple-element.32), channel_id=1, source_target_pairs={{0,9},{1,8},{2,11},{3,10},{4,13},{5,12},{6,15},{7,14},{8,1},{9,0},... | collective-permute-start | bytes 319496 | tf_op jit(solution)/shard_map/ppermute | solution.py:589
  18.6 11.4 %collective-permute-start.9 = (f32[4,48,128]{2,1,0:T(8,128)S(1)}, f32[4,48,128]{2,1,0:T(8,128)S(1)}, u32[]{:S(2)}, u32[]{:S(2)}) collective-permute-start(f32[4,48,128]{2,1,0:T(8,128)S(1)} %get-tuple-element.39), channel_id=1, source_target_pairs={{0,2},{1,3},{2,0},{3,1},{4,6},{5,7},{6,4},{7,5},{8,10},{9,11},{10,... | collective-permute-start | bytes 294920 | tf_op jit(solution)/shard_map/ppermute | solution.py:589
  20.9 9.9 %collective-permute-start.10 = (f32[4,48,128]{2,1,0:T(8,128)S(1)}, f32[4,48,128]{2,1,0:T(8,128)S(1)}, u32[]{:S(2)}, u32[]{:S(2)}) collective-permute-start(f32[4,48,128]{2,1,0:T(8,128)S(1)} %get-tuple-element.40), channel_id=1, source_target_pairs={{0,2},{1,3},{2,0},{3,1},{4,6},{5,7},{6,4},{7,5},{8,10},{9,11},{10,... | collective-permute-start | bytes 294920 | tf_op jit(solution)/shard_map/ppermute | solution.py:589
  21.0 7.0 %collective-permute-start.11 = (f32[48,128]{1,0:T(8,128)S(1)}, f32[48,128]{1,0:T(8,128)S(1)}, u32[]{:S(2)}, u32[]{:S(2)}) collective-permute-start(f32[48,128]{1,0:T(8,128)S(1)} %get-tuple-element.41), channel_id=1, source_target_pairs={{0,3},{1,2},{2,1},{3,0},{4,7},{5,6},{6,5},{7,4},{8,11},{9,10},{10,... | collective-permute-start | bytes 73736 | tf_op jit(solution)/shard_map/ppermute | solution.py:589
  30.9 4.1 %collective-permute-start.12 = (f32[4,48,128]{2,1,0:T(8,128)S(1)}, f32[4,48,128]{2,1,0:T(8,128)S(1)}, u32[]{:S(2)}, u32[]{:S(2)}) collective-permute-start(f32[4,48,128]{2,1,0:T(8,128)S(1)} %get-tuple-element.44), channel_id=1, source_target_pairs={{0,4},{1,5},{2,6},{3,7},{4,0},{5,1},{6,2},{7,3},{8,12},{9,13},{10,... | collective-permute-start | bytes 294920 | tf_op jit(solution)/shard_map/ppermute | solution.py:589
  31.9 6.2 %collective-permute-start.13 = (f32[4,48,128]{2,1,0:T(8,128)S(1)}, f32[4,48,128]{2,1,0:T(8,128)S(1)}, u32[]{:S(2)}, u32[]{:S(2)}) collective-permute-start(f32[4,48,128]{2,1,0:T(8,128)S(1)} %get-tuple-element.45), channel_id=1, source_target_pairs={{4,8},{8,4},{5,9},{9,5},{6,10},{10,6},{7,11},{11,7},{20,24},{24,20... | collective-permute-start | bytes 294920 | tf_op jit(solution)/shard_map/ppermute | solution.py:594
  38.3 4.6 %collective-permute-start.15 = (f32[48,128]{1,0:T(8,128)S(1)}, f32[48,128]{1,0:T(8,128)S(1)}, u32[]{:S(2)}, u32[]{:S(2)}) collective-permute-start(f32[48,128]{1,0:T(8,128)S(1)} %adjoint_edges.1), channel_id=1, source_target_pairs={{0,3},{1,2},{2,1},{3,0},{4,7},{5,6},{6,5},{7,4},{8,11},{9,10},{10,... | collective-permute-start | bytes 73736 | tf_op jit(solution)/shard_map/ppermute | solution.py:589
  41.4 2.7 %collective-permute-start.14 = (f32[48,128]{1,0:T(8,128)S(1)}, f32[48,128]{1,0:T(8,128)S(1)}, u32[]{:S(2)}, u32[]{:S(2)}) collective-permute-start(f32[48,128]{1,0:T(8,128)S(1)} %adjoint_edges.1), channel_id=1, source_target_pairs={{0,1},{1,0},{2,3},{3,2},{4,5},{5,4},{6,7},{7,6},{8,9},{9,8},{10,11... | collective-permute-start | bytes 73736 | tf_op jit(solution)/shard_map/ppermute | solution.py:589

commit v4 on v3

--- a/solution.py
+++ b/solution.py
@@ -44,10 +44,9 @@
     return lines
 
 
-def edge_columns(lines):
-    lane = lax.broadcasted_iota(jnp.int32, lines[0][1].shape, 1)
+def edge_columns(lines, result):
+    lane = lax.broadcasted_iota(jnp.int32, result.shape, 1)
     owner = ((lane + 4) // 8) % 16
-    result = jnp.zeros_like(lines[0][1])
     for k, line in lines:
         result = jnp.where(owner == k, pltpu.roll(line, (8 * k) % LANES, 1), result)
     return result
@@ -161,7 +160,8 @@
     return first, last
 
 
-def state_edges_kernel(n_row, pair_at, paired, turned, pair, cross, one, other):
+def state_edges_kernel(n_row, pair_at, paired, turned, pair, cross, *refs):
+    one, other = refs[-2:]
     first, last = state_edges(n_row, turned, pair, pair_at, cross)
     if paired:
         lower = first_of_pair("fcol")
@@ -169,13 +169,13 @@
     one[...], other[...] = first, last
 
 
-def all_state_edges(n_row, pair_at, paired, turned, pair, cross):
+def all_state_edges(n_row, pair_at, paired, turned, pair, cross, after=()):
     return pl.pallas_call(
         functools.partial(state_edges_kernel, n_row, pair_at, paired),
         out_shape=[jax.ShapeDtypeStruct((turned.shape[2], LANES), F32)] * 2,
         compiler_params=PARAMS,
         name="state_edges",
-    )(turned, pair, cross)
+    )(turned, pair, cross, *after)
 
 
 FIELDS = 7
@@ -185,7 +185,7 @@
     return 0.5 * time_step if which % 2 == 0 else time_step
 
 
-def widen_kernel(n_row, pair_at, edge_at, paired, turned, pair, cross, one, other, gravity, *refs):
+def widen_kernel(n_row, pair_at, paired, turned, pair, cross, one, other, gravity, *refs):
     wide, pull = refs[-2:]
     _, tile_rows, channels, columns = turned.shape
     levels = channels // 3
@@ -202,7 +202,7 @@
     def along_x(values):
         return pltpu.roll(values, 2 * columns - 1, 1) - pltpu.roll(values, 1, 1)
 
-    left, right = from_sides(one[edge_at : edge_at + channels, :], other[...], paired)
+    left, right = from_sides(one[...], other[...], paired)
     lane = lax.broadcasted_iota(jnp.int32, (channels, columns), 1)
     rims = {
         (which, k): jnp.where(
@@ -233,11 +233,11 @@
                 begin += levels
 
 
-def widen(n_row, pair_at, edge_at, paired, turned, pair, cross, one, other, gravity, after=()):
+def widen(n_row, pair_at, paired, turned, pair, cross, one, other, gravity, after=()):
     stages, tile_rows, channels, columns = turned.shape
     in_vmem = pl.BlockSpec(memory_space=pltpu.VMEM)
     return pl.pallas_call(
-        functools.partial(widen_kernel, n_row, pair_at, edge_at, paired),
+        functools.partial(widen_kernel, n_row, pair_at, paired),
         in_specs=[in_vmem] * 5 + [pl.BlockSpec(memory_space=pltpu.SMEM)] + [in_vmem] * len(after),
         out_shape=(
             jax.ShapeDtypeStruct((stages, tile_rows + 2 * HALO, channels // 3 * FIELDS, 2 * columns), F32),
@@ -248,7 +248,7 @@
     )(turned, pair, cross, one, other, gravity, *after)
 
 
-def slot_blocks(cot, where, tiles, share, tile_rows, columns, onehot, high, low):
+def slot_blocks(cot, where, tiles, share, tile_rows, columns, onehot, parts):
     channels, points = cot.shape
     lines = points // LANES
     groups = tiles.shape[0] // share
@@ -287,9 +287,10 @@
             for i in range(1, share):
                 mine = mine + named[g * share + i : g * share + i + 1, :]
             mine = mine.astype(BF16)
-            high[g * rows : (g + 1) * rows, part] = data_high * mine
-            low[g * rows : (g + 1) * rows, part] = data_low * mine
-    packed = dot_nt(high[...], onehot[...]) + dot_nt(low[...], onehot[...])
+            parts[g * rows : (g + 1) * rows, part] = data_high * mine
+            parts[(groups + g) * rows : (groups + g + 1) * rows, part] = data_low * mine
+    both = dot_nt(parts[...], onehot[...])
+    packed = both[: groups * rows, :] + both[groups * rows :, :]
     upper = lax.broadcasted_iota(jnp.int32, (8, LANES), 0) < 4
     for g in range(groups):
         block = packed[g * rows : (g + 1) * rows, :]
@@ -310,8 +311,7 @@
 def pack_scratch(channels, points, groups):
     return [
         pltpu.VMEM((GROUP, points), BF16),
-        pltpu.VMEM((groups * (channels + 8), points), BF16),
-        pltpu.VMEM((groups * (channels + 8), points), BF16),
+        pltpu.VMEM((2 * groups * (channels + 8), points), BF16),
     ]
 
 
@@ -347,55 +347,32 @@
     return tiles.astype(F32)
 
 
-def pack_own_kernel(tiles, tile_rows, columns, cot, where, out, *scratch):
-    for g, pieces in enumerate(slot_blocks(cot, where, partner_tiles(tiles), 1, tile_rows, columns, *scratch)):
-        store_block(out.at[g], 0, pieces)
-
-
-def pack_own(tiles, cot, where, tile_rows, columns):
-    channels, points = cot.shape
-    groups = len(tiles)
-    return pl.pallas_call(
-        functools.partial(pack_own_kernel, tiles, tile_rows, columns),
-        out_shape=jax.ShapeDtypeStruct((groups, 2 * channels + 8, LANES), F32),
-        scratch_shapes=pack_scratch(channels, points, groups),
-        compiler_params=PARAMS,
-        name="pack_own",
-    )(cot, where)
-
-
-def pack_partner_kernel(tiles, tailed, tile_rows, columns, cot, where, own, *refs):
-    if tailed is not None:
-        tail, *refs = refs
-    outs, scratch = refs[:-3], refs[-3:]
-    size = own.shape[1]
-    blocks = slot_blocks(cot, where, partner_tiles(tiles), 1, tile_rows, columns, *scratch)
-    for g, pieces in enumerate(blocks):
-        outs[g][:size, :] = own[g]
-        store_block(outs[g], size, pieces)
-        if tiles[g] == tailed:
-            outs[g][2 * size :, :] = tail[...]
-
-
-def pack_partner(tiles, cot, where, own, tile_rows, columns, tailed=None, tail=None):
-    channels, points = cot.shape
-    rows = 2 * own.shape[1]
-    sizes = [rows + (tail.shape[0] if tile == tailed else 0) for tile in tiles]
-    blocks = pl.pallas_call(
-        functools.partial(pack_partner_kernel, tiles, tailed, tile_rows, columns),
-        out_shape=[jax.ShapeDtypeStruct((size, LANES), F32) for size in sizes],
-        scratch_shapes=pack_scratch(channels, points, len(tiles)),
-        compiler_params=PARAMS,
-        name="pack_partner",
-    )(cot, where, own, *([] if tail is None else [tail]))
-    return dict(zip(tiles, blocks))
+def pack_chip_kernel(tiles, tile_rows, columns, cot, where, pair_cot, pair_where, *refs):
+    outs, scratch = refs[-4 - len(tiles) : -4], refs[-4:]
+    begin = 0
+    for i, points in enumerate(((cot, where), (pair_cot, pair_where))):
+        blocks = slot_blocks(*points, partner_tiles(tiles), 1, tile_rows, columns, *scratch[2 * i : 2 * i + 2])
+        for out, pieces in zip(outs, blocks):
+            store_block(out, begin, pieces)
+        begin += 2 * cot.shape[0] + 8
+
+
+def pack_chip(tiles, points, tile_rows, columns, after=()):
+    channels, count = points[0].shape
+    return pl.pallas_call(
+        functools.partial(pack_chip_kernel, tiles, tile_rows, columns),
+        out_shape=[jax.ShapeDtypeStruct((2 * (2 * channels + 8), LANES), F32)] * len(tiles),
+        scratch_shapes=pack_scratch(channels, count, len(tiles)) * 2,
+        compiler_params=PARAMS,
+        name="pack_chip",
+    )(*points, *after)
 
 
 def scatter_kernel(count, first, later, *refs):
     blocks, refs = refs[:count], refs[count:]
     if not first:
         total, refs = refs[0], refs[1:]
-    outs, (high, low, weight) = refs[later:-3], refs[-3:]
+    outs, (parts, weight) = refs[later:-2], refs[-2:]
     part_rows, channels, columns = outs[0].shape
     tile_rows = part_rows * len(outs)
     rows = 2 * channels + 8
@@ -423,10 +400,11 @@
                 row_weight = hat(lines, row, along_rows)
                 for r in range(tile_rows):
                     product_high, product_low = split(values * row_weight[r : r + 1, :])
-                    high[r * channels : (r + 1) * channels, part] = product_high
-                    low[r * channels : (r + 1) * channels, part] = product_low
-    both = dot_nt(high[...], weight[...])
-    sums = both[:, :columns] + both[:, columns:] + dot_nt(low[...], weight[:columns, :])
+                    parts[r * channels : (r + 1) * channels, part] = product_high
+                    parts[(tile_rows + r) * channels : (tile_rows + r + 1) * channels, part] = product_low
+    both = dot_nt(parts[...], weight[...])
+    sums = both[:, :columns] + both[:, columns:]
+    sums = sums[: tile_rows * channels, :] + sums[tile_rows * channels :, :]
     for r in range(tile_rows):
         line = sums[r * channels : (r + 1) * channels, :]
         if not first:
@@ -440,8 +418,7 @@
         functools.partial(scatter_kernel, len(blocks), total is None, len(after)),
         out_shape=[jax.ShapeDtypeStruct((tile_rows // parts, channels, columns), F32)] * parts,
         scratch_shapes=[
-            pltpu.VMEM((tile_rows * channels, slots), BF16),
-            pltpu.VMEM((tile_rows * channels, slots), BF16),
+            pltpu.VMEM((2 * tile_rows * channels, slots), BF16),
             pltpu.VMEM((2 * columns, slots), BF16),
         ],
         compiler_params=PARAMS,
@@ -482,17 +459,41 @@
     return extended_rows(tile, *rims, HALO, first_of_pair(), row_masks(n_row))
 
 
-def adjoint_edges_kernel(n_row, canvas, pair, cross, edges):
-    edges[...] = edge_columns(adjoint_rows(n_row, canvas, pair, cross))
-
-
-def adjoint_edges(n_row, canvas, pair, cross):
-    return pl.pallas_call(
-        functools.partial(adjoint_edges_kernel, n_row),
-        out_shape=jax.ShapeDtypeStruct(canvas.shape[1:], F32),
-        compiler_params=PARAMS,
-        name="adjoint_edges",
-    )(canvas, pair, cross)
+def cross_edges_kernel(canvas, cross, *refs):
+    edges = refs[-1]
+    lower = first_of_pair()
+    tile_rows = canvas.shape[0]
+    empty = jnp.zeros(edges.shape, F32)
+    lines = [(k, jnp.where(lower, cross[k], empty)) for k in range(HALO)]
+    lines += [(HALO + r, canvas[r]) for r in range(tile_rows)]
+    lines += [(HALO + tile_rows + k, jnp.where(lower, empty, cross[k])) for k in range(HALO)]
+    edges[...] = edge_columns(lines, empty)
+
+
+def pair_edges_kernel(n_row, tile_rows, partial, pair, edges):
+    lower, masks = first_of_pair(), row_masks(n_row)
+    result = partial[...]
+    empty = jnp.zeros(edges.shape, F32)
+    lane = lax.broadcasted_iota(jnp.int32, edges.shape, 1)
+    row = ((lane + 4) // 8) % 16
+    result = jnp.where(row < HALO, masks[0], jnp.where(row < HALO + tile_rows, 1.0, masks[1])) * result
+    lines = [(k, jnp.where(lower, empty, pair[k])) for k in range(HALO)]
+    lines += [(HALO + tile_rows + k, jnp.where(lower, pair[k], empty)) for k in range(HALO)]
+    edges[...] = result + edge_columns(lines, empty)
+
+
+def adjoint_edges(n_row, canvas, pair, cross, after=()):
+    tile_rows, channels, _ = canvas.shape
+    edges = jax.ShapeDtypeStruct((channels, LANES), F32)
+    partial = pl.pallas_call(
+        cross_edges_kernel, out_shape=edges, compiler_params=PARAMS, name="cross_edges"
+    )(canvas, cross, *after)
+    return pl.pallas_call(
+        functools.partial(pair_edges_kernel, n_row, tile_rows),
+        out_shape=edges,
+        compiler_params=PARAMS,
+        name="pair_edges",
+    )(partial, pair)
 
 
 def steps_kernel(n_row, paired, canvas, pair, cross, one, other, gravity, wide, out, start, middle, after, last):
@@ -643,33 +644,31 @@
     pair = exchanged(sent, (1, 0))
     cross = exchanged_across(to_cross)
     if paired:
-        own = pack_own(FAR, cot, sent, tile_rows, columns)
-        packed = pack_partner(FAR, partner_cot, pair, own, tile_rows, columns)
-        got = [packed[0, 2]] + [exchanged(packed[tile], (tile[0], tile[1] ^ 2)) for tile in FAR[1:]]
-        one, other = all_state_edges(n_row, pair_at, paired, turned, pair, cross)
-        own = pack_own(NEAR, cot, sent, tile_rows, columns)
-        packed = pack_partner(NEAR, partner_cot, pair, own, tile_rows, columns, (0, 1), one)
-        total = scatter(got[:2], None, *size, [packed[0, 0]])[0]
-        far = [exchanged(part, (0, 2)) for part in scatter(got[2:], total, *size, parts=2)]
-        got = {tile: exchanged(packed[tile], tile) for tile in NEAR[1:]}
-        other = exchanged(other, (0, 3))
-        total = scatter([packed[0, 0], got[2, 0]], None, *size)[0]
-        total = scatter([got[0, 1], got[2, 1]], total, *size)[0]
-        wide, pull = widen(
-            n_row, pair_at, 2 * own.shape[1], paired, turned, pair, cross, got[0, 1], other, gravity, [total]
-        )
-        canvas = finish(total, far, [pull])
+        chip_points = cot, sent, partner_cot, pair
+        packed = pack_chip(FAR, chip_points, tile_rows, columns)
+        got = [packed[0]] + [exchanged(block, (df, dz ^ 2)) for block, (df, dz) in zip(packed[1:], FAR[1:])]
+        packed = pack_chip(NEAR, chip_points, tile_rows, columns, [cross, packed[0]])
+        total = scatter(got[:2], None, *size, packed[:1])[0]
+        sums = scatter(got[2:], total, *size, parts=2)
+        far = [exchanged(part, (0, 2)) for part in sums]
+        got = [packed[0]] + [exchanged(block, tile) for block, tile in zip(packed[1:], NEAR[1:])]
+        one, other = all_state_edges(n_row, pair_at, paired, turned, pair, cross, sums)
+        one, other = exchanged(one, (0, 1)), exchanged(other, (0, 3))
+        total = scatter(got[:2], None, *size)[0]
+        total = scatter(got[2:], total, *size)[0]
+        wide, pull = widen(n_row, pair_at, paired, turned, pair, cross, one, other, gravity)
+        canvas = finish(total, far, [one, other])
     else:
         packed = pack_all(cot, sent, tile_count, share, tile_rows, columns)
         got = from_everyone(packed, channels, tile_count)
         one, other = all_state_edges(n_row, pair_at, paired, turned, pair, cross)
         one, other = shifted(one, "fcol", 1), shifted(other, "fcol", -1)
-        wide, pull = widen(n_row, pair_at, 0, paired, turned, pair, cross, one, other, gravity)
+        wide, pull = widen(n_row, pair_at, paired, turned, pair, cross, one, other, gravity)
         canvas = finish(scatter([got.reshape(-1, LANES)], None, *size)[0])
 
     canvas, to_pair, to_cross = canvas
     pair, cross = exchanged(to_pair, (1, 0)), exchanged_across(to_cross)
-    edges = adjoint_edges(n_row, canvas, pair, cross)
+    edges = adjoint_edges(n_row, canvas, pair, cross, [pull])
     if paired:
         sides = exchanged(edges, (0, 1)), exchanged(edges, (0, 3))
     else:

time: 46.9 us -> 45.1 us (0.962)
  the two profiles are of different devices: /device:TPU:1 before, /device:TPU:0 now
where the time goes in v4:
time: 45.1 us; the launch traced here: 44.9 us
  starting transfers between devices  23.3 us (52%)
  Pallas kernels  13.6 us (30%)
  waiting for transfers between devices  7.83 us (17%)
    ppermute x15, starting transfers between devices, exchanged(): return lax.ppermute(values, ('frow', 'fcol'), pairs)  22 us
    ppermute x15, waiting for transfers between devices, exchanged(): return lax.ppermute(values, ('frow', 'fcol'), pairs)  7.82 us
    pallas_call x4, Pallas kernels, scatter(): pl.pallas_call(functools.partial(scatter_kernel, len(blocks), total is No...  3.8 us
    pallas_call x2, Pallas kernels, pack_chip(): pl.pallas_call(functools.partial(pack_chip_kernel, tiles, tile_rows, colu...  2.9 us
    pallas_call x1, Pallas kernels, steps(): pl.pallas_call(functools.partial(steps_kernel, n_row, paired), out_shape=...  2.61 us
    pallas_call x1, Pallas kernels, widen(): pl.pallas_call(functools.partial(widen_kernel, n_row, pair_at, paired), i...  1.92 us
    pallas_call x1, Pallas kernels, prepare(): pl.pallas_call(functools.partial(prepare_kernel, order), in_specs=[in_hbm...  1.38 us
    ppermute x2, starting transfers between devices, exchanged_across(): lax.ppermute(values, 'frow', [(f, (f + 1 ^ 1) - 1) for f in range(1, n_ro...  1.33 us
  transfers between devices with their start and end apart: 17, of which 6 were waited for; matrix products, arithmetic and copies ran while one was open for 0% of the time, Pallas kernels for 24%

profile of v4, /device:TPU:0, one launch (start us, length us, event | category | flops | bytes accessed | tf_op | source)
XLA Modules:
  0.0 44.9 jit_solution(4057733333488147843)
XLA Ops:
  0.0 0.0 copy-start
  0.0 0.5 %collective-permute-start = (f32[48,2048]{1,0:T(8,128)}, f32[48,2048]{1,0:T(8,128)S(1)}, u32[]{:S(2)}, u32[]{:S(2)}) collective-permute-start(f32[48,2048]{1,0:T(8,128)} %bitcast.6), channel_id=1, source_target_pairs={{0,4},{1,5},{2,6},{3,7},{4,0},{5,1},{6,2},{7,3},{8,12},{9,13},{10,... | collective-permute-start | bytes 1179656 | tf_op jit(solution)/shard_map/ppermute | solution.py:590
  0.5 1.4 %prepare.1 = (f32[544,128]{1,0:T(8,128)S(1)}, f32[480,128]{1,0:T(8,128)S(1)}, f32[4,8,48,128]{3,2,1,0:T(8,128)S(1)}, f32[48,2048]{1,0:T(8,128)S(1)}) custom-call(s32[16,128]{1,0:T(8,128)} %bitcast.8, s32[16,128]{1,0:T(8,128)} %bitcast.9, f32[2,2048]{1,0:T(2,128)} %frac.1, f32[4,384,128]{2,1,0:T(8,128)} %bitcast.5, f32[48,2048]{1,0:T(8,128)} %bitcast.7), custom_call_target="tpu_custom_call" | custom-call | tf_op jit(solution)/shard_map/prepare/pallas_call | solution.py:105
  1.8 0.1 collective-permute-start.1
  2.0 0.7 %collective-permute-start.2 = (f32[480,128]{1,0:T(8,128)S(1)}, f32[480,128]{1,0:T(8,128)S(1)}, u32[]{:S(2)}, u32[]{:S(2)}) collective-permute-start(f32[480,128]{1,0:T(8,128)S(1)} %get-tuple-element.28), channel_id=1, source_target_pairs={{4,8},{8,4},{5,9},{9,5},{6,10},{10,6},{7,11},{11,7},{20,24},{24,20... | collective-permute-start | bytes 737288 | tf_op jit(solution)/shard_map/ppermute | solution.py:595
  2.6 0.8 %collective-permute-done.1.pair_where.pair = f32[544,128]{1,0:T(8,128)S(1)} collective-permute-done((f32[544,128]{1,0:T(8,128)S(1)}, f32[544,128]{1,0:T(8,128)S(1)}, u32[]{:S(2)}, u32[]{:S(2)}) %collective-permute-start.1) | collective-permute-done | bytes 278560 | tf_op jit(solution)/shard_map/ppermute | solution.py:590
  3.5 0.0 collective-permute-done.pair_cot
  3.5 1.5 %pack_chip.2 = (f32[208,128]{1,0:T(8,128)S(1)}, f32[208,128]{1,0:T(8,128)S(1)}, f32[208,128]{1,0:T(8,128)S(1)}, f32[208,128]{1,0:T(8,128)S(1)}) custom-call(f32[48,2048]{1,0:T(8,128)S(1)} %get-tuple-element.26.cot, f32[544,128]{1,0:T(8,128)S(1)} %get-tuple-element.27.where, f32[48,2048]{1,0:T(8,128)S(1)} %collective-permute-done.pair_cot, ...), custom_call_target="tpu_custom_call" | custom-call | tf_op jit(solution)/shard_map/pack_chip/pallas_call | solution.py:362
  4.9 3.4 %collective-permute-start.8 = (f32[208,128]{1,0:T(8,128)S(1)}, f32[208,128]{1,0:T(8,128)S(1)}, u32[]{:S(2)}, u32[]{:S(2)}) collective-permute-start(f32[208,128]{1,0:T(8,128)S(1)} %get-tuple-element.36), channel_id=1, source_target_pairs={{0,8},{1,9},{2,10},{3,11},{4,12},{5,13},{6,14},{7,15},{8,0},{9,1},... | collective-permute-start | bytes 319496 | tf_op jit(solution)/shard_map/ppermute | solution.py:590
  8.4 1.7 %collective-permute-start.6 = (f32[208,128]{1,0:T(8,128)S(1)}, f32[208,128]{1,0:T(8,128)S(1)}, u32[]{:S(2)}, u32[]{:S(2)}) collective-permute-start(f32[208,128]{1,0:T(8,128)S(1)} %get-tuple-element.34), channel_id=1, source_target_pairs={{0,1},{1,0},{2,3},{3,2},{4,5},{5,4},{6,7},{7,6},{8,9},{9,8},{10,11... | collective-permute-start | bytes 319496 | tf_op jit(solution)/shard_map/ppermute | solution.py:590
  10.1 0.0 collective-permute-start.7
  10.1 0.0 collective-permute-done.2.refs_0_.cross
  10.1 1.5 %pack_chip.3 = (f32[208,128]{1,0:T(8,128)S(1)}, f32[208,128]{1,0:T(8,128)S(1)}, f32[208,128]{1,0:T(8,128)S(1)}, f32[208,128]{1,0:T(8,128)S(1)}) custom-call(f32[48,2048]{1,0:T(8,128)S(1)} %get-tuple-element.26.cot, f32[544,128]{1,0:T(8,128)S(1)} %get-tuple-element.27.where, f32[48,2048]{1,0:T(8,128)S(1)} %collective-permute-done.pair_cot, ...), custom_call_target="tpu_custom_call" | custom-call | tf_op jit(solution)/shard_map/pack_chip/pallas_call | solution.py:362
  11.6 1.6 %collective-permute-start.3 = (f32[208,128]{1,0:T(8,128)S(1)}, f32[208,128]{1,0:T(8,128)S(1)}, u32[]{:S(2)}, u32[]{:S(2)}) collective-permute-start(f32[208,128]{1,0:T(8,128)S(1)} %get-tuple-element.30), channel_id=1, source_target_pairs={{0,1},{1,0},{2,3},{3,2},{4,5},{5,4},{6,7},{7,6},{8,9},{9,8},{10,11... | collective-permute-start | bytes 319496 | tf_op jit(solution)/shard_map/ppermute | solution.py:590
  13.2 2.6 %collective-permute-start.5 = (f32[208,128]{1,0:T(8,128)S(1)}, f32[208,128]{1,0:T(8,128)S(1)}, u32[]{:S(2)}, u32[]{:S(2)}) collective-permute-start(f32[208,128]{1,0:T(8,128)S(1)} %get-tuple-element.33), channel_id=1, source_target_pairs={{0,8},{1,9},{2,10},{3,11},{4,12},{5,13},{6,14},{7,15},{8,0},{9,1},... | collective-permute-start | bytes 319496 | tf_op jit(solution)/shard_map/ppermute | solution.py:590
  15.8 0.0 collective-permute-done.8.refs_1_
  15.8 0.1 collective-permute-start.4
  15.9 1.0 %scatter_points.6.refs_2_ = f32[8,48,128]{2,1,0:T(8,128)S(1)} custom-call(f32[208,128]{1,0:T(8,128)S(1)} %get-tuple-element.29.refs_1_.refs_0_, f32[208,128]{1,0:T(8,128)S(1)} %collective-permute-done.8.refs_1_, f32[208,128]{1,0:T(8,128)S(1)} %get-tuple-element.32.refs_0_.refs_2_), custom_call_target="tpu_custom_call" | custom-call | tf_op jit(solution)/shard_map/scatter_points/pallas_call | solution.py:417
  16.9 0.0 collective-permute-done.6.refs_0_
  16.9 0.0 collective-permute-done.7.refs_1_
  16.9 1.0 %scatter_points.7 = (f32[4,48,128]{2,1,0:T(8,128)S(1)}, f32[4,48,128]{2,1,0:T(8,128)S(1)}) custom-call(f32[208,128]{1,0:T(8,128)S(1)} %collective-permute-done.6.refs_0_, f32[208,128]{1,0:T(8,128)S(1)} %collective-permute-done.7.refs_1_, f32[8,48,128]{2,1,0:T(8,128)S(1)} %scatter_points.6.refs_2_), custom_call_target="tpu_custom_call" | custom-call | tf_op jit(solution)/shard_map/scatter_points/pallas_call | solution.py:417
  17.9 2.7 %collective-permute-start.9 = (f32[4,48,128]{2,1,0:T(8,128)S(1)}, f32[4,48,128]{2,1,0:T(8,128)S(1)}, u32[]{:S(2)}, u32[]{:S(2)}) collective-permute-start(f32[4,48,128]{2,1,0:T(8,128)S(1)} %get-tuple-element.37.refs_0_), channel_id=1, source_target_pairs={{0,2},{1,3},{2,0},{3,1},{4,6},{5,7},{6,4},{7,5},{8,10},{9,11},{10,... | collective-permute-start | bytes 294920 | tf_op jit(solution)/shard_map/ppermute | solution.py:590
  20.5 0.3 collective-permute-start.10
  20.9 0.6 %state_edges.1 = (f32[48,128]{1,0:T(8,128)S(1)}, f32[48,128]{1,0:T(8,128)S(1)}) custom-call(f32[4,8,48,128]{3,2,1,0:T(8,128)S(1)} %get-tuple-element.39.turned, f32[544,128]{1,0:T(8,128)S(1)} %collective-permute-done.1.pair_where.pair, f32[480,128]{1,0:T(8,128)S(1)} %collective-permute-done.2.refs_0_.cross, f32[4,48,128]{2,1,0:T(8,128)S(1)} %get-tuple-element.37.refs_0_, ...), custom_call_target="tpu_custom_call" | custom-call | tf_op jit(solution)/shard_map/state_edges/pallas_call | solution.py:173
  21.5 0.0 collective-permute-done.3.refs_0_
  21.5 1.4 %collective-permute-start.11 = (f32[48,128]{1,0:T(8,128)S(1)}, f32[48,128]{1,0:T(8,128)S(1)}, u32[]{:S(2)}, u32[]{:S(2)}) collective-permute-start(f32[48,128]{1,0:T(8,128)S(1)} %get-tuple-element.40), channel_id=1, source_target_pairs={{0,1},{1,0},{2,3},{3,2},{4,5},{5,4},{6,7},{7,6},{8,9},{9,8},{10,11... | collective-permute-start | bytes 73736 | tf_op jit(solution)/shard_map/ppermute | solution.py:590
  22.9 0.0 collective-permute-done.5.refs_1_
  22.9 2.7 %collective-permute-start.12 = (f32[48,128]{1,0:T(8,128)S(1)}, f32[48,128]{1,0:T(8,128)S(1)}, u32[]{:S(2)}, u32[]{:S(2)}) collective-permute-start(f32[48,128]{1,0:T(8,128)S(1)} %get-tuple-element.41), channel_id=1, source_target_pairs={{0,3},{1,2},{2,1},{3,0},{4,7},{5,6},{6,5},{7,4},{8,11},{9,10},{10,... | collective-permute-start | bytes 73736 | tf_op jit(solution)/shard_map/ppermute | solution.py:590
  25.6 0.9 %scatter_points.4.refs_2_ = f32[8,48,128]{2,1,0:T(8,128)S(1)} custom-call(f32[208,128]{1,0:T(8,128)S(1)} %get-tuple-element.32.refs_0_.refs_2_, f32[208,128]{1,0:T(8,128)S(1)} %collective-permute-done.5.refs_1_), custom_call_target="tpu_custom_call" | custom-call | tf_op jit(solution)/shard_map/scatter_points/pallas_call | solution.py:417
  26.6 0.0 collective-permute-done.4.refs_1_
  26.6 0.9 %scatter_points.5.total = f32[8,48,128]{2,1,0:T(8,128)S(1)} custom-call(f32[208,128]{1,0:T(8,128)S(1)} %collective-permute-done.3.refs_0_, f32[208,128]{1,0:T(8,128)S(1)} %collective-permute-done.4.refs_1_, f32[8,48,128]{2,1,0:T(8,128)S(1)} %scatter_points.4.refs_2_), custom_call_target="tpu_custom_call" | custom-call | tf_op jit(solution)/shard_map/scatter_points/pallas_call | solution.py:417
  27.6 0.0 collective-permute-done.11.refs_2_.one
  27.6 1.1 %collective-permute-done.12.refs_3_.other = f32[48,128]{1,0:T(8,128)S(1)} collective-permute-done((f32[48,128]{1,0:T(8,128)S(1)}, f32[48,128]{1,0:T(8,128)S(1)}, u32[]{:S(2)}, u32[]{:S(2)}) %collective-permute-start.12) | collective-permute-done | bytes 24608 | tf_op jit(solution)/shard_map/ppermute | solution.py:590
  28.6 0.3 collective-permute-done.9.refs_0_
  28.9 1.8 %collective-permute-done.10.refs_1_ = f32[4,48,128]{2,1,0:T(8,128)S(1)} collective-permute-done((f32[4,48,128]{2,1,0:T(8,128)S(1)}, f32[4,48,128]{2,1,0:T(8,128)S(1)}, u32[]{:S(2)}, u32[]{:S(2)}) %collective-permute-start.10) | collective-permute-done | bytes 98336 | tf_op jit(solution)/shard_map/ppermute | solution.py:590
  30.7 0.7 %collective-permute-start.14 = (f32[4,48,128]{2,1,0:T(8,128)S(1)}, f32[4,48,128]{2,1,0:T(8,128)S(1)}, u32[]{:S(2)}, u32[]{:S(2)}) collective-permute-start(f32[4,48,128]{2,1,0:T(8,128)S(1)} %get-tuple-element.44), channel_id=1, source_target_pairs={{4,8},{8,4},{5,9},{9,5},{6,10},{10,6},{7,11},{11,7},{20,24},{24,20... | collective-permute-start | bytes 294920 | tf_op jit(solution)/shard_map/ppermute | solution.py:595
  31.4 1.9 %collective-permute-start.13 = (f32[4,48,128]{2,1,0:T(8,128)S(1)}, f32[4,48,128]{2,1,0:T(8,128)S(1)}, u32[]{:S(2)}, u32[]{:S(2)}) collective-permute-start(f32[4,48,128]{2,1,0:T(8,128)S(1)} %get-tuple-element.43), channel_id=1, source_target_pairs={{0,4},{1,5},{2,6},{3,7},{4,0},{5,1},{6,2},{7,3},{8,12},{9,13},{10,... | collective-permute-start | bytes 294920 | tf_op jit(solution)/shard_map/ppermute | solution.py:590
  33.3 0.0 copy-done
  33.3 1.9 %widen_states.1 = (f32[4,16,112,256]{3,2,1,0:T(8,128)S(1)}, f32[16,256]{1,0:T(8,128)S(1)}) custom-call(f32[4,8,48,128]{3,2,1,0:T(8,128)S(1)} %get-tuple-element.39.turned, f32[544,128]{1,0:T(8,128)S(1)} %collective-permute-done.1.pair_where.pair, f32[480,128]{1,0:T(8,128)S(1)} %collective-permute-done.2.refs_0_.cross, ...), custom_call_target="tpu_custom_call" | custom-call | tf_op jit(solution)/shard_map/widen_states/pallas_call | solution.py:239
  35.3 0.0 collective-permute-done.14.cross
  35.3 0.2 cross_edges.1.partial
  35.4 0.0 collective-permute-done.13.pair
  35.5 0.1 pair_edges.1
  35.6 2.9 %collective-permute-start.16 = (f32[48,128]{1,0:T(8,128)S(1)}, f32[48,128]{1,0:T(8,128)S(1)}, u32[]{:S(2)}, u32[]{:S(2)}) collective-permute-start(f32[48,128]{1,0:T(8,128)S(1)} %pair_edges.1), channel_id=1, source_target_pairs={{0,3},{1,2},{2,1},{3,0},{4,7},{5,6},{6,5},{7,4},{8,11},{9,10},{10,... | collective-permute-start | bytes 73736 | tf_op jit(solution)/shard_map/ppermute | solution.py:590
  38.5 0.0 collective-permute-start.15
  38.5 3.0 %collective-permute-done.16.other = f32[48,128]{1,0:T(8,128)S(1)} collective-permute-done((f32[48,128]{1,0:T(8,128)S(1)}, f32[48,128]{1,0:T(8,128)S(1)}, u32[]{:S(2)}, u32[]{:S(2)}) %collective-permute-start.16) | collective-permute-done | bytes 24608 | tf_op jit(solution)/shard_map/ppermute | solution.py:590
  41.4 0.9 %collective-permute-done.15.one = f32[48,128]{1,0:T(8,128)S(1)} collective-permute-done((f32[48,128]{1,0:T(8,128)S(1)}, f32[48,128]{1,0:T(8,128)S(1)}, u32[]{:S(2)}, u32[]{:S(2)}) %collective-permute-start.15) | collective-permute-done | bytes 24608 | tf_op jit(solution)/shard_map/ppermute | solution.py:590
  42.3 2.6 %adjoint_steps.1 = f32[384,128]{1,0:T(8,128)} custom-call(f32[8,48,128]{2,1,0:T(8,128)S(1)} %get-tuple-element.42.canvas, f32[4,48,128]{2,1,0:T(8,128)S(1)} %collective-permute-done.13.pair, f32[4,48,128]{2,1,0:T(8,128)S(1)} %collective-permute-done.14.cross, f32[48,128]{1,0:T(8,128)S(1)} %collective-permute-done.15.one, ...), custom_call_target="tpu_custom_call" | custom-call | tf_op jit(solution)/shard_map/adjoint_steps/pallas_call | solution.py:572
  (1 shorter events, 0.0 us)
Async XLA Ops:
  0.0 33.3 %copy-start = (f32[16]{0:T(128)S(1)}, f32[16]{0:T(128)}, u32[]{:S(2)}) copy-start(f32[16]{0:T(128)} %gravity.1) | copy-start | bytes 196
  0.0 3.5 %collective-permute-start = (f32[48,2048]{1,0:T(8,128)}, f32[48,2048]{1,0:T(8,128)S(1)}, u32[]{:S(2)}, u32[]{:S(2)}) collective-permute-start(f32[48,2048]{1,0:T(8,128)} %bitcast.6), channel_id=1, source_target_pairs={{0,4},{1,5},{2,6},{3,7},{4,0},{5,1},{6,2},{7,3},{8,12},{9,13},{10,... | collective-permute-start | bytes 1179656 | tf_op jit(solution)/shard_map/ppermute | solution.py:590
  1.8 1.6 %collective-permute-start.1 = (f32[544,128]{1,0:T(8,128)S(1)}, f32[544,128]{1,0:T(8,128)S(1)}, u32[]{:S(2)}, u32[]{:S(2)}) collective-permute-start(f32[544,128]{1,0:T(8,128)S(1)} %get-tuple-element.27.where), channel_id=1, source_target_pairs={{0,4},{1,5},{2,6},{3,7},{4,0},{5,1},{6,2},{7,3},{8,12},{9,13},{10,... | collective-permute-start | bytes 835592 | tf_op jit(solution)/shard_map/ppermute | solution.py:590
  2.0 8.1 %collective-permute-start.2 = (f32[480,128]{1,0:T(8,128)S(1)}, f32[480,128]{1,0:T(8,128)S(1)}, u32[]{:S(2)}, u32[]{:S(2)}) collective-permute-start(f32[480,128]{1,0:T(8,128)S(1)} %get-tuple-element.28), channel_id=1, source_target_pairs={{4,8},{8,4},{5,9},{9,5},{6,10},{10,6},{7,11},{11,7},{20,24},{24,20... | collective-permute-start | bytes 737288 | tf_op jit(solution)/shard_map/ppermute | solution.py:595
  4.9 10.8 %collective-permute-start.8 = (f32[208,128]{1,0:T(8,128)S(1)}, f32[208,128]{1,0:T(8,128)S(1)}, u32[]{:S(2)}, u32[]{:S(2)}) collective-permute-start(f32[208,128]{1,0:T(8,128)S(1)} %get-tuple-element.36), channel_id=1, source_target_pairs={{0,8},{1,9},{2,10},{3,11},{4,12},{5,13},{6,14},{7,15},{8,0},{9,1},... | collective-permute-start | bytes 319496 | tf_op jit(solution)/shard_map/ppermute | solution.py:590
  8.4 8.5 %collective-permute-start.6 = (f32[208,128]{1,0:T(8,128)S(1)}, f32[208,128]{1,0:T(8,128)S(1)}, u32[]{:S(2)}, u32[]{:S(2)}) collective-permute-start(f32[208,128]{1,0:T(8,128)S(1)} %get-tuple-element.34), channel_id=1, source_target_pairs={{0,1},{1,0},{2,3},{3,2},{4,5},{5,4},{6,7},{7,6},{8,9},{9,8},{10,11... | collective-permute-start | bytes 319496 | tf_op jit(solution)/shard_map/ppermute | solution.py:590
  10.1 6.8 %collective-permute-start.7 = (f32[208,128]{1,0:T(8,128)S(1)}, f32[208,128]{1,0:T(8,128)S(1)}, u32[]{:S(2)}, u32[]{:S(2)}) collective-permute-start(f32[208,128]{1,0:T(8,128)S(1)} %get-tuple-element.35), channel_id=1, source_target_pairs={{0,9},{1,8},{2,11},{3,10},{4,13},{5,12},{6,15},{7,14},{8,1},{9,0},... | collective-permute-start | bytes 319496 | tf_op jit(solution)/shard_map/ppermute | solution.py:590
  11.6 9.9 %collective-permute-start.3 = (f32[208,128]{1,0:T(8,128)S(1)}, f32[208,128]{1,0:T(8,128)S(1)}, u32[]{:S(2)}, u32[]{:S(2)}) collective-permute-start(f32[208,128]{1,0:T(8,128)S(1)} %get-tuple-element.30), channel_id=1, source_target_pairs={{0,1},{1,0},{2,3},{3,2},{4,5},{5,4},{6,7},{7,6},{8,9},{9,8},{10,11... | collective-permute-start | bytes 319496 | tf_op jit(solution)/shard_map/ppermute | solution.py:590
  13.2 9.7 %collective-permute-start.5 = (f32[208,128]{1,0:T(8,128)S(1)}, f32[208,128]{1,0:T(8,128)S(1)}, u32[]{:S(2)}, u32[]{:S(2)}) collective-permute-start(f32[208,128]{1,0:T(8,128)S(1)} %get-tuple-element.33), channel_id=1, source_target_pairs={{0,8},{1,9},{2,10},{3,11},{4,12},{5,13},{6,14},{7,15},{8,0},{9,1},... | collective-permute-start | bytes 319496 | tf_op jit(solution)/shard_map/ppermute | solution.py:590
  15.8 10.8 %collective-permute-start.4 = (f32[208,128]{1,0:T(8,128)S(1)}, f32[208,128]{1,0:T(8,128)S(1)}, u32[]{:S(2)}, u32[]{:S(2)}) collective-permute-start(f32[208,128]{1,0:T(8,128)S(1)} %get-tuple-element.31), channel_id=1, source_target_pairs={{0,9},{1,8},{2,11},{3,10},{4,13},{5,12},{6,15},{7,14},{8,1},{9,0},... | collective-permute-start | bytes 319496 | tf_op jit(solution)/shard_map/ppermute | solution.py:590
  17.9 11.1 %collective-permute-start.9 = (f32[4,48,128]{2,1,0:T(8,128)S(1)}, f32[4,48,128]{2,1,0:T(8,128)S(1)}, u32[]{:S(2)}, u32[]{:S(2)}) collective-permute-start(f32[4,48,128]{2,1,0:T(8,128)S(1)} %get-tuple-element.37.refs_0_), channel_id=1, source_target_pairs={{0,2},{1,3},{2,0},{3,1},{4,6},{5,7},{6,4},{7,5},{8,10},{9,11},{10,... | collective-permute-start | bytes 294920 | tf_op jit(solution)/shard_map/ppermute | solution.py:590
  20.5 10.2 %collective-permute-start.10 = (f32[4,48,128]{2,1,0:T(8,128)S(1)}, f32[4,48,128]{2,1,0:T(8,128)S(1)}, u32[]{:S(2)}, u32[]{:S(2)}) collective-permute-start(f32[4,48,128]{2,1,0:T(8,128)S(1)} %get-tuple-element.38.refs_1_), channel_id=1, source_target_pairs={{0,2},{1,3},{2,0},{3,1},{4,6},{5,7},{6,4},{7,5},{8,10},{9,11},{10,... | collective-permute-start | bytes 294920 | tf_op jit(solution)/shard_map/ppermute | solution.py:590
  21.5 6.0 %collective-permute-start.11 = (f32[48,128]{1,0:T(8,128)S(1)}, f32[48,128]{1,0:T(8,128)S(1)}, u32[]{:S(2)}, u32[]{:S(2)}) collective-permute-start(f32[48,128]{1,0:T(8,128)S(1)} %get-tuple-element.40), channel_id=1, source_target_pairs={{0,1},{1,0},{2,3},{3,2},{4,5},{5,4},{6,7},{7,6},{8,9},{9,8},{10,11... | collective-permute-start | bytes 73736 | tf_op jit(solution)/shard_map/ppermute | solution.py:590
  22.9 5.7 %collective-permute-start.12 = (f32[48,128]{1,0:T(8,128)S(1)}, f32[48,128]{1,0:T(8,128)S(1)}, u32[]{:S(2)}, u32[]{:S(2)}) collective-permute-start(f32[48,128]{1,0:T(8,128)S(1)} %get-tuple-element.41), channel_id=1, source_target_pairs={{0,3},{1,2},{2,1},{3,0},{4,7},{5,6},{6,5},{7,4},{8,11},{9,10},{10,... | collective-permute-start | bytes 73736 | tf_op jit(solution)/shard_map/ppermute | solution.py:590
  30.7 4.5 %collective-permute-start.14 = (f32[4,48,128]{2,1,0:T(8,128)S(1)}, f32[4,48,128]{2,1,0:T(8,128)S(1)}, u32[]{:S(2)}, u32[]{:S(2)}) collective-permute-start(f32[4,48,128]{2,1,0:T(8,128)S(1)} %get-tuple-element.44), channel_id=1, source_target_pairs={{4,8},{8,4},{5,9},{9,5},{6,10},{10,6},{7,11},{11,7},{20,24},{24,20... | collective-permute-start | bytes 294920 | tf_op jit(solution)/shard_map/ppermute | solution.py:595
  31.4 4.0 %collective-permute-start.13 = (f32[4,48,128]{2,1,0:T(8,128)S(1)}, f32[4,48,128]{2,1,0:T(8,128)S(1)}, u32[]{:S(2)}, u32[]{:S(2)}) collective-permute-start(f32[4,48,128]{2,1,0:T(8,128)S(1)} %get-tuple-element.43), channel_id=1, source_target_pairs={{0,4},{1,5},{2,6},{3,7},{4,0},{5,1},{6,2},{7,3},{8,12},{9,13},{10,... | collective-permute-start | bytes 294920 | tf_op jit(solution)/shard_map/ppermute | solution.py:590
  35.6 5.9 %collective-permute-start.16 = (f32[48,128]{1,0:T(8,128)S(1)}, f32[48,128]{1,0:T(8,128)S(1)}, u32[]{:S(2)}, u32[]{:S(2)}) collective-permute-start(f32[48,128]{1,0:T(8,128)S(1)} %pair_edges.1), channel_id=1, source_target_pairs={{0,3},{1,2},{2,1},{3,0},{4,7},{5,6},{6,5},{7,4},{8,11},{9,10},{10,... | collective-permute-start | bytes 73736 | tf_op jit(solution)/shard_map/ppermute | solution.py:590
  38.5 3.8 %collective-permute-start.15 = (f32[48,128]{1,0:T(8,128)S(1)}, f32[48,128]{1,0:T(8,128)S(1)}, u32[]{:S(2)}, u32[]{:S(2)}) collective-permute-start(f32[48,128]{1,0:T(8,128)S(1)} %pair_edges.1), channel_id=1, source_target_pairs={{0,1},{1,0},{2,3},{3,2},{4,5},{5,4},{6,7},{7,6},{8,9},{9,8},{10,11... | collective-permute-start | bytes 73736 | tf_op jit(solution)/shard_map/ppermute | solution.py:590

commit v5 on v4

--- a/solution.py
+++ b/solution.py
@@ -185,67 +185,97 @@
     return 0.5 * time_step if which % 2 == 0 else time_step
 
 
-def widen_kernel(n_row, pair_at, paired, turned, pair, cross, one, other, gravity, *refs):
+def store_fields(wide, which, lines, levels, base_row, total_rows):
+    weight = stage_weight(which)
+    channels = 3 * levels
+    for k, line in lines:
+        wide[which, k, :channels, :] = (0.5 * weight) * line
+    winds = slice(levels, channels)
+    for k in range(lines[0][0] + 1, lines[-1][0]):
+        values = wide[which, k, winds, :]
+        change = pltpu.roll(values, LANES - 1, 1) - pltpu.roll(values, 1, 1)
+        slope = wide[which, k + 1, winds, :] - wide[which, k - 1, winds, :]
+        rotation = weight * (coriolis_peak * (2.0 * ((base_row + k - HALO).astype(F32) + 0.5) / total_rows - 1.0))
+        begin = channels
+        for value in (change[:levels], change[levels:] + rotation, slope[:levels] - rotation, slope[levels:]):
+            wide[which, k, begin : begin + levels, :] = value
+            begin += levels
+
+
+def tile_fields_kernel(n_row, pair_at, turned, pair, cross, gravity, *refs):
     wide, pull = refs[-2:]
-    _, tile_rows, channels, columns = turned.shape
+    stages, tile_rows, channels, _ = turned.shape
     levels = channels // 3
-    total_rows = tile_rows * n_row
-    base_row = lax.axis_index("frow") * tile_rows
-    lower, masks = first_of_pair(), row_masks(n_row)
-
     level = lax.broadcasted_iota(jnp.int32, pull.shape, 0)
     pulls = jnp.zeros(pull.shape, F32)
     for i in range(levels):
         pulls = jnp.where(level == i, gravity[i], pulls)
     pull[...] = pulls
-
-    def along_x(values):
-        return pltpu.roll(values, 2 * columns - 1, 1) - pltpu.roll(values, 1, 1)
-
+    lower, masks = first_of_pair(), row_masks(n_row)
+    for which in range(stages):
+        lines = state_rows(which, turned, pair, pair_at, cross, lower, masks)
+        store_fields(wide, which, lines, levels, lax.axis_index("frow") * tile_rows, tile_rows * n_row)
+
+
+def tile_fields(n_row, pair_at, turned, pair, cross, gravity, after=()):
+    stages, tile_rows, channels, columns = turned.shape
+    in_vmem = pl.BlockSpec(memory_space=pltpu.VMEM)
+    return pl.pallas_call(
+        functools.partial(tile_fields_kernel, n_row, pair_at),
+        in_specs=[in_vmem] * 3 + [pl.BlockSpec(memory_space=pltpu.SMEM)] + [in_vmem] * len(after),
+        out_shape=(
+            jax.ShapeDtypeStruct((stages, tile_rows + 2 * HALO, channels // 3 * FIELDS, columns), F32),
+            jax.ShapeDtypeStruct((channels // 3, columns), F32),
+        ),
+        compiler_params=PARAMS,
+        name="tile_fields",
+    )(turned, pair, cross, gravity, *after)
+
+
+PART = 8
+BEYOND_AT = 32
+
+
+def edge_windows(line):
+    lane = lax.broadcasted_iota(jnp.int32, line.shape, 1)
+    return jnp.where((lane >= BEYOND_AT // 2) & (lane < 2 * BEYOND_AT), pltpu.roll(line, BEYOND_AT, 1), line)
+
+
+def with_rim(window, rim):
+    lane = lax.broadcasted_iota(jnp.int32, window.shape, 1)
+    beyond = (lane >= LANES - HALO) | ((lane >= BEYOND_AT) & (lane < BEYOND_AT + HALO))
+    return jnp.where(beyond, rim, window)
+
+
+def edge_fields_kernel(n_row, pair_at, paired, turned, pair, cross, one, other, wide):
+    stages, tile_rows, channels, columns = turned.shape
+    lower, masks = first_of_pair(), row_masks(n_row)
     left, right = from_sides(one[...], other[...], paired)
     lane = lax.broadcasted_iota(jnp.int32, (channels, columns), 1)
     rims = {
         (which, k): jnp.where(
             lane < columns // 2,
-            pltpu.roll(right, (-at) % columns, 1),
+            pltpu.roll(right, (BEYOND_AT - at) % columns, 1),
             pltpu.roll(left, (-at - count) % columns, 1),
         )
-        for which, k, count, at in edge_plan(turned.shape[0], tile_rows)
+        for which, k, count, at in edge_plan(stages, tile_rows)
     }
-
-    for which in range(turned.shape[0]):
-        weight = stage_weight(which)
-        lines = state_rows(which, turned, pair, pair_at, cross, lower, masks)
-        first, final = lines[0][0], lines[-1][0]
-        for k, line in lines:
-            rim = rims.get((which, k), jnp.zeros_like(line))
-            scaled = (0.5 * weight) * jnp.concatenate([line, rim], axis=1)
-            wide[which, k, :channels, :] = scaled
-        for k in range(first + 1, final):
-            winds = slice(levels, channels)
-            change = along_x(wide[which, k, winds, :])
-            slope = wide[which, k + 1, winds, :] - wide[which, k - 1, winds, :]
-            row = (base_row + k - HALO).astype(F32)
-            rotation = weight * (coriolis_peak * (2.0 * (row + 0.5) / total_rows - 1.0))
-            begin = channels
-            for value in (change[:levels], change[levels:] + rotation, slope[:levels] - rotation, slope[levels:]):
-                wide[which, k, begin : begin + levels, :] = value
-                begin += levels
-
-
-def widen(n_row, pair_at, paired, turned, pair, cross, one, other, gravity, after=()):
+    for which in range(stages):
+        lines = [
+            (k, with_rim(edge_windows(line), rims.get((which, k), line)))
+            for k, line in state_rows(which, turned, pair, pair_at, cross, lower, masks)
+        ]
+        store_fields(wide, which, lines, channels // 3, lax.axis_index("frow") * tile_rows, tile_rows * n_row)
+
+
+def edge_fields(n_row, pair_at, paired, turned, pair, cross, one, other):
     stages, tile_rows, channels, columns = turned.shape
-    in_vmem = pl.BlockSpec(memory_space=pltpu.VMEM)
-    return pl.pallas_call(
-        functools.partial(widen_kernel, n_row, pair_at, paired),
-        in_specs=[in_vmem] * 5 + [pl.BlockSpec(memory_space=pltpu.SMEM)] + [in_vmem] * len(after),
-        out_shape=(
-            jax.ShapeDtypeStruct((stages, tile_rows + 2 * HALO, channels // 3 * FIELDS, 2 * columns), F32),
-            jax.ShapeDtypeStruct((channels // 3, 2 * columns), F32),
-        ),
-        compiler_params=PARAMS,
-        name="widen_states",
-    )(turned, pair, cross, one, other, gravity, *after)
+    return pl.pallas_call(
+        functools.partial(edge_fields_kernel, n_row, pair_at, paired),
+        out_shape=jax.ShapeDtypeStruct((stages, tile_rows + 2 * HALO, channels // 3 * FIELDS, columns), F32),
+        compiler_params=PARAMS,
+        name="edge_fields",
+    )(turned, pair, cross, one, other)
 
 
 def slot_blocks(cot, where, tiles, share, tile_rows, columns, onehot, parts):
@@ -266,7 +296,8 @@
     ).astype(F32).astype(BF16)
     index = lax.broadcasted_iota(jnp.int32, tiles.shape, 0)
     begin = ((index % share) * (GROUP // share)).astype(F32)
-    slots = lax.broadcasted_iota(jnp.int32, (GROUP, GROUP), 0).astype(F32)
+    slots = lax.broadcasted_iota(jnp.int32, (GROUP, GROUP), 0).astype(F32).astype(BF16)
+    one, zero = jnp.ones(slots.shape, BF16), jnp.zeros(slots.shape, BF16)
     count = jnp.zeros((tiles.shape[0], 1), F32)
     rows = channels + 8
     for b in range(points // GROUP):
@@ -279,7 +310,7 @@
         ahead = jnp.dot(named.astype(BF16), before, preferred_element_type=F32)
         lane = jnp.sum(named * (ahead + count + begin), axis=0, keepdims=True)
         count = count + jnp.sum(named, axis=1, keepdims=True)
-        onehot[:, part] = (slots == lane).astype(F32).astype(BF16)
+        onehot[:, part] = jnp.where(slots == lane.astype(BF16), one, zero)
         coords = [across(values) for values in (row, col, *offsets)]
         data_high, data_low = split(jnp.concatenate([cot[:, part], *coords, *coords], axis=0))
         for g in range(groups):
@@ -496,31 +527,23 @@
     )(partial, pair)
 
 
-def steps_kernel(n_row, paired, canvas, pair, cross, one, other, gravity, wide, out, start, middle, after, last):
-    tile_rows, channels, columns = canvas.shape
-    levels = channels // 3
-    part = 8
-    masks = row_masks(n_row)
-    left, right = from_sides(one[...], other[...], paired)
-    rim = jnp.where(first_lanes(left), right, left)
-    for k, line in adjoint_rows(n_row, canvas, pair, cross):
-        start[k, :, :columns] = line
-        start[k, :, columns:] = pltpu.roll(rim, (-8 * k) % LANES, 1)
+def run_stages(wide, gravity, levels, masks, tile_rows, buffers, store):
+    start, middle, after, last = buffers
 
     def along_x(values):
-        return pltpu.roll(values, 2 * columns - 1, 1) - pltpu.roll(values, 1, 1)
-
-    def run(stage, adjoint, store):
+        return pltpu.roll(values, LANES - 1, 1) - pltpu.roll(values, 1, 1)
+
+    def run(stage, adjoint, put):
         width = HALO - 1 - stage
         begin, end = HALO - width, HALO + tile_rows + width
-        for low in range(0, levels, part):
-            pull = (0.5 * stage_weight(stage)) * gravity[low : low + part, :]
+        for low in range(0, levels, PART):
+            pull = (0.5 * stage_weight(stage)) * gravity[low : low + PART, :]
 
             def state(k, which):
-                return wide[stage, k, which * levels + low : which * levels + low + part, :]
+                return wide[stage, k, which * levels + low : which * levels + low + PART, :]
 
             def line(k):
-                a, b, c = (adjoint[k, w * levels + low : w * levels + low + part, :] for w in range(3))
+                a, b, c = (adjoint[k, w * levels + low : w * levels + low + PART, :] for w in range(3))
                 v = state(k, 2)
                 return a, b, c, v, v * b, v * c
 
@@ -534,7 +557,7 @@
                 east = h * a_x + along_x(u * b) + (down[4] - up[4]) - b * state(k, 3) - c * state(k, 4)
                 north = h * a_y + along_x(u * c) + (down[5] - up[5]) - b * state(k, 5) - c * state(k, 6)
                 for w, (old, change) in enumerate(zip((a, b, c), (height, east, north))):
-                    store(k, w, low, old, change)
+                    put(k, w, low, old, change)
                 up, here = here, down
 
     def kept(k, value):
@@ -545,37 +568,84 @@
         return value
 
     def half_into(result):
-        def store(k, w, low, old, change):
-            result[k, w * levels + low : w * levels + low + part, :] = kept(k, 0.5 * old + change)
-
-        return store
+        def put(k, w, low, old, change):
+            result[k, w * levels + low : w * levels + low + PART, :] = kept(k, 0.5 * old + change)
+
+        return put
 
     def after_step(adjoint, k, w, low, old, change):
-        return 0.5 * adjoint[k, w * levels + low : w * levels + low + part, :] + old + change
+        return 0.5 * adjoint[k, w * levels + low : w * levels + low + PART, :] + old + change
 
     def to_after(k, w, low, old, change):
-        after[k, w * levels + low : w * levels + low + part, :] = kept(k, after_step(start, k, w, low, old, change))
-
-    def to_out(k, w, low, old, change):
-        place = pl.ds((w * levels + low) * tile_rows + k - HALO, part, stride=tile_rows)
-        out[place, :] = after_step(after, k, w, low, old, change)[:, :columns]
+        after[k, w * levels + low : w * levels + low + PART, :] = kept(k, after_step(start, k, w, low, old, change))
+
+    def to_end(k, w, low, old, change):
+        store(k - HALO, w, low, after_step(after, k, w, low, old, change))
 
     run(0, start, half_into(middle))
     run(1, middle, to_after)
     run(2, after, half_into(last))
-    run(3, last, to_out)
-
-
-def steps(n_row, paired, canvas, pair, cross, one, other, wide, gravity):
+    run(3, last, to_end)
+
+
+def tile_steps_kernel(n_row, canvas, pair, cross, wide, gravity, out, windows, *buffers):
+    tile_rows, channels, _ = canvas.shape
+    levels = channels // 3
+    for k, line in adjoint_rows(n_row, canvas, pair, cross):
+        buffers[0][k] = line
+        windows[k] = edge_windows(line)
+
+    def store(r, w, low, value):
+        out[r, w * levels + low : w * levels + low + PART, :] = value
+
+    run_stages(wide, gravity, levels, row_masks(n_row), tile_rows, buffers, store)
+
+
+def tile_steps(n_row, canvas, pair, cross, wide, gravity):
     tile_rows, channels, columns = canvas.shape
-    extended = pltpu.VMEM((tile_rows + 2 * HALO, channels, 2 * columns), F32)
-    return pl.pallas_call(
-        functools.partial(steps_kernel, n_row, paired),
+    return pl.pallas_call(
+        functools.partial(tile_steps_kernel, n_row),
+        out_shape=(
+            jax.ShapeDtypeStruct(canvas.shape, F32),
+            jax.ShapeDtypeStruct((tile_rows + 2 * HALO, channels, columns), F32),
+        ),
+        scratch_shapes=[pltpu.VMEM((tile_rows + 2 * HALO, channels, columns), F32)] * 4,
+        compiler_params=PARAMS,
+        name="tile_steps",
+    )(canvas, pair, cross, wide, gravity)
+
+
+def edge_steps_kernel(n_row, paired, windows, one, other, wide, gravity, inner, out, *buffers):
+    *buffers, result = buffers
+    tile_rows, channels, _ = inner.shape
+    levels = channels // 3
+    left, right = from_sides(one[...], other[...], paired)
+    rims = jnp.where(first_lanes(left), pltpu.roll(right, BEYOND_AT, 1), left)
+    for k in range(tile_rows + 2 * HALO):
+        buffers[0][k] = with_rim(windows[k], pltpu.roll(rims, (-8 * k) % LANES, 1))
+    lane = lax.broadcasted_iota(jnp.int32, (PART, LANES), 1)
+
+    def store(r, w, low, value):
+        result[r, w * levels + low : w * levels + low + PART, :] = value
+
+    run_stages(wide, gravity, levels, row_masks(n_row), tile_rows, buffers, store)
+    for r in range(tile_rows):
+        for begin in range(0, channels, PART):
+            value = result[r, begin : begin + PART, :]
+            final = pltpu.roll(value, LANES - BEYOND_AT, 1)
+            line = jnp.where(lane >= LANES - HALO, final, inner[r, begin : begin + PART, :])
+            out[pl.ds(begin * tile_rows + r, PART, stride=tile_rows), :] = jnp.where(lane < HALO, value, line)
+
+
+def edge_steps(n_row, paired, windows, one, other, wide, gravity, inner):
+    tile_rows, channels, columns = inner.shape
+    return pl.pallas_call(
+        functools.partial(edge_steps_kernel, n_row, paired),
         out_shape=jax.ShapeDtypeStruct((channels * tile_rows, columns), F32),
-        scratch_shapes=[extended] * 4,
-        compiler_params=PARAMS,
-        name="adjoint_steps",
-    )(canvas, pair, cross, one, other, gravity, wide)
+        scratch_shapes=[pltpu.VMEM(windows.shape, F32)] * 4 + [pltpu.VMEM(inner.shape, F32)],
+        compiler_params=PARAMS,
+        name="edge_steps",
+    )(windows, one, other, wide, gravity, inner)
 
 
 def shifted(values, axis, by):
@@ -656,24 +726,26 @@
         one, other = exchanged(one, (0, 1)), exchanged(other, (0, 3))
         total = scatter(got[:2], None, *size)[0]
         total = scatter(got[2:], total, *size)[0]
-        wide, pull = widen(n_row, pair_at, paired, turned, pair, cross, one, other, gravity)
-        canvas = finish(total, far, [one, other])
+        fields, pull = tile_fields(n_row, pair_at, turned, pair, cross, gravity, [total])
+        canvas = finish(total, far, [one, other, pull])
     else:
         packed = pack_all(cot, sent, tile_count, share, tile_rows, columns)
         got = from_everyone(packed, channels, tile_count)
         one, other = all_state_edges(n_row, pair_at, paired, turned, pair, cross)
         one, other = shifted(one, "fcol", 1), shifted(other, "fcol", -1)
-        wide, pull = widen(n_row, pair_at, paired, turned, pair, cross, one, other, gravity)
+        fields, pull = tile_fields(n_row, pair_at, turned, pair, cross, gravity)
         canvas = finish(scatter([got.reshape(-1, LANES)], None, *size)[0])
 
+    near_edges = edge_fields(n_row, pair_at, paired, turned, pair, cross, one, other)
     canvas, to_pair, to_cross = canvas
     pair, cross = exchanged(to_pair, (1, 0)), exchanged_across(to_cross)
-    edges = adjoint_edges(n_row, canvas, pair, cross, [pull])
+    edges = adjoint_edges(n_row, canvas, pair, cross, [near_edges])
     if paired:
         sides = exchanged(edges, (0, 1)), exchanged(edges, (0, 3))
     else:
         sides = shifted(edges, "fcol", 1), shifted(edges, "fcol", -1)
-    result = steps(n_row, paired, canvas, pair, cross, *sides, wide, pull)
+    inner, windows = tile_steps(n_row, canvas, pair, cross, fields, pull)
+    result = edge_steps(n_row, paired, windows, *sides, near_edges, pull, inner)
     return result.reshape(3, levels, tile_rows, columns)
 
 

time: 45.1 us -> 43.8 us (0.971)
  waiting for transfers between devices: 7.83 us -> 5.01 us
  starting transfers between devices: 23.3 us -> 24.2 us
  Pallas kernels: 13.6 us -> 14.2 us
    ppermute x15, waiting for transfers between devices: 7.82 us -> 5 us  [exchanged(): return lax.ppermute(values, ('frow', 'fcol'), pairs)]
    ppermute x15, starting transfers between devices: 22 us -> 22.8 us  [exchanged(): return lax.ppermute(values, ('frow', 'fcol'), pairs)]
    pallas_call x2 -> x4, Pallas kernels: 4.53 us -> 5.2 us  [the longest x1 1.83 us: edge_steps(): pl.pallas_call(functools.partial(edge_steps_kernel, n_row, paired), out_s...]
  transfers between devices with their start and end apart: 17 -> 17, of which waited for: 6 -> 5; matrix products, arithmetic and copies ran while one was open for 0% -> 0% of each run, Pallas kernels for 24% -> 28%
where the time goes in v5:
time: 43.8 us; the launch traced here: 43.6 us
  starting transfers between devices  24.2 us (55%)
  Pallas kernels  14.2 us (32%)
  waiting for transfers between devices  5.01 us (11%)
    ppermute x15, starting transfers between devices, exchanged(): return lax.ppermute(values, ('frow', 'fcol'), pairs)  22.8 us
    ppermute x15, waiting for transfers between devices, exchanged(): return lax.ppermute(values, ('frow', 'fcol'), pairs)  5 us
    pallas_call x4, Pallas kernels, scatter(): pl.pallas_call(functools.partial(scatter_kernel, len(blocks), total is No...  3.81 us
    pallas_call x2, Pallas kernels, pack_chip(): pl.pallas_call(functools.partial(pack_chip_kernel, tiles, tile_rows, colu...  2.88 us
    pallas_call x1, Pallas kernels, edge_steps(): pl.pallas_call(functools.partial(edge_steps_kernel, n_row, paired), out_s...  1.83 us
    pallas_call x1, Pallas kernels, prepare(): pl.pallas_call(functools.partial(prepare_kernel, order), in_specs=[in_hbm...  1.39 us
    pallas_call x1, Pallas kernels, edge_fields(): pl.pallas_call(functools.partial(edge_fields_kernel, n_row, pair_at, pair...  1.37 us
    ppermute x2, starting transfers between devices, exchanged_across(): lax.ppermute(values, 'frow', [(f, (f + 1 ^ 1) - 1) for f in range(1, n_ro...  1.33 us
  transfers between devices with their start and end apart: 17, of which 5 were waited for; matrix products, arithmetic and copies ran while one was open for 0% of the time, Pallas kernels for 28%

profile of v5, /device:TPU:0, one launch (start us, length us, event | category | flops | bytes accessed | tf_op | source)
XLA Modules:
  0.0 43.6 jit_solution(12670205759811468269)
XLA Ops:
  0.0 0.5 %collective-permute-start = (f32[48,2048]{1,0:T(8,128)}, f32[48,2048]{1,0:T(8,128)S(1)}, u32[]{:S(2)}, u32[]{:S(2)}) collective-permute-start(f32[48,2048]{1,0:T(8,128)} %bitcast.6), channel_id=1, source_target_pairs={{0,4},{1,5},{2,6},{3,7},{4,0},{5,1},{6,2},{7,3},{8,12},{9,13},{10,... | collective-permute-start | bytes 1179656 | tf_op jit(solution)/shard_map/ppermute | solution.py:660
  0.5 1.4 %prepare.1 = (f32[544,128]{1,0:T(8,128)S(1)}, f32[480,128]{1,0:T(8,128)S(1)}, f32[4,8,48,128]{3,2,1,0:T(8,128)S(1)}, f32[48,2048]{1,0:T(8,128)S(1)}) custom-call(s32[16,128]{1,0:T(8,128)} %bitcast.8, s32[16,128]{1,0:T(8,128)} %bitcast.9, f32[2,2048]{1,0:T(2,128)} %frac.1, f32[4,384,128]{2,1,0:T(8,128)} %bitcast.5, f32[48,2048]{1,0:T(8,128)} %bitcast.7), custom_call_target="tpu_custom_call" | custom-call | tf_op jit(solution)/shard_map/prepare/pallas_call | solution.py:105
  1.9 0.1 collective-permute-start.1
  2.0 0.7 %collective-permute-start.2 = (f32[480,128]{1,0:T(8,128)S(1)}, f32[480,128]{1,0:T(8,128)S(1)}, u32[]{:S(2)}, u32[]{:S(2)}) collective-permute-start(f32[480,128]{1,0:T(8,128)S(1)} %get-tuple-element.30), channel_id=1, source_target_pairs={{4,8},{8,4},{5,9},{9,5},{6,10},{10,6},{7,11},{11,7},{20,24},{24,20... | collective-permute-start | bytes 737288 | tf_op jit(solution)/shard_map/ppermute | solution.py:665
  2.7 0.8 %collective-permute-done.1.pair_where.pair = f32[544,128]{1,0:T(8,128)S(1)} collective-permute-done((f32[544,128]{1,0:T(8,128)S(1)}, f32[544,128]{1,0:T(8,128)S(1)}, u32[]{:S(2)}, u32[]{:S(2)}) %collective-permute-start.1) | collective-permute-done | bytes 278560 | tf_op jit(solution)/shard_map/ppermute | solution.py:660
  3.5 0.0 collective-permute-done.pair_cot
  3.5 1.4 %pack_chip.2 = (f32[208,128]{1,0:T(8,128)S(1)}, f32[208,128]{1,0:T(8,128)S(1)}, f32[208,128]{1,0:T(8,128)S(1)}, f32[208,128]{1,0:T(8,128)S(1)}) custom-call(f32[48,2048]{1,0:T(8,128)S(1)} %get-tuple-element.28.cot, f32[544,128]{1,0:T(8,128)S(1)} %get-tuple-element.29.where, f32[48,2048]{1,0:T(8,128)S(1)} %collective-permute-done.pair_cot, ...), custom_call_target="tpu_custom_call" | custom-call | tf_op jit(solution)/shard_map/pack_chip/pallas_call | solution.py:393
  4.9 3.4 %collective-permute-start.8 = (f32[208,128]{1,0:T(8,128)S(1)}, f32[208,128]{1,0:T(8,128)S(1)}, u32[]{:S(2)}, u32[]{:S(2)}) collective-permute-start(f32[208,128]{1,0:T(8,128)S(1)} %get-tuple-element.38), channel_id=1, source_target_pairs={{0,8},{1,9},{2,10},{3,11},{4,12},{5,13},{6,14},{7,15},{8,0},{9,1},... | collective-permute-start | bytes 319496 | tf_op jit(solution)/shard_map/ppermute | solution.py:660
  8.4 1.7 %collective-permute-start.6 = (f32[208,128]{1,0:T(8,128)S(1)}, f32[208,128]{1,0:T(8,128)S(1)}, u32[]{:S(2)}, u32[]{:S(2)}) collective-permute-start(f32[208,128]{1,0:T(8,128)S(1)} %get-tuple-element.36), channel_id=1, source_target_pairs={{0,1},{1,0},{2,3},{3,2},{4,5},{5,4},{6,7},{7,6},{8,9},{9,8},{10,11... | collective-permute-start | bytes 319496 | tf_op jit(solution)/shard_map/ppermute | solution.py:660
  10.1 0.0 collective-permute-start.7
  10.1 0.0 collective-permute-done.2.refs_0_.cross
  10.1 1.4 %pack_chip.3 = (f32[208,128]{1,0:T(8,128)S(1)}, f32[208,128]{1,0:T(8,128)S(1)}, f32[208,128]{1,0:T(8,128)S(1)}, f32[208,128]{1,0:T(8,128)S(1)}) custom-call(f32[48,2048]{1,0:T(8,128)S(1)} %get-tuple-element.28.cot, f32[544,128]{1,0:T(8,128)S(1)} %get-tuple-element.29.where, f32[48,2048]{1,0:T(8,128)S(1)} %collective-permute-done.pair_cot, ...), custom_call_target="tpu_custom_call" | custom-call | tf_op jit(solution)/shard_map/pack_chip/pallas_call | solution.py:393
  11.5 1.6 %collective-permute-start.3 = (f32[208,128]{1,0:T(8,128)S(1)}, f32[208,128]{1,0:T(8,128)S(1)}, u32[]{:S(2)}, u32[]{:S(2)}) collective-permute-start(f32[208,128]{1,0:T(8,128)S(1)} %get-tuple-element.32), channel_id=1, source_target_pairs={{0,1},{1,0},{2,3},{3,2},{4,5},{5,4},{6,7},{7,6},{8,9},{9,8},{10,11... | collective-permute-start | bytes 319496 | tf_op jit(solution)/shard_map/ppermute | solution.py:660
  13.2 2.6 %collective-permute-start.5 = (f32[208,128]{1,0:T(8,128)S(1)}, f32[208,128]{1,0:T(8,128)S(1)}, u32[]{:S(2)}, u32[]{:S(2)}) collective-permute-start(f32[208,128]{1,0:T(8,128)S(1)} %get-tuple-element.35), channel_id=1, source_target_pairs={{0,8},{1,9},{2,10},{3,11},{4,12},{5,13},{6,14},{7,15},{8,0},{9,1},... | collective-permute-start | bytes 319496 | tf_op jit(solution)/shard_map/ppermute | solution.py:660
  15.8 0.0 collective-permute-done.8.refs_1_
  15.8 0.1 collective-permute-start.4
  15.9 1.0 %scatter_points.6.refs_2_ = f32[8,48,128]{2,1,0:T(8,128)S(1)} custom-call(f32[208,128]{1,0:T(8,128)S(1)} %get-tuple-element.31.refs_1_.refs_0_, f32[208,128]{1,0:T(8,128)S(1)} %collective-permute-done.8.refs_1_, f32[208,128]{1,0:T(8,128)S(1)} %get-tuple-element.34.refs_0_.refs_2_), custom_call_target="tpu_custom_call" | custom-call | tf_op jit(solution)/shard_map/scatter_points/pallas_call | solution.py:448
  16.9 0.0 collective-permute-done.6.refs_0_
  16.9 0.0 collective-permute-done.7.refs_1_
  16.9 1.0 %scatter_points.7 = (f32[4,48,128]{2,1,0:T(8,128)S(1)}, f32[4,48,128]{2,1,0:T(8,128)S(1)}) custom-call(f32[208,128]{1,0:T(8,128)S(1)} %collective-permute-done.6.refs_0_, f32[208,128]{1,0:T(8,128)S(1)} %collective-permute-done.7.refs_1_, f32[8,48,128]{2,1,0:T(8,128)S(1)} %scatter_points.6.refs_2_), custom_call_target="tpu_custom_call" | custom-call | tf_op jit(solution)/shard_map/scatter_points/pallas_call | solution.py:448
  17.9 2.7 %collective-permute-start.9 = (f32[4,48,128]{2,1,0:T(8,128)S(1)}, f32[4,48,128]{2,1,0:T(8,128)S(1)}, u32[]{:S(2)}, u32[]{:S(2)}) collective-permute-start(f32[4,48,128]{2,1,0:T(8,128)S(1)} %get-tuple-element.39.refs_0_), channel_id=1, source_target_pairs={{0,2},{1,3},{2,0},{3,1},{4,6},{5,7},{6,4},{7,5},{8,10},{9,11},{10,... | collective-permute-start | bytes 294920 | tf_op jit(solution)/shard_map/ppermute | solution.py:660
  20.5 0.3 collective-permute-start.10
  20.9 0.6 %state_edges.1 = (f32[48,128]{1,0:T(8,128)S(1)}, f32[48,128]{1,0:T(8,128)S(1)}) custom-call(f32[4,8,48,128]{3,2,1,0:T(8,128)S(1)} %get-tuple-element.41.turned, f32[544,128]{1,0:T(8,128)S(1)} %collective-permute-done.1.pair_where.pair, f32[480,128]{1,0:T(8,128)S(1)} %collective-permute-done.2.refs_0_.cross, f32[4,48,128]{2,1,0:T(8,128)S(1)} %get-tuple-element.39.refs_0_, ...), custom_call_target="tpu_custom_call" | custom-call | tf_op jit(solution)/shard_map/state_edges/pallas_call | solution.py:173
  21.5 0.0 collective-permute-done.3.refs_0_
  21.5 1.4 %collective-permute-start.11 = (f32[48,128]{1,0:T(8,128)S(1)}, f32[48,128]{1,0:T(8,128)S(1)}, u32[]{:S(2)}, u32[]{:S(2)}) collective-permute-start(f32[48,128]{1,0:T(8,128)S(1)} %get-tuple-element.42), channel_id=1, source_target_pairs={{0,1},{1,0},{2,3},{3,2},{4,5},{5,4},{6,7},{7,6},{8,9},{9,8},{10,11... | collective-permute-start | bytes 73736 | tf_op jit(solution)/shard_map/ppermute | solution.py:660
  22.9 0.0 collective-permute-done.5.refs_1_
  22.9 2.7 %collective-permute-start.12 = (f32[48,128]{1,0:T(8,128)S(1)}, f32[48,128]{1,0:T(8,128)S(1)}, u32[]{:S(2)}, u32[]{:S(2)}) collective-permute-start(f32[48,128]{1,0:T(8,128)S(1)} %get-tuple-element.43), channel_id=1, source_target_pairs={{0,3},{1,2},{2,1},{3,0},{4,7},{5,6},{6,5},{7,4},{8,11},{9,10},{10,... | collective-permute-start | bytes 73736 | tf_op jit(solution)/shard_map/ppermute | solution.py:660
  25.6 0.9 %scatter_points.4.refs_2_ = f32[8,48,128]{2,1,0:T(8,128)S(1)} custom-call(f32[208,128]{1,0:T(8,128)S(1)} %get-tuple-element.34.refs_0_.refs_2_, f32[208,128]{1,0:T(8,128)S(1)} %collective-permute-done.5.refs_1_), custom_call_target="tpu_custom_call" | custom-call | tf_op jit(solution)/shard_map/scatter_points/pallas_call | solution.py:448
  26.6 0.0 collective-permute-done.4.refs_1_
  26.6 1.0 %scatter_points.5.refs_0_.total = f32[8,48,128]{2,1,0:T(8,128)S(1)} custom-call(f32[208,128]{1,0:T(8,128)S(1)} %collective-permute-done.3.refs_0_, f32[208,128]{1,0:T(8,128)S(1)} %collective-permute-done.4.refs_1_, f32[8,48,128]{2,1,0:T(8,128)S(1)} %scatter_points.4.refs_2_), custom_call_target="tpu_custom_call" | custom-call | tf_op jit(solution)/shard_map/scatter_points/pallas_call | solution.py:448
  27.6 1.0 %tile_fields.1 = (f32[4,16,112,128]{3,2,1,0:T(8,128)S(1)}, f32[16,128]{1,0:T(8,128)S(1)}) custom-call(f32[4,8,48,128]{3,2,1,0:T(8,128)S(1)} %get-tuple-element.41.turned, f32[544,128]{1,0:T(8,128)S(1)} %collective-permute-done.1.pair_where.pair, f32[480,128]{1,0:T(8,128)S(1)} %collective-permute-done.2.refs_0_.cross, f32[16]{0:T(128)S(1)} %copy-done, ...), custom_call_target="tpu_custom_call" | custom-call | tf_op jit(solution)/shard_map/tile_fields/pallas_call | solution.py:223
  28.6 0.0 collective-permute-done.11.refs_2_.one
  28.6 0.1 collective-permute-done.12.refs_3_.other
  28.6 0.3 collective-permute-done.9.refs_0_
  28.9 1.8 %collective-permute-done.10.refs_1_ = f32[4,48,128]{2,1,0:T(8,128)S(1)} collective-permute-done((f32[4,48,128]{2,1,0:T(8,128)S(1)}, f32[4,48,128]{2,1,0:T(8,128)S(1)}, u32[]{:S(2)}, u32[]{:S(2)}) %collective-permute-start.10) | collective-permute-done | bytes 98336 | tf_op jit(solution)/shard_map/ppermute | solution.py:660
  30.8 0.7 %collective-permute-start.14 = (f32[4,48,128]{2,1,0:T(8,128)S(1)}, f32[4,48,128]{2,1,0:T(8,128)S(1)}, u32[]{:S(2)}, u32[]{:S(2)}) collective-permute-start(f32[4,48,128]{2,1,0:T(8,128)S(1)} %get-tuple-element.47), channel_id=1, source_target_pairs={{4,8},{8,4},{5,9},{9,5},{6,10},{10,6},{7,11},{11,7},{20,24},{24,20... | collective-permute-start | bytes 294920 | tf_op jit(solution)/shard_map/ppermute | solution.py:665
  31.4 1.9 %collective-permute-start.13 = (f32[4,48,128]{2,1,0:T(8,128)S(1)}, f32[4,48,128]{2,1,0:T(8,128)S(1)}, u32[]{:S(2)}, u32[]{:S(2)}) collective-permute-start(f32[4,48,128]{2,1,0:T(8,128)S(1)} %get-tuple-element.46), channel_id=1, source_target_pairs={{0,4},{1,5},{2,6},{3,7},{4,0},{5,1},{6,2},{7,3},{8,12},{9,13},{10,... | collective-permute-start | bytes 294920 | tf_op jit(solution)/shard_map/ppermute | solution.py:660
  33.3 1.4 %edge_fields.1.refs_0_.wide = f32[4,16,112,128]{3,2,1,0:T(8,128)S(1)} custom-call(f32[4,8,48,128]{3,2,1,0:T(8,128)S(1)} %get-tuple-element.41.turned, f32[544,128]{1,0:T(8,128)S(1)} %collective-permute-done.1.pair_where.pair, f32[480,128]{1,0:T(8,128)S(1)} %collective-permute-done.2.refs_0_.cross, f32[48,128]{1,0:T(8,128)S(1)} %collective-permute-done.11.refs_2_.one, ...), custom_call_target="tpu_custom_call" | custom-call | tf_op jit(solution)/shard_map/edge_fields/pallas_call | solution.py:273
  34.7 0.0 collective-permute-done.14.cross
  34.7 0.2 cross_edges.1.partial
  34.9 0.0 collective-permute-done.13.pair
  34.9 0.1 pair_edges.1
  35.0 0.9 %collective-permute-start.15 = (f32[48,128]{1,0:T(8,128)S(1)}, f32[48,128]{1,0:T(8,128)S(1)}, u32[]{:S(2)}, u32[]{:S(2)}) collective-permute-start(f32[48,128]{1,0:T(8,128)S(1)} %pair_edges.1), channel_id=1, source_target_pairs={{0,1},{1,0},{2,3},{3,2},{4,5},{5,4},{6,7},{7,6},{8,9},{9,8},{10,11... | collective-permute-start | bytes 73736 | tf_op jit(solution)/shard_map/ppermute | solution.py:660
  35.9 2.8 %collective-permute-start.16 = (f32[48,128]{1,0:T(8,128)S(1)}, f32[48,128]{1,0:T(8,128)S(1)}, u32[]{:S(2)}, u32[]{:S(2)}) collective-permute-start(f32[48,128]{1,0:T(8,128)S(1)} %pair_edges.1), channel_id=1, source_target_pairs={{0,3},{1,2},{2,1},{3,0},{4,7},{5,6},{6,5},{7,4},{8,11},{9,10},{10,... | collective-permute-start | bytes 73736 | tf_op jit(solution)/shard_map/ppermute | solution.py:660
  38.7 1.0 %tile_steps.1 = (f32[8,48,128]{2,1,0:T(8,128)S(1)}, f32[16,48,128]{2,1,0:T(8,128)S(1)}) custom-call(f32[8,48,128]{2,1,0:T(8,128)S(1)} %get-tuple-element.45.canvas, f32[4,48,128]{2,1,0:T(8,128)S(1)} %collective-permute-done.13.pair, f32[4,48,128]{2,1,0:T(8,128)S(1)} %collective-permute-done.14.cross, f32[4,16,112,128]{3,2,1,0:T(8,128)S(1)} %get-tuple-element.48.wide, ...), custom_call_target="tpu_custom_call" | custom-call | tf_op jit(solution)/shard_map/tile_steps/pallas_call | solution.py:606
  39.8 0.0 collective-permute-done.15.one
  39.8 2.0 %collective-permute-done.16.other = f32[48,128]{1,0:T(8,128)S(1)} collective-permute-done((f32[48,128]{1,0:T(8,128)S(1)}, f32[48,128]{1,0:T(8,128)S(1)}, u32[]{:S(2)}, u32[]{:S(2)}) %collective-permute-start.16) | collective-permute-done | bytes 24608 | tf_op jit(solution)/shard_map/ppermute | solution.py:660
  41.8 1.8 %edge_steps.1 = f32[384,128]{1,0:T(8,128)} custom-call(f32[16,48,128]{2,1,0:T(8,128)S(1)} %get-tuple-element.49.windows, f32[48,128]{1,0:T(8,128)S(1)} %collective-permute-done.15.one, f32[48,128]{1,0:T(8,128)S(1)} %collective-permute-done.16.other, f32[4,16,112,128]{3,2,1,0:T(8,128)S(1)} %edge_fields.1.refs_0_.wide, ...), custom_call_target="tpu_custom_call" | custom-call | tf_op jit(solution)/shard_map/edge_steps/pallas_call | solution.py:642
  (3 shorter events, 0.0 us)
Async XLA Ops:
  0.0 3.5 %collective-permute-start = (f32[48,2048]{1,0:T(8,128)}, f32[48,2048]{1,0:T(8,128)S(1)}, u32[]{:S(2)}, u32[]{:S(2)}) collective-permute-start(f32[48,2048]{1,0:T(8,128)} %bitcast.6), channel_id=1, source_target_pairs={{0,4},{1,5},{2,6},{3,7},{4,0},{5,1},{6,2},{7,3},{8,12},{9,13},{10,... | collective-permute-start | bytes 1179656 | tf_op jit(solution)/shard_map/ppermute | solution.py:660
  0.5 27.1 %copy-start = (f32[16]{0:T(128)S(1)}, f32[16]{0:T(128)}, u32[]{:S(2)}) copy-start(f32[16]{0:T(128)} %gravity.1) | copy-start | bytes 196
  1.9 1.6 %collective-permute-start.1 = (f32[544,128]{1,0:T(8,128)S(1)}, f32[544,128]{1,0:T(8,128)S(1)}, u32[]{:S(2)}, u32[]{:S(2)}) collective-permute-start(f32[544,128]{1,0:T(8,128)S(1)} %get-tuple-element.29.where), channel_id=1, source_target_pairs={{0,4},{1,5},{2,6},{3,7},{4,0},{5,1},{6,2},{7,3},{8,12},{9,13},{10,... | collective-permute-start | bytes 835592 | tf_op jit(solution)/shard_map/ppermute | solution.py:660
  2.0 8.1 %collective-permute-start.2 = (f32[480,128]{1,0:T(8,128)S(1)}, f32[480,128]{1,0:T(8,128)S(1)}, u32[]{:S(2)}, u32[]{:S(2)}) collective-permute-start(f32[480,128]{1,0:T(8,128)S(1)} %get-tuple-element.30), channel_id=1, source_target_pairs={{4,8},{8,4},{5,9},{9,5},{6,10},{10,6},{7,11},{11,7},{20,24},{24,20... | collective-permute-start | bytes 737288 | tf_op jit(solution)/shard_map/ppermute | solution.py:665
  4.9 10.9 %collective-permute-start.8 = (f32[208,128]{1,0:T(8,128)S(1)}, f32[208,128]{1,0:T(8,128)S(1)}, u32[]{:S(2)}, u32[]{:S(2)}) collective-permute-start(f32[208,128]{1,0:T(8,128)S(1)} %get-tuple-element.38), channel_id=1, source_target_pairs={{0,8},{1,9},{2,10},{3,11},{4,12},{5,13},{6,14},{7,15},{8,0},{9,1},... | collective-permute-start | bytes 319496 | tf_op jit(solution)/shard_map/ppermute | solution.py:660
  8.4 8.5 %collective-permute-start.6 = (f32[208,128]{1,0:T(8,128)S(1)}, f32[208,128]{1,0:T(8,128)S(1)}, u32[]{:S(2)}, u32[]{:S(2)}) collective-permute-start(f32[208,128]{1,0:T(8,128)S(1)} %get-tuple-element.36), channel_id=1, source_target_pairs={{0,1},{1,0},{2,3},{3,2},{4,5},{5,4},{6,7},{7,6},{8,9},{9,8},{10,11... | collective-permute-start | bytes 319496 | tf_op jit(solution)/shard_map/ppermute | solution.py:660
  10.1 6.8 %collective-permute-start.7 = (f32[208,128]{1,0:T(8,128)S(1)}, f32[208,128]{1,0:T(8,128)S(1)}, u32[]{:S(2)}, u32[]{:S(2)}) collective-permute-start(f32[208,128]{1,0:T(8,128)S(1)} %get-tuple-element.37), channel_id=1, source_target_pairs={{0,9},{1,8},{2,11},{3,10},{4,13},{5,12},{6,15},{7,14},{8,1},{9,0},... | collective-permute-start | bytes 319496 | tf_op jit(solution)/shard_map/ppermute | solution.py:660
  11.5 10.0 %collective-permute-start.3 = (f32[208,128]{1,0:T(8,128)S(1)}, f32[208,128]{1,0:T(8,128)S(1)}, u32[]{:S(2)}, u32[]{:S(2)}) collective-permute-start(f32[208,128]{1,0:T(8,128)S(1)} %get-tuple-element.32), channel_id=1, source_target_pairs={{0,1},{1,0},{2,3},{3,2},{4,5},{5,4},{6,7},{7,6},{8,9},{9,8},{10,11... | collective-permute-start | bytes 319496 | tf_op jit(solution)/shard_map/ppermute | solution.py:660
  13.2 9.8 %collective-permute-start.5 = (f32[208,128]{1,0:T(8,128)S(1)}, f32[208,128]{1,0:T(8,128)S(1)}, u32[]{:S(2)}, u32[]{:S(2)}) collective-permute-start(f32[208,128]{1,0:T(8,128)S(1)} %get-tuple-element.35), channel_id=1, source_target_pairs={{0,8},{1,9},{2,10},{3,11},{4,12},{5,13},{6,14},{7,15},{8,0},{9,1},... | collective-permute-start | bytes 319496 | tf_op jit(solution)/shard_map/ppermute | solution.py:660
  15.8 10.8 %collective-permute-start.4 = (f32[208,128]{1,0:T(8,128)S(1)}, f32[208,128]{1,0:T(8,128)S(1)}, u32[]{:S(2)}, u32[]{:S(2)}) collective-permute-start(f32[208,128]{1,0:T(8,128)S(1)} %get-tuple-element.33), channel_id=1, source_target_pairs={{0,9},{1,8},{2,11},{3,10},{4,13},{5,12},{6,15},{7,14},{8,1},{9,0},... | collective-permute-start | bytes 319496 | tf_op jit(solution)/shard_map/ppermute | solution.py:660
  17.9 11.1 %collective-permute-start.9 = (f32[4,48,128]{2,1,0:T(8,128)S(1)}, f32[4,48,128]{2,1,0:T(8,128)S(1)}, u32[]{:S(2)}, u32[]{:S(2)}) collective-permute-start(f32[4,48,128]{2,1,0:T(8,128)S(1)} %get-tuple-element.39.refs_0_), channel_id=1, source_target_pairs={{0,2},{1,3},{2,0},{3,1},{4,6},{5,7},{6,4},{7,5},{8,10},{9,11},{10,... | collective-permute-start | bytes 294920 | tf_op jit(solution)/shard_map/ppermute | solution.py:660
  20.5 10.2 %collective-permute-start.10 = (f32[4,48,128]{2,1,0:T(8,128)S(1)}, f32[4,48,128]{2,1,0:T(8,128)S(1)}, u32[]{:S(2)}, u32[]{:S(2)}) collective-permute-start(f32[4,48,128]{2,1,0:T(8,128)S(1)} %get-tuple-element.40.refs_1_), channel_id=1, source_target_pairs={{0,2},{1,3},{2,0},{3,1},{4,6},{5,7},{6,4},{7,5},{8,10},{9,11},{10,... | collective-permute-start | bytes 294920 | tf_op jit(solution)/shard_map/ppermute | solution.py:660
  21.5 7.1 %collective-permute-start.11 = (f32[48,128]{1,0:T(8,128)S(1)}, f32[48,128]{1,0:T(8,128)S(1)}, u32[]{:S(2)}, u32[]{:S(2)}) collective-permute-start(f32[48,128]{1,0:T(8,128)S(1)} %get-tuple-element.42), channel_id=1, source_target_pairs={{0,1},{1,0},{2,3},{3,2},{4,5},{5,4},{6,7},{7,6},{8,9},{9,8},{10,11... | collective-permute-start | bytes 73736 | tf_op jit(solution)/shard_map/ppermute | solution.py:660
  22.9 5.7 %collective-permute-start.12 = (f32[48,128]{1,0:T(8,128)S(1)}, f32[48,128]{1,0:T(8,128)S(1)}, u32[]{:S(2)}, u32[]{:S(2)}) collective-permute-start(f32[48,128]{1,0:T(8,128)S(1)} %get-tuple-element.43), channel_id=1, source_target_pairs={{0,3},{1,2},{2,1},{3,0},{4,7},{5,6},{6,5},{7,4},{8,11},{9,10},{10,... | collective-permute-start | bytes 73736 | tf_op jit(solution)/shard_map/ppermute | solution.py:660
  30.8 4.0 %collective-permute-start.14 = (f32[4,48,128]{2,1,0:T(8,128)S(1)}, f32[4,48,128]{2,1,0:T(8,128)S(1)}, u32[]{:S(2)}, u32[]{:S(2)}) collective-permute-start(f32[4,48,128]{2,1,0:T(8,128)S(1)} %get-tuple-element.47), channel_id=1, source_target_pairs={{4,8},{8,4},{5,9},{9,5},{6,10},{10,6},{7,11},{11,7},{20,24},{24,20... | collective-permute-start | bytes 294920 | tf_op jit(solution)/shard_map/ppermute | solution.py:665
  31.4 3.5 %collective-permute-start.13 = (f32[4,48,128]{2,1,0:T(8,128)S(1)}, f32[4,48,128]{2,1,0:T(8,128)S(1)}, u32[]{:S(2)}, u32[]{:S(2)}) collective-permute-start(f32[4,48,128]{2,1,0:T(8,128)S(1)} %get-tuple-element.46), channel_id=1, source_target_pairs={{0,4},{1,5},{2,6},{3,7},{4,0},{5,1},{6,2},{7,3},{8,12},{9,13},{10,... | collective-permute-start | bytes 294920 | tf_op jit(solution)/shard_map/ppermute | solution.py:660
  35.0 4.7 %collective-permute-start.15 = (f32[48,128]{1,0:T(8,128)S(1)}, f32[48,128]{1,0:T(8,128)S(1)}, u32[]{:S(2)}, u32[]{:S(2)}) collective-permute-start(f32[48,128]{1,0:T(8,128)S(1)} %pair_edges.1), channel_id=1, source_target_pairs={{0,1},{1,0},{2,3},{3,2},{4,5},{5,4},{6,7},{7,6},{8,9},{9,8},{10,11... | collective-permute-start | bytes 73736 | tf_op jit(solution)/shard_map/ppermute | solution.py:660
  35.9 5.8 %collective-permute-start.16 = (f32[48,128]{1,0:T(8,128)S(1)}, f32[48,128]{1,0:T(8,128)S(1)}, u32[]{:S(2)}, u32[]{:S(2)}) collective-permute-start(f32[48,128]{1,0:T(8,128)S(1)} %pair_edges.1), channel_id=1, source_target_pairs={{0,3},{1,2},{2,1},{3,0},{4,7},{5,6},{6,5},{7,4},{8,11},{9,10},{10,... | collective-permute-start | bytes 73736 | tf_op jit(solution)/shard_map/ppermute | solution.py:660

commit v6 on v5

--- a/solution.py
+++ b/solution.py
@@ -278,10 +278,10 @@
     )(turned, pair, cross, one, other)
 
 
-def slot_blocks(cot, where, tiles, share, tile_rows, columns, onehot, parts):
+def slot_blocks(cot, where, tiles, share, groups, tile_rows, columns, onehot, parts):
     channels, points = cot.shape
     lines = points // LANES
-    groups = tiles.shape[0] // share
+    named_tiles = tiles.shape[0]
     corner = where[lines : 2 * lines, :]
     row = jnp.zeros_like(corner)
     for k in range(1, tile_rows - 1):
@@ -298,20 +298,21 @@
     begin = ((index % share) * (GROUP // share)).astype(F32)
     slots = lax.broadcasted_iota(jnp.int32, (GROUP, GROUP), 0).astype(F32).astype(BF16)
     one, zero = jnp.ones(slots.shape, BF16), jnp.zeros(slots.shape, BF16)
-    count = jnp.zeros((tiles.shape[0], 1), F32)
+    count = jnp.zeros((named_tiles, 1), F32)
     rows = channels + 8
-    for b in range(points // GROUP):
+
+    def across(values, b):
+        return jnp.concatenate([values[2 * b : 2 * b + 1, :], values[2 * b + 1 : 2 * b + 2, :]], axis=1)
+
+    all_named = [(tiles == across(target, b)).astype(F32) for b in range(points // GROUP)]
+    all_ahead = jnp.dot(jnp.concatenate(all_named, axis=0).astype(BF16), before, preferred_element_type=F32)
+    for b, named in enumerate(all_named):
         part = slice(b * GROUP, (b + 1) * GROUP)
-
-        def across(values):
-            return jnp.concatenate([values[2 * b : 2 * b + 1, :], values[2 * b + 1 : 2 * b + 2, :]], axis=1)
-
-        named = (tiles == across(target)).astype(F32)
-        ahead = jnp.dot(named.astype(BF16), before, preferred_element_type=F32)
+        ahead = all_ahead[b * named_tiles : (b + 1) * named_tiles, :]
         lane = jnp.sum(named * (ahead + count + begin), axis=0, keepdims=True)
         count = count + jnp.sum(named, axis=1, keepdims=True)
         onehot[:, part] = jnp.where(slots == lane.astype(BF16), one, zero)
-        coords = [across(values) for values in (row, col, *offsets)]
+        coords = [across(values, b) for values in (row, col, *offsets)]
         data_high, data_low = split(jnp.concatenate([cot[:, part], *coords, *coords], axis=0))
         for g in range(groups):
             mine = named[g * share : g * share + 1, :]
@@ -348,7 +349,7 @@
 
 def pack_all_kernel(tile_count, share, tile_rows, columns, cot, where, out, *scratch):
     tiles = lax.broadcasted_iota(jnp.int32, (tile_count, GROUP), 0).astype(F32)
-    for g, pieces in enumerate(slot_blocks(cot, where, tiles, share, tile_rows, columns, *scratch)):
+    for g, pieces in enumerate(slot_blocks(cot, where, tiles, share, tile_count // share, tile_rows, columns, *scratch)):
         store_block(out.at[g], 0, pieces)
 
 
@@ -371,8 +372,8 @@
 def partner_tiles(partners):
     at_row, at_col = lax.axis_index("frow"), lax.axis_index("fcol")
     n_col = lax.axis_size("fcol")
-    index = lax.broadcasted_iota(jnp.int32, (len(partners), GROUP), 0)
-    tiles = jnp.zeros(index.shape, jnp.int32)
+    index = lax.broadcasted_iota(jnp.int32, (8, GROUP), 0)
+    tiles = jnp.full(index.shape, -1, jnp.int32)
     for g, (df, dz) in enumerate(partners):
         tiles = jnp.where(index == g, (at_row ^ df) * n_col + (at_col ^ dz), tiles)
     return tiles.astype(F32)
@@ -382,7 +383,9 @@
     outs, scratch = refs[-4 - len(tiles) : -4], refs[-4:]
     begin = 0
     for i, points in enumerate(((cot, where), (pair_cot, pair_where))):
-        blocks = slot_blocks(*points, partner_tiles(tiles), 1, tile_rows, columns, *scratch[2 * i : 2 * i + 2])
+        blocks = slot_blocks(
+            *points, partner_tiles(tiles), 1, len(tiles), tile_rows, columns, *scratch[2 * i : 2 * i + 2]
+        )
         for out, pieces in zip(outs, blocks):
             store_block(out, begin, pieces)
         begin += 2 * cot.shape[0] + 8
@@ -403,19 +406,19 @@
     blocks, refs = refs[:count], refs[count:]
     if not first:
         total, refs = refs[0], refs[1:]
-    outs, (parts, weight) = refs[later:-2], refs[-2:]
+    outs, scratch = refs[later : -2 * count], refs[-2 * count :]
     part_rows, channels, columns = outs[0].shape
     tile_rows = part_rows * len(outs)
     rows = 2 * channels + 8
-    cells = lax.broadcasted_iota(jnp.int32, (columns, LANES), 0).astype(F32)
-    lines = lax.broadcasted_iota(jnp.int32, (tile_rows, LANES), 0).astype(F32)
-
-    def hat(index, corner, fraction):
-        away = index - corner
-        return jnp.where(away == 0.0, 1.0 - fraction, jnp.where(away == 1.0, fraction, 0.0))
-
-    at = 0
-    for block in blocks:
+    cells = lax.broadcasted_iota(jnp.int32, (columns, LANES), 0).astype(F32).astype(BF16)
+    zero = jnp.zeros((channels, LANES), BF16)
+
+    def spread(values, shape):
+        return jnp.broadcast_to(values.astype(BF16), shape)
+
+    sums = None
+    for block, parts, weight in zip(blocks, scratch[::2], scratch[1::2]):
+        at = 0
         for source in range(block.shape[0] // rows):
             for half in range(2):
                 part = slice(at, at + LANES)
@@ -423,19 +426,29 @@
                 begin = source * rows + 2 * channels + 4 * half
                 coords = block[begin : begin + 4, :]
                 row, col, along_rows, along_cols = (coords[k : k + 1, :] for k in range(4))
-                weight_high, weight_low = split(hat(cells, col, along_cols))
-                weight[:columns, part] = weight_high
-                weight[columns:, part] = weight_low
+                corner, beside = cells == spread(col, cells.shape), cells == spread(col + 1.0, cells.shape)
+                for k, (near, far) in enumerate(zip(split(1.0 - along_cols), split(along_cols))):
+                    chosen = jnp.where(
+                        beside, spread(far, cells.shape), jnp.zeros(cells.shape, BF16)
+                    )
+                    weight[k * columns : (k + 1) * columns, part] = jnp.where(corner, spread(near, cells.shape), chosen)
                 begin = source * rows + half * channels
                 values = block[begin : begin + channels, :]
-                row_weight = hat(lines, row, along_rows)
+                upper, lower = split(values * (1.0 - along_rows)), split(values * along_rows)
+                below = None
+                line = spread(row, zero.shape)
                 for r in range(tile_rows):
-                    product_high, product_low = split(values * row_weight[r : r + 1, :])
-                    parts[r * channels : (r + 1) * channels, part] = product_high
-                    parts[(tile_rows + r) * channels : (tile_rows + r + 1) * channels, part] = product_low
-    both = dot_nt(parts[...], weight[...])
-    sums = both[:, :columns] + both[:, columns:]
-    sums = sums[: tile_rows * channels, :] + sums[tile_rows * channels :, :]
+                    here = line == jnp.full(zero.shape, r, BF16)
+                    for k in range(2):
+                        product = zero if below is None else jnp.where(below, lower[k], zero)
+                        product = jnp.where(here, upper[k], product)
+                        begin = (k * tile_rows + r) * channels
+                        parts[begin : begin + channels, part] = product
+                    below = here
+        both = dot_nt(parts[...], weight[...])
+        both = both[:, :columns] + both[:, columns:]
+        both = both[: tile_rows * channels, :] + both[tile_rows * channels :, :]
+        sums = both if sums is None else sums + both
     for r in range(tile_rows):
         line = sums[r * channels : (r + 1) * channels, :]
         if not first:
@@ -444,13 +457,12 @@
 
 
 def scatter(blocks, total, channels, tile_rows, columns, after=(), parts=1):
-    slots = sum(block.shape[0] // (2 * channels + 8) for block in blocks) * GROUP
+    slots = [block.shape[0] // (2 * channels + 8) * GROUP for block in blocks]
     return pl.pallas_call(
         functools.partial(scatter_kernel, len(blocks), total is None, len(after)),
         out_shape=[jax.ShapeDtypeStruct((tile_rows // parts, channels, columns), F32)] * parts,
         scratch_shapes=[
-            pltpu.VMEM((2 * tile_rows * channels, slots), BF16),
-            pltpu.VMEM((2 * columns, slots), BF16),
+            pltpu.VMEM((2 * lines, count), BF16) for count in slots for lines in (tile_rows * channels, columns)
         ],
         compiler_params=PARAMS,
         name="scatter_points",

time: 43.8 us -> 43.2 us (0.986)
  Pallas kernels: 14.2 us -> 13.1 us
  waiting for transfers between devices: 5.01 us -> 5.81 us
    pallas_call x4, Pallas kernels: 3.81 us -> 2.89 us  [scatter(): pl.pallas_call(functools.partial(scatter_kernel, len(blocks), total is No...]
    ppermute x15, waiting for transfers between devices: 5 us -> 5.81 us  [exchanged(): return lax.ppermute(values, ('frow', 'fcol'), pairs)]
  transfers between devices with their start and end apart: 17 -> 17, of which waited for: 5 -> 6; matrix products, arithmetic and copies ran while one was open for 0% -> 0% of each run, Pallas kernels for 28% -> 26%
where the time goes in v6:
time: 43.2 us; the launch traced here: 43.1 us
  starting transfers between devices  24 us (56%)
  Pallas kernels  13.1 us (30%)
  waiting for transfers between devices  5.81 us (13%)
    ppermute x15, starting transfers between devices, exchanged(): return lax.ppermute(values, ('frow', 'fcol'), pairs)  22.7 us
    ppermute x15, waiting for transfers between devices, exchanged(): return lax.ppermute(values, ('frow', 'fcol'), pairs)  5.81 us
    pallas_call x4, Pallas kernels, scatter(): pl.pallas_call(functools.partial(scatter_kernel, len(blocks), total is No...  2.89 us
    pallas_call x2, Pallas kernels, pack_chip(): pl.pallas_call(functools.partial(pack_chip_kernel, tiles, tile_rows, colu...  2.65 us
    pallas_call x1, Pallas kernels, edge_steps(): pl.pallas_call(functools.partial(edge_steps_kernel, n_row, paired), out_s...  1.83 us
    pallas_call x1, Pallas kernels, prepare(): pl.pallas_call(functools.partial(prepare_kernel, order), in_specs=[in_hbm...  1.39 us
    pallas_call x1, Pallas kernels, edge_fields(): pl.pallas_call(functools.partial(edge_fields_kernel, n_row, pair_at, pair...  1.37 us
    ppermute x2, starting transfers between devices, exchanged_across(): lax.ppermute(values, 'frow', [(f, (f + 1 ^ 1) - 1) for f in range(1, n_ro...  1.33 us
  transfers between devices with their start and end apart: 17, of which 6 were waited for; matrix products, arithmetic and copies ran while one was open for 0% of the time, Pallas kernels for 26%

profile of v6, /device:TPU:0, one launch (start us, length us, event | category | flops | bytes accessed | tf_op | source)
XLA Modules:
  0.0 43.1 jit_solution(910316505340554037)
XLA Ops:
  0.0 0.5 %collective-permute-start = (f32[48,2048]{1,0:T(8,128)}, f32[48,2048]{1,0:T(8,128)S(1)}, u32[]{:S(2)}, u32[]{:S(2)}) collective-permute-start(f32[48,2048]{1,0:T(8,128)} %bitcast.6), channel_id=1, source_target_pairs={{0,4},{1,5},{2,6},{3,7},{4,0},{5,1},{6,2},{7,3},{8,12},{9,13},{10,... | collective-permute-start | bytes 1179656 | tf_op jit(solution)/shard_map/ppermute | solution.py:672
  0.5 1.4 %prepare.1 = (f32[544,128]{1,0:T(8,128)S(1)}, f32[480,128]{1,0:T(8,128)S(1)}, f32[4,8,48,128]{3,2,1,0:T(8,128)S(1)}, f32[48,2048]{1,0:T(8,128)S(1)}) custom-call(s32[16,128]{1,0:T(8,128)} %bitcast.8, s32[16,128]{1,0:T(8,128)} %bitcast.9, f32[2,2048]{1,0:T(2,128)} %frac.1, f32[4,384,128]{2,1,0:T(8,128)} %bitcast.5, f32[48,2048]{1,0:T(8,128)} %bitcast.7), custom_call_target="tpu_custom_call" | custom-call | tf_op jit(solution)/shard_map/prepare/pallas_call | solution.py:105
  1.9 0.1 collective-permute-start.1
  2.0 0.7 %collective-permute-start.2 = (f32[480,128]{1,0:T(8,128)S(1)}, f32[480,128]{1,0:T(8,128)S(1)}, u32[]{:S(2)}, u32[]{:S(2)}) collective-permute-start(f32[480,128]{1,0:T(8,128)S(1)} %get-tuple-element.30), channel_id=1, source_target_pairs={{4,8},{8,4},{5,9},{9,5},{6,10},{10,6},{7,11},{11,7},{20,24},{24,20... | collective-permute-start | bytes 737288 | tf_op jit(solution)/shard_map/ppermute | solution.py:677
  2.7 0.8 %collective-permute-done.1.pair_where.pair = f32[544,128]{1,0:T(8,128)S(1)} collective-permute-done((f32[544,128]{1,0:T(8,128)S(1)}, f32[544,128]{1,0:T(8,128)S(1)}, u32[]{:S(2)}, u32[]{:S(2)}) %collective-permute-start.1) | collective-permute-done | bytes 278560 | tf_op jit(solution)/shard_map/ppermute | solution.py:672
  3.5 0.0 collective-permute-done.pair_cot
  3.5 1.3 %pack_chip.2 = (f32[208,128]{1,0:T(8,128)S(1)}, f32[208,128]{1,0:T(8,128)S(1)}, f32[208,128]{1,0:T(8,128)S(1)}, f32[208,128]{1,0:T(8,128)S(1)}) custom-call(f32[48,2048]{1,0:T(8,128)S(1)} %get-tuple-element.28.cot, f32[544,128]{1,0:T(8,128)S(1)} %get-tuple-element.29.where, f32[48,2048]{1,0:T(8,128)S(1)} %collective-permute-done.pair_cot, ...), custom_call_target="tpu_custom_call" | custom-call | tf_op jit(solution)/shard_map/pack_chip/pallas_call | solution.py:396
  4.8 3.4 %collective-permute-start.8 = (f32[208,128]{1,0:T(8,128)S(1)}, f32[208,128]{1,0:T(8,128)S(1)}, u32[]{:S(2)}, u32[]{:S(2)}) collective-permute-start(f32[208,128]{1,0:T(8,128)S(1)} %get-tuple-element.38), channel_id=1, source_target_pairs={{0,8},{1,9},{2,10},{3,11},{4,12},{5,13},{6,14},{7,15},{8,0},{9,1},... | collective-permute-start | bytes 319496 | tf_op jit(solution)/shard_map/ppermute | solution.py:672
  8.3 1.7 %collective-permute-start.6 = (f32[208,128]{1,0:T(8,128)S(1)}, f32[208,128]{1,0:T(8,128)S(1)}, u32[]{:S(2)}, u32[]{:S(2)}) collective-permute-start(f32[208,128]{1,0:T(8,128)S(1)} %get-tuple-element.36), channel_id=1, source_target_pairs={{0,1},{1,0},{2,3},{3,2},{4,5},{5,4},{6,7},{7,6},{8,9},{9,8},{10,11... | collective-permute-start | bytes 319496 | tf_op jit(solution)/shard_map/ppermute | solution.py:672
  10.0 0.0 collective-permute-start.7
  10.0 0.0 collective-permute-done.2.refs_0_.cross
  10.0 1.3 %pack_chip.3 = (f32[208,128]{1,0:T(8,128)S(1)}, f32[208,128]{1,0:T(8,128)S(1)}, f32[208,128]{1,0:T(8,128)S(1)}, f32[208,128]{1,0:T(8,128)S(1)}) custom-call(f32[48,2048]{1,0:T(8,128)S(1)} %get-tuple-element.28.cot, f32[544,128]{1,0:T(8,128)S(1)} %get-tuple-element.29.where, f32[48,2048]{1,0:T(8,128)S(1)} %collective-permute-done.pair_cot, ...), custom_call_target="tpu_custom_call" | custom-call | tf_op jit(solution)/shard_map/pack_chip/pallas_call | solution.py:396
  11.3 1.6 %collective-permute-start.3 = (f32[208,128]{1,0:T(8,128)S(1)}, f32[208,128]{1,0:T(8,128)S(1)}, u32[]{:S(2)}, u32[]{:S(2)}) collective-permute-start(f32[208,128]{1,0:T(8,128)S(1)} %get-tuple-element.32), channel_id=1, source_target_pairs={{0,1},{1,0},{2,3},{3,2},{4,5},{5,4},{6,7},{7,6},{8,9},{9,8},{10,11... | collective-permute-start | bytes 319496 | tf_op jit(solution)/shard_map/ppermute | solution.py:672
  12.9 2.9 %collective-permute-start.5 = (f32[208,128]{1,0:T(8,128)S(1)}, f32[208,128]{1,0:T(8,128)S(1)}, u32[]{:S(2)}, u32[]{:S(2)}) collective-permute-start(f32[208,128]{1,0:T(8,128)S(1)} %get-tuple-element.35), channel_id=1, source_target_pairs={{0,8},{1,9},{2,10},{3,11},{4,12},{5,13},{6,14},{7,15},{8,0},{9,1},... | collective-permute-start | bytes 319496 | tf_op jit(solution)/shard_map/ppermute | solution.py:672
  15.8 0.0 collective-permute-done.8.refs_1_
  15.8 0.0 collective-permute-start.4
  15.8 0.7 %scatter_points.6.refs_2_ = f32[8,48,128]{2,1,0:T(8,128)S(1)} custom-call(f32[208,128]{1,0:T(8,128)S(1)} %get-tuple-element.31.refs_1_.refs_0_, f32[208,128]{1,0:T(8,128)S(1)} %collective-permute-done.8.refs_1_, f32[208,128]{1,0:T(8,128)S(1)} %get-tuple-element.34.refs_0_.refs_2_), custom_call_target="tpu_custom_call" | custom-call | tf_op jit(solution)/shard_map/scatter_points/pallas_call | solution.py:461
  16.6 0.0 collective-permute-done.6.refs_0_
  16.6 0.2 collective-permute-done.7.refs_1_
  16.8 0.7 %scatter_points.7 = (f32[4,48,128]{2,1,0:T(8,128)S(1)}, f32[4,48,128]{2,1,0:T(8,128)S(1)}) custom-call(f32[208,128]{1,0:T(8,128)S(1)} %collective-permute-done.6.refs_0_, f32[208,128]{1,0:T(8,128)S(1)} %collective-permute-done.7.refs_1_, f32[8,48,128]{2,1,0:T(8,128)S(1)} %scatter_points.6.refs_2_), custom_call_target="tpu_custom_call" | custom-call | tf_op jit(solution)/shard_map/scatter_points/pallas_call | solution.py:461
  17.5 2.6 %collective-permute-start.9 = (f32[4,48,128]{2,1,0:T(8,128)S(1)}, f32[4,48,128]{2,1,0:T(8,128)S(1)}, u32[]{:S(2)}, u32[]{:S(2)}) collective-permute-start(f32[4,48,128]{2,1,0:T(8,128)S(1)} %get-tuple-element.39.refs_0_), channel_id=1, source_target_pairs={{0,2},{1,3},{2,0},{3,1},{4,6},{5,7},{6,4},{7,5},{8,10},{9,11},{10,... | collective-permute-start | bytes 294920 | tf_op jit(solution)/shard_map/ppermute | solution.py:672
  20.2 0.3 collective-permute-start.10
  20.5 0.6 %state_edges.1 = (f32[48,128]{1,0:T(8,128)S(1)}, f32[48,128]{1,0:T(8,128)S(1)}) custom-call(f32[4,8,48,128]{3,2,1,0:T(8,128)S(1)} %get-tuple-element.41.turned, f32[544,128]{1,0:T(8,128)S(1)} %collective-permute-done.1.pair_where.pair, f32[480,128]{1,0:T(8,128)S(1)} %collective-permute-done.2.refs_0_.cross, f32[4,48,128]{2,1,0:T(8,128)S(1)} %get-tuple-element.39.refs_0_, ...), custom_call_target="tpu_custom_call" | custom-call | tf_op jit(solution)/shard_map/state_edges/pallas_call | solution.py:173
  21.2 0.0 collective-permute-done.3.refs_0_
  21.2 1.3 %collective-permute-start.11 = (f32[48,128]{1,0:T(8,128)S(1)}, f32[48,128]{1,0:T(8,128)S(1)}, u32[]{:S(2)}, u32[]{:S(2)}) collective-permute-start(f32[48,128]{1,0:T(8,128)S(1)} %get-tuple-element.42), channel_id=1, source_target_pairs={{0,1},{1,0},{2,3},{3,2},{4,5},{5,4},{6,7},{7,6},{8,9},{9,8},{10,11... | collective-permute-start | bytes 73736 | tf_op jit(solution)/shard_map/ppermute | solution.py:672
  22.4 0.0 collective-permute-done.5.refs_1_
  22.4 2.8 %collective-permute-start.12 = (f32[48,128]{1,0:T(8,128)S(1)}, f32[48,128]{1,0:T(8,128)S(1)}, u32[]{:S(2)}, u32[]{:S(2)}) collective-permute-start(f32[48,128]{1,0:T(8,128)S(1)} %get-tuple-element.43), channel_id=1, source_target_pairs={{0,3},{1,2},{2,1},{3,0},{4,7},{5,6},{6,5},{7,4},{8,11},{9,10},{10,... | collective-permute-start | bytes 73736 | tf_op jit(solution)/shard_map/ppermute | solution.py:672
  25.3 0.7 %scatter_points.4.refs_2_ = f32[8,48,128]{2,1,0:T(8,128)S(1)} custom-call(f32[208,128]{1,0:T(8,128)S(1)} %get-tuple-element.34.refs_0_.refs_2_, f32[208,128]{1,0:T(8,128)S(1)} %collective-permute-done.5.refs_1_), custom_call_target="tpu_custom_call" | custom-call | tf_op jit(solution)/shard_map/scatter_points/pallas_call | solution.py:461
  26.0 0.0 collective-permute-done.4.refs_1_
  26.0 0.7 %scatter_points.5.refs_0_.total = f32[8,48,128]{2,1,0:T(8,128)S(1)} custom-call(f32[208,128]{1,0:T(8,128)S(1)} %collective-permute-done.3.refs_0_, f32[208,128]{1,0:T(8,128)S(1)} %collective-permute-done.4.refs_1_, f32[8,48,128]{2,1,0:T(8,128)S(1)} %scatter_points.4.refs_2_), custom_call_target="tpu_custom_call" | custom-call | tf_op jit(solution)/shard_map/scatter_points/pallas_call | solution.py:461
  26.8 1.0 %tile_fields.1 = (f32[4,16,112,128]{3,2,1,0:T(8,128)S(1)}, f32[16,128]{1,0:T(8,128)S(1)}) custom-call(f32[4,8,48,128]{3,2,1,0:T(8,128)S(1)} %get-tuple-element.41.turned, f32[544,128]{1,0:T(8,128)S(1)} %collective-permute-done.1.pair_where.pair, f32[480,128]{1,0:T(8,128)S(1)} %collective-permute-done.2.refs_0_.cross, f32[16]{0:T(128)S(1)} %copy-done, ...), custom_call_target="tpu_custom_call" | custom-call | tf_op jit(solution)/shard_map/tile_fields/pallas_call | solution.py:223
  27.8 0.0 collective-permute-done.11.refs_2_.one
  27.8 0.4 collective-permute-done.12.refs_3_.other
  28.2 0.3 collective-permute-done.9.refs_0_
  28.5 1.9 %collective-permute-done.10.refs_1_ = f32[4,48,128]{2,1,0:T(8,128)S(1)} collective-permute-done((f32[4,48,128]{2,1,0:T(8,128)S(1)}, f32[4,48,128]{2,1,0:T(8,128)S(1)}, u32[]{:S(2)}, u32[]{:S(2)}) %collective-permute-start.10) | collective-permute-done | bytes 98336 | tf_op jit(solution)/shard_map/ppermute | solution.py:672
  30.4 0.7 %collective-permute-start.14 = (f32[4,48,128]{2,1,0:T(8,128)S(1)}, f32[4,48,128]{2,1,0:T(8,128)S(1)}, u32[]{:S(2)}, u32[]{:S(2)}) collective-permute-start(f32[4,48,128]{2,1,0:T(8,128)S(1)} %get-tuple-element.47), channel_id=1, source_target_pairs={{4,8},{8,4},{5,9},{9,5},{6,10},{10,6},{7,11},{11,7},{20,24},{24,20... | collective-permute-start | bytes 294920 | tf_op jit(solution)/shard_map/ppermute | solution.py:677
  31.1 1.8 %collective-permute-start.13 = (f32[4,48,128]{2,1,0:T(8,128)S(1)}, f32[4,48,128]{2,1,0:T(8,128)S(1)}, u32[]{:S(2)}, u32[]{:S(2)}) collective-permute-start(f32[4,48,128]{2,1,0:T(8,128)S(1)} %get-tuple-element.46), channel_id=1, source_target_pairs={{0,4},{1,5},{2,6},{3,7},{4,0},{5,1},{6,2},{7,3},{8,12},{9,13},{10,... | collective-permute-start | bytes 294920 | tf_op jit(solution)/shard_map/ppermute | solution.py:672
  32.9 1.4 %edge_fields.1.refs_0_.wide = f32[4,16,112,128]{3,2,1,0:T(8,128)S(1)} custom-call(f32[4,8,48,128]{3,2,1,0:T(8,128)S(1)} %get-tuple-element.41.turned, f32[544,128]{1,0:T(8,128)S(1)} %collective-permute-done.1.pair_where.pair, f32[480,128]{1,0:T(8,128)S(1)} %collective-permute-done.2.refs_0_.cross, f32[48,128]{1,0:T(8,128)S(1)} %collective-permute-done.11.refs_2_.one, ...), custom_call_target="tpu_custom_call" | custom-call | tf_op jit(solution)/shard_map/edge_fields/pallas_call | solution.py:273
  34.3 0.0 collective-permute-done.14.cross
  34.3 0.2 cross_edges.1.partial
  34.5 0.0 collective-permute-done.13.pair
  34.5 0.1 pair_edges.1
  34.6 0.9 %collective-permute-start.15 = (f32[48,128]{1,0:T(8,128)S(1)}, f32[48,128]{1,0:T(8,128)S(1)}, u32[]{:S(2)}, u32[]{:S(2)}) collective-permute-start(f32[48,128]{1,0:T(8,128)S(1)} %pair_edges.1), channel_id=1, source_target_pairs={{0,1},{1,0},{2,3},{3,2},{4,5},{5,4},{6,7},{7,6},{8,9},{9,8},{10,11... | collective-permute-start | bytes 73736 | tf_op jit(solution)/shard_map/ppermute | solution.py:672
  35.5 2.6 %collective-permute-start.16 = (f32[48,128]{1,0:T(8,128)S(1)}, f32[48,128]{1,0:T(8,128)S(1)}, u32[]{:S(2)}, u32[]{:S(2)}) collective-permute-start(f32[48,128]{1,0:T(8,128)S(1)} %pair_edges.1), channel_id=1, source_target_pairs={{0,3},{1,2},{2,1},{3,0},{4,7},{5,6},{6,5},{7,4},{8,11},{9,10},{10,... | collective-permute-start | bytes 73736 | tf_op jit(solution)/shard_map/ppermute | solution.py:672
  38.1 1.0 %tile_steps.1 = (f32[8,48,128]{2,1,0:T(8,128)S(1)}, f32[16,48,128]{2,1,0:T(8,128)S(1)}) custom-call(f32[8,48,128]{2,1,0:T(8,128)S(1)} %get-tuple-element.45.canvas, f32[4,48,128]{2,1,0:T(8,128)S(1)} %collective-permute-done.13.pair, f32[4,48,128]{2,1,0:T(8,128)S(1)} %collective-permute-done.14.cross, f32[4,16,112,128]{3,2,1,0:T(8,128)S(1)} %get-tuple-element.48.wide, ...), custom_call_target="tpu_custom_call" | custom-call | tf_op jit(solution)/shard_map/tile_steps/pallas_call | solution.py:618
  39.1 0.0 collective-permute-done.15.one
  39.1 2.1 %collective-permute-done.16.other = f32[48,128]{1,0:T(8,128)S(1)} collective-permute-done((f32[48,128]{1,0:T(8,128)S(1)}, f32[48,128]{1,0:T(8,128)S(1)}, u32[]{:S(2)}, u32[]{:S(2)}) %collective-permute-start.16) | collective-permute-done | bytes 24608 | tf_op jit(solution)/shard_map/ppermute | solution.py:672
  41.3 1.8 %edge_steps.1 = f32[384,128]{1,0:T(8,128)} custom-call(f32[16,48,128]{2,1,0:T(8,128)S(1)} %get-tuple-element.49.windows, f32[48,128]{1,0:T(8,128)S(1)} %collective-permute-done.15.one, f32[48,128]{1,0:T(8,128)S(1)} %collective-permute-done.16.other, f32[4,16,112,128]{3,2,1,0:T(8,128)S(1)} %edge_fields.1.refs_0_.wide, ...), custom_call_target="tpu_custom_call" | custom-call | tf_op jit(solution)/shard_map/edge_steps/pallas_call | solution.py:654
  (3 shorter events, 0.0 us)
Async XLA Ops:
  0.0 3.5 %collective-permute-start = (f32[48,2048]{1,0:T(8,128)}, f32[48,2048]{1,0:T(8,128)S(1)}, u32[]{:S(2)}, u32[]{:S(2)}) collective-permute-start(f32[48,2048]{1,0:T(8,128)} %bitcast.6), channel_id=1, source_target_pairs={{0,4},{1,5},{2,6},{3,7},{4,0},{5,1},{6,2},{7,3},{8,12},{9,13},{10,... | collective-permute-start | bytes 1179656 | tf_op jit(solution)/shard_map/ppermute | solution.py:672
  0.5 26.3 %copy-start = (f32[16]{0:T(128)S(1)}, f32[16]{0:T(128)}, u32[]{:S(2)}) copy-start(f32[16]{0:T(128)} %gravity.1) | copy-start | bytes 196
  1.9 1.6 %collective-permute-start.1 = (f32[544,128]{1,0:T(8,128)S(1)}, f32[544,128]{1,0:T(8,128)S(1)}, u32[]{:S(2)}, u32[]{:S(2)}) collective-permute-start(f32[544,128]{1,0:T(8,128)S(1)} %get-tuple-element.29.where), channel_id=1, source_target_pairs={{0,4},{1,5},{2,6},{3,7},{4,0},{5,1},{6,2},{7,3},{8,12},{9,13},{10,... | collective-permute-start | bytes 835592 | tf_op jit(solution)/shard_map/ppermute | solution.py:672
  2.0 8.0 %collective-permute-start.2 = (f32[480,128]{1,0:T(8,128)S(1)}, f32[480,128]{1,0:T(8,128)S(1)}, u32[]{:S(2)}, u32[]{:S(2)}) collective-permute-start(f32[480,128]{1,0:T(8,128)S(1)} %get-tuple-element.30), channel_id=1, source_target_pairs={{4,8},{8,4},{5,9},{9,5},{6,10},{10,6},{7,11},{11,7},{20,24},{24,20... | collective-permute-start | bytes 737288 | tf_op jit(solution)/shard_map/ppermute | solution.py:677
  4.8 11.0 %collective-permute-start.8 = (f32[208,128]{1,0:T(8,128)S(1)}, f32[208,128]{1,0:T(8,128)S(1)}, u32[]{:S(2)}, u32[]{:S(2)}) collective-permute-start(f32[208,128]{1,0:T(8,128)S(1)} %get-tuple-element.38), channel_id=1, source_target_pairs={{0,8},{1,9},{2,10},{3,11},{4,12},{5,13},{6,14},{7,15},{8,0},{9,1},... | collective-permute-start | bytes 319496 | tf_op jit(solution)/shard_map/ppermute | solution.py:672
  8.3 8.3 %collective-permute-start.6 = (f32[208,128]{1,0:T(8,128)S(1)}, f32[208,128]{1,0:T(8,128)S(1)}, u32[]{:S(2)}, u32[]{:S(2)}) collective-permute-start(f32[208,128]{1,0:T(8,128)S(1)} %get-tuple-element.36), channel_id=1, source_target_pairs={{0,1},{1,0},{2,3},{3,2},{4,5},{5,4},{6,7},{7,6},{8,9},{9,8},{10,11... | collective-permute-start | bytes 319496 | tf_op jit(solution)/shard_map/ppermute | solution.py:672
  10.0 6.8 %collective-permute-start.7 = (f32[208,128]{1,0:T(8,128)S(1)}, f32[208,128]{1,0:T(8,128)S(1)}, u32[]{:S(2)}, u32[]{:S(2)}) collective-permute-start(f32[208,128]{1,0:T(8,128)S(1)} %get-tuple-element.37), channel_id=1, source_target_pairs={{0,9},{1,8},{2,11},{3,10},{4,13},{5,12},{6,15},{7,14},{8,1},{9,0},... | collective-permute-start | bytes 319496 | tf_op jit(solution)/shard_map/ppermute | solution.py:672
  11.3 9.8 %collective-permute-start.3 = (f32[208,128]{1,0:T(8,128)S(1)}, f32[208,128]{1,0:T(8,128)S(1)}, u32[]{:S(2)}, u32[]{:S(2)}) collective-permute-start(f32[208,128]{1,0:T(8,128)S(1)} %get-tuple-element.32), channel_id=1, source_target_pairs={{0,1},{1,0},{2,3},{3,2},{4,5},{5,4},{6,7},{7,6},{8,9},{9,8},{10,11... | collective-permute-start | bytes 319496 | tf_op jit(solution)/shard_map/ppermute | solution.py:672
  12.9 9.5 %collective-permute-start.5 = (f32[208,128]{1,0:T(8,128)S(1)}, f32[208,128]{1,0:T(8,128)S(1)}, u32[]{:S(2)}, u32[]{:S(2)}) collective-permute-start(f32[208,128]{1,0:T(8,128)S(1)} %get-tuple-element.35), channel_id=1, source_target_pairs={{0,8},{1,9},{2,10},{3,11},{4,12},{5,13},{6,14},{7,15},{8,0},{9,1},... | collective-permute-start | bytes 319496 | tf_op jit(solution)/shard_map/ppermute | solution.py:672
  15.8 10.2 %collective-permute-start.4 = (f32[208,128]{1,0:T(8,128)S(1)}, f32[208,128]{1,0:T(8,128)S(1)}, u32[]{:S(2)}, u32[]{:S(2)}) collective-permute-start(f32[208,128]{1,0:T(8,128)S(1)} %get-tuple-element.33), channel_id=1, source_target_pairs={{0,9},{1,8},{2,11},{3,10},{4,13},{5,12},{6,15},{7,14},{8,1},{9,0},... | collective-permute-start | bytes 319496 | tf_op jit(solution)/shard_map/ppermute | solution.py:672
  17.5 11.0 %collective-permute-start.9 = (f32[4,48,128]{2,1,0:T(8,128)S(1)}, f32[4,48,128]{2,1,0:T(8,128)S(1)}, u32[]{:S(2)}, u32[]{:S(2)}) collective-permute-start(f32[4,48,128]{2,1,0:T(8,128)S(1)} %get-tuple-element.39.refs_0_), channel_id=1, source_target_pairs={{0,2},{1,3},{2,0},{3,1},{4,6},{5,7},{6,4},{7,5},{8,10},{9,11},{10,... | collective-permute-start | bytes 294920 | tf_op jit(solution)/shard_map/ppermute | solution.py:672
  20.2 10.2 %collective-permute-start.10 = (f32[4,48,128]{2,1,0:T(8,128)S(1)}, f32[4,48,128]{2,1,0:T(8,128)S(1)}, u32[]{:S(2)}, u32[]{:S(2)}) collective-permute-start(f32[4,48,128]{2,1,0:T(8,128)S(1)} %get-tuple-element.40.refs_1_), channel_id=1, source_target_pairs={{0,2},{1,3},{2,0},{3,1},{4,6},{5,7},{6,4},{7,5},{8,10},{9,11},{10,... | collective-permute-start | bytes 294920 | tf_op jit(solution)/shard_map/ppermute | solution.py:672
  21.2 6.6 %collective-permute-start.11 = (f32[48,128]{1,0:T(8,128)S(1)}, f32[48,128]{1,0:T(8,128)S(1)}, u32[]{:S(2)}, u32[]{:S(2)}) collective-permute-start(f32[48,128]{1,0:T(8,128)S(1)} %get-tuple-element.42), channel_id=1, source_target_pairs={{0,1},{1,0},{2,3},{3,2},{4,5},{5,4},{6,7},{7,6},{8,9},{9,8},{10,11... | collective-permute-start | bytes 73736 | tf_op jit(solution)/shard_map/ppermute | solution.py:672
  22.4 5.7 %collective-permute-start.12 = (f32[48,128]{1,0:T(8,128)S(1)}, f32[48,128]{1,0:T(8,128)S(1)}, u32[]{:S(2)}, u32[]{:S(2)}) collective-permute-start(f32[48,128]{1,0:T(8,128)S(1)} %get-tuple-element.43), channel_id=1, source_target_pairs={{0,3},{1,2},{2,1},{3,0},{4,7},{5,6},{6,5},{7,4},{8,11},{9,10},{10,... | collective-permute-start | bytes 73736 | tf_op jit(solution)/shard_map/ppermute | solution.py:672
  30.4 3.9 %collective-permute-start.14 = (f32[4,48,128]{2,1,0:T(8,128)S(1)}, f32[4,48,128]{2,1,0:T(8,128)S(1)}, u32[]{:S(2)}, u32[]{:S(2)}) collective-permute-start(f32[4,48,128]{2,1,0:T(8,128)S(1)} %get-tuple-element.47), channel_id=1, source_target_pairs={{4,8},{8,4},{5,9},{9,5},{6,10},{10,6},{7,11},{11,7},{20,24},{24,20... | collective-permute-start | bytes 294920 | tf_op jit(solution)/shard_map/ppermute | solution.py:677
  31.1 3.4 %collective-permute-start.13 = (f32[4,48,128]{2,1,0:T(8,128)S(1)}, f32[4,48,128]{2,1,0:T(8,128)S(1)}, u32[]{:S(2)}, u32[]{:S(2)}) collective-permute-start(f32[4,48,128]{2,1,0:T(8,128)S(1)} %get-tuple-element.46), channel_id=1, source_target_pairs={{0,4},{1,5},{2,6},{3,7},{4,0},{5,1},{6,2},{7,3},{8,12},{9,13},{10,... | collective-permute-start | bytes 294920 | tf_op jit(solution)/shard_map/ppermute | solution.py:672
  34.6 4.5 %collective-permute-start.15 = (f32[48,128]{1,0:T(8,128)S(1)}, f32[48,128]{1,0:T(8,128)S(1)}, u32[]{:S(2)}, u32[]{:S(2)}) collective-permute-start(f32[48,128]{1,0:T(8,128)S(1)} %pair_edges.1), channel_id=1, source_target_pairs={{0,1},{1,0},{2,3},{3,2},{4,5},{5,4},{6,7},{7,6},{8,9},{9,8},{10,11... | collective-permute-start | bytes 73736 | tf_op jit(solution)/shard_map/ppermute | solution.py:672
  35.5 5.8 %collective-permute-start.16 = (f32[48,128]{1,0:T(8,128)S(1)}, f32[48,128]{1,0:T(8,128)S(1)}, u32[]{:S(2)}, u32[]{:S(2)}) collective-permute-start(f32[48,128]{1,0:T(8,128)S(1)} %pair_edges.1), channel_id=1, source_target_pairs={{0,3},{1,2},{2,1},{3,0},{4,7},{5,6},{6,5},{7,4},{8,11},{9,10},{10,... | collective-permute-start | bytes 73736 | tf_op jit(solution)/shard_map/ppermute | solution.py:672

commit v7 on v6

--- a/solution.py
+++ b/solution.py
@@ -185,11 +185,13 @@
     return 0.5 * time_step if which % 2 == 0 else time_step
 
 
-def store_fields(wide, which, lines, levels, base_row, total_rows):
+def store_fields(wide, which, lines, levels, base_row, total_rows, own=None):
     weight = stage_weight(which)
     channels = 3 * levels
     for k, line in lines:
         wide[which, k, :channels, :] = (0.5 * weight) * line
+        if own is not None:
+            own[which, k] = edge_windows(line)
     winds = slice(levels, channels)
     for k in range(lines[0][0] + 1, lines[-1][0]):
         values = wide[which, k, winds, :]
@@ -202,8 +204,48 @@
             begin += levels
 
 
+PART = 8
+BEYOND_AT = 32
+TURN = LANES // 2
+
+
+def ring_lanes():
+    return lax.broadcasted_iota(jnp.int32, (PART, LANES), 1)
+
+
+def by_half(values, ring):
+    lane = ring_lanes()
+    second = (lane >= TURN - LANES // 8) & (lane < LANES - LANES // 8)
+    fields = []
+    for begin in range(0, values.shape[0], 2 * PART):
+        first, last = values[begin : begin + PART], values[begin + PART : begin + 2 * PART]
+        fields.append(jnp.where(second, ring(last, TURN), ring(first, 0)))
+    return jnp.concatenate(fields, axis=0)
+
+
+def turned_by(values, shift):
+    shift %= LANES
+    return pltpu.roll(values, shift, 1) if shift else values
+
+
+def edge_windows(line):
+    lane = ring_lanes()
+
+    def ring(values, turn):
+        ends = (lane >= turn + BEYOND_AT // 2) & (lane < turn + BEYOND_AT)
+        return jnp.where(ends, turned_by(values, BEYOND_AT + turn), turned_by(values, turn))
+
+    return by_half(line, ring)
+
+
+def with_rim(window, rim):
+    lane = lax.broadcasted_iota(jnp.int32, window.shape, 1) % TURN
+    beyond = (lane >= TURN - HALO) | ((lane >= BEYOND_AT) & (lane < BEYOND_AT + HALO))
+    return jnp.where(beyond, rim, window)
+
+
 def tile_fields_kernel(n_row, pair_at, turned, pair, cross, gravity, *refs):
-    wide, pull = refs[-2:]
+    wide, pull, edge_pull, own = refs[-4:]
     stages, tile_rows, channels, _ = turned.shape
     levels = channels // 3
     level = lax.broadcasted_iota(jnp.int32, pull.shape, 0)
@@ -211,10 +253,11 @@
     for i in range(levels):
         pulls = jnp.where(level == i, gravity[i], pulls)
     pull[...] = pulls
+    edge_pull[...] = by_half(pulls, lambda values, _: values)
     lower, masks = first_of_pair(), row_masks(n_row)
     for which in range(stages):
         lines = state_rows(which, turned, pair, pair_at, cross, lower, masks)
-        store_fields(wide, which, lines, levels, lax.axis_index("frow") * tile_rows, tile_rows * n_row)
+        store_fields(wide, which, lines, levels, lax.axis_index("frow") * tile_rows, tile_rows * n_row, own)
 
 
 def tile_fields(n_row, pair_at, turned, pair, cross, gravity, after=()):
@@ -226,56 +269,51 @@
         out_shape=(
             jax.ShapeDtypeStruct((stages, tile_rows + 2 * HALO, channels // 3 * FIELDS, columns), F32),
             jax.ShapeDtypeStruct((channels // 3, columns), F32),
+            jax.ShapeDtypeStruct((PART, columns), F32),
+            jax.ShapeDtypeStruct((stages, tile_rows + 2 * HALO, 3 * PART, columns), F32),
         ),
         compiler_params=PARAMS,
         name="tile_fields",
     )(turned, pair, cross, gravity, *after)
 
 
-PART = 8
-BEYOND_AT = 32
-
-
-def edge_windows(line):
-    lane = lax.broadcasted_iota(jnp.int32, line.shape, 1)
-    return jnp.where((lane >= BEYOND_AT // 2) & (lane < 2 * BEYOND_AT), pltpu.roll(line, BEYOND_AT, 1), line)
-
-
-def with_rim(window, rim):
-    lane = lax.broadcasted_iota(jnp.int32, window.shape, 1)
-    beyond = (lane >= LANES - HALO) | ((lane >= BEYOND_AT) & (lane < BEYOND_AT + HALO))
-    return jnp.where(beyond, rim, window)
-
-
-def edge_fields_kernel(n_row, pair_at, paired, turned, pair, cross, one, other, wide):
-    stages, tile_rows, channels, columns = turned.shape
-    lower, masks = first_of_pair(), row_masks(n_row)
+def edge_fields_kernel(n_row, paired, own, one, other, wide):
+    stages, extended, _, columns = own.shape
+    tile_rows = extended - 2 * HALO
     left, right = from_sides(one[...], other[...], paired)
-    lane = lax.broadcasted_iota(jnp.int32, (channels, columns), 1)
-    rims = {
-        (which, k): jnp.where(
-            lane < columns // 2,
-            pltpu.roll(right, (BEYOND_AT - at) % columns, 1),
-            pltpu.roll(left, (-at - count) % columns, 1),
-        )
-        for which, k, count, at in edge_plan(stages, tile_rows)
-    }
+    lane = ring_lanes()
+    sides = jnp.concatenate([left, right], axis=1)
+
+    def rim_of(count, at):
+        def ring(values, turn):
+            beyond = (lane >= BEYOND_AT + turn) & (lane < BEYOND_AT + HALO + turn)
+            from_left, from_right = values[:, :columns], values[:, columns:]
+            return jnp.where(
+                beyond, turned_by(from_right, BEYOND_AT + turn - at), turned_by(from_left, turn - at - count)
+            )
+
+        return by_half(sides, ring)
+
+    rims = {(which, k): rim_of(count, at) for which, k, count, at in edge_plan(stages, tile_rows)}
     for which in range(stages):
-        lines = [
-            (k, with_rim(edge_windows(line), rims.get((which, k), line)))
-            for k, line in state_rows(which, turned, pair, pair_at, cross, lower, masks)
-        ]
-        store_fields(wide, which, lines, channels // 3, lax.axis_index("frow") * tile_rows, tile_rows * n_row)
-
-
-def edge_fields(n_row, pair_at, paired, turned, pair, cross, one, other):
-    stages, tile_rows, channels, columns = turned.shape
-    return pl.pallas_call(
-        functools.partial(edge_fields_kernel, n_row, pair_at, paired),
-        out_shape=jax.ShapeDtypeStruct((stages, tile_rows + 2 * HALO, channels // 3 * FIELDS, columns), F32),
+        width = HALO - which
+        lines = []
+        for k in range(HALO - width, HALO + tile_rows + width):
+            line = own[which, k]
+            if (which, k) in rims:
+                line = with_rim(line, rims[which, k])
+            lines.append((k, line))
+        store_fields(wide, which, lines, PART, lax.axis_index("frow") * tile_rows, tile_rows * n_row)
+
+
+def edge_fields(n_row, paired, own, one, other):
+    stages, extended, _, columns = own.shape
+    return pl.pallas_call(
+        functools.partial(edge_fields_kernel, n_row, paired),
+        out_shape=jax.ShapeDtypeStruct((stages, extended, PART * FIELDS, columns), F32),
         compiler_params=PARAMS,
         name="edge_fields",
-    )(turned, pair, cross, one, other)
+    )(own, one, other)
 
 
 def slot_blocks(cot, where, tiles, share, groups, tile_rows, columns, onehot, parts):
@@ -407,8 +445,9 @@
     if not first:
         total, refs = refs[0], refs[1:]
     outs, scratch = refs[later : -2 * count], refs[-2 * count :]
-    part_rows, channels, columns = outs[0].shape
-    tile_rows = part_rows * len(outs)
+    _, channels, columns = outs[0].shape
+    places = [(out, r) for out in outs for r in range(out.shape[0])]
+    tile_rows = len(places)
     rows = 2 * channels + 8
     cells = lax.broadcasted_iota(jnp.int32, (columns, LANES), 0).astype(F32).astype(BF16)
     zero = jnp.zeros((channels, LANES), BF16)
@@ -453,14 +492,15 @@
         line = sums[r * channels : (r + 1) * channels, :]
         if not first:
             line = line + total[r]
-        outs[r // part_rows][r % part_rows] = line
-
-
-def scatter(blocks, total, channels, tile_rows, columns, after=(), parts=1):
+        out, at = places[r]
+        out[at] = line
+
+
+def scatter(blocks, total, channels, tile_rows, columns, after=(), parts=None):
     slots = [block.shape[0] // (2 * channels + 8) * GROUP for block in blocks]
     return pl.pallas_call(
         functools.partial(scatter_kernel, len(blocks), total is None, len(after)),
-        out_shape=[jax.ShapeDtypeStruct((tile_rows // parts, channels, columns), F32)] * parts,
+        out_shape=[jax.ShapeDtypeStruct((count, channels, columns), F32) for count in parts or (tile_rows,)],
         scratch_shapes=[
             pltpu.VMEM((2 * lines, count), BF16) for count in slots for lines in (tile_rows * channels, columns)
         ],
@@ -472,11 +512,12 @@
 def finish_kernel(count, total, *refs):
     parts, (canvas, to_pair, to_cross) = refs[:count], refs[-3:]
     tile_rows = canvas.shape[0]
+    places = [(part, at) for part in parts for at in range(part.shape[0])]
     for r in range(tile_rows):
         line = total[r]
         if parts:
-            size = parts[0].shape[0]
-            line = line + parts[r // size][r % size]
+            part, at = places[r]
+            line = line + part[at]
         canvas[r] = line
     lower = first_of_pair()
     for k in range(HALO):
@@ -619,7 +660,7 @@
         functools.partial(tile_steps_kernel, n_row),
         out_shape=(
             jax.ShapeDtypeStruct(canvas.shape, F32),
-            jax.ShapeDtypeStruct((tile_rows + 2 * HALO, channels, columns), F32),
+            jax.ShapeDtypeStruct((tile_rows + 2 * HALO, 3 * PART, columns), F32),
         ),
         scratch_shapes=[pltpu.VMEM((tile_rows + 2 * HALO, channels, columns), F32)] * 4,
         compiler_params=PARAMS,
@@ -634,19 +675,22 @@
     left, right = from_sides(one[...], other[...], paired)
     rims = jnp.where(first_lanes(left), pltpu.roll(right, BEYOND_AT, 1), left)
     for k in range(tile_rows + 2 * HALO):
-        buffers[0][k] = with_rim(windows[k], pltpu.roll(rims, (-8 * k) % LANES, 1))
-    lane = lax.broadcasted_iota(jnp.int32, (PART, LANES), 1)
+        rim = by_half(rims, lambda values, turn: turned_by(values, turn - 8 * k))
+        buffers[0][k] = with_rim(windows[k], rim)
+    lane = ring_lanes()
 
     def store(r, w, low, value):
-        result[r, w * levels + low : w * levels + low + PART, :] = value
-
-    run_stages(wide, gravity, levels, row_masks(n_row), tile_rows, buffers, store)
+        result[r, w * PART : (w + 1) * PART, :] = value
+
+    run_stages(wide, gravity, PART, row_masks(n_row), tile_rows, buffers, store)
     for r in range(tile_rows):
         for begin in range(0, channels, PART):
-            value = result[r, begin : begin + PART, :]
-            final = pltpu.roll(value, LANES - BEYOND_AT, 1)
+            field, turn = begin // levels, begin % levels // PART * TURN
+            value = result[r, field * PART : (field + 1) * PART, :]
+            first = pltpu.roll(value, turn, 1) if turn else value
+            final = pltpu.roll(value, LANES - BEYOND_AT - turn, 1)
             line = jnp.where(lane >= LANES - HALO, final, inner[r, begin : begin + PART, :])
-            out[pl.ds(begin * tile_rows + r, PART, stride=tile_rows), :] = jnp.where(lane < HALO, value, line)
+            out[pl.ds(begin * tile_rows + r, PART, stride=tile_rows), :] = jnp.where(lane < HALO, first, line)
 
 
 def edge_steps(n_row, paired, windows, one, other, wide, gravity, inner):
@@ -654,7 +698,7 @@
     return pl.pallas_call(
         functools.partial(edge_steps_kernel, n_row, paired),
         out_shape=jax.ShapeDtypeStruct((channels * tile_rows, columns), F32),
-        scratch_shapes=[pltpu.VMEM(windows.shape, F32)] * 4 + [pltpu.VMEM(inner.shape, F32)],
+        scratch_shapes=[pltpu.VMEM(windows.shape, F32)] * 4 + [pltpu.VMEM((tile_rows, 3 * PART, columns), F32)],
         compiler_params=PARAMS,
         name="edge_steps",
     )(windows, one, other, wide, gravity, inner)
@@ -731,24 +775,24 @@
         got = [packed[0]] + [exchanged(block, (df, dz ^ 2)) for block, (df, dz) in zip(packed[1:], FAR[1:])]
         packed = pack_chip(NEAR, chip_points, tile_rows, columns, [cross, packed[0]])
         total = scatter(got[:2], None, *size, packed[:1])[0]
-        sums = scatter(got[2:], total, *size, parts=2)
+        sums = scatter(got[2:], total, *size, parts=(5, tile_rows - 5))
         far = [exchanged(part, (0, 2)) for part in sums]
         got = [packed[0]] + [exchanged(block, tile) for block, tile in zip(packed[1:], NEAR[1:])]
         one, other = all_state_edges(n_row, pair_at, paired, turned, pair, cross, sums)
         one, other = exchanged(one, (0, 1)), exchanged(other, (0, 3))
         total = scatter(got[:2], None, *size)[0]
         total = scatter(got[2:], total, *size)[0]
-        fields, pull = tile_fields(n_row, pair_at, turned, pair, cross, gravity, [total])
+        fields, pull, edge_pull, own = tile_fields(n_row, pair_at, turned, pair, cross, gravity, [total])
         canvas = finish(total, far, [one, other, pull])
     else:
         packed = pack_all(cot, sent, tile_count, share, tile_rows, columns)
         got = from_everyone(packed, channels, tile_count)
         one, other = all_state_edges(n_row, pair_at, paired, turned, pair, cross)
         one, other = shifted(one, "fcol", 1), shifted(other, "fcol", -1)
-        fields, pull = tile_fields(n_row, pair_at, turned, pair, cross, gravity)
+        fields, pull, edge_pull, own = tile_fields(n_row, pair_at, turned, pair, cross, gravity)
         canvas = finish(scatter([got.reshape(-1, LANES)], None, *size)[0])
 
-    near_edges = edge_fields(n_row, pair_at, paired, turned, pair, cross, one, other)
+    near_edges = edge_fields(n_row, paired, own, one, other)
     canvas, to_pair, to_cross = canvas
     pair, cross = exchanged(to_pair, (1, 0)), exchanged_across(to_cross)
     edges = adjoint_edges(n_row, canvas, pair, cross, [near_edges])
@@ -757,7 +801,7 @@
     else:
         sides = shifted(edges, "fcol", 1), shifted(edges, "fcol", -1)
     inner, windows = tile_steps(n_row, canvas, pair, cross, fields, pull)
-    result = edge_steps(n_row, paired, windows, *sides, near_edges, pull, inner)
+    result = edge_steps(n_row, paired, windows, *sides, near_edges, edge_pull, inner)
     return result.reshape(3, levels, tile_rows, columns)
 
 

time: 43.2 us -> 42.1 us (0.975)
  waiting for transfers between devices: 5.81 us -> 3.89 us
  starting transfers between devices: 24 us -> 25.2 us
    ppermute x15, waiting for transfers between devices: 5.81 us -> 3.88 us  [exchanged(): return lax.ppermute(values, ('frow', 'fcol'), pairs)]
    ppermute x15, starting transfers between devices: 22.7 us -> 23.8 us  [exchanged(): return lax.ppermute(values, ('frow', 'fcol'), pairs)]
    pallas_call x1, Pallas kernels: 1.37 us -> 0.87 us  [edge_fields(): pl.pallas_call(functools.partial(edge_fields_kernel, n_row, paired), out_...]
    pallas_call x1, Pallas kernels: 1 us -> 1.49 us  [tile_fields(): pl.pallas_call(functools.partial(tile_fields_kernel, n_row, pair_at), in_...]
    pallas_call x1, Pallas kernels: 1.83 us -> 1.39 us  [edge_steps(): pl.pallas_call(functools.partial(edge_steps_kernel, n_row, paired), out_s...]
  transfers between devices with their start and end apart: 17 -> 17, of which waited for: 6 -> 4; matrix products, arithmetic and copies ran while one was open for 0% -> 0% of each run, Pallas kernels for 26% -> 27%
where the time goes in v7:
time: 42.1 us; the launch traced here: 42 us
  starting transfers between devices  25.2 us (60%)
  Pallas kernels  12.7 us (30%)
  waiting for transfers between devices  3.89 us (9%)
    ppermute x15, starting transfers between devices, exchanged(): return lax.ppermute(values, ('frow', 'fcol'), pairs)  23.8 us
    ppermute x15, waiting for transfers between devices, exchanged(): return lax.ppermute(values, ('frow', 'fcol'), pairs)  3.88 us
    pallas_call x4, Pallas kernels, scatter(): pl.pallas_call(functools.partial(scatter_kernel, len(blocks), total is No...  2.89 us
    pallas_call x2, Pallas kernels, pack_chip(): pl.pallas_call(functools.partial(pack_chip_kernel, tiles, tile_rows, colu...  2.65 us
    pallas_call x1, Pallas kernels, tile_fields(): pl.pallas_call(functools.partial(tile_fields_kernel, n_row, pair_at), in_...  1.49 us
    pallas_call x1, Pallas kernels, prepare(): pl.pallas_call(functools.partial(prepare_kernel, order), in_specs=[in_hbm...  1.39 us
    pallas_call x1, Pallas kernels, edge_steps(): pl.pallas_call(functools.partial(edge_steps_kernel, n_row, paired), out_s...  1.39 us
    ppermute x2, starting transfers between devices, exchanged_across(): lax.ppermute(values, 'frow', [(f, (f + 1 ^ 1) - 1) for f in range(1, n_ro...  1.33 us
  transfers between devices with their start and end apart: 17, of which 4 were waited for; matrix products, arithmetic and copies ran while one was open for 0% of the time, Pallas kernels for 27%

profile of v7, /device:TPU:0, one launch (start us, length us, event | category | flops | bytes accessed | tf_op | source)
XLA Modules:
  0.0 42.0 jit_solution(7500182922243530012)
XLA Ops:
  0.0 0.5 %collective-permute-start = (f32[48,2048]{1,0:T(8,128)}, f32[48,2048]{1,0:T(8,128)S(1)}, u32[]{:S(2)}, u32[]{:S(2)}) collective-permute-start(f32[48,2048]{1,0:T(8,128)} %bitcast.6), channel_id=1, source_target_pairs={{0,4},{1,5},{2,6},{3,7},{4,0},{5,1},{6,2},{7,3},{8,12},{9,13},{10,... | collective-permute-start | bytes 1179656 | tf_op jit(solution)/shard_map/ppermute | solution.py:716
  0.5 1.4 %prepare.1 = (f32[544,128]{1,0:T(8,128)S(1)}, f32[480,128]{1,0:T(8,128)S(1)}, f32[4,8,48,128]{3,2,1,0:T(8,128)S(1)}, f32[48,2048]{1,0:T(8,128)S(1)}) custom-call(s32[16,128]{1,0:T(8,128)} %bitcast.8, s32[16,128]{1,0:T(8,128)} %bitcast.9, f32[2,2048]{1,0:T(2,128)} %frac.1, f32[4,384,128]{2,1,0:T(8,128)} %bitcast.5, f32[48,2048]{1,0:T(8,128)} %bitcast.7), custom_call_target="tpu_custom_call" | custom-call | tf_op jit(solution)/shard_map/prepare/pallas_call | solution.py:105
  1.9 0.1 collective-permute-start.1
  2.0 0.7 %collective-permute-start.2 = (f32[480,128]{1,0:T(8,128)S(1)}, f32[480,128]{1,0:T(8,128)S(1)}, u32[]{:S(2)}, u32[]{:S(2)}) collective-permute-start(f32[480,128]{1,0:T(8,128)S(1)} %get-tuple-element.32), channel_id=1, source_target_pairs={{4,8},{8,4},{5,9},{9,5},{6,10},{10,6},{7,11},{11,7},{20,24},{24,20... | collective-permute-start | bytes 737288 | tf_op jit(solution)/shard_map/ppermute | solution.py:721
  2.7 0.8 %collective-permute-done.1.pair_where.pair = f32[544,128]{1,0:T(8,128)S(1)} collective-permute-done((f32[544,128]{1,0:T(8,128)S(1)}, f32[544,128]{1,0:T(8,128)S(1)}, u32[]{:S(2)}, u32[]{:S(2)}) %collective-permute-start.1) | collective-permute-done | bytes 278560 | tf_op jit(solution)/shard_map/ppermute | solution.py:716
  3.5 0.0 collective-permute-done.pair_cot
  3.5 1.3 %pack_chip.2 = (f32[208,128]{1,0:T(8,128)S(1)}, f32[208,128]{1,0:T(8,128)S(1)}, f32[208,128]{1,0:T(8,128)S(1)}, f32[208,128]{1,0:T(8,128)S(1)}) custom-call(f32[48,2048]{1,0:T(8,128)S(1)} %get-tuple-element.30.cot, f32[544,128]{1,0:T(8,128)S(1)} %get-tuple-element.31.where, f32[48,2048]{1,0:T(8,128)S(1)} %collective-permute-done.pair_cot, ...), custom_call_target="tpu_custom_call" | custom-call | tf_op jit(solution)/shard_map/pack_chip/pallas_call | solution.py:434
  4.8 3.4 %collective-permute-start.8 = (f32[208,128]{1,0:T(8,128)S(1)}, f32[208,128]{1,0:T(8,128)S(1)}, u32[]{:S(2)}, u32[]{:S(2)}) collective-permute-start(f32[208,128]{1,0:T(8,128)S(1)} %get-tuple-element.40), channel_id=1, source_target_pairs={{0,8},{1,9},{2,10},{3,11},{4,12},{5,13},{6,14},{7,15},{8,0},{9,1},... | collective-permute-start | bytes 319496 | tf_op jit(solution)/shard_map/ppermute | solution.py:716
  8.3 1.7 %collective-permute-start.6 = (f32[208,128]{1,0:T(8,128)S(1)}, f32[208,128]{1,0:T(8,128)S(1)}, u32[]{:S(2)}, u32[]{:S(2)}) collective-permute-start(f32[208,128]{1,0:T(8,128)S(1)} %get-tuple-element.38), channel_id=1, source_target_pairs={{0,1},{1,0},{2,3},{3,2},{4,5},{5,4},{6,7},{7,6},{8,9},{9,8},{10,11... | collective-permute-start | bytes 319496 | tf_op jit(solution)/shard_map/ppermute | solution.py:716
  10.0 0.0 collective-permute-start.7
  10.0 0.0 collective-permute-done.2.refs_0_.cross
  10.0 1.3 %pack_chip.3 = (f32[208,128]{1,0:T(8,128)S(1)}, f32[208,128]{1,0:T(8,128)S(1)}, f32[208,128]{1,0:T(8,128)S(1)}, f32[208,128]{1,0:T(8,128)S(1)}) custom-call(f32[48,2048]{1,0:T(8,128)S(1)} %get-tuple-element.30.cot, f32[544,128]{1,0:T(8,128)S(1)} %get-tuple-element.31.where, f32[48,2048]{1,0:T(8,128)S(1)} %collective-permute-done.pair_cot, ...), custom_call_target="tpu_custom_call" | custom-call | tf_op jit(solution)/shard_map/pack_chip/pallas_call | solution.py:434
  11.3 1.6 %collective-permute-start.3 = (f32[208,128]{1,0:T(8,128)S(1)}, f32[208,128]{1,0:T(8,128)S(1)}, u32[]{:S(2)}, u32[]{:S(2)}) collective-permute-start(f32[208,128]{1,0:T(8,128)S(1)} %get-tuple-element.34), channel_id=1, source_target_pairs={{0,1},{1,0},{2,3},{3,2},{4,5},{5,4},{6,7},{7,6},{8,9},{9,8},{10,11... | collective-permute-start | bytes 319496 | tf_op jit(solution)/shard_map/ppermute | solution.py:716
  12.9 2.9 %collective-permute-start.5 = (f32[208,128]{1,0:T(8,128)S(1)}, f32[208,128]{1,0:T(8,128)S(1)}, u32[]{:S(2)}, u32[]{:S(2)}) collective-permute-start(f32[208,128]{1,0:T(8,128)S(1)} %get-tuple-element.37), channel_id=1, source_target_pairs={{0,8},{1,9},{2,10},{3,11},{4,12},{5,13},{6,14},{7,15},{8,0},{9,1},... | collective-permute-start | bytes 319496 | tf_op jit(solution)/shard_map/ppermute | solution.py:716
  15.8 0.0 collective-permute-done.8.refs_1_
  15.8 0.7 %scatter_points.6.refs_2_ = f32[8,48,128]{2,1,0:T(8,128)S(1)} custom-call(f32[208,128]{1,0:T(8,128)S(1)} %get-tuple-element.33.refs_1_.refs_0_, f32[208,128]{1,0:T(8,128)S(1)} %collective-permute-done.8.refs_1_, f32[208,128]{1,0:T(8,128)S(1)} %get-tuple-element.36.refs_0_.refs_2_), custom_call_target="tpu_custom_call" | custom-call | tf_op jit(solution)/shard_map/scatter_points/pallas_call | solution.py:501
  16.5 0.0 collective-permute-done.6.refs_0_
  16.5 0.3 collective-permute-done.7.refs_1_
  16.8 0.7 %scatter_points.7 = (f32[5,48,128]{2,1,0:T(8,128)S(1)}, f32[3,48,128]{2,1,0:T(8,128)S(1)}) custom-call(f32[208,128]{1,0:T(8,128)S(1)} %collective-permute-done.6.refs_0_, f32[208,128]{1,0:T(8,128)S(1)} %collective-permute-done.7.refs_1_, f32[8,48,128]{2,1,0:T(8,128)S(1)} %scatter_points.6.refs_2_), custom_call_target="tpu_custom_call" | custom-call | tf_op jit(solution)/shard_map/scatter_points/pallas_call | solution.py:501
  17.5 2.7 %collective-permute-start.9 = (f32[5,48,128]{2,1,0:T(8,128)S(1)}, f32[5,48,128]{2,1,0:T(8,128)S(1)}, u32[]{:S(2)}, u32[]{:S(2)}) collective-permute-start(f32[5,48,128]{2,1,0:T(8,128)S(1)} %get-tuple-element.41.refs_0_), channel_id=1, source_target_pairs={{0,2},{1,3},{2,0},{3,1},{4,6},{5,7},{6,4},{7,5},{8,10},{9,11},{10,... | collective-permute-start | bytes 368648 | tf_op jit(solution)/shard_map/ppermute | solution.py:716
  20.2 1.7 %collective-permute-start.4 = (f32[208,128]{1,0:T(8,128)S(1)}, f32[208,128]{1,0:T(8,128)S(1)}, u32[]{:S(2)}, u32[]{:S(2)}) collective-permute-start(f32[208,128]{1,0:T(8,128)S(1)} %get-tuple-element.35), channel_id=1, source_target_pairs={{0,9},{1,8},{2,11},{3,10},{4,13},{5,12},{6,15},{7,14},{8,1},{9,0},... | collective-permute-start | bytes 319496 | tf_op jit(solution)/shard_map/ppermute | solution.py:716
  21.9 0.3 collective-permute-start.10
  22.2 0.6 %state_edges.1 = (f32[48,128]{1,0:T(8,128)S(1)}, f32[48,128]{1,0:T(8,128)S(1)}) custom-call(f32[4,8,48,128]{3,2,1,0:T(8,128)S(1)} %get-tuple-element.43.turned, f32[544,128]{1,0:T(8,128)S(1)} %collective-permute-done.1.pair_where.pair, f32[480,128]{1,0:T(8,128)S(1)} %collective-permute-done.2.refs_0_.cross, f32[5,48,128]{2,1,0:T(8,128)S(1)} %get-tuple-element.41.refs_0_, ...), custom_call_target="tpu_custom_call" | custom-call | tf_op jit(solution)/shard_map/state_edges/pallas_call | solution.py:173
  22.9 0.0 collective-permute-done.3.refs_0_
  22.9 0.1 collective-permute-start.11
  23.0 0.0 collective-permute-done.5.refs_1_
  23.0 4.0 %collective-permute-start.12 = (f32[48,128]{1,0:T(8,128)S(1)}, f32[48,128]{1,0:T(8,128)S(1)}, u32[]{:S(2)}, u32[]{:S(2)}) collective-permute-start(f32[48,128]{1,0:T(8,128)S(1)} %get-tuple-element.45), channel_id=1, source_target_pairs={{0,3},{1,2},{2,1},{3,0},{4,7},{5,6},{6,5},{7,4},{8,11},{9,10},{10,... | collective-permute-start | bytes 73736 | tf_op jit(solution)/shard_map/ppermute | solution.py:716
  27.0 0.7 %scatter_points.4.refs_2_ = f32[8,48,128]{2,1,0:T(8,128)S(1)} custom-call(f32[208,128]{1,0:T(8,128)S(1)} %get-tuple-element.36.refs_0_.refs_2_, f32[208,128]{1,0:T(8,128)S(1)} %collective-permute-done.5.refs_1_), custom_call_target="tpu_custom_call" | custom-call | tf_op jit(solution)/shard_map/scatter_points/pallas_call | solution.py:501
  27.8 0.0 collective-permute-done.4.refs_1_
  27.8 0.7 %scatter_points.5.refs_0_.total = f32[8,48,128]{2,1,0:T(8,128)S(1)} custom-call(f32[208,128]{1,0:T(8,128)S(1)} %collective-permute-done.3.refs_0_, f32[208,128]{1,0:T(8,128)S(1)} %collective-permute-done.4.refs_1_, f32[8,48,128]{2,1,0:T(8,128)S(1)} %scatter_points.4.refs_2_), custom_call_target="tpu_custom_call" | custom-call | tf_op jit(solution)/shard_map/scatter_points/pallas_call | solution.py:501
  28.5 1.5 %tile_fields.1 = (f32[4,16,112,128]{3,2,1,0:T(8,128)S(1)}, f32[16,128]{1,0:T(8,128)S(1)}, f32[8,128]{1,0:T(8,128)S(1)}, f32[4,16,24,128]{3,2,1,0:T(8,128)S(1)}) custom-call(f32[4,8,48,128]{3,2,1,0:T(8,128)S(1)} %get-tuple-element.43.turned, f32[544,128]{1,0:T(8,128)S(1)} %collective-permute-done.1.pair_where.pair, ...), custom_call_target="tpu_custom_call" | custom-call | tf_op jit(solution)/shard_map/tile_fields/pallas_call | solution.py:266
  30.0 0.0 collective-permute-done.11.refs_2_.one
  30.0 0.0 collective-permute-done.12.refs_3_.other
  30.0 0.0 collective-permute-done.10.refs_1_
  30.0 0.0 collective-permute-done.9.refs_0_
  30.1 0.7 %collective-permute-start.14 = (f32[4,48,128]{2,1,0:T(8,128)S(1)}, f32[4,48,128]{2,1,0:T(8,128)S(1)}, u32[]{:S(2)}, u32[]{:S(2)}) collective-permute-start(f32[4,48,128]{2,1,0:T(8,128)S(1)} %get-tuple-element.49), channel_id=1, source_target_pairs={{4,8},{8,4},{5,9},{9,5},{6,10},{10,6},{7,11},{11,7},{20,24},{24,20... | collective-permute-start | bytes 294920 | tf_op jit(solution)/shard_map/ppermute | solution.py:721
  30.8 2.0 %collective-permute-start.13 = (f32[4,48,128]{2,1,0:T(8,128)S(1)}, f32[4,48,128]{2,1,0:T(8,128)S(1)}, u32[]{:S(2)}, u32[]{:S(2)}) collective-permute-start(f32[4,48,128]{2,1,0:T(8,128)S(1)} %get-tuple-element.48), channel_id=1, source_target_pairs={{0,4},{1,5},{2,6},{3,7},{4,0},{5,1},{6,2},{7,3},{8,12},{9,13},{10,... | collective-permute-start | bytes 294920 | tf_op jit(solution)/shard_map/ppermute | solution.py:716
  32.7 0.9 %edge_fields.1.refs_0_.wide = f32[4,16,56,128]{3,2,1,0:T(8,128)S(1)} custom-call(f32[4,16,24,128]{3,2,1,0:T(8,128)S(1)} %get-tuple-element.52.own, f32[48,128]{1,0:T(8,128)S(1)} %collective-permute-done.11.refs_2_.one, f32[48,128]{1,0:T(8,128)S(1)} %collective-permute-done.12.refs_3_.other), custom_call_target="tpu_custom_call" | custom-call | tf_op jit(solution)/shard_map/edge_fields/pallas_call | solution.py:311
  33.6 0.0 collective-permute-done.14.cross
  33.6 0.2 cross_edges.1.partial
  33.8 0.0 collective-permute-done.13.pair
  33.8 0.1 pair_edges.1
  33.9 2.8 %collective-permute-start.16 = (f32[48,128]{1,0:T(8,128)S(1)}, f32[48,128]{1,0:T(8,128)S(1)}, u32[]{:S(2)}, u32[]{:S(2)}) collective-permute-start(f32[48,128]{1,0:T(8,128)S(1)} %pair_edges.1), channel_id=1, source_target_pairs={{0,3},{1,2},{2,1},{3,0},{4,7},{5,6},{6,5},{7,4},{8,11},{9,10},{10,... | collective-permute-start | bytes 73736 | tf_op jit(solution)/shard_map/ppermute | solution.py:716
  36.8 0.0 collective-permute-start.15
  36.8 1.1 %tile_steps.1 = (f32[8,48,128]{2,1,0:T(8,128)S(1)}, f32[16,24,128]{2,1,0:T(8,128)S(1)}) custom-call(f32[8,48,128]{2,1,0:T(8,128)S(1)} %get-tuple-element.47.canvas, f32[4,48,128]{2,1,0:T(8,128)S(1)} %collective-permute-done.13.pair, f32[4,48,128]{2,1,0:T(8,128)S(1)} %collective-permute-done.14.cross, f32[4,16,112,128]{3,2,1,0:T(8,128)S(1)} %get-tuple-element.50.wide, ...), custom_call_target="tpu_custom_call" | custom-call | tf_op jit(solution)/shard_map/tile_steps/pallas_call | solution.py:659
  37.8 1.8 %collective-permute-done.16.other = f32[48,128]{1,0:T(8,128)S(1)} collective-permute-done((f32[48,128]{1,0:T(8,128)S(1)}, f32[48,128]{1,0:T(8,128)S(1)}, u32[]{:S(2)}, u32[]{:S(2)}) %collective-permute-start.16) | collective-permute-done | bytes 24608 | tf_op jit(solution)/shard_map/ppermute | solution.py:716
  39.6 0.9 %collective-permute-done.15.one = f32[48,128]{1,0:T(8,128)S(1)} collective-permute-done((f32[48,128]{1,0:T(8,128)S(1)}, f32[48,128]{1,0:T(8,128)S(1)}, u32[]{:S(2)}, u32[]{:S(2)}) %collective-permute-start.15) | collective-permute-done | bytes 24608 | tf_op jit(solution)/shard_map/ppermute | solution.py:716
  40.6 1.4 %edge_steps.1 = f32[384,128]{1,0:T(8,128)} custom-call(f32[16,24,128]{2,1,0:T(8,128)S(1)} %get-tuple-element.51.windows, f32[48,128]{1,0:T(8,128)S(1)} %collective-permute-done.15.one, f32[48,128]{1,0:T(8,128)S(1)} %collective-permute-done.16.other, f32[4,16,56,128]{3,2,1,0:T(8,128)S(1)} %edge_fields.1.refs_0_.wide, f32[8,128]{1,0:T(8,128)S(1)} %get-tuple-element.53.gravity, ...), custom_call_target="tpu_custom_call" | custom-call | tf_op jit(solution)/shard_map/edge_steps/pallas_call | solution.py:698
  (3 shorter events, 0.0 us)
Async XLA Ops:
  0.0 3.5 %collective-permute-start = (f32[48,2048]{1,0:T(8,128)}, f32[48,2048]{1,0:T(8,128)S(1)}, u32[]{:S(2)}, u32[]{:S(2)}) collective-permute-start(f32[48,2048]{1,0:T(8,128)} %bitcast.6), channel_id=1, source_target_pairs={{0,4},{1,5},{2,6},{3,7},{4,0},{5,1},{6,2},{7,3},{8,12},{9,13},{10,... | collective-permute-start | bytes 1179656 | tf_op jit(solution)/shard_map/ppermute | solution.py:716
  0.5 28.1 %copy-start = (f32[16]{0:T(128)S(1)}, f32[16]{0:T(128)}, u32[]{:S(2)}) copy-start(f32[16]{0:T(128)} %gravity.1) | copy-start | bytes 196
  1.9 1.6 %collective-permute-start.1 = (f32[544,128]{1,0:T(8,128)S(1)}, f32[544,128]{1,0:T(8,128)S(1)}, u32[]{:S(2)}, u32[]{:S(2)}) collective-permute-start(f32[544,128]{1,0:T(8,128)S(1)} %get-tuple-element.31.where), channel_id=1, source_target_pairs={{0,4},{1,5},{2,6},{3,7},{4,0},{5,1},{6,2},{7,3},{8,12},{9,13},{10,... | collective-permute-start | bytes 835592 | tf_op jit(solution)/shard_map/ppermute | solution.py:716
  2.0 8.0 %collective-permute-start.2 = (f32[480,128]{1,0:T(8,128)S(1)}, f32[480,128]{1,0:T(8,128)S(1)}, u32[]{:S(2)}, u32[]{:S(2)}) collective-permute-start(f32[480,128]{1,0:T(8,128)S(1)} %get-tuple-element.32), channel_id=1, source_target_pairs={{4,8},{8,4},{5,9},{9,5},{6,10},{10,6},{7,11},{11,7},{20,24},{24,20... | collective-permute-start | bytes 737288 | tf_op jit(solution)/shard_map/ppermute | solution.py:721
  4.8 11.0 %collective-permute-start.8 = (f32[208,128]{1,0:T(8,128)S(1)}, f32[208,128]{1,0:T(8,128)S(1)}, u32[]{:S(2)}, u32[]{:S(2)}) collective-permute-start(f32[208,128]{1,0:T(8,128)S(1)} %get-tuple-element.40), channel_id=1, source_target_pairs={{0,8},{1,9},{2,10},{3,11},{4,12},{5,13},{6,14},{7,15},{8,0},{9,1},... | collective-permute-start | bytes 319496 | tf_op jit(solution)/shard_map/ppermute | solution.py:716
  8.3 8.3 %collective-permute-start.6 = (f32[208,128]{1,0:T(8,128)S(1)}, f32[208,128]{1,0:T(8,128)S(1)}, u32[]{:S(2)}, u32[]{:S(2)}) collective-permute-start(f32[208,128]{1,0:T(8,128)S(1)} %get-tuple-element.38), channel_id=1, source_target_pairs={{0,1},{1,0},{2,3},{3,2},{4,5},{5,4},{6,7},{7,6},{8,9},{9,8},{10,11... | collective-permute-start | bytes 319496 | tf_op jit(solution)/shard_map/ppermute | solution.py:716
  10.0 6.8 %collective-permute-start.7 = (f32[208,128]{1,0:T(8,128)S(1)}, f32[208,128]{1,0:T(8,128)S(1)}, u32[]{:S(2)}, u32[]{:S(2)}) collective-permute-start(f32[208,128]{1,0:T(8,128)S(1)} %get-tuple-element.39), channel_id=1, source_target_pairs={{0,9},{1,8},{2,11},{3,10},{4,13},{5,12},{6,15},{7,14},{8,1},{9,0},... | collective-permute-start | bytes 319496 | tf_op jit(solution)/shard_map/ppermute | solution.py:716
  11.3 11.6 %collective-permute-start.3 = (f32[208,128]{1,0:T(8,128)S(1)}, f32[208,128]{1,0:T(8,128)S(1)}, u32[]{:S(2)}, u32[]{:S(2)}) collective-permute-start(f32[208,128]{1,0:T(8,128)S(1)} %get-tuple-element.34), channel_id=1, source_target_pairs={{0,1},{1,0},{2,3},{3,2},{4,5},{5,4},{6,7},{7,6},{8,9},{9,8},{10,11... | collective-permute-start | bytes 319496 | tf_op jit(solution)/shard_map/ppermute | solution.py:716
  12.9 10.1 %collective-permute-start.5 = (f32[208,128]{1,0:T(8,128)S(1)}, f32[208,128]{1,0:T(8,128)S(1)}, u32[]{:S(2)}, u32[]{:S(2)}) collective-permute-start(f32[208,128]{1,0:T(8,128)S(1)} %get-tuple-element.37), channel_id=1, source_target_pairs={{0,8},{1,9},{2,10},{3,11},{4,12},{5,13},{6,14},{7,15},{8,0},{9,1},... | collective-permute-start | bytes 319496 | tf_op jit(solution)/shard_map/ppermute | solution.py:716
  17.5 12.5 %collective-permute-start.9 = (f32[5,48,128]{2,1,0:T(8,128)S(1)}, f32[5,48,128]{2,1,0:T(8,128)S(1)}, u32[]{:S(2)}, u32[]{:S(2)}) collective-permute-start(f32[5,48,128]{2,1,0:T(8,128)S(1)} %get-tuple-element.41.refs_0_), channel_id=1, source_target_pairs={{0,2},{1,3},{2,0},{3,1},{4,6},{5,7},{6,4},{7,5},{8,10},{9,11},{10,... | collective-permute-start | bytes 368648 | tf_op jit(solution)/shard_map/ppermute | solution.py:716
  20.2 7.6 %collective-permute-start.4 = (f32[208,128]{1,0:T(8,128)S(1)}, f32[208,128]{1,0:T(8,128)S(1)}, u32[]{:S(2)}, u32[]{:S(2)}) collective-permute-start(f32[208,128]{1,0:T(8,128)S(1)} %get-tuple-element.35), channel_id=1, source_target_pairs={{0,9},{1,8},{2,11},{3,10},{4,13},{5,12},{6,15},{7,14},{8,1},{9,0},... | collective-permute-start | bytes 319496 | tf_op jit(solution)/shard_map/ppermute | solution.py:716
  21.9 8.1 %collective-permute-start.10 = (f32[3,48,128]{2,1,0:T(8,128)S(1)}, f32[3,48,128]{2,1,0:T(8,128)S(1)}, u32[]{:S(2)}, u32[]{:S(2)}) collective-permute-start(f32[3,48,128]{2,1,0:T(8,128)S(1)} %get-tuple-element.42.refs_1_), channel_id=1, source_target_pairs={{0,2},{1,3},{2,0},{3,1},{4,6},{5,7},{6,4},{7,5},{8,10},{9,11},{10,... | collective-permute-start | bytes 221192 | tf_op jit(solution)/shard_map/ppermute | solution.py:716
  22.9 7.1 %collective-permute-start.11 = (f32[48,128]{1,0:T(8,128)S(1)}, f32[48,128]{1,0:T(8,128)S(1)}, u32[]{:S(2)}, u32[]{:S(2)}) collective-permute-start(f32[48,128]{1,0:T(8,128)S(1)} %get-tuple-element.44), channel_id=1, source_target_pairs={{0,1},{1,0},{2,3},{3,2},{4,5},{5,4},{6,7},{7,6},{8,9},{9,8},{10,11... | collective-permute-start | bytes 73736 | tf_op jit(solution)/shard_map/ppermute | solution.py:716
  23.0 7.0 %collective-permute-start.12 = (f32[48,128]{1,0:T(8,128)S(1)}, f32[48,128]{1,0:T(8,128)S(1)}, u32[]{:S(2)}, u32[]{:S(2)}) collective-permute-start(f32[48,128]{1,0:T(8,128)S(1)} %get-tuple-element.45), channel_id=1, source_target_pairs={{0,3},{1,2},{2,1},{3,0},{4,7},{5,6},{6,5},{7,4},{8,11},{9,10},{10,... | collective-permute-start | bytes 73736 | tf_op jit(solution)/shard_map/ppermute | solution.py:716
  30.1 3.5 %collective-permute-start.14 = (f32[4,48,128]{2,1,0:T(8,128)S(1)}, f32[4,48,128]{2,1,0:T(8,128)S(1)}, u32[]{:S(2)}, u32[]{:S(2)}) collective-permute-start(f32[4,48,128]{2,1,0:T(8,128)S(1)} %get-tuple-element.49), channel_id=1, source_target_pairs={{4,8},{8,4},{5,9},{9,5},{6,10},{10,6},{7,11},{11,7},{20,24},{24,20... | collective-permute-start | bytes 294920 | tf_op jit(solution)/shard_map/ppermute | solution.py:721
  30.8 3.0 %collective-permute-start.13 = (f32[4,48,128]{2,1,0:T(8,128)S(1)}, f32[4,48,128]{2,1,0:T(8,128)S(1)}, u32[]{:S(2)}, u32[]{:S(2)}) collective-permute-start(f32[4,48,128]{2,1,0:T(8,128)S(1)} %get-tuple-element.48), channel_id=1, source_target_pairs={{0,4},{1,5},{2,6},{3,7},{4,0},{5,1},{6,2},{7,3},{8,12},{9,13},{10,... | collective-permute-start | bytes 294920 | tf_op jit(solution)/shard_map/ppermute | solution.py:716
  33.9 5.7 %collective-permute-start.16 = (f32[48,128]{1,0:T(8,128)S(1)}, f32[48,128]{1,0:T(8,128)S(1)}, u32[]{:S(2)}, u32[]{:S(2)}) collective-permute-start(f32[48,128]{1,0:T(8,128)S(1)} %pair_edges.1), channel_id=1, source_target_pairs={{0,3},{1,2},{2,1},{3,0},{4,7},{5,6},{6,5},{7,4},{8,11},{9,10},{10,... | collective-permute-start | bytes 73736 | tf_op jit(solution)/shard_map/ppermute | solution.py:716
  36.8 3.8 %collective-permute-start.15 = (f32[48,128]{1,0:T(8,128)S(1)}, f32[48,128]{1,0:T(8,128)S(1)}, u32[]{:S(2)}, u32[]{:S(2)}) collective-permute-start(f32[48,128]{1,0:T(8,128)S(1)} %pair_edges.1), channel_id=1, source_target_pairs={{0,1},{1,0},{2,3},{3,2},{4,5},{5,4},{6,7},{7,6},{8,9},{9,8},{10,11... | collective-permute-start | bytes 73736 | tf_op jit(solution)/shard_map/ppermute | solution.py:716

commit v8 on v7

--- a/solution.py
+++ b/solution.py
@@ -163,10 +163,10 @@
 def state_edges_kernel(n_row, pair_at, paired, turned, pair, cross, *refs):
     one, other = refs[-2:]
     first, last = state_edges(n_row, turned, pair, pair_at, cross)
+    one[...], other[...] = last, first
     if paired:
         lower = first_of_pair("fcol")
-        first, last = jnp.where(lower, last, first), jnp.where(lower, first, last)
-    one[...], other[...] = first, last
+        one[...], other[...] = jnp.where(lower, last, first), jnp.where(lower, first, last)
 
 
 def all_state_edges(n_row, pair_at, paired, turned, pair, cross, after=()):

time: 42.1 us -> 42.1 us (level)
  no operation moved by 1% of the time
where the time goes in v8:
time: 42.1 us; the launch traced here: 42 us
  starting transfers between devices  25.2 us (60%)
  Pallas kernels  12.7 us (30%)
  waiting for transfers between devices  3.89 us (9%)
    ppermute x15, starting transfers between devices, exchanged(): return lax.ppermute(values, ('frow', 'fcol'), pairs)  23.8 us
    ppermute x15, waiting for transfers between devices, exchanged(): return lax.ppermute(values, ('frow', 'fcol'), pairs)  3.88 us
    pallas_call x4, Pallas kernels, scatter(): pl.pallas_call(functools.partial(scatter_kernel, len(blocks), total is No...  2.89 us
    pallas_call x2, Pallas kernels, pack_chip(): pl.pallas_call(functools.partial(pack_chip_kernel, tiles, tile_rows, colu...  2.65 us
    pallas_call x1, Pallas kernels, tile_fields(): pl.pallas_call(functools.partial(tile_fields_kernel, n_row, pair_at), in_...  1.49 us
    pallas_call x1, Pallas kernels, prepare(): pl.pallas_call(functools.partial(prepare_kernel, order), in_specs=[in_hbm...  1.39 us
    pallas_call x1, Pallas kernels, edge_steps(): pl.pallas_call(functools.partial(edge_steps_kernel, n_row, paired), out_s...  1.39 us
    ppermute x2, starting transfers between devices, exchanged_across(): lax.ppermute(values, 'frow', [(f, (f + 1 ^ 1) - 1) for f in range(1, n_ro...  1.33 us
  transfers between devices with their start and end apart: 17, of which 4 were waited for; matrix products, arithmetic and copies ran while one was open for 0% of the time, Pallas kernels for 27%

profile of v8, /device:TPU:0, one launch (start us, length us, event | category | flops | bytes accessed | tf_op | source)
XLA Modules:
  0.0 42.0 jit_solution(7500182922243530012)
XLA Ops:
  0.0 0.5 %collective-permute-start = (f32[48,2048]{1,0:T(8,128)}, f32[48,2048]{1,0:T(8,128)S(1)}, u32[]{:S(2)}, u32[]{:S(2)}) collective-permute-start(f32[48,2048]{1,0:T(8,128)} %bitcast.6), channel_id=1, source_target_pairs={{0,4},{1,5},{2,6},{3,7},{4,0},{5,1},{6,2},{7,3},{8,12},{9,13},{10,... | collective-permute-start | bytes 1179656 | tf_op jit(solution)/shard_map/ppermute | solution.py:716
  0.5 1.4 %prepare.1 = (f32[544,128]{1,0:T(8,128)S(1)}, f32[480,128]{1,0:T(8,128)S(1)}, f32[4,8,48,128]{3,2,1,0:T(8,128)S(1)}, f32[48,2048]{1,0:T(8,128)S(1)}) custom-call(s32[16,128]{1,0:T(8,128)} %bitcast.8, s32[16,128]{1,0:T(8,128)} %bitcast.9, f32[2,2048]{1,0:T(2,128)} %frac.1, f32[4,384,128]{2,1,0:T(8,128)} %bitcast.5, f32[48,2048]{1,0:T(8,128)} %bitcast.7), custom_call_target="tpu_custom_call" | custom-call | tf_op jit(solution)/shard_map/prepare/pallas_call | solution.py:105
  1.9 0.1 collective-permute-start.1
  2.0 0.7 %collective-permute-start.2 = (f32[480,128]{1,0:T(8,128)S(1)}, f32[480,128]{1,0:T(8,128)S(1)}, u32[]{:S(2)}, u32[]{:S(2)}) collective-permute-start(f32[480,128]{1,0:T(8,128)S(1)} %get-tuple-element.32), channel_id=1, source_target_pairs={{4,8},{8,4},{5,9},{9,5},{6,10},{10,6},{7,11},{11,7},{20,24},{24,20... | collective-permute-start | bytes 737288 | tf_op jit(solution)/shard_map/ppermute | solution.py:721
  2.7 0.8 %collective-permute-done.1.pair_where.pair = f32[544,128]{1,0:T(8,128)S(1)} collective-permute-done((f32[544,128]{1,0:T(8,128)S(1)}, f32[544,128]{1,0:T(8,128)S(1)}, u32[]{:S(2)}, u32[]{:S(2)}) %collective-permute-start.1) | collective-permute-done | bytes 278560 | tf_op jit(solution)/shard_map/ppermute | solution.py:716
  3.5 0.0 collective-permute-done.pair_cot
  3.5 1.3 %pack_chip.2 = (f32[208,128]{1,0:T(8,128)S(1)}, f32[208,128]{1,0:T(8,128)S(1)}, f32[208,128]{1,0:T(8,128)S(1)}, f32[208,128]{1,0:T(8,128)S(1)}) custom-call(f32[48,2048]{1,0:T(8,128)S(1)} %get-tuple-element.30.cot, f32[544,128]{1,0:T(8,128)S(1)} %get-tuple-element.31.where, f32[48,2048]{1,0:T(8,128)S(1)} %collective-permute-done.pair_cot, ...), custom_call_target="tpu_custom_call" | custom-call | tf_op jit(solution)/shard_map/pack_chip/pallas_call | solution.py:434
  4.8 3.4 %collective-permute-start.8 = (f32[208,128]{1,0:T(8,128)S(1)}, f32[208,128]{1,0:T(8,128)S(1)}, u32[]{:S(2)}, u32[]{:S(2)}) collective-permute-start(f32[208,128]{1,0:T(8,128)S(1)} %get-tuple-element.40), channel_id=1, source_target_pairs={{0,8},{1,9},{2,10},{3,11},{4,12},{5,13},{6,14},{7,15},{8,0},{9,1},... | collective-permute-start | bytes 319496 | tf_op jit(solution)/shard_map/ppermute | solution.py:716
  8.3 1.7 %collective-permute-start.6 = (f32[208,128]{1,0:T(8,128)S(1)}, f32[208,128]{1,0:T(8,128)S(1)}, u32[]{:S(2)}, u32[]{:S(2)}) collective-permute-start(f32[208,128]{1,0:T(8,128)S(1)} %get-tuple-element.38), channel_id=1, source_target_pairs={{0,1},{1,0},{2,3},{3,2},{4,5},{5,4},{6,7},{7,6},{8,9},{9,8},{10,11... | collective-permute-start | bytes 319496 | tf_op jit(solution)/shard_map/ppermute | solution.py:716
  10.0 0.0 collective-permute-start.7
  10.0 0.0 collective-permute-done.2.refs_0_.cross
  10.0 1.3 %pack_chip.3 = (f32[208,128]{1,0:T(8,128)S(1)}, f32[208,128]{1,0:T(8,128)S(1)}, f32[208,128]{1,0:T(8,128)S(1)}, f32[208,128]{1,0:T(8,128)S(1)}) custom-call(f32[48,2048]{1,0:T(8,128)S(1)} %get-tuple-element.30.cot, f32[544,128]{1,0:T(8,128)S(1)} %get-tuple-element.31.where, f32[48,2048]{1,0:T(8,128)S(1)} %collective-permute-done.pair_cot, ...), custom_call_target="tpu_custom_call" | custom-call | tf_op jit(solution)/shard_map/pack_chip/pallas_call | solution.py:434
  11.3 1.6 %collective-permute-start.3 = (f32[208,128]{1,0:T(8,128)S(1)}, f32[208,128]{1,0:T(8,128)S(1)}, u32[]{:S(2)}, u32[]{:S(2)}) collective-permute-start(f32[208,128]{1,0:T(8,128)S(1)} %get-tuple-element.34), channel_id=1, source_target_pairs={{0,1},{1,0},{2,3},{3,2},{4,5},{5,4},{6,7},{7,6},{8,9},{9,8},{10,11... | collective-permute-start | bytes 319496 | tf_op jit(solution)/shard_map/ppermute | solution.py:716
  12.9 2.9 %collective-permute-start.5 = (f32[208,128]{1,0:T(8,128)S(1)}, f32[208,128]{1,0:T(8,128)S(1)}, u32[]{:S(2)}, u32[]{:S(2)}) collective-permute-start(f32[208,128]{1,0:T(8,128)S(1)} %get-tuple-element.37), channel_id=1, source_target_pairs={{0,8},{1,9},{2,10},{3,11},{4,12},{5,13},{6,14},{7,15},{8,0},{9,1},... | collective-permute-start | bytes 319496 | tf_op jit(solution)/shard_map/ppermute | solution.py:716
  15.8 0.0 collective-permute-done.8.refs_1_
  15.8 0.7 %scatter_points.6.refs_2_ = f32[8,48,128]{2,1,0:T(8,128)S(1)} custom-call(f32[208,128]{1,0:T(8,128)S(1)} %get-tuple-element.33.refs_1_.refs_0_, f32[208,128]{1,0:T(8,128)S(1)} %collective-permute-done.8.refs_1_, f32[208,128]{1,0:T(8,128)S(1)} %get-tuple-element.36.refs_0_.refs_2_), custom_call_target="tpu_custom_call" | custom-call | tf_op jit(solution)/shard_map/scatter_points/pallas_call | solution.py:501
  16.5 0.0 collective-permute-done.6.refs_0_
  16.5 0.3 collective-permute-done.7.refs_1_
  16.8 0.7 %scatter_points.7 = (f32[5,48,128]{2,1,0:T(8,128)S(1)}, f32[3,48,128]{2,1,0:T(8,128)S(1)}) custom-call(f32[208,128]{1,0:T(8,128)S(1)} %collective-permute-done.6.refs_0_, f32[208,128]{1,0:T(8,128)S(1)} %collective-permute-done.7.refs_1_, f32[8,48,128]{2,1,0:T(8,128)S(1)} %scatter_points.6.refs_2_), custom_call_target="tpu_custom_call" | custom-call | tf_op jit(solution)/shard_map/scatter_points/pallas_call | solution.py:501
  17.5 2.7 %collective-permute-start.9 = (f32[5,48,128]{2,1,0:T(8,128)S(1)}, f32[5,48,128]{2,1,0:T(8,128)S(1)}, u32[]{:S(2)}, u32[]{:S(2)}) collective-permute-start(f32[5,48,128]{2,1,0:T(8,128)S(1)} %get-tuple-element.41.refs_0_), channel_id=1, source_target_pairs={{0,2},{1,3},{2,0},{3,1},{4,6},{5,7},{6,4},{7,5},{8,10},{9,11},{10,... | collective-permute-start | bytes 368648 | tf_op jit(solution)/shard_map/ppermute | solution.py:716
  20.2 1.7 %collective-permute-start.4 = (f32[208,128]{1,0:T(8,128)S(1)}, f32[208,128]{1,0:T(8,128)S(1)}, u32[]{:S(2)}, u32[]{:S(2)}) collective-permute-start(f32[208,128]{1,0:T(8,128)S(1)} %get-tuple-element.35), channel_id=1, source_target_pairs={{0,9},{1,8},{2,11},{3,10},{4,13},{5,12},{6,15},{7,14},{8,1},{9,0},... | collective-permute-start | bytes 319496 | tf_op jit(solution)/shard_map/ppermute | solution.py:716
  21.9 0.3 collective-permute-start.10
  22.2 0.6 %state_edges.1 = (f32[48,128]{1,0:T(8,128)S(1)}, f32[48,128]{1,0:T(8,128)S(1)}) custom-call(f32[4,8,48,128]{3,2,1,0:T(8,128)S(1)} %get-tuple-element.43.turned, f32[544,128]{1,0:T(8,128)S(1)} %collective-permute-done.1.pair_where.pair, f32[480,128]{1,0:T(8,128)S(1)} %collective-permute-done.2.refs_0_.cross, f32[5,48,128]{2,1,0:T(8,128)S(1)} %get-tuple-element.41.refs_0_, ...), custom_call_target="tpu_custom_call" | custom-call | tf_op jit(solution)/shard_map/state_edges/pallas_call | solution.py:173
  22.9 0.0 collective-permute-done.3.refs_0_
  22.9 0.1 collective-permute-start.11
  23.0 0.0 collective-permute-done.5.refs_1_
  23.0 4.0 %collective-permute-start.12 = (f32[48,128]{1,0:T(8,128)S(1)}, f32[48,128]{1,0:T(8,128)S(1)}, u32[]{:S(2)}, u32[]{:S(2)}) collective-permute-start(f32[48,128]{1,0:T(8,128)S(1)} %get-tuple-element.45), channel_id=1, source_target_pairs={{0,3},{1,2},{2,1},{3,0},{4,7},{5,6},{6,5},{7,4},{8,11},{9,10},{10,... | collective-permute-start | bytes 73736 | tf_op jit(solution)/shard_map/ppermute | solution.py:716
  27.0 0.7 %scatter_points.4.refs_2_ = f32[8,48,128]{2,1,0:T(8,128)S(1)} custom-call(f32[208,128]{1,0:T(8,128)S(1)} %get-tuple-element.36.refs_0_.refs_2_, f32[208,128]{1,0:T(8,128)S(1)} %collective-permute-done.5.refs_1_), custom_call_target="tpu_custom_call" | custom-call | tf_op jit(solution)/shard_map/scatter_points/pallas_call | solution.py:501
  27.8 0.0 collective-permute-done.4.refs_1_
  27.8 0.7 %scatter_points.5.refs_0_.total = f32[8,48,128]{2,1,0:T(8,128)S(1)} custom-call(f32[208,128]{1,0:T(8,128)S(1)} %collective-permute-done.3.refs_0_, f32[208,128]{1,0:T(8,128)S(1)} %collective-permute-done.4.refs_1_, f32[8,48,128]{2,1,0:T(8,128)S(1)} %scatter_points.4.refs_2_), custom_call_target="tpu_custom_call" | custom-call | tf_op jit(solution)/shard_map/scatter_points/pallas_call | solution.py:501
  28.5 1.5 %tile_fields.1 = (f32[4,16,112,128]{3,2,1,0:T(8,128)S(1)}, f32[16,128]{1,0:T(8,128)S(1)}, f32[8,128]{1,0:T(8,128)S(1)}, f32[4,16,24,128]{3,2,1,0:T(8,128)S(1)}) custom-call(f32[4,8,48,128]{3,2,1,0:T(8,128)S(1)} %get-tuple-element.43.turned, f32[544,128]{1,0:T(8,128)S(1)} %collective-permute-done.1.pair_where.pair, ...), custom_call_target="tpu_custom_call" | custom-call | tf_op jit(solution)/shard_map/tile_fields/pallas_call | solution.py:266
  30.0 0.0 collective-permute-done.11.refs_2_.one
  30.0 0.0 collective-permute-done.12.refs_3_.other
  30.0 0.0 collective-permute-done.10.refs_1_
  30.0 0.0 collective-permute-done.9.refs_0_
  30.1 0.7 %collective-permute-start.14 = (f32[4,48,128]{2,1,0:T(8,128)S(1)}, f32[4,48,128]{2,1,0:T(8,128)S(1)}, u32[]{:S(2)}, u32[]{:S(2)}) collective-permute-start(f32[4,48,128]{2,1,0:T(8,128)S(1)} %get-tuple-element.49), channel_id=1, source_target_pairs={{4,8},{8,4},{5,9},{9,5},{6,10},{10,6},{7,11},{11,7},{20,24},{24,20... | collective-permute-start | bytes 294920 | tf_op jit(solution)/shard_map/ppermute | solution.py:721
  30.8 2.0 %collective-permute-start.13 = (f32[4,48,128]{2,1,0:T(8,128)S(1)}, f32[4,48,128]{2,1,0:T(8,128)S(1)}, u32[]{:S(2)}, u32[]{:S(2)}) collective-permute-start(f32[4,48,128]{2,1,0:T(8,128)S(1)} %get-tuple-element.48), channel_id=1, source_target_pairs={{0,4},{1,5},{2,6},{3,7},{4,0},{5,1},{6,2},{7,3},{8,12},{9,13},{10,... | collective-permute-start | bytes 294920 | tf_op jit(solution)/shard_map/ppermute | solution.py:716
  32.7 0.9 %edge_fields.1.refs_0_.wide = f32[4,16,56,128]{3,2,1,0:T(8,128)S(1)} custom-call(f32[4,16,24,128]{3,2,1,0:T(8,128)S(1)} %get-tuple-element.52.own, f32[48,128]{1,0:T(8,128)S(1)} %collective-permute-done.11.refs_2_.one, f32[48,128]{1,0:T(8,128)S(1)} %collective-permute-done.12.refs_3_.other), custom_call_target="tpu_custom_call" | custom-call | tf_op jit(solution)/shard_map/edge_fields/pallas_call | solution.py:311
  33.6 0.0 collective-permute-done.14.cross
  33.6 0.2 cross_edges.1.partial
  33.8 0.0 collective-permute-done.13.pair
  33.8 0.1 pair_edges.1
  33.9 2.8 %collective-permute-start.16 = (f32[48,128]{1,0:T(8,128)S(1)}, f32[48,128]{1,0:T(8,128)S(1)}, u32[]{:S(2)}, u32[]{:S(2)}) collective-permute-start(f32[48,128]{1,0:T(8,128)S(1)} %pair_edges.1), channel_id=1, source_target_pairs={{0,3},{1,2},{2,1},{3,0},{4,7},{5,6},{6,5},{7,4},{8,11},{9,10},{10,... | collective-permute-start | bytes 73736 | tf_op jit(solution)/shard_map/ppermute | solution.py:716
  36.8 0.0 collective-permute-start.15
  36.8 1.1 %tile_steps.1 = (f32[8,48,128]{2,1,0:T(8,128)S(1)}, f32[16,24,128]{2,1,0:T(8,128)S(1)}) custom-call(f32[8,48,128]{2,1,0:T(8,128)S(1)} %get-tuple-element.47.canvas, f32[4,48,128]{2,1,0:T(8,128)S(1)} %collective-permute-done.13.pair, f32[4,48,128]{2,1,0:T(8,128)S(1)} %collective-permute-done.14.cross, f32[4,16,112,128]{3,2,1,0:T(8,128)S(1)} %get-tuple-element.50.wide, ...), custom_call_target="tpu_custom_call" | custom-call | tf_op jit(solution)/shard_map/tile_steps/pallas_call | solution.py:659
  37.8 1.8 %collective-permute-done.16.other = f32[48,128]{1,0:T(8,128)S(1)} collective-permute-done((f32[48,128]{1,0:T(8,128)S(1)}, f32[48,128]{1,0:T(8,128)S(1)}, u32[]{:S(2)}, u32[]{:S(2)}) %collective-permute-start.16) | collective-permute-done | bytes 24608 | tf_op jit(solution)/shard_map/ppermute | solution.py:716
  39.6 0.9 %collective-permute-done.15.one = f32[48,128]{1,0:T(8,128)S(1)} collective-permute-done((f32[48,128]{1,0:T(8,128)S(1)}, f32[48,128]{1,0:T(8,128)S(1)}, u32[]{:S(2)}, u32[]{:S(2)}) %collective-permute-start.15) | collective-permute-done | bytes 24608 | tf_op jit(solution)/shard_map/ppermute | solution.py:716
  40.6 1.4 %edge_steps.1 = f32[384,128]{1,0:T(8,128)} custom-call(f32[16,24,128]{2,1,0:T(8,128)S(1)} %get-tuple-element.51.windows, f32[48,128]{1,0:T(8,128)S(1)} %collective-permute-done.15.one, f32[48,128]{1,0:T(8,128)S(1)} %collective-permute-done.16.other, f32[4,16,56,128]{3,2,1,0:T(8,128)S(1)} %edge_fields.1.refs_0_.wide, f32[8,128]{1,0:T(8,128)S(1)} %get-tuple-element.53.gravity, ...), custom_call_target="tpu_custom_call" | custom-call | tf_op jit(solution)/shard_map/edge_steps/pallas_call | solution.py:698
  (3 shorter events, 0.0 us)
Async XLA Ops:
  0.0 3.5 %collective-permute-start = (f32[48,2048]{1,0:T(8,128)}, f32[48,2048]{1,0:T(8,128)S(1)}, u32[]{:S(2)}, u32[]{:S(2)}) collective-permute-start(f32[48,2048]{1,0:T(8,128)} %bitcast.6), channel_id=1, source_target_pairs={{0,4},{1,5},{2,6},{3,7},{4,0},{5,1},{6,2},{7,3},{8,12},{9,13},{10,... | collective-permute-start | bytes 1179656 | tf_op jit(solution)/shard_map/ppermute | solution.py:716
  0.5 28.1 %copy-start = (f32[16]{0:T(128)S(1)}, f32[16]{0:T(128)}, u32[]{:S(2)}) copy-start(f32[16]{0:T(128)} %gravity.1) | copy-start | bytes 196
  1.9 1.6 %collective-permute-start.1 = (f32[544,128]{1,0:T(8,128)S(1)}, f32[544,128]{1,0:T(8,128)S(1)}, u32[]{:S(2)}, u32[]{:S(2)}) collective-permute-start(f32[544,128]{1,0:T(8,128)S(1)} %get-tuple-element.31.where), channel_id=1, source_target_pairs={{0,4},{1,5},{2,6},{3,7},{4,0},{5,1},{6,2},{7,3},{8,12},{9,13},{10,... | collective-permute-start | bytes 835592 | tf_op jit(solution)/shard_map/ppermute | solution.py:716
  2.0 8.0 %collective-permute-start.2 = (f32[480,128]{1,0:T(8,128)S(1)}, f32[480,128]{1,0:T(8,128)S(1)}, u32[]{:S(2)}, u32[]{:S(2)}) collective-permute-start(f32[480,128]{1,0:T(8,128)S(1)} %get-tuple-element.32), channel_id=1, source_target_pairs={{4,8},{8,4},{5,9},{9,5},{6,10},{10,6},{7,11},{11,7},{20,24},{24,20... | collective-permute-start | bytes 737288 | tf_op jit(solution)/shard_map/ppermute | solution.py:721
  4.8 11.0 %collective-permute-start.8 = (f32[208,128]{1,0:T(8,128)S(1)}, f32[208,128]{1,0:T(8,128)S(1)}, u32[]{:S(2)}, u32[]{:S(2)}) collective-permute-start(f32[208,128]{1,0:T(8,128)S(1)} %get-tuple-element.40), channel_id=1, source_target_pairs={{0,8},{1,9},{2,10},{3,11},{4,12},{5,13},{6,14},{7,15},{8,0},{9,1},... | collective-permute-start | bytes 319496 | tf_op jit(solution)/shard_map/ppermute | solution.py:716
  8.3 8.3 %collective-permute-start.6 = (f32[208,128]{1,0:T(8,128)S(1)}, f32[208,128]{1,0:T(8,128)S(1)}, u32[]{:S(2)}, u32[]{:S(2)}) collective-permute-start(f32[208,128]{1,0:T(8,128)S(1)} %get-tuple-element.38), channel_id=1, source_target_pairs={{0,1},{1,0},{2,3},{3,2},{4,5},{5,4},{6,7},{7,6},{8,9},{9,8},{10,11... | collective-permute-start | bytes 319496 | tf_op jit(solution)/shard_map/ppermute | solution.py:716
  10.0 6.8 %collective-permute-start.7 = (f32[208,128]{1,0:T(8,128)S(1)}, f32[208,128]{1,0:T(8,128)S(1)}, u32[]{:S(2)}, u32[]{:S(2)}) collective-permute-start(f32[208,128]{1,0:T(8,128)S(1)} %get-tuple-element.39), channel_id=1, source_target_pairs={{0,9},{1,8},{2,11},{3,10},{4,13},{5,12},{6,15},{7,14},{8,1},{9,0},... | collective-permute-start | bytes 319496 | tf_op jit(solution)/shard_map/ppermute | solution.py:716
  11.3 11.6 %collective-permute-start.3 = (f32[208,128]{1,0:T(8,128)S(1)}, f32[208,128]{1,0:T(8,128)S(1)}, u32[]{:S(2)}, u32[]{:S(2)}) collective-permute-start(f32[208,128]{1,0:T(8,128)S(1)} %get-tuple-element.34), channel_id=1, source_target_pairs={{0,1},{1,0},{2,3},{3,2},{4,5},{5,4},{6,7},{7,6},{8,9},{9,8},{10,11... | collective-permute-start | bytes 319496 | tf_op jit(solution)/shard_map/ppermute | solution.py:716
  12.9 10.1 %collective-permute-start.5 = (f32[208,128]{1,0:T(8,128)S(1)}, f32[208,128]{1,0:T(8,128)S(1)}, u32[]{:S(2)}, u32[]{:S(2)}) collective-permute-start(f32[208,128]{1,0:T(8,128)S(1)} %get-tuple-element.37), channel_id=1, source_target_pairs={{0,8},{1,9},{2,10},{3,11},{4,12},{5,13},{6,14},{7,15},{8,0},{9,1},... | collective-permute-start | bytes 319496 | tf_op jit(solution)/shard_map/ppermute | solution.py:716
  17.5 12.5 %collective-permute-start.9 = (f32[5,48,128]{2,1,0:T(8,128)S(1)}, f32[5,48,128]{2,1,0:T(8,128)S(1)}, u32[]{:S(2)}, u32[]{:S(2)}) collective-permute-start(f32[5,48,128]{2,1,0:T(8,128)S(1)} %get-tuple-element.41.refs_0_), channel_id=1, source_target_pairs={{0,2},{1,3},{2,0},{3,1},{4,6},{5,7},{6,4},{7,5},{8,10},{9,11},{10,... | collective-permute-start | bytes 368648 | tf_op jit(solution)/shard_map/ppermute | solution.py:716
  20.2 7.6 %collective-permute-start.4 = (f32[208,128]{1,0:T(8,128)S(1)}, f32[208,128]{1,0:T(8,128)S(1)}, u32[]{:S(2)}, u32[]{:S(2)}) collective-permute-start(f32[208,128]{1,0:T(8,128)S(1)} %get-tuple-element.35), channel_id=1, source_target_pairs={{0,9},{1,8},{2,11},{3,10},{4,13},{5,12},{6,15},{7,14},{8,1},{9,0},... | collective-permute-start | bytes 319496 | tf_op jit(solution)/shard_map/ppermute | solution.py:716
  21.9 8.1 %collective-permute-start.10 = (f32[3,48,128]{2,1,0:T(8,128)S(1)}, f32[3,48,128]{2,1,0:T(8,128)S(1)}, u32[]{:S(2)}, u32[]{:S(2)}) collective-permute-start(f32[3,48,128]{2,1,0:T(8,128)S(1)} %get-tuple-element.42.refs_1_), channel_id=1, source_target_pairs={{0,2},{1,3},{2,0},{3,1},{4,6},{5,7},{6,4},{7,5},{8,10},{9,11},{10,... | collective-permute-start | bytes 221192 | tf_op jit(solution)/shard_map/ppermute | solution.py:716
  22.9 7.1 %collective-permute-start.11 = (f32[48,128]{1,0:T(8,128)S(1)}, f32[48,128]{1,0:T(8,128)S(1)}, u32[]{:S(2)}, u32[]{:S(2)}) collective-permute-start(f32[48,128]{1,0:T(8,128)S(1)} %get-tuple-element.44), channel_id=1, source_target_pairs={{0,1},{1,0},{2,3},{3,2},{4,5},{5,4},{6,7},{7,6},{8,9},{9,8},{10,11... | collective-permute-start | bytes 73736 | tf_op jit(solution)/shard_map/ppermute | solution.py:716
  23.0 7.0 %collective-permute-start.12 = (f32[48,128]{1,0:T(8,128)S(1)}, f32[48,128]{1,0:T(8,128)S(1)}, u32[]{:S(2)}, u32[]{:S(2)}) collective-permute-start(f32[48,128]{1,0:T(8,128)S(1)} %get-tuple-element.45), channel_id=1, source_target_pairs={{0,3},{1,2},{2,1},{3,0},{4,7},{5,6},{6,5},{7,4},{8,11},{9,10},{10,... | collective-permute-start | bytes 73736 | tf_op jit(solution)/shard_map/ppermute | solution.py:716
  30.1 3.5 %collective-permute-start.14 = (f32[4,48,128]{2,1,0:T(8,128)S(1)}, f32[4,48,128]{2,1,0:T(8,128)S(1)}, u32[]{:S(2)}, u32[]{:S(2)}) collective-permute-start(f32[4,48,128]{2,1,0:T(8,128)S(1)} %get-tuple-element.49), channel_id=1, source_target_pairs={{4,8},{8,4},{5,9},{9,5},{6,10},{10,6},{7,11},{11,7},{20,24},{24,20... | collective-permute-start | bytes 294920 | tf_op jit(solution)/shard_map/ppermute | solution.py:721
  30.8 3.0 %collective-permute-start.13 = (f32[4,48,128]{2,1,0:T(8,128)S(1)}, f32[4,48,128]{2,1,0:T(8,128)S(1)}, u32[]{:S(2)}, u32[]{:S(2)}) collective-permute-start(f32[4,48,128]{2,1,0:T(8,128)S(1)} %get-tuple-element.48), channel_id=1, source_target_pairs={{0,4},{1,5},{2,6},{3,7},{4,0},{5,1},{6,2},{7,3},{8,12},{9,13},{10,... | collective-permute-start | bytes 294920 | tf_op jit(solution)/shard_map/ppermute | solution.py:716
  33.9 5.7 %collective-permute-start.16 = (f32[48,128]{1,0:T(8,128)S(1)}, f32[48,128]{1,0:T(8,128)S(1)}, u32[]{:S(2)}, u32[]{:S(2)}) collective-permute-start(f32[48,128]{1,0:T(8,128)S(1)} %pair_edges.1), channel_id=1, source_target_pairs={{0,3},{1,2},{2,1},{3,0},{4,7},{5,6},{6,5},{7,4},{8,11},{9,10},{10,... | collective-permute-start | bytes 73736 | tf_op jit(solution)/shard_map/ppermute | solution.py:716
  36.8 3.8 %collective-permute-start.15 = (f32[48,128]{1,0:T(8,128)S(1)}, f32[48,128]{1,0:T(8,128)S(1)}, u32[]{:S(2)}, u32[]{:S(2)}) collective-permute-start(f32[48,128]{1,0:T(8,128)S(1)} %pair_edges.1), channel_id=1, source_target_pairs={{0,1},{1,0},{2,3},{3,2},{4,5},{5,4},{6,7},{7,6},{8,9},{9,8},{10,11... | collective-permute-start | bytes 73736 | tf_op jit(solution)/shard_map/ppermute | solution.py:716

commit v9 on v8

--- a/solution.py
+++ b/solution.py
@@ -774,14 +774,14 @@
         packed = pack_chip(FAR, chip_points, tile_rows, columns)
         got = [packed[0]] + [exchanged(block, (df, dz ^ 2)) for block, (df, dz) in zip(packed[1:], FAR[1:])]
         packed = pack_chip(NEAR, chip_points, tile_rows, columns, [cross, packed[0]])
-        total = scatter(got[:2], None, *size, packed[:1])[0]
-        sums = scatter(got[2:], total, *size, parts=(5, tile_rows - 5))
+        total = scatter(got[:3], None, *size, packed[:1])[0]
+        sums = scatter(got[3:], total, *size, parts=(5, tile_rows - 5))
         far = [exchanged(part, (0, 2)) for part in sums]
         got = [packed[0]] + [exchanged(block, tile) for block, tile in zip(packed[1:], NEAR[1:])]
         one, other = all_state_edges(n_row, pair_at, paired, turned, pair, cross, sums)
         one, other = exchanged(one, (0, 1)), exchanged(other, (0, 3))
-        total = scatter(got[:2], None, *size)[0]
-        total = scatter(got[2:], total, *size)[0]
+        total = scatter(got[:3], None, *size)[0]
+        total = scatter(got[3:], total, *size)[0]
         fields, pull, edge_pull, own = tile_fields(n_row, pair_at, turned, pair, cross, gravity, [total])
         canvas = finish(total, far, [one, other, pull])
     else:

time: 42.1 us -> 42.3 us (level)
  transfers between devices with their start and end apart: 17 -> 17, of which waited for: 4 -> 3; matrix products, arithmetic and copies ran while one was open for 0% -> 0% of each run, Pallas kernels for 27% -> 27%
where the time goes in v9:
time: 42.3 us; the launch traced here: 42.1 us
  starting transfers between devices  25.2 us (60%)
  Pallas kernels  12.9 us (30%)
  waiting for transfers between devices  3.81 us (9%)
    ppermute x15, starting transfers between devices, exchanged(): return lax.ppermute(values, ('frow', 'fcol'), pairs)  23.9 us
    ppermute x15, waiting for transfers between devices, exchanged(): return lax.ppermute(values, ('frow', 'fcol'), pairs)  3.81 us
    pallas_call x4, Pallas kernels, scatter(): pl.pallas_call(functools.partial(scatter_kernel, len(blocks), total is No...  3.08 us
    pallas_call x2, Pallas kernels, pack_chip(): pl.pallas_call(functools.partial(pack_chip_kernel, tiles, tile_rows, colu...  2.65 us
    pallas_call x1, Pallas kernels, tile_fields(): pl.pallas_call(functools.partial(tile_fields_kernel, n_row, pair_at), in_...  1.49 us
    pallas_call x1, Pallas kernels, prepare(): pl.pallas_call(functools.partial(prepare_kernel, order), in_specs=[in_hbm...  1.39 us
    pallas_call x1, Pallas kernels, edge_steps(): pl.pallas_call(functools.partial(edge_steps_kernel, n_row, paired), out_s...  1.39 us
    ppermute x2, starting transfers between devices, exchanged_across(): lax.ppermute(values, 'frow', [(f, (f + 1 ^ 1) - 1) for f in range(1, n_ro...  1.33 us
  transfers between devices with their start and end apart: 17, of which 3 were waited for; matrix products, arithmetic and copies ran while one was open for 0% of the time, Pallas kernels for 27%

profile of v9, /device:TPU:0, one launch (start us, length us, event | category | flops | bytes accessed | tf_op | source)
XLA Modules:
  0.0 42.1 jit_solution(6541318170090705418)
XLA Ops:
  0.0 0.5 %collective-permute-start = (f32[48,2048]{1,0:T(8,128)}, f32[48,2048]{1,0:T(8,128)S(1)}, u32[]{:S(2)}, u32[]{:S(2)}) collective-permute-start(f32[48,2048]{1,0:T(8,128)} %bitcast.6), channel_id=1, source_target_pairs={{0,4},{1,5},{2,6},{3,7},{4,0},{5,1},{6,2},{7,3},{8,12},{9,13},{10,... | collective-permute-start | bytes 1179656 | tf_op jit(solution)/shard_map/ppermute | solution.py:716
  0.5 1.4 %prepare.1 = (f32[544,128]{1,0:T(8,128)S(1)}, f32[480,128]{1,0:T(8,128)S(1)}, f32[4,8,48,128]{3,2,1,0:T(8,128)S(1)}, f32[48,2048]{1,0:T(8,128)S(1)}) custom-call(s32[16,128]{1,0:T(8,128)} %bitcast.8, s32[16,128]{1,0:T(8,128)} %bitcast.9, f32[2,2048]{1,0:T(2,128)} %frac.1, f32[4,384,128]{2,1,0:T(8,128)} %bitcast.5, f32[48,2048]{1,0:T(8,128)} %bitcast.7), custom_call_target="tpu_custom_call" | custom-call | tf_op jit(solution)/shard_map/prepare/pallas_call | solution.py:105
  1.9 0.1 collective-permute-start.1
  2.0 0.7 %collective-permute-start.2 = (f32[480,128]{1,0:T(8,128)S(1)}, f32[480,128]{1,0:T(8,128)S(1)}, u32[]{:S(2)}, u32[]{:S(2)}) collective-permute-start(f32[480,128]{1,0:T(8,128)S(1)} %get-tuple-element.32), channel_id=1, source_target_pairs={{4,8},{8,4},{5,9},{9,5},{6,10},{10,6},{7,11},{11,7},{20,24},{24,20... | collective-permute-start | bytes 737288 | tf_op jit(solution)/shard_map/ppermute | solution.py:721
  2.7 0.8 %collective-permute-done.1.pair_where.pair = f32[544,128]{1,0:T(8,128)S(1)} collective-permute-done((f32[544,128]{1,0:T(8,128)S(1)}, f32[544,128]{1,0:T(8,128)S(1)}, u32[]{:S(2)}, u32[]{:S(2)}) %collective-permute-start.1) | collective-permute-done | bytes 278560 | tf_op jit(solution)/shard_map/ppermute | solution.py:716
  3.5 0.0 collective-permute-done.pair_cot
  3.5 1.3 %pack_chip.2 = (f32[208,128]{1,0:T(8,128)S(1)}, f32[208,128]{1,0:T(8,128)S(1)}, f32[208,128]{1,0:T(8,128)S(1)}, f32[208,128]{1,0:T(8,128)S(1)}) custom-call(f32[48,2048]{1,0:T(8,128)S(1)} %get-tuple-element.30.cot, f32[544,128]{1,0:T(8,128)S(1)} %get-tuple-element.31.where, f32[48,2048]{1,0:T(8,128)S(1)} %collective-permute-done.pair_cot, ...), custom_call_target="tpu_custom_call" | custom-call | tf_op jit(solution)/shard_map/pack_chip/pallas_call | solution.py:434
  4.8 3.4 %collective-permute-start.7 = (f32[208,128]{1,0:T(8,128)S(1)}, f32[208,128]{1,0:T(8,128)S(1)}, u32[]{:S(2)}, u32[]{:S(2)}) collective-permute-start(f32[208,128]{1,0:T(8,128)S(1)} %get-tuple-element.39), channel_id=1, source_target_pairs={{0,8},{1,9},{2,10},{3,11},{4,12},{5,13},{6,14},{7,15},{8,0},{9,1},... | collective-permute-start | bytes 319496 | tf_op jit(solution)/shard_map/ppermute | solution.py:716
  8.3 1.7 %collective-permute-start.8 = (f32[208,128]{1,0:T(8,128)S(1)}, f32[208,128]{1,0:T(8,128)S(1)}, u32[]{:S(2)}, u32[]{:S(2)}) collective-permute-start(f32[208,128]{1,0:T(8,128)S(1)} %get-tuple-element.40), channel_id=1, source_target_pairs={{0,1},{1,0},{2,3},{3,2},{4,5},{5,4},{6,7},{7,6},{8,9},{9,8},{10,11... | collective-permute-start | bytes 319496 | tf_op jit(solution)/shard_map/ppermute | solution.py:716
  10.0 0.0 collective-permute-start.6
  10.0 0.0 collective-permute-done.2.refs_0_.cross
  10.0 1.3 %pack_chip.3 = (f32[208,128]{1,0:T(8,128)S(1)}, f32[208,128]{1,0:T(8,128)S(1)}, f32[208,128]{1,0:T(8,128)S(1)}, f32[208,128]{1,0:T(8,128)S(1)}) custom-call(f32[48,2048]{1,0:T(8,128)S(1)} %get-tuple-element.30.cot, f32[544,128]{1,0:T(8,128)S(1)} %get-tuple-element.31.where, f32[48,2048]{1,0:T(8,128)S(1)} %collective-permute-done.pair_cot, ...), custom_call_target="tpu_custom_call" | custom-call | tf_op jit(solution)/shard_map/pack_chip/pallas_call | solution.py:434
  11.3 3.0 %collective-permute-start.4 = (f32[208,128]{1,0:T(8,128)S(1)}, f32[208,128]{1,0:T(8,128)S(1)}, u32[]{:S(2)}, u32[]{:S(2)}) collective-permute-start(f32[208,128]{1,0:T(8,128)S(1)} %get-tuple-element.36), channel_id=1, source_target_pairs={{0,8},{1,9},{2,10},{3,11},{4,12},{5,13},{6,14},{7,15},{8,0},{9,1},... | collective-permute-start | bytes 319496 | tf_op jit(solution)/shard_map/ppermute | solution.py:716
  14.4 1.4 %collective-permute-start.5 = (f32[208,128]{1,0:T(8,128)S(1)}, f32[208,128]{1,0:T(8,128)S(1)}, u32[]{:S(2)}, u32[]{:S(2)}) collective-permute-start(f32[208,128]{1,0:T(8,128)S(1)} %get-tuple-element.37), channel_id=1, source_target_pairs={{0,1},{1,0},{2,3},{3,2},{4,5},{5,4},{6,7},{7,6},{8,9},{9,8},{10,11... | collective-permute-start | bytes 319496 | tf_op jit(solution)/shard_map/ppermute | solution.py:716
  15.8 0.0 collective-permute-done.7.refs_1_
  15.8 0.0 collective-permute-done.8.refs_2_
  15.8 1.1 %scatter_points.6.refs_1_ = f32[8,48,128]{2,1,0:T(8,128)S(1)} custom-call(f32[208,128]{1,0:T(8,128)S(1)} %get-tuple-element.33.refs_1_.refs_0_, f32[208,128]{1,0:T(8,128)S(1)} %collective-permute-done.7.refs_1_, f32[208,128]{1,0:T(8,128)S(1)} %collective-permute-done.8.refs_2_, f32[208,128]{1,0:T(8,128)S(1)} %get-tuple-element.35.refs_0_.refs_3_), custom_call_target="tpu_custom_call" | custom-call | tf_op jit(solution)/shard_map/scatter_points/pallas_call | solution.py:501
  16.9 0.0 collective-permute-done.6.refs_0_
  16.9 0.5 %scatter_points.7 = (f32[5,48,128]{2,1,0:T(8,128)S(1)}, f32[3,48,128]{2,1,0:T(8,128)S(1)}) custom-call(f32[208,128]{1,0:T(8,128)S(1)} %collective-permute-done.6.refs_0_, f32[8,48,128]{2,1,0:T(8,128)S(1)} %scatter_points.6.refs_1_), custom_call_target="tpu_custom_call" | custom-call | tf_op jit(solution)/shard_map/scatter_points/pallas_call | solution.py:501
  17.4 2.7 %collective-permute-start.9 = (f32[5,48,128]{2,1,0:T(8,128)S(1)}, f32[5,48,128]{2,1,0:T(8,128)S(1)}, u32[]{:S(2)}, u32[]{:S(2)}) collective-permute-start(f32[5,48,128]{2,1,0:T(8,128)S(1)} %get-tuple-element.41.refs_0_), channel_id=1, source_target_pairs={{0,2},{1,3},{2,0},{3,1},{4,6},{5,7},{6,4},{7,5},{8,10},{9,11},{10,... | collective-permute-start | bytes 368648 | tf_op jit(solution)/shard_map/ppermute | solution.py:716
  20.0 1.6 %collective-permute-start.3 = (f32[208,128]{1,0:T(8,128)S(1)}, f32[208,128]{1,0:T(8,128)S(1)}, u32[]{:S(2)}, u32[]{:S(2)}) collective-permute-start(f32[208,128]{1,0:T(8,128)S(1)} %get-tuple-element.34), channel_id=1, source_target_pairs={{0,9},{1,8},{2,11},{3,10},{4,13},{5,12},{6,15},{7,14},{8,1},{9,0},... | collective-permute-start | bytes 319496 | tf_op jit(solution)/shard_map/ppermute | solution.py:716
  21.6 0.3 collective-permute-start.10
  22.0 0.6 %state_edges.1 = (f32[48,128]{1,0:T(8,128)S(1)}, f32[48,128]{1,0:T(8,128)S(1)}) custom-call(f32[4,8,48,128]{3,2,1,0:T(8,128)S(1)} %get-tuple-element.43.turned, f32[544,128]{1,0:T(8,128)S(1)} %collective-permute-done.1.pair_where.pair, f32[480,128]{1,0:T(8,128)S(1)} %collective-permute-done.2.refs_0_.cross, f32[5,48,128]{2,1,0:T(8,128)S(1)} %get-tuple-element.41.refs_0_, ...), custom_call_target="tpu_custom_call" | custom-call | tf_op jit(solution)/shard_map/state_edges/pallas_call | solution.py:173
  22.6 0.0 collective-permute-done.4.refs_1_
  22.6 0.1 collective-permute-start.11
  22.7 0.0 collective-permute-done.5.refs_2_
  22.7 4.0 %collective-permute-start.12 = (f32[48,128]{1,0:T(8,128)S(1)}, f32[48,128]{1,0:T(8,128)S(1)}, u32[]{:S(2)}, u32[]{:S(2)}) collective-permute-start(f32[48,128]{1,0:T(8,128)S(1)} %get-tuple-element.45), channel_id=1, source_target_pairs={{0,3},{1,2},{2,1},{3,0},{4,7},{5,6},{6,5},{7,4},{8,11},{9,10},{10,... | collective-permute-start | bytes 73736 | tf_op jit(solution)/shard_map/ppermute | solution.py:716
  26.8 1.1 %scatter_points.4.refs_1_ = f32[8,48,128]{2,1,0:T(8,128)S(1)} custom-call(f32[208,128]{1,0:T(8,128)S(1)} %get-tuple-element.35.refs_0_.refs_3_, f32[208,128]{1,0:T(8,128)S(1)} %collective-permute-done.4.refs_1_, f32[208,128]{1,0:T(8,128)S(1)} %collective-permute-done.5.refs_2_), custom_call_target="tpu_custom_call" | custom-call | tf_op jit(solution)/shard_map/scatter_points/pallas_call | solution.py:501
  27.8 0.0 collective-permute-done.3.refs_0_
  27.8 0.5 %scatter_points.5.refs_0_.total = f32[8,48,128]{2,1,0:T(8,128)S(1)} custom-call(f32[208,128]{1,0:T(8,128)S(1)} %collective-permute-done.3.refs_0_, f32[8,48,128]{2,1,0:T(8,128)S(1)} %scatter_points.4.refs_1_), custom_call_target="tpu_custom_call" | custom-call | tf_op jit(solution)/shard_map/scatter_points/pallas_call | solution.py:501
  28.3 1.5 %tile_fields.1 = (f32[4,16,112,128]{3,2,1,0:T(8,128)S(1)}, f32[16,128]{1,0:T(8,128)S(1)}, f32[8,128]{1,0:T(8,128)S(1)}, f32[4,16,24,128]{3,2,1,0:T(8,128)S(1)}) custom-call(f32[4,8,48,128]{3,2,1,0:T(8,128)S(1)} %get-tuple-element.43.turned, f32[544,128]{1,0:T(8,128)S(1)} %collective-permute-done.1.pair_where.pair, ...), custom_call_target="tpu_custom_call" | custom-call | tf_op jit(solution)/shard_map/tile_fields/pallas_call | solution.py:266
  29.8 0.0 collective-permute-done.11.refs_2_.one
  29.8 0.0 collective-permute-done.12.refs_3_.other
  29.8 0.0 collective-permute-done.10.refs_1_
  29.9 0.0 collective-permute-done.9.refs_0_
  29.9 0.7 %collective-permute-start.14 = (f32[4,48,128]{2,1,0:T(8,128)S(1)}, f32[4,48,128]{2,1,0:T(8,128)S(1)}, u32[]{:S(2)}, u32[]{:S(2)}) collective-permute-start(f32[4,48,128]{2,1,0:T(8,128)S(1)} %get-tuple-element.49), channel_id=1, source_target_pairs={{4,8},{8,4},{5,9},{9,5},{6,10},{10,6},{7,11},{11,7},{20,24},{24,20... | collective-permute-start | bytes 294920 | tf_op jit(solution)/shard_map/ppermute | solution.py:721
  30.6 1.9 %collective-permute-start.13 = (f32[4,48,128]{2,1,0:T(8,128)S(1)}, f32[4,48,128]{2,1,0:T(8,128)S(1)}, u32[]{:S(2)}, u32[]{:S(2)}) collective-permute-start(f32[4,48,128]{2,1,0:T(8,128)S(1)} %get-tuple-element.48), channel_id=1, source_target_pairs={{0,4},{1,5},{2,6},{3,7},{4,0},{5,1},{6,2},{7,3},{8,12},{9,13},{10,... | collective-permute-start | bytes 294920 | tf_op jit(solution)/shard_map/ppermute | solution.py:716
  32.4 0.9 %edge_fields.1.refs_0_.wide = f32[4,16,56,128]{3,2,1,0:T(8,128)S(1)} custom-call(f32[4,16,24,128]{3,2,1,0:T(8,128)S(1)} %get-tuple-element.52.own, f32[48,128]{1,0:T(8,128)S(1)} %collective-permute-done.11.refs_2_.one, f32[48,128]{1,0:T(8,128)S(1)} %collective-permute-done.12.refs_3_.other), custom_call_target="tpu_custom_call" | custom-call | tf_op jit(solution)/shard_map/edge_fields/pallas_call | solution.py:311
  33.3 0.0 collective-permute-done.14.cross
  33.3 0.2 cross_edges.1.partial
  33.5 0.0 collective-permute-done.13.pair
  33.5 0.1 pair_edges.1
  33.6 3.1 %collective-permute-start.16 = (f32[48,128]{1,0:T(8,128)S(1)}, f32[48,128]{1,0:T(8,128)S(1)}, u32[]{:S(2)}, u32[]{:S(2)}) collective-permute-start(f32[48,128]{1,0:T(8,128)S(1)} %pair_edges.1), channel_id=1, source_target_pairs={{0,3},{1,2},{2,1},{3,0},{4,7},{5,6},{6,5},{7,4},{8,11},{9,10},{10,... | collective-permute-start | bytes 73736 | tf_op jit(solution)/shard_map/ppermute | solution.py:716
  36.7 0.0 collective-permute-start.15
  36.7 1.1 %tile_steps.1 = (f32[8,48,128]{2,1,0:T(8,128)S(1)}, f32[16,24,128]{2,1,0:T(8,128)S(1)}) custom-call(f32[8,48,128]{2,1,0:T(8,128)S(1)} %get-tuple-element.47.canvas, f32[4,48,128]{2,1,0:T(8,128)S(1)} %collective-permute-done.13.pair, f32[4,48,128]{2,1,0:T(8,128)S(1)} %collective-permute-done.14.cross, f32[4,16,112,128]{3,2,1,0:T(8,128)S(1)} %get-tuple-element.50.wide, ...), custom_call_target="tpu_custom_call" | custom-call | tf_op jit(solution)/shard_map/tile_steps/pallas_call | solution.py:659
  37.8 1.5 %collective-permute-done.16.other = f32[48,128]{1,0:T(8,128)S(1)} collective-permute-done((f32[48,128]{1,0:T(8,128)S(1)}, f32[48,128]{1,0:T(8,128)S(1)}, u32[]{:S(2)}, u32[]{:S(2)}) %collective-permute-start.16) | collective-permute-done | bytes 24608 | tf_op jit(solution)/shard_map/ppermute | solution.py:716
  39.3 1.4 %collective-permute-done.15.one = f32[48,128]{1,0:T(8,128)S(1)} collective-permute-done((f32[48,128]{1,0:T(8,128)S(1)}, f32[48,128]{1,0:T(8,128)S(1)}, u32[]{:S(2)}, u32[]{:S(2)}) %collective-permute-start.15) | collective-permute-done | bytes 24608 | tf_op jit(solution)/shard_map/ppermute | solution.py:716
  40.8 1.4 %edge_steps.1 = f32[384,128]{1,0:T(8,128)} custom-call(f32[16,24,128]{2,1,0:T(8,128)S(1)} %get-tuple-element.51.windows, f32[48,128]{1,0:T(8,128)S(1)} %collective-permute-done.15.one, f32[48,128]{1,0:T(8,128)S(1)} %collective-permute-done.16.other, f32[4,16,56,128]{3,2,1,0:T(8,128)S(1)} %edge_fields.1.refs_0_.wide, f32[8,128]{1,0:T(8,128)S(1)} %get-tuple-element.53.gravity, ...), custom_call_target="tpu_custom_call" | custom-call | tf_op jit(solution)/shard_map/edge_steps/pallas_call | solution.py:698
  (3 shorter events, 0.0 us)
Async XLA Ops:
  0.0 3.5 %collective-permute-start = (f32[48,2048]{1,0:T(8,128)}, f32[48,2048]{1,0:T(8,128)S(1)}, u32[]{:S(2)}, u32[]{:S(2)}) collective-permute-start(f32[48,2048]{1,0:T(8,128)} %bitcast.6), channel_id=1, source_target_pairs={{0,4},{1,5},{2,6},{3,7},{4,0},{5,1},{6,2},{7,3},{8,12},{9,13},{10,... | collective-permute-start | bytes 1179656 | tf_op jit(solution)/shard_map/ppermute | solution.py:716
  0.5 27.9 %copy-start = (f32[16]{0:T(128)S(1)}, f32[16]{0:T(128)}, u32[]{:S(2)}) copy-start(f32[16]{0:T(128)} %gravity.1) | copy-start | bytes 196
  1.9 1.6 %collective-permute-start.1 = (f32[544,128]{1,0:T(8,128)S(1)}, f32[544,128]{1,0:T(8,128)S(1)}, u32[]{:S(2)}, u32[]{:S(2)}) collective-permute-start(f32[544,128]{1,0:T(8,128)S(1)} %get-tuple-element.31.where), channel_id=1, source_target_pairs={{0,4},{1,5},{2,6},{3,7},{4,0},{5,1},{6,2},{7,3},{8,12},{9,13},{10,... | collective-permute-start | bytes 835592 | tf_op jit(solution)/shard_map/ppermute | solution.py:716
  2.0 8.0 %collective-permute-start.2 = (f32[480,128]{1,0:T(8,128)S(1)}, f32[480,128]{1,0:T(8,128)S(1)}, u32[]{:S(2)}, u32[]{:S(2)}) collective-permute-start(f32[480,128]{1,0:T(8,128)S(1)} %get-tuple-element.32), channel_id=1, source_target_pairs={{4,8},{8,4},{5,9},{9,5},{6,10},{10,6},{7,11},{11,7},{20,24},{24,20... | collective-permute-start | bytes 737288 | tf_op jit(solution)/shard_map/ppermute | solution.py:721
  4.8 11.0 %collective-permute-start.7 = (f32[208,128]{1,0:T(8,128)S(1)}, f32[208,128]{1,0:T(8,128)S(1)}, u32[]{:S(2)}, u32[]{:S(2)}) collective-permute-start(f32[208,128]{1,0:T(8,128)S(1)} %get-tuple-element.39), channel_id=1, source_target_pairs={{0,8},{1,9},{2,10},{3,11},{4,12},{5,13},{6,14},{7,15},{8,0},{9,1},... | collective-permute-start | bytes 319496 | tf_op jit(solution)/shard_map/ppermute | solution.py:716
  8.3 7.5 %collective-permute-start.8 = (f32[208,128]{1,0:T(8,128)S(1)}, f32[208,128]{1,0:T(8,128)S(1)}, u32[]{:S(2)}, u32[]{:S(2)}) collective-permute-start(f32[208,128]{1,0:T(8,128)S(1)} %get-tuple-element.40), channel_id=1, source_target_pairs={{0,1},{1,0},{2,3},{3,2},{4,5},{5,4},{6,7},{7,6},{8,9},{9,8},{10,11... | collective-permute-start | bytes 319496 | tf_op jit(solution)/shard_map/ppermute | solution.py:716
  10.0 6.9 %collective-permute-start.6 = (f32[208,128]{1,0:T(8,128)S(1)}, f32[208,128]{1,0:T(8,128)S(1)}, u32[]{:S(2)}, u32[]{:S(2)}) collective-permute-start(f32[208,128]{1,0:T(8,128)S(1)} %get-tuple-element.38), channel_id=1, source_target_pairs={{0,9},{1,8},{2,11},{3,10},{4,13},{5,12},{6,15},{7,14},{8,1},{9,0},... | collective-permute-start | bytes 319496 | tf_op jit(solution)/shard_map/ppermute | solution.py:716
  11.3 11.3 %collective-permute-start.4 = (f32[208,128]{1,0:T(8,128)S(1)}, f32[208,128]{1,0:T(8,128)S(1)}, u32[]{:S(2)}, u32[]{:S(2)}) collective-permute-start(f32[208,128]{1,0:T(8,128)S(1)} %get-tuple-element.36), channel_id=1, source_target_pairs={{0,8},{1,9},{2,10},{3,11},{4,12},{5,13},{6,14},{7,15},{8,0},{9,1},... | collective-permute-start | bytes 319496 | tf_op jit(solution)/shard_map/ppermute | solution.py:716
  14.4 8.4 %collective-permute-start.5 = (f32[208,128]{1,0:T(8,128)S(1)}, f32[208,128]{1,0:T(8,128)S(1)}, u32[]{:S(2)}, u32[]{:S(2)}) collective-permute-start(f32[208,128]{1,0:T(8,128)S(1)} %get-tuple-element.37), channel_id=1, source_target_pairs={{0,1},{1,0},{2,3},{3,2},{4,5},{5,4},{6,7},{7,6},{8,9},{9,8},{10,11... | collective-permute-start | bytes 319496 | tf_op jit(solution)/shard_map/ppermute | solution.py:716
  17.4 12.5 %collective-permute-start.9 = (f32[5,48,128]{2,1,0:T(8,128)S(1)}, f32[5,48,128]{2,1,0:T(8,128)S(1)}, u32[]{:S(2)}, u32[]{:S(2)}) collective-permute-start(f32[5,48,128]{2,1,0:T(8,128)S(1)} %get-tuple-element.41.refs_0_), channel_id=1, source_target_pairs={{0,2},{1,3},{2,0},{3,1},{4,6},{5,7},{6,4},{7,5},{8,10},{9,11},{10,... | collective-permute-start | bytes 368648 | tf_op jit(solution)/shard_map/ppermute | solution.py:716
  20.0 7.8 %collective-permute-start.3 = (f32[208,128]{1,0:T(8,128)S(1)}, f32[208,128]{1,0:T(8,128)S(1)}, u32[]{:S(2)}, u32[]{:S(2)}) collective-permute-start(f32[208,128]{1,0:T(8,128)S(1)} %get-tuple-element.34), channel_id=1, source_target_pairs={{0,9},{1,8},{2,11},{3,10},{4,13},{5,12},{6,15},{7,14},{8,1},{9,0},... | collective-permute-start | bytes 319496 | tf_op jit(solution)/shard_map/ppermute | solution.py:716
  21.6 8.2 %collective-permute-start.10 = (f32[3,48,128]{2,1,0:T(8,128)S(1)}, f32[3,48,128]{2,1,0:T(8,128)S(1)}, u32[]{:S(2)}, u32[]{:S(2)}) collective-permute-start(f32[3,48,128]{2,1,0:T(8,128)S(1)} %get-tuple-element.42.refs_1_), channel_id=1, source_target_pairs={{0,2},{1,3},{2,0},{3,1},{4,6},{5,7},{6,4},{7,5},{8,10},{9,11},{10,... | collective-permute-start | bytes 221192 | tf_op jit(solution)/shard_map/ppermute | solution.py:716
  22.6 7.2 %collective-permute-start.11 = (f32[48,128]{1,0:T(8,128)S(1)}, f32[48,128]{1,0:T(8,128)S(1)}, u32[]{:S(2)}, u32[]{:S(2)}) collective-permute-start(f32[48,128]{1,0:T(8,128)S(1)} %get-tuple-element.44), channel_id=1, source_target_pairs={{0,1},{1,0},{2,3},{3,2},{4,5},{5,4},{6,7},{7,6},{8,9},{9,8},{10,11... | collective-permute-start | bytes 73736 | tf_op jit(solution)/shard_map/ppermute | solution.py:716
  22.7 7.1 %collective-permute-start.12 = (f32[48,128]{1,0:T(8,128)S(1)}, f32[48,128]{1,0:T(8,128)S(1)}, u32[]{:S(2)}, u32[]{:S(2)}) collective-permute-start(f32[48,128]{1,0:T(8,128)S(1)} %get-tuple-element.45), channel_id=1, source_target_pairs={{0,3},{1,2},{2,1},{3,0},{4,7},{5,6},{6,5},{7,4},{8,11},{9,10},{10,... | collective-permute-start | bytes 73736 | tf_op jit(solution)/shard_map/ppermute | solution.py:716
  29.9 3.4 %collective-permute-start.14 = (f32[4,48,128]{2,1,0:T(8,128)S(1)}, f32[4,48,128]{2,1,0:T(8,128)S(1)}, u32[]{:S(2)}, u32[]{:S(2)}) collective-permute-start(f32[4,48,128]{2,1,0:T(8,128)S(1)} %get-tuple-element.49), channel_id=1, source_target_pairs={{4,8},{8,4},{5,9},{9,5},{6,10},{10,6},{7,11},{11,7},{20,24},{24,20... | collective-permute-start | bytes 294920 | tf_op jit(solution)/shard_map/ppermute | solution.py:721
  30.6 2.9 %collective-permute-start.13 = (f32[4,48,128]{2,1,0:T(8,128)S(1)}, f32[4,48,128]{2,1,0:T(8,128)S(1)}, u32[]{:S(2)}, u32[]{:S(2)}) collective-permute-start(f32[4,48,128]{2,1,0:T(8,128)S(1)} %get-tuple-element.48), channel_id=1, source_target_pairs={{0,4},{1,5},{2,6},{3,7},{4,0},{5,1},{6,2},{7,3},{8,12},{9,13},{10,... | collective-permute-start | bytes 294920 | tf_op jit(solution)/shard_map/ppermute | solution.py:716
  33.6 5.7 %collective-permute-start.16 = (f32[48,128]{1,0:T(8,128)S(1)}, f32[48,128]{1,0:T(8,128)S(1)}, u32[]{:S(2)}, u32[]{:S(2)}) collective-permute-start(f32[48,128]{1,0:T(8,128)S(1)} %pair_edges.1), channel_id=1, source_target_pairs={{0,3},{1,2},{2,1},{3,0},{4,7},{5,6},{6,5},{7,4},{8,11},{9,10},{10,... | collective-permute-start | bytes 73736 | tf_op jit(solution)/shard_map/ppermute | solution.py:716
  36.7 4.0 %collective-permute-start.15 = (f32[48,128]{1,0:T(8,128)S(1)}, f32[48,128]{1,0:T(8,128)S(1)}, u32[]{:S(2)}, u32[]{:S(2)}) collective-permute-start(f32[48,128]{1,0:T(8,128)S(1)} %pair_edges.1), channel_id=1, source_target_pairs={{0,1},{1,0},{2,3},{3,2},{4,5},{5,4},{6,7},{7,6},{8,9},{9,8},{10,11... | collective-permute-start | bytes 73736 | tf_op jit(solution)/shard_map/ppermute | solution.py:716

commit v10 on v9

--- a/solution.py
+++ b/solution.py
@@ -669,7 +669,7 @@
 
 
 def edge_steps_kernel(n_row, paired, windows, one, other, wide, gravity, inner, out, *buffers):
-    *buffers, result = buffers
+    *buffers, result, merged, sems = buffers
     tile_rows, channels, _ = inner.shape
     levels = channels // 3
     left, right = from_sides(one[...], other[...], paired)
@@ -683,14 +683,21 @@
         result[r, w * PART : (w + 1) * PART, :] = value
 
     run_stages(wide, gravity, PART, row_masks(n_row), tile_rows, buffers, store)
-    for r in range(tile_rows):
-        for begin in range(0, channels, PART):
-            field, turn = begin // levels, begin % levels // PART * TURN
-            value = result[r, field * PART : (field + 1) * PART, :]
-            first = pltpu.roll(value, turn, 1) if turn else value
-            final = pltpu.roll(value, LANES - BEYOND_AT - turn, 1)
-            line = jnp.where(lane >= LANES - HALO, final, inner[r, begin : begin + PART, :])
-            out[pl.ds(begin * tile_rows + r, PART, stride=tile_rows), :] = jnp.where(lane < HALO, first, line)
+    copies = []
+    for w in range(3):
+        for begin in range(w * levels, (w + 1) * levels, PART):
+            turn = begin % levels // PART * TURN
+            for r in range(tile_rows):
+                value = result[r, w * PART : (w + 1) * PART, :]
+                final = turned_by(value, LANES - BEYOND_AT - turn)
+                line = jnp.where(lane >= LANES - HALO, final, inner[r, begin : begin + PART, :])
+                line = jnp.where(lane < HALO, turned_by(value, turn), line)
+                merged[pl.ds(begin * tile_rows + r, PART, stride=tile_rows), :] = line
+        field = pl.ds(w * levels * tile_rows, levels * tile_rows)
+        copies.append(pltpu.make_async_copy(merged.at[field, :], out.at[field, :], sems.at[w]))
+        copies[-1].start()
+    for copy in copies:
+        copy.wait()
 
 
 def edge_steps(n_row, paired, windows, one, other, wide, gravity, inner):
@@ -698,7 +705,13 @@
     return pl.pallas_call(
         functools.partial(edge_steps_kernel, n_row, paired),
         out_shape=jax.ShapeDtypeStruct((channels * tile_rows, columns), F32),
-        scratch_shapes=[pltpu.VMEM(windows.shape, F32)] * 4 + [pltpu.VMEM((tile_rows, 3 * PART, columns), F32)],
+        out_specs=pl.BlockSpec(memory_space=pltpu.HBM),
+        scratch_shapes=[pltpu.VMEM(windows.shape, F32)] * 4
+        + [
+            pltpu.VMEM((tile_rows, 3 * PART, columns), F32),
+            pltpu.VMEM((channels * tile_rows, columns), F32),
+            pltpu.SemaphoreType.DMA((3,)),
+        ],
         compiler_params=PARAMS,
         name="edge_steps",
     )(windows, one, other, wide, gravity, inner)

time: 42.3 us -> 42.3 us (level)
  no operation moved by 1% of the time
where the time goes in v10:
time: 42.3 us; the launch traced here: 42.2 us
  starting transfers between devices  25.2 us (60%)
  Pallas kernels  12.9 us (30%)
  waiting for transfers between devices  3.81 us (9%)
    ppermute x15, starting transfers between devices, exchanged(): return lax.ppermute(values, ('frow', 'fcol'), pairs)  23.9 us
    ppermute x15, waiting for transfers between devices, exchanged(): return lax.ppermute(values, ('frow', 'fcol'), pairs)  3.81 us
    pallas_call x4, Pallas kernels, scatter(): pl.pallas_call(functools.partial(scatter_kernel, len(blocks), total is No...  3.08 us
    pallas_call x2, Pallas kernels, pack_chip(): pl.pallas_call(functools.partial(pack_chip_kernel, tiles, tile_rows, colu...  2.65 us
    pallas_call x1, Pallas kernels, tile_fields(): pl.pallas_call(functools.partial(tile_fields_kernel, n_row, pair_at), in_...  1.49 us
    pallas_call x1, Pallas kernels, edge_steps(): pl.pallas_call(functools.partial(edge_steps_kernel, n_row, paired), out_s...  1.42 us
    pallas_call x1, Pallas kernels, prepare(): pl.pallas_call(functools.partial(prepare_kernel, order), in_specs=[in_hbm...  1.39 us
    ppermute x2, starting transfers between devices, exchanged_across(): lax.ppermute(values, 'frow', [(f, (f + 1 ^ 1) - 1) for f in range(1, n_ro...  1.33 us
  transfers between devices with their start and end apart: 17, of which 3 were waited for; matrix products, arithmetic and copies ran while one was open for 0% of the time, Pallas kernels for 27%

profile of v10, /device:TPU:0, one launch (start us, length us, event | category | flops | bytes accessed | tf_op | source)
XLA Modules:
  0.0 42.2 jit_solution(15221025905023488621)
XLA Ops:
  0.0 0.5 %collective-permute-start = (f32[48,2048]{1,0:T(8,128)}, f32[48,2048]{1,0:T(8,128)S(1)}, u32[]{:S(2)}, u32[]{:S(2)}) collective-permute-start(f32[48,2048]{1,0:T(8,128)} %bitcast.6), channel_id=1, source_target_pairs={{0,4},{1,5},{2,6},{3,7},{4,0},{5,1},{6,2},{7,3},{8,12},{9,13},{10,... | collective-permute-start | bytes 1179656 | tf_op jit(solution)/shard_map/ppermute | solution.py:729
  0.5 1.4 %prepare.1 = (f32[544,128]{1,0:T(8,128)S(1)}, f32[480,128]{1,0:T(8,128)S(1)}, f32[4,8,48,128]{3,2,1,0:T(8,128)S(1)}, f32[48,2048]{1,0:T(8,128)S(1)}) custom-call(s32[16,128]{1,0:T(8,128)} %bitcast.8, s32[16,128]{1,0:T(8,128)} %bitcast.9, f32[2,2048]{1,0:T(2,128)} %frac.1, f32[4,384,128]{2,1,0:T(8,128)} %bitcast.5, f32[48,2048]{1,0:T(8,128)} %bitcast.7), custom_call_target="tpu_custom_call" | custom-call | tf_op jit(solution)/shard_map/prepare/pallas_call | solution.py:105
  1.9 0.1 collective-permute-start.1
  2.0 0.7 %collective-permute-start.2 = (f32[480,128]{1,0:T(8,128)S(1)}, f32[480,128]{1,0:T(8,128)S(1)}, u32[]{:S(2)}, u32[]{:S(2)}) collective-permute-start(f32[480,128]{1,0:T(8,128)S(1)} %get-tuple-element.32), channel_id=1, source_target_pairs={{4,8},{8,4},{5,9},{9,5},{6,10},{10,6},{7,11},{11,7},{20,24},{24,20... | collective-permute-start | bytes 737288 | tf_op jit(solution)/shard_map/ppermute | solution.py:734
  2.7 0.8 %collective-permute-done.1.pair_where.pair = f32[544,128]{1,0:T(8,128)S(1)} collective-permute-done((f32[544,128]{1,0:T(8,128)S(1)}, f32[544,128]{1,0:T(8,128)S(1)}, u32[]{:S(2)}, u32[]{:S(2)}) %collective-permute-start.1) | collective-permute-done | bytes 278560 | tf_op jit(solution)/shard_map/ppermute | solution.py:729
  3.5 0.0 collective-permute-done.pair_cot
  3.5 1.3 %pack_chip.2 = (f32[208,128]{1,0:T(8,128)S(1)}, f32[208,128]{1,0:T(8,128)S(1)}, f32[208,128]{1,0:T(8,128)S(1)}, f32[208,128]{1,0:T(8,128)S(1)}) custom-call(f32[48,2048]{1,0:T(8,128)S(1)} %get-tuple-element.30.cot, f32[544,128]{1,0:T(8,128)S(1)} %get-tuple-element.31.where, f32[48,2048]{1,0:T(8,128)S(1)} %collective-permute-done.pair_cot, ...), custom_call_target="tpu_custom_call" | custom-call | tf_op jit(solution)/shard_map/pack_chip/pallas_call | solution.py:434
  4.8 3.4 %collective-permute-start.7 = (f32[208,128]{1,0:T(8,128)S(1)}, f32[208,128]{1,0:T(8,128)S(1)}, u32[]{:S(2)}, u32[]{:S(2)}) collective-permute-start(f32[208,128]{1,0:T(8,128)S(1)} %get-tuple-element.39), channel_id=1, source_target_pairs={{0,8},{1,9},{2,10},{3,11},{4,12},{5,13},{6,14},{7,15},{8,0},{9,1},... | collective-permute-start | bytes 319496 | tf_op jit(solution)/shard_map/ppermute | solution.py:729
  8.3 1.7 %collective-permute-start.8 = (f32[208,128]{1,0:T(8,128)S(1)}, f32[208,128]{1,0:T(8,128)S(1)}, u32[]{:S(2)}, u32[]{:S(2)}) collective-permute-start(f32[208,128]{1,0:T(8,128)S(1)} %get-tuple-element.40), channel_id=1, source_target_pairs={{0,1},{1,0},{2,3},{3,2},{4,5},{5,4},{6,7},{7,6},{8,9},{9,8},{10,11... | collective-permute-start | bytes 319496 | tf_op jit(solution)/shard_map/ppermute | solution.py:729
  10.0 0.0 collective-permute-start.6
  10.0 0.0 collective-permute-done.2.refs_0_.cross
  10.0 1.3 %pack_chip.3 = (f32[208,128]{1,0:T(8,128)S(1)}, f32[208,128]{1,0:T(8,128)S(1)}, f32[208,128]{1,0:T(8,128)S(1)}, f32[208,128]{1,0:T(8,128)S(1)}) custom-call(f32[48,2048]{1,0:T(8,128)S(1)} %get-tuple-element.30.cot, f32[544,128]{1,0:T(8,128)S(1)} %get-tuple-element.31.where, f32[48,2048]{1,0:T(8,128)S(1)} %collective-permute-done.pair_cot, ...), custom_call_target="tpu_custom_call" | custom-call | tf_op jit(solution)/shard_map/pack_chip/pallas_call | solution.py:434
  11.3 3.0 %collective-permute-start.4 = (f32[208,128]{1,0:T(8,128)S(1)}, f32[208,128]{1,0:T(8,128)S(1)}, u32[]{:S(2)}, u32[]{:S(2)}) collective-permute-start(f32[208,128]{1,0:T(8,128)S(1)} %get-tuple-element.36), channel_id=1, source_target_pairs={{0,8},{1,9},{2,10},{3,11},{4,12},{5,13},{6,14},{7,15},{8,0},{9,1},... | collective-permute-start | bytes 319496 | tf_op jit(solution)/shard_map/ppermute | solution.py:729
  14.4 1.4 %collective-permute-start.5 = (f32[208,128]{1,0:T(8,128)S(1)}, f32[208,128]{1,0:T(8,128)S(1)}, u32[]{:S(2)}, u32[]{:S(2)}) collective-permute-start(f32[208,128]{1,0:T(8,128)S(1)} %get-tuple-element.37), channel_id=1, source_target_pairs={{0,1},{1,0},{2,3},{3,2},{4,5},{5,4},{6,7},{7,6},{8,9},{9,8},{10,11... | collective-permute-start | bytes 319496 | tf_op jit(solution)/shard_map/ppermute | solution.py:729
  15.8 0.0 collective-permute-done.7.refs_1_
  15.8 0.0 collective-permute-done.8.refs_2_
  15.8 1.1 %scatter_points.6.refs_1_ = f32[8,48,128]{2,1,0:T(8,128)S(1)} custom-call(f32[208,128]{1,0:T(8,128)S(1)} %get-tuple-element.33.refs_1_.refs_0_, f32[208,128]{1,0:T(8,128)S(1)} %collective-permute-done.7.refs_1_, f32[208,128]{1,0:T(8,128)S(1)} %collective-permute-done.8.refs_2_, f32[208,128]{1,0:T(8,128)S(1)} %get-tuple-element.35.refs_0_.refs_3_), custom_call_target="tpu_custom_call" | custom-call | tf_op jit(solution)/shard_map/scatter_points/pallas_call | solution.py:501
  16.9 0.0 collective-permute-done.6.refs_0_
  16.9 0.5 %scatter_points.7 = (f32[5,48,128]{2,1,0:T(8,128)S(1)}, f32[3,48,128]{2,1,0:T(8,128)S(1)}) custom-call(f32[208,128]{1,0:T(8,128)S(1)} %collective-permute-done.6.refs_0_, f32[8,48,128]{2,1,0:T(8,128)S(1)} %scatter_points.6.refs_1_), custom_call_target="tpu_custom_call" | custom-call | tf_op jit(solution)/shard_map/scatter_points/pallas_call | solution.py:501
  17.4 2.7 %collective-permute-start.9 = (f32[5,48,128]{2,1,0:T(8,128)S(1)}, f32[5,48,128]{2,1,0:T(8,128)S(1)}, u32[]{:S(2)}, u32[]{:S(2)}) collective-permute-start(f32[5,48,128]{2,1,0:T(8,128)S(1)} %get-tuple-element.41.refs_0_), channel_id=1, source_target_pairs={{0,2},{1,3},{2,0},{3,1},{4,6},{5,7},{6,4},{7,5},{8,10},{9,11},{10,... | collective-permute-start | bytes 368648 | tf_op jit(solution)/shard_map/ppermute | solution.py:729
  20.0 1.6 %collective-permute-start.3 = (f32[208,128]{1,0:T(8,128)S(1)}, f32[208,128]{1,0:T(8,128)S(1)}, u32[]{:S(2)}, u32[]{:S(2)}) collective-permute-start(f32[208,128]{1,0:T(8,128)S(1)} %get-tuple-element.34), channel_id=1, source_target_pairs={{0,9},{1,8},{2,11},{3,10},{4,13},{5,12},{6,15},{7,14},{8,1},{9,0},... | collective-permute-start | bytes 319496 | tf_op jit(solution)/shard_map/ppermute | solution.py:729
  21.6 0.3 collective-permute-start.10
  22.0 0.6 %state_edges.1 = (f32[48,128]{1,0:T(8,128)S(1)}, f32[48,128]{1,0:T(8,128)S(1)}) custom-call(f32[4,8,48,128]{3,2,1,0:T(8,128)S(1)} %get-tuple-element.43.turned, f32[544,128]{1,0:T(8,128)S(1)} %collective-permute-done.1.pair_where.pair, f32[480,128]{1,0:T(8,128)S(1)} %collective-permute-done.2.refs_0_.cross, f32[5,48,128]{2,1,0:T(8,128)S(1)} %get-tuple-element.41.refs_0_, ...), custom_call_target="tpu_custom_call" | custom-call | tf_op jit(solution)/shard_map/state_edges/pallas_call | solution.py:173
  22.6 0.0 collective-permute-done.4.refs_1_
  22.6 0.1 collective-permute-start.11
  22.7 0.0 collective-permute-done.5.refs_2_
  22.7 4.0 %collective-permute-start.12 = (f32[48,128]{1,0:T(8,128)S(1)}, f32[48,128]{1,0:T(8,128)S(1)}, u32[]{:S(2)}, u32[]{:S(2)}) collective-permute-start(f32[48,128]{1,0:T(8,128)S(1)} %get-tuple-element.45), channel_id=1, source_target_pairs={{0,3},{1,2},{2,1},{3,0},{4,7},{5,6},{6,5},{7,4},{8,11},{9,10},{10,... | collective-permute-start | bytes 73736 | tf_op jit(solution)/shard_map/ppermute | solution.py:729
  26.8 1.1 %scatter_points.4.refs_1_ = f32[8,48,128]{2,1,0:T(8,128)S(1)} custom-call(f32[208,128]{1,0:T(8,128)S(1)} %get-tuple-element.35.refs_0_.refs_3_, f32[208,128]{1,0:T(8,128)S(1)} %collective-permute-done.4.refs_1_, f32[208,128]{1,0:T(8,128)S(1)} %collective-permute-done.5.refs_2_), custom_call_target="tpu_custom_call" | custom-call | tf_op jit(solution)/shard_map/scatter_points/pallas_call | solution.py:501
  27.8 0.0 collective-permute-done.3.refs_0_
  27.8 0.5 %scatter_points.5.refs_0_.total = f32[8,48,128]{2,1,0:T(8,128)S(1)} custom-call(f32[208,128]{1,0:T(8,128)S(1)} %collective-permute-done.3.refs_0_, f32[8,48,128]{2,1,0:T(8,128)S(1)} %scatter_points.4.refs_1_), custom_call_target="tpu_custom_call" | custom-call | tf_op jit(solution)/shard_map/scatter_points/pallas_call | solution.py:501
  28.3 1.5 %tile_fields.1 = (f32[4,16,112,128]{3,2,1,0:T(8,128)S(1)}, f32[16,128]{1,0:T(8,128)S(1)}, f32[8,128]{1,0:T(8,128)S(1)}, f32[4,16,24,128]{3,2,1,0:T(8,128)S(1)}) custom-call(f32[4,8,48,128]{3,2,1,0:T(8,128)S(1)} %get-tuple-element.43.turned, f32[544,128]{1,0:T(8,128)S(1)} %collective-permute-done.1.pair_where.pair, ...), custom_call_target="tpu_custom_call" | custom-call | tf_op jit(solution)/shard_map/tile_fields/pallas_call | solution.py:266
  29.8 0.0 collective-permute-done.11.refs_2_.one
  29.8 0.0 collective-permute-done.12.refs_3_.other
  29.8 0.0 collective-permute-done.10.refs_1_
  29.9 0.0 collective-permute-done.9.refs_0_
  29.9 0.7 %collective-permute-start.14 = (f32[4,48,128]{2,1,0:T(8,128)S(1)}, f32[4,48,128]{2,1,0:T(8,128)S(1)}, u32[]{:S(2)}, u32[]{:S(2)}) collective-permute-start(f32[4,48,128]{2,1,0:T(8,128)S(1)} %get-tuple-element.49), channel_id=1, source_target_pairs={{4,8},{8,4},{5,9},{9,5},{6,10},{10,6},{7,11},{11,7},{20,24},{24,20... | collective-permute-start | bytes 294920 | tf_op jit(solution)/shard_map/ppermute | solution.py:734
  30.6 1.9 %collective-permute-start.13 = (f32[4,48,128]{2,1,0:T(8,128)S(1)}, f32[4,48,128]{2,1,0:T(8,128)S(1)}, u32[]{:S(2)}, u32[]{:S(2)}) collective-permute-start(f32[4,48,128]{2,1,0:T(8,128)S(1)} %get-tuple-element.48), channel_id=1, source_target_pairs={{0,4},{1,5},{2,6},{3,7},{4,0},{5,1},{6,2},{7,3},{8,12},{9,13},{10,... | collective-permute-start | bytes 294920 | tf_op jit(solution)/shard_map/ppermute | solution.py:729
  32.4 0.9 %edge_fields.1.refs_0_.wide = f32[4,16,56,128]{3,2,1,0:T(8,128)S(1)} custom-call(f32[4,16,24,128]{3,2,1,0:T(8,128)S(1)} %get-tuple-element.52.own, f32[48,128]{1,0:T(8,128)S(1)} %collective-permute-done.11.refs_2_.one, f32[48,128]{1,0:T(8,128)S(1)} %collective-permute-done.12.refs_3_.other), custom_call_target="tpu_custom_call" | custom-call | tf_op jit(solution)/shard_map/edge_fields/pallas_call | solution.py:311
  33.3 0.0 collective-permute-done.14.cross
  33.3 0.2 cross_edges.1.partial
  33.5 0.0 collective-permute-done.13.pair
  33.5 0.1 pair_edges.1
  33.6 3.1 %collective-permute-start.16 = (f32[48,128]{1,0:T(8,128)S(1)}, f32[48,128]{1,0:T(8,128)S(1)}, u32[]{:S(2)}, u32[]{:S(2)}) collective-permute-start(f32[48,128]{1,0:T(8,128)S(1)} %pair_edges.1), channel_id=1, source_target_pairs={{0,3},{1,2},{2,1},{3,0},{4,7},{5,6},{6,5},{7,4},{8,11},{9,10},{10,... | collective-permute-start | bytes 73736 | tf_op jit(solution)/shard_map/ppermute | solution.py:729
  36.7 0.0 collective-permute-start.15
  36.7 1.1 %tile_steps.1 = (f32[8,48,128]{2,1,0:T(8,128)S(1)}, f32[16,24,128]{2,1,0:T(8,128)S(1)}) custom-call(f32[8,48,128]{2,1,0:T(8,128)S(1)} %get-tuple-element.47.canvas, f32[4,48,128]{2,1,0:T(8,128)S(1)} %collective-permute-done.13.pair, f32[4,48,128]{2,1,0:T(8,128)S(1)} %collective-permute-done.14.cross, f32[4,16,112,128]{3,2,1,0:T(8,128)S(1)} %get-tuple-element.50.wide, ...), custom_call_target="tpu_custom_call" | custom-call | tf_op jit(solution)/shard_map/tile_steps/pallas_call | solution.py:659
  37.8 1.5 %collective-permute-done.16.other = f32[48,128]{1,0:T(8,128)S(1)} collective-permute-done((f32[48,128]{1,0:T(8,128)S(1)}, f32[48,128]{1,0:T(8,128)S(1)}, u32[]{:S(2)}, u32[]{:S(2)}) %collective-permute-start.16) | collective-permute-done | bytes 24608 | tf_op jit(solution)/shard_map/ppermute | solution.py:729
  39.3 1.4 %collective-permute-done.15.one = f32[48,128]{1,0:T(8,128)S(1)} collective-permute-done((f32[48,128]{1,0:T(8,128)S(1)}, f32[48,128]{1,0:T(8,128)S(1)}, u32[]{:S(2)}, u32[]{:S(2)}) %collective-permute-start.15) | collective-permute-done | bytes 24608 | tf_op jit(solution)/shard_map/ppermute | solution.py:729
  40.8 1.4 %edge_steps.1 = f32[384,128]{1,0:T(8,128)} custom-call(f32[16,24,128]{2,1,0:T(8,128)S(1)} %get-tuple-element.51.windows, f32[48,128]{1,0:T(8,128)S(1)} %collective-permute-done.15.one, f32[48,128]{1,0:T(8,128)S(1)} %collective-permute-done.16.other, f32[4,16,56,128]{3,2,1,0:T(8,128)S(1)} %edge_fields.1.refs_0_.wide, f32[8,128]{1,0:T(8,128)S(1)} %get-tuple-element.53.gravity, ...), custom_call_target="tpu_custom_call" | custom-call | tf_op jit(solution)/shard_map/edge_steps/pallas_call | solution.py:705
  (3 shorter events, 0.0 us)
Async XLA Ops:
  0.0 3.5 %collective-permute-start = (f32[48,2048]{1,0:T(8,128)}, f32[48,2048]{1,0:T(8,128)S(1)}, u32[]{:S(2)}, u32[]{:S(2)}) collective-permute-start(f32[48,2048]{1,0:T(8,128)} %bitcast.6), channel_id=1, source_target_pairs={{0,4},{1,5},{2,6},{3,7},{4,0},{5,1},{6,2},{7,3},{8,12},{9,13},{10,... | collective-permute-start | bytes 1179656 | tf_op jit(solution)/shard_map/ppermute | solution.py:729
  0.5 27.9 %copy-start = (f32[16]{0:T(128)S(1)}, f32[16]{0:T(128)}, u32[]{:S(2)}) copy-start(f32[16]{0:T(128)} %gravity.1) | copy-start | bytes 196
  1.9 1.6 %collective-permute-start.1 = (f32[544,128]{1,0:T(8,128)S(1)}, f32[544,128]{1,0:T(8,128)S(1)}, u32[]{:S(2)}, u32[]{:S(2)}) collective-permute-start(f32[544,128]{1,0:T(8,128)S(1)} %get-tuple-element.31.where), channel_id=1, source_target_pairs={{0,4},{1,5},{2,6},{3,7},{4,0},{5,1},{6,2},{7,3},{8,12},{9,13},{10,... | collective-permute-start | bytes 835592 | tf_op jit(solution)/shard_map/ppermute | solution.py:729
  2.0 8.0 %collective-permute-start.2 = (f32[480,128]{1,0:T(8,128)S(1)}, f32[480,128]{1,0:T(8,128)S(1)}, u32[]{:S(2)}, u32[]{:S(2)}) collective-permute-start(f32[480,128]{1,0:T(8,128)S(1)} %get-tuple-element.32), channel_id=1, source_target_pairs={{4,8},{8,4},{5,9},{9,5},{6,10},{10,6},{7,11},{11,7},{20,24},{24,20... | collective-permute-start | bytes 737288 | tf_op jit(solution)/shard_map/ppermute | solution.py:734
  4.8 11.0 %collective-permute-start.7 = (f32[208,128]{1,0:T(8,128)S(1)}, f32[208,128]{1,0:T(8,128)S(1)}, u32[]{:S(2)}, u32[]{:S(2)}) collective-permute-start(f32[208,128]{1,0:T(8,128)S(1)} %get-tuple-element.39), channel_id=1, source_target_pairs={{0,8},{1,9},{2,10},{3,11},{4,12},{5,13},{6,14},{7,15},{8,0},{9,1},... | collective-permute-start | bytes 319496 | tf_op jit(solution)/shard_map/ppermute | solution.py:729
  8.3 7.5 %collective-permute-start.8 = (f32[208,128]{1,0:T(8,128)S(1)}, f32[208,128]{1,0:T(8,128)S(1)}, u32[]{:S(2)}, u32[]{:S(2)}) collective-permute-start(f32[208,128]{1,0:T(8,128)S(1)} %get-tuple-element.40), channel_id=1, source_target_pairs={{0,1},{1,0},{2,3},{3,2},{4,5},{5,4},{6,7},{7,6},{8,9},{9,8},{10,11... | collective-permute-start | bytes 319496 | tf_op jit(solution)/shard_map/ppermute | solution.py:729
  10.0 6.9 %collective-permute-start.6 = (f32[208,128]{1,0:T(8,128)S(1)}, f32[208,128]{1,0:T(8,128)S(1)}, u32[]{:S(2)}, u32[]{:S(2)}) collective-permute-start(f32[208,128]{1,0:T(8,128)S(1)} %get-tuple-element.38), channel_id=1, source_target_pairs={{0,9},{1,8},{2,11},{3,10},{4,13},{5,12},{6,15},{7,14},{8,1},{9,0},... | collective-permute-start | bytes 319496 | tf_op jit(solution)/shard_map/ppermute | solution.py:729
  11.3 11.3 %collective-permute-start.4 = (f32[208,128]{1,0:T(8,128)S(1)}, f32[208,128]{1,0:T(8,128)S(1)}, u32[]{:S(2)}, u32[]{:S(2)}) collective-permute-start(f32[208,128]{1,0:T(8,128)S(1)} %get-tuple-element.36), channel_id=1, source_target_pairs={{0,8},{1,9},{2,10},{3,11},{4,12},{5,13},{6,14},{7,15},{8,0},{9,1},... | collective-permute-start | bytes 319496 | tf_op jit(solution)/shard_map/ppermute | solution.py:729
  14.4 8.4 %collective-permute-start.5 = (f32[208,128]{1,0:T(8,128)S(1)}, f32[208,128]{1,0:T(8,128)S(1)}, u32[]{:S(2)}, u32[]{:S(2)}) collective-permute-start(f32[208,128]{1,0:T(8,128)S(1)} %get-tuple-element.37), channel_id=1, source_target_pairs={{0,1},{1,0},{2,3},{3,2},{4,5},{5,4},{6,7},{7,6},{8,9},{9,8},{10,11... | collective-permute-start | bytes 319496 | tf_op jit(solution)/shard_map/ppermute | solution.py:729
  17.4 12.5 %collective-permute-start.9 = (f32[5,48,128]{2,1,0:T(8,128)S(1)}, f32[5,48,128]{2,1,0:T(8,128)S(1)}, u32[]{:S(2)}, u32[]{:S(2)}) collective-permute-start(f32[5,48,128]{2,1,0:T(8,128)S(1)} %get-tuple-element.41.refs_0_), channel_id=1, source_target_pairs={{0,2},{1,3},{2,0},{3,1},{4,6},{5,7},{6,4},{7,5},{8,10},{9,11},{10,... | collective-permute-start | bytes 368648 | tf_op jit(solution)/shard_map/ppermute | solution.py:729
  20.0 7.8 %collective-permute-start.3 = (f32[208,128]{1,0:T(8,128)S(1)}, f32[208,128]{1,0:T(8,128)S(1)}, u32[]{:S(2)}, u32[]{:S(2)}) collective-permute-start(f32[208,128]{1,0:T(8,128)S(1)} %get-tuple-element.34), channel_id=1, source_target_pairs={{0,9},{1,8},{2,11},{3,10},{4,13},{5,12},{6,15},{7,14},{8,1},{9,0},... | collective-permute-start | bytes 319496 | tf_op jit(solution)/shard_map/ppermute | solution.py:729
  21.6 8.2 %collective-permute-start.10 = (f32[3,48,128]{2,1,0:T(8,128)S(1)}, f32[3,48,128]{2,1,0:T(8,128)S(1)}, u32[]{:S(2)}, u32[]{:S(2)}) collective-permute-start(f32[3,48,128]{2,1,0:T(8,128)S(1)} %get-tuple-element.42.refs_1_), channel_id=1, source_target_pairs={{0,2},{1,3},{2,0},{3,1},{4,6},{5,7},{6,4},{7,5},{8,10},{9,11},{10,... | collective-permute-start | bytes 221192 | tf_op jit(solution)/shard_map/ppermute | solution.py:729
  22.6 7.2 %collective-permute-start.11 = (f32[48,128]{1,0:T(8,128)S(1)}, f32[48,128]{1,0:T(8,128)S(1)}, u32[]{:S(2)}, u32[]{:S(2)}) collective-permute-start(f32[48,128]{1,0:T(8,128)S(1)} %get-tuple-element.44), channel_id=1, source_target_pairs={{0,1},{1,0},{2,3},{3,2},{4,5},{5,4},{6,7},{7,6},{8,9},{9,8},{10,11... | collective-permute-start | bytes 73736 | tf_op jit(solution)/shard_map/ppermute | solution.py:729
  22.7 7.1 %collective-permute-start.12 = (f32[48,128]{1,0:T(8,128)S(1)}, f32[48,128]{1,0:T(8,128)S(1)}, u32[]{:S(2)}, u32[]{:S(2)}) collective-permute-start(f32[48,128]{1,0:T(8,128)S(1)} %get-tuple-element.45), channel_id=1, source_target_pairs={{0,3},{1,2},{2,1},{3,0},{4,7},{5,6},{6,5},{7,4},{8,11},{9,10},{10,... | collective-permute-start | bytes 73736 | tf_op jit(solution)/shard_map/ppermute | solution.py:729
  29.9 3.4 %collective-permute-start.14 = (f32[4,48,128]{2,1,0:T(8,128)S(1)}, f32[4,48,128]{2,1,0:T(8,128)S(1)}, u32[]{:S(2)}, u32[]{:S(2)}) collective-permute-start(f32[4,48,128]{2,1,0:T(8,128)S(1)} %get-tuple-element.49), channel_id=1, source_target_pairs={{4,8},{8,4},{5,9},{9,5},{6,10},{10,6},{7,11},{11,7},{20,24},{24,20... | collective-permute-start | bytes 294920 | tf_op jit(solution)/shard_map/ppermute | solution.py:734
  30.6 2.9 %collective-permute-start.13 = (f32[4,48,128]{2,1,0:T(8,128)S(1)}, f32[4,48,128]{2,1,0:T(8,128)S(1)}, u32[]{:S(2)}, u32[]{:S(2)}) collective-permute-start(f32[4,48,128]{2,1,0:T(8,128)S(1)} %get-tuple-element.48), channel_id=1, source_target_pairs={{0,4},{1,5},{2,6},{3,7},{4,0},{5,1},{6,2},{7,3},{8,12},{9,13},{10,... | collective-permute-start | bytes 294920 | tf_op jit(solution)/shard_map/ppermute | solution.py:729
  33.6 5.7 %collective-permute-start.16 = (f32[48,128]{1,0:T(8,128)S(1)}, f32[48,128]{1,0:T(8,128)S(1)}, u32[]{:S(2)}, u32[]{:S(2)}) collective-permute-start(f32[48,128]{1,0:T(8,128)S(1)} %pair_edges.1), channel_id=1, source_target_pairs={{0,3},{1,2},{2,1},{3,0},{4,7},{5,6},{6,5},{7,4},{8,11},{9,10},{10,... | collective-permute-start | bytes 73736 | tf_op jit(solution)/shard_map/ppermute | solution.py:729
  36.7 4.0 %collective-permute-start.15 = (f32[48,128]{1,0:T(8,128)S(1)}, f32[48,128]{1,0:T(8,128)S(1)}, u32[]{:S(2)}, u32[]{:S(2)}) collective-permute-start(f32[48,128]{1,0:T(8,128)S(1)} %pair_edges.1), channel_id=1, source_target_pairs={{0,1},{1,0},{2,3},{3,2},{4,5},{5,4},{6,7},{7,6},{8,9},{9,8},{10,11... | collective-permute-start | bytes 73736 | tf_op jit(solution)/shard_map/ppermute | solution.py:729

commit v11 on v9

--- a/solution.py
+++ b/solution.py
@@ -403,7 +403,7 @@
     )(cot, where)
 
 
-NEAR = ((0, 0), (2, 0), (0, 1), (2, 1))
+NEAR = ((0, 0), (2, 1), (2, 0), (0, 1))
 FAR = ((0, 2), (2, 2), (0, 3), (2, 3))
 
 

time: 42.3 us -> 42.4 us (level)
  starting transfers between devices: 25.2 us -> 24.6 us
  waiting for transfers between devices: 3.81 us -> 4.36 us
    ppermute x15, starting transfers between devices: 23.9 us -> 23.3 us  [exchanged(): return lax.ppermute(values, ('frow', 'fcol'), pairs)]
    ppermute x15, waiting for transfers between devices: 3.81 us -> 4.35 us  [exchanged(): return lax.ppermute(values, ('frow', 'fcol'), pairs)]
  transfers between devices with their start and end apart: 17 -> 17, of which waited for: 3 -> 5; matrix products, arithmetic and copies ran while one was open for 0% -> 0% of each run, Pallas kernels for 27% -> 27%
where the time goes in v11:
time: 42.4 us; the launch traced here: 42.1 us
  starting transfers between devices  24.6 us (58%)
  Pallas kernels  12.9 us (30%)
  waiting for transfers between devices  4.36 us (10%)
    ppermute x15, starting transfers between devices, exchanged(): return lax.ppermute(values, ('frow', 'fcol'), pairs)  23.3 us
    ppermute x15, waiting for transfers between devices, exchanged(): return lax.ppermute(values, ('frow', 'fcol'), pairs)  4.35 us
    pallas_call x4, Pallas kernels, scatter(): pl.pallas_call(functools.partial(scatter_kernel, len(blocks), total is No...  3.08 us
    pallas_call x2, Pallas kernels, pack_chip(): pl.pallas_call(functools.partial(pack_chip_kernel, tiles, tile_rows, colu...  2.65 us
    pallas_call x1, Pallas kernels, tile_fields(): pl.pallas_call(functools.partial(tile_fields_kernel, n_row, pair_at), in_...  1.49 us
    pallas_call x1, Pallas kernels, prepare(): pl.pallas_call(functools.partial(prepare_kernel, order), in_specs=[in_hbm...  1.39 us
    pallas_call x1, Pallas kernels, edge_steps(): pl.pallas_call(functools.partial(edge_steps_kernel, n_row, paired), out_s...  1.39 us
    ppermute x2, starting transfers between devices, exchanged_across(): lax.ppermute(values, 'frow', [(f, (f + 1 ^ 1) - 1) for f in range(1, n_ro...  1.33 us
  transfers between devices with their start and end apart: 17, of which 5 were waited for; matrix products, arithmetic and copies ran while one was open for 0% of the time, Pallas kernels for 27%

profile of v11, /device:TPU:0, one launch (start us, length us, event | category | flops | bytes accessed | tf_op | source)
XLA Modules:
  0.0 42.1 jit_solution(11462969390103278485)
XLA Ops:
  0.0 0.5 %collective-permute-start = (f32[48,2048]{1,0:T(8,128)}, f32[48,2048]{1,0:T(8,128)S(1)}, u32[]{:S(2)}, u32[]{:S(2)}) collective-permute-start(f32[48,2048]{1,0:T(8,128)} %bitcast.6), channel_id=1, source_target_pairs={{0,4},{1,5},{2,6},{3,7},{4,0},{5,1},{6,2},{7,3},{8,12},{9,13},{10,... | collective-permute-start | bytes 1179656 | tf_op jit(solution)/shard_map/ppermute | solution.py:716
  0.5 1.4 %prepare.1 = (f32[544,128]{1,0:T(8,128)S(1)}, f32[480,128]{1,0:T(8,128)S(1)}, f32[4,8,48,128]{3,2,1,0:T(8,128)S(1)}, f32[48,2048]{1,0:T(8,128)S(1)}) custom-call(s32[16,128]{1,0:T(8,128)} %bitcast.8, s32[16,128]{1,0:T(8,128)} %bitcast.9, f32[2,2048]{1,0:T(2,128)} %frac.1, f32[4,384,128]{2,1,0:T(8,128)} %bitcast.5, f32[48,2048]{1,0:T(8,128)} %bitcast.7), custom_call_target="tpu_custom_call" | custom-call | tf_op jit(solution)/shard_map/prepare/pallas_call | solution.py:105
  1.9 0.1 collective-permute-start.1
  2.0 0.7 %collective-permute-start.2 = (f32[480,128]{1,0:T(8,128)S(1)}, f32[480,128]{1,0:T(8,128)S(1)}, u32[]{:S(2)}, u32[]{:S(2)}) collective-permute-start(f32[480,128]{1,0:T(8,128)S(1)} %get-tuple-element.32), channel_id=1, source_target_pairs={{4,8},{8,4},{5,9},{9,5},{6,10},{10,6},{7,11},{11,7},{20,24},{24,20... | collective-permute-start | bytes 737288 | tf_op jit(solution)/shard_map/ppermute | solution.py:721
  2.7 0.8 %collective-permute-done.1.pair_where.pair = f32[544,128]{1,0:T(8,128)S(1)} collective-permute-done((f32[544,128]{1,0:T(8,128)S(1)}, f32[544,128]{1,0:T(8,128)S(1)}, u32[]{:S(2)}, u32[]{:S(2)}) %collective-permute-start.1) | collective-permute-done | bytes 278560 | tf_op jit(solution)/shard_map/ppermute | solution.py:716
  3.5 0.0 collective-permute-done.pair_cot
  3.5 1.3 %pack_chip.2 = (f32[208,128]{1,0:T(8,128)S(1)}, f32[208,128]{1,0:T(8,128)S(1)}, f32[208,128]{1,0:T(8,128)S(1)}, f32[208,128]{1,0:T(8,128)S(1)}) custom-call(f32[48,2048]{1,0:T(8,128)S(1)} %get-tuple-element.30.cot, f32[544,128]{1,0:T(8,128)S(1)} %get-tuple-element.31.where, f32[48,2048]{1,0:T(8,128)S(1)} %collective-permute-done.pair_cot, ...), custom_call_target="tpu_custom_call" | custom-call | tf_op jit(solution)/shard_map/pack_chip/pallas_call | solution.py:434
  4.8 3.4 %collective-permute-start.7 = (f32[208,128]{1,0:T(8,128)S(1)}, f32[208,128]{1,0:T(8,128)S(1)}, u32[]{:S(2)}, u32[]{:S(2)}) collective-permute-start(f32[208,128]{1,0:T(8,128)S(1)} %get-tuple-element.39), channel_id=1, source_target_pairs={{0,8},{1,9},{2,10},{3,11},{4,12},{5,13},{6,14},{7,15},{8,0},{9,1},... | collective-permute-start | bytes 319496 | tf_op jit(solution)/shard_map/ppermute | solution.py:716
  8.3 1.7 %collective-permute-start.8 = (f32[208,128]{1,0:T(8,128)S(1)}, f32[208,128]{1,0:T(8,128)S(1)}, u32[]{:S(2)}, u32[]{:S(2)}) collective-permute-start(f32[208,128]{1,0:T(8,128)S(1)} %get-tuple-element.40), channel_id=1, source_target_pairs={{0,1},{1,0},{2,3},{3,2},{4,5},{5,4},{6,7},{7,6},{8,9},{9,8},{10,11... | collective-permute-start | bytes 319496 | tf_op jit(solution)/shard_map/ppermute | solution.py:716
  10.0 0.0 collective-permute-start.6
  10.0 0.0 collective-permute-done.2.refs_0_.cross
  10.0 1.3 %pack_chip.3 = (f32[208,128]{1,0:T(8,128)S(1)}, f32[208,128]{1,0:T(8,128)S(1)}, f32[208,128]{1,0:T(8,128)S(1)}, f32[208,128]{1,0:T(8,128)S(1)}) custom-call(f32[48,2048]{1,0:T(8,128)S(1)} %get-tuple-element.30.cot, f32[544,128]{1,0:T(8,128)S(1)} %get-tuple-element.31.where, f32[48,2048]{1,0:T(8,128)S(1)} %collective-permute-done.pair_cot, ...), custom_call_target="tpu_custom_call" | custom-call | tf_op jit(solution)/shard_map/pack_chip/pallas_call | solution.py:434
  11.3 3.9 %collective-permute-start.4 = (f32[208,128]{1,0:T(8,128)S(1)}, f32[208,128]{1,0:T(8,128)S(1)}, u32[]{:S(2)}, u32[]{:S(2)}) collective-permute-start(f32[208,128]{1,0:T(8,128)S(1)} %get-tuple-element.36), channel_id=1, source_target_pairs={{0,9},{1,8},{2,11},{3,10},{4,13},{5,12},{6,15},{7,14},{8,1},{9,0},... | collective-permute-start | bytes 319496 | tf_op jit(solution)/shard_map/ppermute | solution.py:716
  15.2 0.0 collective-permute-start.5
  15.2 0.0 collective-permute-done.7.refs_1_
  15.2 0.0 collective-permute-done.8.refs_2_
  15.2 1.1 %scatter_points.6.refs_1_ = f32[8,48,128]{2,1,0:T(8,128)S(1)} custom-call(f32[208,128]{1,0:T(8,128)S(1)} %get-tuple-element.33.refs_1_.refs_0_, f32[208,128]{1,0:T(8,128)S(1)} %collective-permute-done.7.refs_1_, f32[208,128]{1,0:T(8,128)S(1)} %collective-permute-done.8.refs_2_, f32[208,128]{1,0:T(8,128)S(1)} %get-tuple-element.35.refs_0_.refs_3_), custom_call_target="tpu_custom_call" | custom-call | tf_op jit(solution)/shard_map/scatter_points/pallas_call | solution.py:501
  16.3 0.0 collective-permute-done.6.refs_0_
  16.3 0.5 %scatter_points.7 = (f32[5,48,128]{2,1,0:T(8,128)S(1)}, f32[3,48,128]{2,1,0:T(8,128)S(1)}) custom-call(f32[208,128]{1,0:T(8,128)S(1)} %collective-permute-done.6.refs_0_, f32[8,48,128]{2,1,0:T(8,128)S(1)} %scatter_points.6.refs_1_), custom_call_target="tpu_custom_call" | custom-call | tf_op jit(solution)/shard_map/scatter_points/pallas_call | solution.py:501
  16.8 2.7 %collective-permute-start.9 = (f32[5,48,128]{2,1,0:T(8,128)S(1)}, f32[5,48,128]{2,1,0:T(8,128)S(1)}, u32[]{:S(2)}, u32[]{:S(2)}) collective-permute-start(f32[5,48,128]{2,1,0:T(8,128)S(1)} %get-tuple-element.41.refs_0_), channel_id=1, source_target_pairs={{0,2},{1,3},{2,0},{3,1},{4,6},{5,7},{6,4},{7,5},{8,10},{9,11},{10,... | collective-permute-start | bytes 368648 | tf_op jit(solution)/shard_map/ppermute | solution.py:716
  19.4 1.0 %collective-permute-start.3 = (f32[208,128]{1,0:T(8,128)S(1)}, f32[208,128]{1,0:T(8,128)S(1)}, u32[]{:S(2)}, u32[]{:S(2)}) collective-permute-start(f32[208,128]{1,0:T(8,128)S(1)} %get-tuple-element.34), channel_id=1, source_target_pairs={{0,1},{1,0},{2,3},{3,2},{4,5},{5,4},{6,7},{7,6},{8,9},{9,8},{10,11... | collective-permute-start | bytes 319496 | tf_op jit(solution)/shard_map/ppermute | solution.py:716
  20.4 0.1 collective-permute-start.10
  20.5 0.6 %state_edges.1 = (f32[48,128]{1,0:T(8,128)S(1)}, f32[48,128]{1,0:T(8,128)S(1)}) custom-call(f32[4,8,48,128]{3,2,1,0:T(8,128)S(1)} %get-tuple-element.43.turned, f32[544,128]{1,0:T(8,128)S(1)} %collective-permute-done.1.pair_where.pair, f32[480,128]{1,0:T(8,128)S(1)} %collective-permute-done.2.refs_0_.cross, f32[5,48,128]{2,1,0:T(8,128)S(1)} %get-tuple-element.41.refs_0_, ...), custom_call_target="tpu_custom_call" | custom-call | tf_op jit(solution)/shard_map/state_edges/pallas_call | solution.py:173
  21.2 0.0 collective-permute-done.4.refs_1_
  21.2 1.3 %collective-permute-start.11 = (f32[48,128]{1,0:T(8,128)S(1)}, f32[48,128]{1,0:T(8,128)S(1)}, u32[]{:S(2)}, u32[]{:S(2)}) collective-permute-start(f32[48,128]{1,0:T(8,128)S(1)} %get-tuple-element.44), channel_id=1, source_target_pairs={{0,1},{1,0},{2,3},{3,2},{4,5},{5,4},{6,7},{7,6},{8,9},{9,8},{10,11... | collective-permute-start | bytes 73736 | tf_op jit(solution)/shard_map/ppermute | solution.py:716
  22.5 0.0 collective-permute-done.5.refs_2_
  22.5 3.0 %collective-permute-start.12 = (f32[48,128]{1,0:T(8,128)S(1)}, f32[48,128]{1,0:T(8,128)S(1)}, u32[]{:S(2)}, u32[]{:S(2)}) collective-permute-start(f32[48,128]{1,0:T(8,128)S(1)} %get-tuple-element.45), channel_id=1, source_target_pairs={{0,3},{1,2},{2,1},{3,0},{4,7},{5,6},{6,5},{7,4},{8,11},{9,10},{10,... | collective-permute-start | bytes 73736 | tf_op jit(solution)/shard_map/ppermute | solution.py:716
  25.5 1.1 %scatter_points.4.refs_1_ = f32[8,48,128]{2,1,0:T(8,128)S(1)} custom-call(f32[208,128]{1,0:T(8,128)S(1)} %get-tuple-element.35.refs_0_.refs_3_, f32[208,128]{1,0:T(8,128)S(1)} %collective-permute-done.4.refs_1_, f32[208,128]{1,0:T(8,128)S(1)} %collective-permute-done.5.refs_2_), custom_call_target="tpu_custom_call" | custom-call | tf_op jit(solution)/shard_map/scatter_points/pallas_call | solution.py:501
  26.6 0.0 collective-permute-done.3.refs_0_
  26.6 0.5 %scatter_points.5.refs_0_.total = f32[8,48,128]{2,1,0:T(8,128)S(1)} custom-call(f32[208,128]{1,0:T(8,128)S(1)} %collective-permute-done.3.refs_0_, f32[8,48,128]{2,1,0:T(8,128)S(1)} %scatter_points.4.refs_1_), custom_call_target="tpu_custom_call" | custom-call | tf_op jit(solution)/shard_map/scatter_points/pallas_call | solution.py:501
  27.1 1.5 %tile_fields.1 = (f32[4,16,112,128]{3,2,1,0:T(8,128)S(1)}, f32[16,128]{1,0:T(8,128)S(1)}, f32[8,128]{1,0:T(8,128)S(1)}, f32[4,16,24,128]{3,2,1,0:T(8,128)S(1)}) custom-call(f32[4,8,48,128]{3,2,1,0:T(8,128)S(1)} %get-tuple-element.43.turned, f32[544,128]{1,0:T(8,128)S(1)} %collective-permute-done.1.pair_where.pair, ...), custom_call_target="tpu_custom_call" | custom-call | tf_op jit(solution)/shard_map/tile_fields/pallas_call | solution.py:266
  28.6 0.0 collective-permute-done.11.refs_2_.one
  28.6 0.4 %collective-permute-done.12.refs_3_.other = f32[48,128]{1,0:T(8,128)S(1)} collective-permute-done((f32[48,128]{1,0:T(8,128)S(1)}, f32[48,128]{1,0:T(8,128)S(1)}, u32[]{:S(2)}, u32[]{:S(2)}) %collective-permute-start.12) | collective-permute-done | bytes 24608 | tf_op jit(solution)/shard_map/ppermute | solution.py:716
  29.0 0.3 collective-permute-done.10.refs_1_
  29.3 0.0 collective-permute-done.9.refs_0_
  29.4 0.7 %collective-permute-start.14 = (f32[4,48,128]{2,1,0:T(8,128)S(1)}, f32[4,48,128]{2,1,0:T(8,128)S(1)}, u32[]{:S(2)}, u32[]{:S(2)}) collective-permute-start(f32[4,48,128]{2,1,0:T(8,128)S(1)} %get-tuple-element.49), channel_id=1, source_target_pairs={{4,8},{8,4},{5,9},{9,5},{6,10},{10,6},{7,11},{11,7},{20,24},{24,20... | collective-permute-start | bytes 294920 | tf_op jit(solution)/shard_map/ppermute | solution.py:721
  30.1 2.9 %collective-permute-start.13 = (f32[4,48,128]{2,1,0:T(8,128)S(1)}, f32[4,48,128]{2,1,0:T(8,128)S(1)}, u32[]{:S(2)}, u32[]{:S(2)}) collective-permute-start(f32[4,48,128]{2,1,0:T(8,128)S(1)} %get-tuple-element.48), channel_id=1, source_target_pairs={{0,4},{1,5},{2,6},{3,7},{4,0},{5,1},{6,2},{7,3},{8,12},{9,13},{10,... | collective-permute-start | bytes 294920 | tf_op jit(solution)/shard_map/ppermute | solution.py:716
  33.0 0.9 %edge_fields.1.refs_0_.wide = f32[4,16,56,128]{3,2,1,0:T(8,128)S(1)} custom-call(f32[4,16,24,128]{3,2,1,0:T(8,128)S(1)} %get-tuple-element.52.own, f32[48,128]{1,0:T(8,128)S(1)} %collective-permute-done.11.refs_2_.one, f32[48,128]{1,0:T(8,128)S(1)} %collective-permute-done.12.refs_3_.other), custom_call_target="tpu_custom_call" | custom-call | tf_op jit(solution)/shard_map/edge_fields/pallas_call | solution.py:311
  33.8 0.0 collective-permute-done.14.cross
  33.9 0.2 cross_edges.1.partial
  34.0 0.0 collective-permute-done.13.pair
  34.0 0.1 pair_edges.1
  34.2 2.7 %collective-permute-start.16 = (f32[48,128]{1,0:T(8,128)S(1)}, f32[48,128]{1,0:T(8,128)S(1)}, u32[]{:S(2)}, u32[]{:S(2)}) collective-permute-start(f32[48,128]{1,0:T(8,128)S(1)} %pair_edges.1), channel_id=1, source_target_pairs={{0,3},{1,2},{2,1},{3,0},{4,7},{5,6},{6,5},{7,4},{8,11},{9,10},{10,... | collective-permute-start | bytes 73736 | tf_op jit(solution)/shard_map/ppermute | solution.py:716
  36.9 0.0 collective-permute-start.15
  36.9 1.1 %tile_steps.1 = (f32[8,48,128]{2,1,0:T(8,128)S(1)}, f32[16,24,128]{2,1,0:T(8,128)S(1)}) custom-call(f32[8,48,128]{2,1,0:T(8,128)S(1)} %get-tuple-element.47.canvas, f32[4,48,128]{2,1,0:T(8,128)S(1)} %collective-permute-done.13.pair, f32[4,48,128]{2,1,0:T(8,128)S(1)} %collective-permute-done.14.cross, f32[4,16,112,128]{3,2,1,0:T(8,128)S(1)} %get-tuple-element.50.wide, ...), custom_call_target="tpu_custom_call" | custom-call | tf_op jit(solution)/shard_map/tile_steps/pallas_call | solution.py:659
  37.9 2.0 %collective-permute-done.16.other = f32[48,128]{1,0:T(8,128)S(1)} collective-permute-done((f32[48,128]{1,0:T(8,128)S(1)}, f32[48,128]{1,0:T(8,128)S(1)}, u32[]{:S(2)}, u32[]{:S(2)}) %collective-permute-start.16) | collective-permute-done | bytes 24608 | tf_op jit(solution)/shard_map/ppermute | solution.py:716
  40.0 0.7 %collective-permute-done.15.one = f32[48,128]{1,0:T(8,128)S(1)} collective-permute-done((f32[48,128]{1,0:T(8,128)S(1)}, f32[48,128]{1,0:T(8,128)S(1)}, u32[]{:S(2)}, u32[]{:S(2)}) %collective-permute-start.15) | collective-permute-done | bytes 24608 | tf_op jit(solution)/shard_map/ppermute | solution.py:716
  40.7 1.4 %edge_steps.1 = f32[384,128]{1,0:T(8,128)} custom-call(f32[16,24,128]{2,1,0:T(8,128)S(1)} %get-tuple-element.51.windows, f32[48,128]{1,0:T(8,128)S(1)} %collective-permute-done.15.one, f32[48,128]{1,0:T(8,128)S(1)} %collective-permute-done.16.other, f32[4,16,56,128]{3,2,1,0:T(8,128)S(1)} %edge_fields.1.refs_0_.wide, f32[8,128]{1,0:T(8,128)S(1)} %get-tuple-element.53.gravity, ...), custom_call_target="tpu_custom_call" | custom-call | tf_op jit(solution)/shard_map/edge_steps/pallas_call | solution.py:698
  (3 shorter events, 0.0 us)
Async XLA Ops:
  0.0 3.5 %collective-permute-start = (f32[48,2048]{1,0:T(8,128)}, f32[48,2048]{1,0:T(8,128)S(1)}, u32[]{:S(2)}, u32[]{:S(2)}) collective-permute-start(f32[48,2048]{1,0:T(8,128)} %bitcast.6), channel_id=1, source_target_pairs={{0,4},{1,5},{2,6},{3,7},{4,0},{5,1},{6,2},{7,3},{8,12},{9,13},{10,... | collective-permute-start | bytes 1179656 | tf_op jit(solution)/shard_map/ppermute | solution.py:716
  0.5 26.6 %copy-start = (f32[16]{0:T(128)S(1)}, f32[16]{0:T(128)}, u32[]{:S(2)}) copy-start(f32[16]{0:T(128)} %gravity.1) | copy-start | bytes 196
  1.9 1.6 %collective-permute-start.1 = (f32[544,128]{1,0:T(8,128)S(1)}, f32[544,128]{1,0:T(8,128)S(1)}, u32[]{:S(2)}, u32[]{:S(2)}) collective-permute-start(f32[544,128]{1,0:T(8,128)S(1)} %get-tuple-element.31.where), channel_id=1, source_target_pairs={{0,4},{1,5},{2,6},{3,7},{4,0},{5,1},{6,2},{7,3},{8,12},{9,13},{10,... | collective-permute-start | bytes 835592 | tf_op jit(solution)/shard_map/ppermute | solution.py:716
  2.0 8.0 %collective-permute-start.2 = (f32[480,128]{1,0:T(8,128)S(1)}, f32[480,128]{1,0:T(8,128)S(1)}, u32[]{:S(2)}, u32[]{:S(2)}) collective-permute-start(f32[480,128]{1,0:T(8,128)S(1)} %get-tuple-element.32), channel_id=1, source_target_pairs={{4,8},{8,4},{5,9},{9,5},{6,10},{10,6},{7,11},{11,7},{20,24},{24,20... | collective-permute-start | bytes 737288 | tf_op jit(solution)/shard_map/ppermute | solution.py:721
  4.8 10.4 %collective-permute-start.7 = (f32[208,128]{1,0:T(8,128)S(1)}, f32[208,128]{1,0:T(8,128)S(1)}, u32[]{:S(2)}, u32[]{:S(2)}) collective-permute-start(f32[208,128]{1,0:T(8,128)S(1)} %get-tuple-element.39), channel_id=1, source_target_pairs={{0,8},{1,9},{2,10},{3,11},{4,12},{5,13},{6,14},{7,15},{8,0},{9,1},... | collective-permute-start | bytes 319496 | tf_op jit(solution)/shard_map/ppermute | solution.py:716
  8.3 7.0 %collective-permute-start.8 = (f32[208,128]{1,0:T(8,128)S(1)}, f32[208,128]{1,0:T(8,128)S(1)}, u32[]{:S(2)}, u32[]{:S(2)}) collective-permute-start(f32[208,128]{1,0:T(8,128)S(1)} %get-tuple-element.40), channel_id=1, source_target_pairs={{0,1},{1,0},{2,3},{3,2},{4,5},{5,4},{6,7},{7,6},{8,9},{9,8},{10,11... | collective-permute-start | bytes 319496 | tf_op jit(solution)/shard_map/ppermute | solution.py:716
  10.0 6.3 %collective-permute-start.6 = (f32[208,128]{1,0:T(8,128)S(1)}, f32[208,128]{1,0:T(8,128)S(1)}, u32[]{:S(2)}, u32[]{:S(2)}) collective-permute-start(f32[208,128]{1,0:T(8,128)S(1)} %get-tuple-element.38), channel_id=1, source_target_pairs={{0,9},{1,8},{2,11},{3,10},{4,13},{5,12},{6,15},{7,14},{8,1},{9,0},... | collective-permute-start | bytes 319496 | tf_op jit(solution)/shard_map/ppermute | solution.py:716
  11.3 9.9 %collective-permute-start.4 = (f32[208,128]{1,0:T(8,128)S(1)}, f32[208,128]{1,0:T(8,128)S(1)}, u32[]{:S(2)}, u32[]{:S(2)}) collective-permute-start(f32[208,128]{1,0:T(8,128)S(1)} %get-tuple-element.36), channel_id=1, source_target_pairs={{0,9},{1,8},{2,11},{3,10},{4,13},{5,12},{6,15},{7,14},{8,1},{9,0},... | collective-permute-start | bytes 319496 | tf_op jit(solution)/shard_map/ppermute | solution.py:716
  15.2 7.3 %collective-permute-start.5 = (f32[208,128]{1,0:T(8,128)S(1)}, f32[208,128]{1,0:T(8,128)S(1)}, u32[]{:S(2)}, u32[]{:S(2)}) collective-permute-start(f32[208,128]{1,0:T(8,128)S(1)} %get-tuple-element.37), channel_id=1, source_target_pairs={{0,8},{1,9},{2,10},{3,11},{4,12},{5,13},{6,14},{7,15},{8,0},{9,1},... | collective-permute-start | bytes 319496 | tf_op jit(solution)/shard_map/ppermute | solution.py:716
  16.8 12.6 %collective-permute-start.9 = (f32[5,48,128]{2,1,0:T(8,128)S(1)}, f32[5,48,128]{2,1,0:T(8,128)S(1)}, u32[]{:S(2)}, u32[]{:S(2)}) collective-permute-start(f32[5,48,128]{2,1,0:T(8,128)S(1)} %get-tuple-element.41.refs_0_), channel_id=1, source_target_pairs={{0,2},{1,3},{2,0},{3,1},{4,6},{5,7},{6,4},{7,5},{8,10},{9,11},{10,... | collective-permute-start | bytes 368648 | tf_op jit(solution)/shard_map/ppermute | solution.py:716
  19.4 7.1 %collective-permute-start.3 = (f32[208,128]{1,0:T(8,128)S(1)}, f32[208,128]{1,0:T(8,128)S(1)}, u32[]{:S(2)}, u32[]{:S(2)}) collective-permute-start(f32[208,128]{1,0:T(8,128)S(1)} %get-tuple-element.34), channel_id=1, source_target_pairs={{0,1},{1,0},{2,3},{3,2},{4,5},{5,4},{6,7},{7,6},{8,9},{9,8},{10,11... | collective-permute-start | bytes 319496 | tf_op jit(solution)/shard_map/ppermute | solution.py:716
  20.4 8.9 %collective-permute-start.10 = (f32[3,48,128]{2,1,0:T(8,128)S(1)}, f32[3,48,128]{2,1,0:T(8,128)S(1)}, u32[]{:S(2)}, u32[]{:S(2)}) collective-permute-start(f32[3,48,128]{2,1,0:T(8,128)S(1)} %get-tuple-element.42.refs_1_), channel_id=1, source_target_pairs={{0,2},{1,3},{2,0},{3,1},{4,6},{5,7},{6,4},{7,5},{8,10},{9,11},{10,... | collective-permute-start | bytes 221192 | tf_op jit(solution)/shard_map/ppermute | solution.py:716
  21.2 7.4 %collective-permute-start.11 = (f32[48,128]{1,0:T(8,128)S(1)}, f32[48,128]{1,0:T(8,128)S(1)}, u32[]{:S(2)}, u32[]{:S(2)}) collective-permute-start(f32[48,128]{1,0:T(8,128)S(1)} %get-tuple-element.44), channel_id=1, source_target_pairs={{0,1},{1,0},{2,3},{3,2},{4,5},{5,4},{6,7},{7,6},{8,9},{9,8},{10,11... | collective-permute-start | bytes 73736 | tf_op jit(solution)/shard_map/ppermute | solution.py:716
  22.5 6.5 %collective-permute-start.12 = (f32[48,128]{1,0:T(8,128)S(1)}, f32[48,128]{1,0:T(8,128)S(1)}, u32[]{:S(2)}, u32[]{:S(2)}) collective-permute-start(f32[48,128]{1,0:T(8,128)S(1)} %get-tuple-element.45), channel_id=1, source_target_pairs={{0,3},{1,2},{2,1},{3,0},{4,7},{5,6},{6,5},{7,4},{8,11},{9,10},{10,... | collective-permute-start | bytes 73736 | tf_op jit(solution)/shard_map/ppermute | solution.py:716
  29.4 4.5 %collective-permute-start.14 = (f32[4,48,128]{2,1,0:T(8,128)S(1)}, f32[4,48,128]{2,1,0:T(8,128)S(1)}, u32[]{:S(2)}, u32[]{:S(2)}) collective-permute-start(f32[4,48,128]{2,1,0:T(8,128)S(1)} %get-tuple-element.49), channel_id=1, source_target_pairs={{4,8},{8,4},{5,9},{9,5},{6,10},{10,6},{7,11},{11,7},{20,24},{24,20... | collective-permute-start | bytes 294920 | tf_op jit(solution)/shard_map/ppermute | solution.py:721
  30.1 4.0 %collective-permute-start.13 = (f32[4,48,128]{2,1,0:T(8,128)S(1)}, f32[4,48,128]{2,1,0:T(8,128)S(1)}, u32[]{:S(2)}, u32[]{:S(2)}) collective-permute-start(f32[4,48,128]{2,1,0:T(8,128)S(1)} %get-tuple-element.48), channel_id=1, source_target_pairs={{0,4},{1,5},{2,6},{3,7},{4,0},{5,1},{6,2},{7,3},{8,12},{9,13},{10,... | collective-permute-start | bytes 294920 | tf_op jit(solution)/shard_map/ppermute | solution.py:716
  34.2 5.8 %collective-permute-start.16 = (f32[48,128]{1,0:T(8,128)S(1)}, f32[48,128]{1,0:T(8,128)S(1)}, u32[]{:S(2)}, u32[]{:S(2)}) collective-permute-start(f32[48,128]{1,0:T(8,128)S(1)} %pair_edges.1), channel_id=1, source_target_pairs={{0,3},{1,2},{2,1},{3,0},{4,7},{5,6},{6,5},{7,4},{8,11},{9,10},{10,... | collective-permute-start | bytes 73736 | tf_op jit(solution)/shard_map/ppermute | solution.py:716
  36.9 3.8 %collective-permute-start.15 = (f32[48,128]{1,0:T(8,128)S(1)}, f32[48,128]{1,0:T(8,128)S(1)}, u32[]{:S(2)}, u32[]{:S(2)}) collective-permute-start(f32[48,128]{1,0:T(8,128)S(1)} %pair_edges.1), channel_id=1, source_target_pairs={{0,1},{1,0},{2,3},{3,2},{4,5},{5,4},{6,7},{7,6},{8,9},{9,8},{10,11... | collective-permute-start | bytes 73736 | tf_op jit(solution)/shard_map/ppermute | solution.py:716
